TPU v7x, 256 devices: a whole 4x4x8 slice. The times are simulated.
256 devices in a mesh: replica: 16 (over x_lo, y, core), shard: 16 (over x_hi, z).
Axes of the slice: x: 4 (x_hi: 2, x_lo: 2; x = x_hi * 2 + x_lo), y: 4, z: 8, core: 2. Of those that a mesh axis runs over, the one named last changes fastest.
Arguments:
- hidden: bfloat16 [4, 512, 5120], P(None, 'replica', 'shard'), may hold values from -6 to 6
- norm_gain: float32 [5120], replicated, may hold values from 0.1 to 1.9
- query_gain: float32 [128], replicated, may hold values from 0.1 to 1.9
- key_gain: float32 [128], replicated, may hold values from 0.1 to 1.9
- base_query: bfloat16 [5120, 4096], P(None, 'shard'), may hold values from -0.078125 to 0.078125
- base_key: bfloat16 [5120, 2048], P(None, 'shard'), may hold values from -0.078125 to 0.078125
- base_value: bfloat16 [5120, 2048], P(None, 'shard'), may hold values from -0.078125 to 0.078125
- base_output: bfloat16 [5120, 4096], P(None, 'shard'), may hold values from -0.09375 to 0.09375
- delta_query: bfloat16 [5120, 4096], P(('replica', 'shard')), may hold values from -4 to 4
- scale_query: int32 [5120, 32], P(('replica', 'shard')), may hold values from 6 to 9
- key_delta_codes: bfloat16 [5120, 1024], P(('replica', 'shard')), may hold values from -4 to 4
- key_scale_codes: int32 [5120, 8], P(('replica', 'shard')), may hold values from 6 to 9
- value_delta_codes: bfloat16 [5120, 1024], P(('replica', 'shard')), may hold values from -4 to 4
- value_scale_codes: int32 [5120, 8], P(('replica', 'shard')), may hold values from 6 to 9
- delta_output: bfloat16 [5120, 4096], P(('replica', 'shard')), may hold values from -4 to 4
- scale_output: int32 [5120, 32], P(('replica', 'shard')), may hold values from 6 to 9
- cache_keys: bfloat16 [512, 64, 2048], P('replica', None, 'shard')
- cache_values: bfloat16 [512, 64, 2048], P('replica', None, 'shard'), may hold values from -6 to 6
- lengths: int32 [512], P('replica'), may hold values from 1 to 64, as said below
- stale_rows: int32 [16, 128], P('replica'), may hold values from 0 to 31
- stale_steps: int32 [16, 128], P('replica'), may hold values from 0 to 3
- stale_back: int32 [16, 128], P('replica'), may hold values from 0 to 67
Outputs:
- attention_out: bfloat16 [4, 512, 5120], P(None, 'replica', 'shard')
- log_ratio: float32 [16, 128], P('replica')
Inputs may be any that keep to these rules, and one draw needn't show every extreme that they name: `lengths`: the first row of each engine's 32 rows has 64.
All inputs are finite; a program needn't handle non-finite values.
Results may differ from a plain program's by a relative error of at most 0.02.
The roundings to bfloat16 on the way count: a program that leaves them out, or rounds other values in their place, can miss the bound.
Values may be sent and summed in bfloat16 or wider, within the bound.
No kernel may reach another device: no remote copies, remote signals or barrier semaphores. Data moves between devices by JAX's collectives and lax.ppermute only.
A program may use at most 128 MiB of HBM per device.

v0:
```python
import jax
import jax.numpy as jnp
from jax import lax
from jax.sharding import PartitionSpec as P

HQ = 32
KEY_VALUE_HEADS = 8
HEAD_SIZE = 128


EPSILON = 1e-06
THETA = 1000000.0


def rms_scale(value, gain):
    return value * lax.rsqrt(jnp.mean(value * value, axis=-1, keepdims=True) + EPSILON) * gain


def rotate(value, position):
    half = value.shape[-1] // 2
    freq = THETA ** (-(jnp.arange(half).astype(jnp.float32) * 2.0) / value.shape[-1])
    angle = position.astype(jnp.float32)[..., None, None] * freq
    cosine = jnp.cos(angle)
    sine = jnp.sin(angle)
    first = value[..., :half]
    second = value[..., half:]
    return jnp.concatenate(
        [first * cosine - second * sine, second * cosine + first * sine], axis=-1
    )


def dequantize(codes, exponents):
    rows_here, width = codes.shape
    heads = exponents.shape[1]
    factor = 1.0 / jnp.left_shift(jnp.ones_like(exponents), exponents).astype(jnp.float32)
    scaled = (
        codes.astype(jnp.float32).reshape(rows_here, heads, width // heads) * factor[:, :, None]
    )
    return scaled.reshape(rows_here, width).astype(jnp.bfloat16)


def expand_slots(values, repeat_count):
    rows_here, width = values.shape
    heads = width // HEAD_SIZE
    spread = jnp.broadcast_to(
        values.reshape(rows_here, heads, 1, HEAD_SIZE), (rows_here, heads, repeat_count, HEAD_SIZE)
    )
    return spread.reshape(rows_here, heads * repeat_count * HEAD_SIZE)


def refresh(base, delta):
    return (base.astype(jnp.float32) + delta.astype(jnp.float32)).astype(jnp.bfloat16)


def reorder(item, groups, blocks):
    rows_here = item.shape[0] // (groups * blocks)
    shaped = item.reshape(groups, blocks, rows_here, item.shape[1])
    return shaped.transpose(1, 0, 2, 3).reshape(groups * blocks * rows_here, item.shape[1])


def project(normed, weight, gain, position):
    lead = normed.shape[:-1]
    raw = jnp.dot(normed.reshape(-1, normed.shape[-1]), weight, preferred_element_type=jnp.float32)
    raw = raw.reshape(lead + (weight.shape[1] // HEAD_SIZE, HEAD_SIZE))
    return rotate(rms_scale(raw, gain), position).astype(jnp.bfloat16)


def log_scores(query, cache_k, fresh_k, lens, steps):
    a_len, r_len, heads, width = query.shape
    slots = cache_k.shape[2]
    grouped = query.reshape(a_len, r_len, slots, heads // slots, width)
    past = jnp.einsum("arkgd,rckd->arkgc", grouped, cache_k, preferred_element_type=jnp.float32)
    fresh = jnp.einsum("arkgd,urkd->arkgu", grouped, fresh_k, preferred_element_type=jnp.float32)
    scores = jnp.concatenate([past, fresh], axis=-1) * width ** (-0.5)
    past_ok = jnp.arange(cache_k.shape[1])[None, :] < lens[:, None]
    past_ok = jnp.broadcast_to(past_ok[None, :, None, None, :], past.shape)
    fresh_ok = jnp.arange(fresh_k.shape[0])[None, None, :] <= steps[:, :, None]
    fresh_ok = jnp.broadcast_to(fresh_ok[:, :, None, None, :], fresh.shape)
    allowed = jnp.concatenate([past_ok, fresh_ok], axis=-1)
    scores = jnp.where(allowed, scores, -jnp.inf)
    shifted = scores - jnp.max(scores, axis=-1, keepdims=True)
    total = jnp.sum(jnp.exp(shifted), axis=-1, keepdims=True)
    logp = shifted - jnp.log(total)
    probs = (jnp.exp(shifted) / total).astype(jnp.bfloat16)
    return (logp.reshape(a_len, r_len, heads, -1), probs)


def combine(probs, cache_v, fresh_v):
    a_len, r_len, slots, group, positions = probs.shape
    ctx_len = cache_v.shape[1]
    past = jnp.einsum(
        "arkgc,rckd->arkgd", probs[..., :ctx_len], cache_v, preferred_element_type=jnp.float32
    )
    fresh = jnp.einsum(
        "arkgu,urkd->arkgd", probs[..., ctx_len:], fresh_v, preferred_element_type=jnp.float32
    )
    return (past + fresh).astype(jnp.bfloat16).reshape(a_len, r_len, slots * group * HEAD_SIZE)


def pick(logp, index):
    return jnp.take_along_axis(logp, index[:, None, None], axis=2)[:, :, 0]


def local(
    hidden,
    norm_gain,
    query_gain,
    key_gain,
    base_query,
    base_key,
    base_value,
    base_output,
    delta_query,
    scale_query,
    key_delta_codes,
    key_scale_codes,
    value_delta_codes,
    value_scale_codes,
    delta_output,
    scale_output,
    cache_keys,
    cache_values,
    lengths,
    stale_rows,
    stale_steps,
    stale_back,
):
    repeat_count = max(KEY_VALUE_HEADS, lax.axis_size("shard")) // KEY_VALUE_HEADS
    narrow = (
        dequantize(delta_query, scale_query),
        dequantize(key_delta_codes, key_scale_codes),
        dequantize(value_delta_codes, value_scale_codes),
        dequantize(delta_output, scale_output),
    )
    collected = (
        lax.all_gather(narrow[0], "replica", axis=0, tiled=True),
        lax.all_gather(narrow[1], "replica", axis=0, tiled=True),
        lax.all_gather(narrow[2], "replica", axis=0, tiled=True),
        lax.all_gather(narrow[3], "replica", axis=0, tiled=True),
    )
    widened = (
        collected[0],
        expand_slots(collected[1], repeat_count),
        expand_slots(collected[2], repeat_count),
        collected[3],
    )
    moved = (
        lax.all_to_all(widened[0], "shard", split_axis=1, concat_axis=0, tiled=True),
        lax.all_to_all(widened[1], "shard", split_axis=1, concat_axis=0, tiled=True),
        lax.all_to_all(widened[2], "shard", split_axis=1, concat_axis=0, tiled=True),
        lax.all_to_all(widened[3], "shard", split_axis=1, concat_axis=0, tiled=True),
    )
    groups = lax.axis_size("shard")
    blocks = lax.axis_size("replica")
    ordered = tuple((reorder(item, groups, blocks) for item in moved))
    new_query = refresh(base_query, ordered[0])
    new_key = refresh(base_key, ordered[1])
    new_value = refresh(base_value, ordered[2])
    new_output = refresh(base_output, ordered[3])
    whole = lax.all_gather(hidden, "shard", axis=2, tiled=True)
    normed = rms_scale(whole.astype(jnp.float32), norm_gain).astype(jnp.bfloat16)
    steps_count, rows_count, width = normed.shape
    ctx_len = cache_keys.shape[1]
    step_ids = jnp.arange(steps_count)
    positions = lengths[None, :] + step_ids[:, None]
    query = project(normed, new_query, query_gain, positions)
    fresh_k = project(normed, new_key, key_gain, positions)
    fresh_v = jnp.dot(normed.reshape(-1, width), new_value, preferred_element_type=jnp.float32)
    fresh_v = fresh_v.reshape(steps_count, rows_count, -1, HEAD_SIZE).astype(jnp.bfloat16)
    cache_k = cache_keys.reshape(rows_count, ctx_len, -1, HEAD_SIZE)
    cache_v = cache_values.reshape(rows_count, ctx_len, -1, HEAD_SIZE)
    step_grid = jnp.broadcast_to(step_ids[:, None], (steps_count, rows_count))
    logp_new, probs = log_scores(query, cache_k, fresh_k, lengths, step_grid)
    attended = combine(probs, cache_v, fresh_v)
    partial_value = lax.dot_general(
        attended.reshape(steps_count * rows_count, -1),
        new_output,
        (((1,), (1,)), ((), ())),
        preferred_element_type=jnp.float32,
    )
    partial_value = partial_value.reshape(steps_count, rows_count, width)
    attention_out = lax.psum_scatter(
        partial_value.astype(jnp.bfloat16), "shard", scatter_dimension=2, tiled=True
    )
    rows_s = stale_rows[0]
    steps_s = stale_steps[0]
    back_s = stale_back[0]
    lens_s = lengths[rows_s]
    place = lens_s + steps_s - back_s % (lens_s + steps_s + 1)
    index = jnp.where(place >= lens_s, ctx_len + place - lens_s, place)
    picked_new = pick(logp_new[steps_s, rows_s], index)
    sample_x = normed[steps_s, rows_s]
    query_old = project(sample_x[None], base_query, query_gain, (lens_s + steps_s)[None])
    keys_old = project(normed[:, rows_s], base_key, key_gain, positions[:, rows_s])
    logp_old, unused = log_scores(query_old, cache_k[rows_s], keys_old, lens_s, steps_s[None])
    picked_old = pick(logp_old[0], index)
    local_terms = jnp.sum(picked_new - picked_old, axis=1)
    summed = lax.psum(local_terms, "shard")
    log_ratio = (summed / HQ)[None, :]
    return (attention_out, log_ratio)


def solution(mesh):
    return jax.shard_map(
        local,
        mesh=mesh,
        in_specs=(
            P(None, "replica", "shard"),
            P(),
            P(),
            P(),
            P(None, "shard"),
            P(None, "shard"),
            P(None, "shard"),
            P(None, "shard"),
            P(("replica", "shard"), None),
            P(("replica", "shard"), None),
            P(("replica", "shard"), None),
            P(("replica", "shard"), None),
            P(("replica", "shard"), None),
            P(("replica", "shard"), None),
            P(("replica", "shard"), None),
            P(("replica", "shard"), None),
            P("replica", None, "shard"),
            P("replica", None, "shard"),
            P("replica"),
            P("replica", None),
            P("replica", None),
            P("replica", None),
        ),
        out_specs=(P(None, "replica", "shard"), P("replica", None)),
        check_vma=False,
    )
```

profile of v0, /device:TPU:32, one launch (start us, length us, event | category | flops | bytes accessed | tf_op | source)
XLA Modules:
  0.0 585.0 jit_solution(15704858531428098670)
XLA Ops:
  10.4 23.2 %all-gather.1 = bf16[16,20,1024]{2,1,0:T(8,128)(2,1)S(1)} all-gather(bf16[1,20,1024]{2,1,0:T(8,128)(2,1)S(1)} %fusion.64), channel_id=1, replica_groups=mesh['replica'=16,'shard'=16] {'replica'}, dimensions={0}, use_global_device_ids=true | all-gather | bytes 696320 | tf_op jit(solution)/shard_map/all_gather | solution.py:137
  35.4 10.9 %all-to-all-start.1 = ((bf16[320,16,128]{2,0,1:T(8,128)(2,1)}), bf16[320,16,128]{2,0,1:T(8,128)(2,1)S(1)}, u32[]{:S(2)}, u32[]{:S(2)}) async-start(bf16[320,16,128]{2,0,1:T(8,128)(2,1)} %bitcast.16), calls=%async_computation.1 | async-start | bytes 2621440 | tf_op jit(solution)/shard_map/all_to_all | solution.py:149
  47.7 22.2 %all-gather.2 = bf16[16,20,1024]{2,1,0:T(8,128)(2,1)S(1)} all-gather(bf16[1,20,1024]{2,1,0:T(8,128)(2,1)S(1)} %fusion.65), channel_id=1, replica_groups=mesh['replica'=16,'shard'=16] {'replica'}, dimensions={0}, use_global_device_ids=true | all-gather | bytes 696320 | tf_op jit(solution)/shard_map/all_gather | solution.py:138
  70.9 10.0 %all-to-all-done.1 = bf16[320,16,128]{2,0,1:T(8,128)(2,1)S(1)} async-done(((bf16[320,16,128]{2,0,1:T(8,128)(2,1)}), bf16[320,16,128]{2,0,1:T(8,128)(2,1)S(1)}, u32[]{:S(2)}, u32[]{:S(2)}) %all-to-all-start.1) | async-done | bytes 1310752 | tf_op jit(solution)/shard_map/all_to_all | solution.py:149
  82.5 6.2 %all-to-all-start.2 = ((bf16[320,16,128]{2,0,1:T(8,128)(2,1)}), bf16[320,16,128]{2,0,1:T(8,128)(2,1)}, u32[]{:S(2)}, u32[]{:S(2)}) async-start(bf16[320,16,128]{2,0,1:T(8,128)(2,1)} %bitcast.32), calls=%async_computation.2 | async-start | bytes 2621440 | tf_op jit(solution)/shard_map/all_to_all | solution.py:150
  98.5 27.5 %all-to-all-done.2 = bf16[320,16,128]{2,0,1:T(8,128)(2,1)} async-done(((bf16[320,16,128]{2,0,1:T(8,128)(2,1)}), bf16[320,16,128]{2,0,1:T(8,128)(2,1)}, u32[]{:S(2)}, u32[]{:S(2)}) %all-to-all-start.2) | async-done | bytes 1310752 | tf_op jit(solution)/shard_map/all_to_all | solution.py:150
  126.0 6.4 %all-to-all-start = ((bf16[320,16,256]{2,0,1:T(8,128)(2,1)}), bf16[320,16,256]{2,0,1:T(8,128)(2,1)}, u32[]{:S(2)}, u32[]{:S(2)}) async-start(bf16[320,16,256]{2,0,1:T(8,128)(2,1)} %copy.177), calls=%async_computation | async-start | bytes 5242880 | tf_op jit(solution)/shard_map/all_to_all | solution.py:148
  146.9 68.9 %all-gather.8.cloned.1.call-done = bf16[4,32,5120]{1,0,2:T(4,128)(2,1)} async-done(((bf16[4,32,320]{1,0,2:T(4,128)(2,1)}), bf16[4,32,5120]{1,0,2:T(4,128)(2,1)}) %all-gather.8.cloned.1.call-update) | async-done | bytes 1310736 | tf_op jit(solution)/shard_map/all_gather | solution.py:160
  215.8 6.0 %copy.176 = bf16[4,32,5120]{2,1,0:T(8,128)(2,1)S(1)} copy(bf16[4,32,5120]{1,0,2:T(4,128)(2,1)} %all-gather.8.cloned.1.call-done) | data formatting | bytes 2621440 | tf_op jit(solution)/shard_map/all_gather | solution.py:160
  225.8 5.7 gather_fusion.3
  234.3 9.1 %gather_fusion.4 = bf16[128,4,5120]{2,1,0:T(4,128)(2,1)} fusion(bf16[4,32,5120]{2,0,1:T(4,128)(2,1)S(1)} %copy.203, s32[1024]{0:T(1024)S(1)} %pad_clamp_fusion), kind=kCustom, calls=%fused_computation.6 | custom fusion | bytes 10486272 | tf_op jit(solution)/shard_map/gather | solution.py:194
  243.5 6.4 %copy.204 = bf16[4,128,5120]{2,1,0:T(8,128)(2,1)} copy(bf16[4,128,5120]{2,0,1:T(4,128)(2,1)} %bitcast.223) | data formatting | bytes 10485760 | tf_op jit(solution)/shard_map/gather | solution.py:194
  263.3 5.5 all_to_all.46
  273.0 8.8 %all-to-all-start.3 = ((bf16[320,16,256]{2,0,1:T(8,128)(2,1)}), bf16[320,16,256]{2,0,1:T(8,128)(2,1)}, u32[]{:S(2)}, u32[]{:S(2)}) async-start(bf16[320,16,256]{2,0,1:T(8,128)(2,1)} %copy.196), calls=%async_computation.3 | async-start | bytes 5242880 | tf_op jit(solution)/shard_map/all_to_all | solution.py:151
  281.9 5.3 multiply_reduce_fusion
  290.4 6.6 %copy.179 = f32[16,16,20,256]{3,2,1,0:T(8,128)} copy(f32[16,16,20,256]{3,1,2,0:T(8,128)S(1)} %bitcast.224) | data formatting | bytes 10485760 | tf_op jit(solution)/shard_map/convert_element_type | solution.py:52
  297.0 6.9 %reshape.943 = f32[5120,256]{1,0:T(8,128)} reshape(f32[16,16,20,256]{3,2,1,0:T(8,128)} %copy.179) | data formatting | bytes 10485760 | tf_op jit(solution)/shard_map/convert_element_type | solution.py:52
  303.9 5.4 fusion.3
  319.2 22.5 %all-to-all-done.3 = bf16[320,16,256]{2,0,1:T(8,128)(2,1)} async-done(((bf16[320,16,256]{2,0,1:T(8,128)(2,1)}), bf16[320,16,256]{2,0,1:T(8,128)(2,1)}, u32[]{:S(2)}, u32[]{:S(2)}) %all-to-all-start.3) | async-done | bytes 2621472 | tf_op jit(solution)/shard_map/all_to_all | solution.py:151
  345.0 6.5 %copy.198 = f32[16,16,20,256]{3,2,1,0:T(8,128)} copy(f32[16,16,20,256]{3,1,2,0:T(8,128)S(1)} %bitcast.225) | data formatting | bytes 10485760 | tf_op jit(solution)/shard_map/convert_element_type | solution.py:52
  351.5 6.7 %reshape.946 = f32[5120,256]{1,0:T(8,128)} reshape(f32[16,16,20,256]{3,2,1,0:T(8,128)} %copy.198) | data formatting | bytes 10485760 | tf_op jit(solution)/shard_map/convert_element_type | solution.py:52
  367.8 7.3 %reshape.1045 = bf16[5120,128]{1,0:T(8,128)(2,1)} reshape(bf16[5120,4,32]{2,1,0:T(4,128)(2,1)} %bitcast.226) | data formatting | bytes 2621440
  399.1 39.3 %psum.7 = f32[128]{0:T(128)S(1)} all-reduce(f32[128]{0:T(128)S(1)} %fusion.57), channel_id=1, replica_groups=mesh['replica'=16,'shard'=16] {'shard'}, use_global_device_ids=true, to_apply=%region_11.13 | all-reduce | flops 128 | bytes 1024 | tf_op jit(solution)/shard_map/psum | solution.py:198
  438.9 137.5 %reduce-scatter.4.cloned.1.call-done = bf16[320,128]{1,0:T(8,128)(2,1)} async-done(((bf16[5120,128]{1,0:T(8,128)(2,1)}), bf16[320,128]{1,0:T(8,128)(2,1)}) %reduce-scatter.4.cloned.1.call-update) | async-done | bytes 81936
  (221 shorter events, 109.0 us)
Async XLA Ops:
  7.2 126.0 %copy-start = (bf16[32,64,128]{2,1,0:T(8,128)(2,1)S(1)}, bf16[32,64,128]{2,1,0:T(8,128)(2,1)}, u32[]{:S(2)}) copy-start(bf16[32,64,128]{2,1,0:T(8,128)(2,1)} %param.40) | copy-start | bytes 1572868
  7.2 84.5 %all-gather.10.cloned.1.call-start = ((), (), s32[]{:S(2)}) async-start(), calls=%async_computation.6 | async-start | bytes 3342336 | tf_op jit(solution)/shard_map/all_gather | solution.py:136
  34.1 12.4 %copy-start.24 = (bf16[4,32,320]{2,1,0:T(8,128)(2,1)S(1)}, bf16[4,32,320]{2,1,0:T(8,128)(2,1)}, u32[]{:S(2)}) copy-start(bf16[4,32,320]{2,1,0:T(8,128)(2,1)} %param.24) | copy-start | bytes 245764
  34.1 13.3 %copy-start.33 = (s32[20,8]{0,1:T(8,128)S(1)}, s32[20,8]{0,1:T(8,128)}, u32[]{:S(2)}) copy-start(s32[20,8]{0,1:T(8,128)} %param.37) | copy-start | bytes 1924
  34.1 13.6 %copy-start.27 = (bf16[20,1024]{1,0:T(8,128)(2,1)S(1)}, bf16[20,1024]{1,0:T(8,128)(2,1)}, u32[]{:S(2)}) copy-start(bf16[20,1024]{1,0:T(8,128)(2,1)} %param.36) | copy-start | bytes 122884
  35.4 45.5 %all-to-all-start.1 = ((bf16[320,16,128]{2,0,1:T(8,128)(2,1)}), bf16[320,16,128]{2,0,1:T(8,128)(2,1)S(1)}, u32[]{:S(2)}, u32[]{:S(2)}) async-start(bf16[320,16,128]{2,0,1:T(8,128)(2,1)} %bitcast.16), calls=%async_computation.1 | async-start | bytes 2621440 | tf_op jit(solution)/shard_map/all_to_all | solution.py:149
  46.4 24.0 %copy-start.29 = (s32[20,32]{1,0:T(8,128)S(1)}, s32[20,32]{1,0:T(8,128)}, u32[]{:S(2)}) copy-start(s32[20,32]{1,0:T(8,128)} %param.39) | copy-start | bytes 7684
  46.4 169.4 %all-gather.8.cloned.1.call-start = ((), (), s32[]{:S(2)}) async-start(), calls=%async_computation.5 | async-start | bytes 5570560 | tf_op jit(solution)/shard_map/all_gather | solution.py:160
  70.6 18.1 %copy-start.16 = (bf16[20,4096]{1,0:T(8,128)(2,1)S(1)}, bf16[20,4096]{1,0:T(8,128)(2,1)}, u32[]{:S(2)}) copy-start(bf16[20,4096]{1,0:T(8,128)(2,1)} %param.38) | copy-start | bytes 491524
  70.9 18.6 %copy-start.37 = (s32[1,128]{1,0:T(1,128)S(1)}, s32[1,128]{1,0:T(1,128)}, u32[]{:S(2)}) copy-start(s32[1,128]{1,0:T(1,128)} %param.44) | copy-start | bytes 1540
  70.9 18.6 %copy-start.40 = (s32[1,128]{1,0:T(1,128)S(1)}, s32[1,128]{1,0:T(1,128)}, u32[]{:S(2)}) copy-start(s32[1,128]{1,0:T(1,128)} %param.43) | copy-start | bytes 1540
  70.9 18.6 %copy-start.1 = (s32[32]{0:T(128)S(1)}, s32[32]{0:T(128)}, u32[]{:S(2)}) copy-start(s32[32]{0:T(128)} %param.42) | copy-start | bytes 388
  70.9 19.8 %copy-start.39 = (s32[1,128]{1,0:T(1,128)S(1)}, s32[1,128]{1,0:T(1,128)}, u32[]{:S(2)}) copy-start(s32[1,128]{1,0:T(1,128)} %param.45) | copy-start | bytes 1540
  81.0 8.5 %copy-start.4 = (bf16[320,16,128]{2,0,1:T(8,128)(2,1)}, bf16[320,16,128]{2,0,1:T(8,128)(2,1)S(1)}, u32[]{:S(2)}) copy-start(bf16[320,16,128]{2,0,1:T(8,128)(2,1)S(1)} %all-to-all-done.1) | copy-start | bytes 3932164
  82.5 43.5 %all-to-all-start.2 = ((bf16[320,16,128]{2,0,1:T(8,128)(2,1)}), bf16[320,16,128]{2,0,1:T(8,128)(2,1)}, u32[]{:S(2)}, u32[]{:S(2)}) async-start(bf16[320,16,128]{2,0,1:T(8,128)(2,1)} %bitcast.32), calls=%async_computation.2 | async-start | bytes 2621440 | tf_op jit(solution)/shard_map/all_to_all | solution.py:150
  88.7 174.7 %all-gather.12.cloned.1.call-start = ((), (), s32[]{:S(2)}) async-start(), calls=%async_computation.7 | async-start | bytes 3342336 | tf_op jit(solution)/shard_map/all_gather | solution.py:139
  91.7 40.7 %copy-start.19 = (f32[4,32]{0,1:T(8,128)}, f32[4,32]{0,1:T(8,128)S(1)}, u32[]{:S(2)}) copy-start(f32[4,32]{0,1:T(8,128)S(1)} %get-tuple-element.24) | copy-start | bytes 1540
  126.0 147.0 %all-to-all-start = ((bf16[320,16,256]{2,0,1:T(8,128)(2,1)}), bf16[320,16,256]{2,0,1:T(8,128)(2,1)}, u32[]{:S(2)}, u32[]{:S(2)}) async-start(bf16[320,16,256]{2,0,1:T(8,128)(2,1)} %copy.177), calls=%async_computation | async-start | bytes 5242880 | tf_op jit(solution)/shard_map/all_to_all | solution.py:148
  146.9 75.3 %copy-start.28 = (f32[5120]{0:T(1024)S(1)}, f32[5120]{0:T(1024)}, u32[]{:S(2)}) copy-start(f32[5120]{0:T(1024)} %param.25) | copy-start | bytes 61444
  273.0 8.9 %copy-start.8 = (bf16[5120,128]{1,0:T(8,128)(2,1)S(1)}, bf16[5120,128]{1,0:T(8,128)(2,1)}, u32[]{:S(2)}) copy-start(bf16[5120,128]{1,0:T(8,128)(2,1)} %param.29) | copy-start | bytes 3932164
  273.0 68.7 %all-to-all-start.3 = ((bf16[320,16,256]{2,0,1:T(8,128)(2,1)}), bf16[320,16,256]{2,0,1:T(8,128)(2,1)}, u32[]{:S(2)}, u32[]{:S(2)}) async-start(bf16[320,16,256]{2,0,1:T(8,128)(2,1)} %copy.196), calls=%async_computation.3 | async-start | bytes 5242880 | tf_op jit(solution)/shard_map/all_to_all | solution.py:151
  281.8 294.6 %reduce-scatter.4.cloned.1.call-start = ((), (), s32[]{:S(2)}) async-start(), calls=%async_computation.8 | async-start | bytes 1392640
  367.8 8.9 %copy-start.12 = (f32[128,64]{1,0:T(8,128)S(1)}, f32[128,64]{1,0:T(8,128)}, u32[]{:S(2)}) copy-start(f32[128,64]{1,0:T(8,128)} %get-tuple-element.19) | copy-start | bytes 98308
  367.8 8.9 %copy-start.13 = (f32[128,64]{1,0:T(8,128)S(1)}, f32[128,64]{1,0:T(8,128)}, u32[]{:S(2)}) copy-start(f32[128,64]{1,0:T(8,128)} %get-tuple-element.20) | copy-start | bytes 98308
  (25 other events, 108.7 us)
Sparse Core Ops, SparseCore 0:
  10.2 42.9 all-gather.9
  55.8 159.9 all-gather.7
  217.7 37.7 all-gather.11
  375.2 201.1 reduce-scatter.3
where the time goes:
time: 593 us; the launch traced here: 585 us
  waiting for transfers between devices  267 us (45%)
  local copies, waits for them, and re-layouts  132 us (22%)
  blocking collectives  84.7 us (14%)
  other arithmetic  32.7 us (6%)
  starting transfers between devices  32.5 us (5%)
  matrix products  21.8 us (4%)
  between operations  15 us (3%)
    unnamed x5, waiting for transfers between devices  138 us
    all_gather x1, waiting for transfers between devices, local(): whole = lax.all_gather(hidden, 'shard', axis=2, tiled=True)  68.9 us
    convert_element_type x8, local copies, waits for them, and re-layouts, refresh(): delta.astype(jnp.float32)  40.1 us
    psum x1, blocking collectives, local(): summed = lax.psum(local_terms, 'shard')  39.3 us
    all_to_all x1, waiting for transfers between devices, local(): lax.all_to_all(widened[2], 'shard', split_axis=1, concat_axis=0, tiled=True)  27.5 us
    all_gather x1, blocking collectives, local(): lax.all_gather(narrow[1], 'replica', axis=0, tiled=True)  23.2 us
    all_to_all x1, waiting for transfers between devices, local(): lax.all_to_all(widened[3], 'shard', split_axis=1, concat_axis=0, tiled=True)  22.5 us
    all_gather x1, blocking collectives, local(): lax.all_gather(narrow[2], 'replica', axis=0, tiled=True)  22.2 us
  transfers between devices with their start and end apart: 8, of which 5 were waited for; matrix products, arithmetic and copies ran while one was open for 24% of the time, Pallas kernels for 0%

commit v1 on v0

v1 whole, which is shorter than its diff:
```python
import functools

import jax
import jax.numpy as jnp
from jax import lax
from jax.experimental import pallas as pl
from jax.experimental.pallas import tpu as pltpu
from jax.sharding import PartitionSpec as P

HQ = 32
HEAD = 128
WIDTH = 5120
STEPS = 4
ROWS = 32
TOKENS = STEPS * ROWS
CTX = 64
PARTS = 16
OWN = WIDTH // PARTS
CUT = 20
COLS = 768
GROUP = 8
GROUPS = ROWS // GROUP
TAIL = 16
EPSILON = 1e-06
THETA = 1000000.0
SCALE = HEAD ** (-0.5)
NEG = -1e30
CHUNKS = 8
CHUNK = WIDTH // CHUNKS
F32 = jnp.float32
BF16 = jnp.bfloat16
VMEM = pltpu.VMEM


def factors(codes):
    out = jnp.ones(codes.shape, F32)
    for bit in range(5):
        out = out * jnp.where((codes >> bit) & 1 == 1, F32(2.0 ** -(2**bit)), F32(1.0))
    return out


def pack_kernel(dq, sq, dk, sk, dv, sv, do, so, out, buf):
    fq, fk, fv, fo = factors(sq[...]), factors(sk[...]), factors(sv[...]), factors(so[...])

    def piece(codes, factor, head):
        return codes[:, head * HEAD : (head + 1) * HEAD].astype(F32) * factor[:, head : head + 1]

    for dest in range(PARTS):
        half = dest // 2
        pieces = (
            piece(dq, fq, 2 * dest),
            piece(dq, fq, 2 * dest + 1),
            piece(dk, fk, half),
            piece(dv, fv, half),
            piece(do, fo, 2 * dest),
            piece(do, fo, 2 * dest + 1),
        )
        for c, value in enumerate(pieces):
            buf[dest % 2, CUT * c : CUT * (c + 1), :] = value
        out[dest] = buf[dest % 2].astype(BF16)


def refresh_kernel(block, recv, bq, bk, bv, bo, out, buf, delta):
    for src in range(PARTS):
        buf[src % 2] = recv[src].astype(F32)
        for c in range(6):
            delta[CUT * src : CUT * (src + 1), HEAD * c : HEAD * (c + 1)] = buf[
                src % 2, CUT * c : CUT * (c + 1), :
            ]
    out[:, 0:256] = (bq[...].astype(F32) + delta[:, 0:256]).astype(BF16)
    out[:, 256:384] = (bk[...].astype(F32) + delta[:, 256:384]).astype(BF16)
    out[:, 384:512] = (bv[...].astype(F32) + delta[:, 384:512]).astype(BF16)
    out[:, 512:768] = (bo[...].astype(F32) + delta[:, 512:768]).astype(BF16)


def dot_nt(a, b):
    return lax.dot_general(a, b, (((1,), (1,)), ((), ())), preferred_element_type=F32)


def dot(a, b):
    return jnp.dot(a, b, preferred_element_type=F32)


def head_norm_rotate(raw, gain, cosine, sine):
    value = raw * lax.rsqrt(jnp.mean(raw * raw, axis=-1, keepdims=True) + EPSILON) * gain
    swapped = jnp.concatenate([value[:, HEAD // 2 :], value[:, : HEAD // 2]], axis=-1)
    return value * cosine + swapped * sine


def group_scores(group, query, cache, fresh, lens):
    picked = [
        query[h * TOKENS + t * ROWS + group * GROUP : h * TOKENS + t * ROWS + (group + 1) * GROUP, :]
        for h in range(2)
        for t in range(STEPS)
    ]
    q = jnp.concatenate(picked, axis=0).astype(BF16)
    past = dot_nt(q, cache) * SCALE
    new = dot_nt(q, fresh) * SCALE
    n = 2 * STEPS * GROUP
    length = jnp.concatenate([lens[group * GROUP : (group + 1) * GROUP, :]] * (2 * STEPS), axis=0)
    column = lax.broadcasted_iota(jnp.int32, past.shape, 1)
    line = lax.broadcasted_iota(jnp.int32, past.shape, 0)
    past_ok = ((column >> 6) == (line & 7)) & ((column & 63) < length[:, 0:1])
    column = lax.broadcasted_iota(jnp.int32, (n, TOKENS), 1)
    line = lax.broadcasted_iota(jnp.int32, (n, TOKENS), 0)
    new_ok = ((column & 31) == group * GROUP + (line & 7)) & ((column >> 5) <= ((line >> 3) & 3))
    past = jnp.where(past_ok, past, NEG)
    new = jnp.where(new_ok, new, NEG)
    top = jnp.maximum(
        jnp.max(past, axis=-1, keepdims=True), jnp.max(new, axis=-1, keepdims=True)
    )
    past = jnp.exp(past - top)
    new = jnp.exp(new - top)
    total = jnp.sum(past, axis=-1, keepdims=True) + jnp.sum(new, axis=-1, keepdims=True)
    return past, new, total, top + jnp.log(total)


def put_groups(group, ref, value):
    for h in range(2):
        for t in range(STEPS):
            at = h * TOKENS + t * ROWS + group * GROUP
            i = (h * STEPS + t) * GROUP
            ref[at : at + GROUP, :] = value[i : i + GROUP, :]


def sample_logp(query, keys, one_query, lse):
    out = []
    for h in range(2):
        q = dot(one_query, query[h * TOKENS : (h + 1) * TOKENS, :].astype(BF16))
        score = jnp.sum(q * keys, axis=-1, keepdims=True) * SCALE
        line = lse[h * TOKENS : (h + 1) * TOKENS, :].T
        picked = jnp.sum(one_query.astype(F32) * line, axis=-1, keepdims=True)
        out.append(jnp.broadcast_to(score - picked, (TOKENS, HEAD)))
    return out


def prepare_kernel(
    xt, gain, qg, kg, cosine, sine, lens, token, place, base_q, base_k, cache,
    normed, keys_out, one_q_out, one_f_out, old_out,
    total, query, lse,
):
    total[...] = jnp.zeros_like(total)
    for k in range(WIDTH // HEAD):
        x = xt[k * HEAD : (k + 1) * HEAD, :].astype(F32)
        total[...] += jnp.sum(x * x, axis=0, keepdims=True)
    scale = lax.rsqrt(total[...] * (1.0 / WIDTH) + EPSILON)
    for k in range(WIDTH // HEAD):
        x = xt[k * HEAD : (k + 1) * HEAD, :].astype(F32) * scale
        normed[:, k * HEAD : (k + 1) * HEAD] = (
            x.T * gain[:, k * HEAD : (k + 1) * HEAD]
        ).astype(BF16)
    raw = dot(normed[...], base_q[...])
    raw_k = dot(normed[...], base_k[...])
    cos, sin = cosine[...], sine[...]
    for h in range(2):
        query[h * TOKENS : (h + 1) * TOKENS, :] = (
            head_norm_rotate(raw[:, h * HEAD : (h + 1) * HEAD], qg[...], cos, sin)
            .astype(BF16)
            .astype(F32)
        )
    fresh = head_norm_rotate(raw_k, kg[...], cos, sin).astype(BF16)
    for g in range(GROUPS):
        _, _, _, log_sum = group_scores(
            g, query, cache[g * GROUP * CTX : (g + 1) * GROUP * CTX, :], fresh, lens
        )
        put_groups(g, lse, jnp.broadcast_to(log_sum, (log_sum.shape[0], HEAD)))
    tokens = jnp.broadcast_to(token[...], (TOKENS, TOKENS)).T
    places = jnp.broadcast_to(place[...], (TOKENS, TOKENS)).T
    lane = lax.broadcasted_iota(jnp.int32, (TOKENS, TOKENS), 1)
    one_q = jnp.where(tokens == lane, F32(1.0), F32(0.0)).astype(BF16)
    one_f = jnp.where(places == lane + ROWS * CTX, F32(1.0), F32(0.0)).astype(BF16)
    keys = jnp.zeros((TOKENS, HEAD), F32)
    for k in range(ROWS * CTX // HEAD):
        one = jnp.where(places == lane + k * HEAD, F32(1.0), F32(0.0)).astype(BF16)
        keys = keys + dot(one, cache[k * HEAD : (k + 1) * HEAD, :])
    keys_out[...] = keys
    one_q_out[...] = one_q
    one_f_out[...] = one_f
    old = sample_logp(query, keys + dot(one_f, fresh), one_q, lse)
    old_out[0] = old[0]
    old_out[1] = old[1]


def main_kernel(
    normed, weight, qg, kg, cosine, sine, lens, cache, values, keys, one_q, one_f, old,
    out,
    held, query, lse, mixed, sems,
):
    copies = [
        pltpu.make_async_copy(
            weight.at[pl.ds(c * CHUNK, CHUNK)], held.at[pl.ds(c * CHUNK, CHUNK)], sems.at[c]
        )
        for c in range(CHUNKS)
    ]
    for copy in copies:
        copy.start()
    raw = jnp.zeros((TOKENS, 512), F32)
    for c in range(CHUNKS):
        copies[c].wait()
        raw = raw + dot(
            normed[:, c * CHUNK : (c + 1) * CHUNK], held[c * CHUNK : (c + 1) * CHUNK, 0:512]
        )
    cos, sin = cosine[...], sine[...]
    for h in range(2):
        query[h * TOKENS : (h + 1) * TOKENS, :] = (
            head_norm_rotate(raw[:, h * HEAD : (h + 1) * HEAD], qg[...], cos, sin)
            .astype(BF16)
            .astype(F32)
        )
    fresh = head_norm_rotate(raw[:, 256:384], kg[...], cos, sin).astype(BF16)
    fresh_v = raw[:, 384:512].astype(BF16)
    for g in range(GROUPS):
        at = slice(g * GROUP * CTX, (g + 1) * GROUP * CTX)
        past, new, total, log_sum = group_scores(g, query, cache[at, :], fresh, lens)
        put_groups(g, lse, jnp.broadcast_to(log_sum, (log_sum.shape[0], HEAD)))
        mix = dot((past / total).astype(BF16), values[at, :])
        mix = mix + dot((new / total).astype(BF16), fresh_v)
        put_groups(g, mixed, mix)
    attended = jnp.concatenate([mixed[0:TOKENS, :], mixed[TOKENS:, :]], axis=1).astype(BF16)
    for p in range(PARTS):
        part = dot_nt(held[p * OWN : (p + 1) * OWN, 512:768], attended)
        out[p, 0:OWN, :] = part.astype(BF16)
    now = sample_logp(query, keys[...] + dot(one_f[...], fresh), one_q[...], lse)
    term = (now[0] - old[0]) + (now[1] - old[1])
    line = term.T[0:1, :]
    high = line.astype(BF16).astype(F32)
    middle = (line - high).astype(BF16).astype(F32)
    low = line - high - middle
    tail = jnp.concatenate([high, middle, low, jnp.zeros((TAIL - 3, TOKENS), F32)], axis=0)
    tail = tail.astype(BF16)
    for p in range(PARTS):
        out[p, OWN : OWN + TAIL, :] = tail


def finish_kernel(recv, out, ratio):
    for k, n in ((0, 128), (128, 128), (256, 80)):
        total = recv[0, k : k + n, :].astype(F32)
        for src in range(1, PARTS):
            total = total + recv[src, k : k + n, :].astype(F32)
        if n == 128:
            out[:, k : k + n] = total.T.astype(BF16)
        else:
            tail = total[64:67, :]
            ratio[...] = ((tail[2:3, :] + tail[1:2, :]) + tail[0:1, :]) * (1.0 / HQ)
            out[:, k : k + 64] = total[0:64, :].T.astype(BF16)


def params(mib):
    return pltpu.CompilerParams(vmem_limit_bytes=mib * 1024 * 1024)


def shape(dims, dtype):
    return jax.ShapeDtypeStruct(dims, dtype)


def whole():
    return pl.BlockSpec(memory_space=VMEM)


def local(
    hidden,
    norm_gain,
    query_gain,
    key_gain,
    base_query,
    base_key,
    base_value,
    base_output,
    delta_query,
    scale_query,
    key_delta_codes,
    key_scale_codes,
    value_delta_codes,
    value_scale_codes,
    delta_output,
    scale_output,
    cache_keys,
    cache_values,
    lengths,
    stale_rows,
    stale_steps,
    stale_back,
):
    packed = pl.pallas_call(
        pack_kernel,
        name="pack",
        out_shape=shape((PARTS, 6 * CUT, HEAD), BF16),
        in_specs=[whole()] * 8,
        out_specs=whole(),
        scratch_shapes=[VMEM((2, 6 * CUT, HEAD), F32)],
        compiler_params=params(16),
    )(
        delta_query,
        scale_query,
        key_delta_codes,
        key_scale_codes,
        value_delta_codes,
        value_scale_codes,
        delta_output,
        scale_output,
    )
    arrived = lax.all_to_all(packed, "shard", split_axis=0, concat_axis=0, tiled=False)
    arrived, hidden, lengths, stale_rows, stale_steps, stale_back = lax.optimization_barrier(
        (arrived, hidden, lengths, stale_rows, stale_steps, stale_back)
    )
    block = lax.axis_index("replica").astype(jnp.int32).reshape(1)
    fresh_rows = pl.pallas_call(
        refresh_kernel,
        name="refresh",
        out_shape=shape((OWN, COLS), BF16),
        grid_spec=pltpu.PrefetchScalarGridSpec(
            num_scalar_prefetch=1,
            grid=(1,),
            in_specs=[
                pl.BlockSpec((PARTS, 6 * CUT, HEAD), lambda i, b: (0, 0, 0)),
                pl.BlockSpec((OWN, 256), lambda i, b: (b[0], 0)),
                pl.BlockSpec((OWN, 128), lambda i, b: (b[0], 0)),
                pl.BlockSpec((OWN, 128), lambda i, b: (b[0], 0)),
                pl.BlockSpec((OWN, 256), lambda i, b: (b[0], 0)),
            ],
            out_specs=pl.BlockSpec((OWN, COLS), lambda i, b: (0, 0)),
            scratch_shapes=[VMEM((2, 6 * CUT, HEAD), F32), VMEM((OWN, COLS), F32)],
        ),
        compiler_params=params(16),
    )(block, arrived, base_query, base_key, base_value, base_output)
    weight = lax.all_gather(fresh_rows, "replica", axis=0, tiled=True)

    mine = hidden.reshape(TOKENS, OWN).T
    spread = jnp.broadcast_to(mine[None], (PARTS, OWN, TOKENS))
    xt = lax.all_to_all(spread, "shard", split_axis=0, concat_axis=0, tiled=False)
    xt = xt.reshape(WIDTH, TOKENS)

    position = (lengths[None, :] + jnp.arange(STEPS)[:, None]).reshape(TOKENS)
    freq = THETA ** (-(jnp.arange(HEAD // 2).astype(F32) * 2.0) / HEAD)
    angle = position.astype(F32)[:, None] * freq
    cos, sin = jnp.cos(angle), jnp.sin(angle)
    cosine = jnp.concatenate([cos, cos], axis=1)
    sine = jnp.concatenate([-sin, sin], axis=1)
    lens = jnp.broadcast_to(lengths[:, None], (ROWS, HEAD))

    rows_s, steps_s, back_s = stale_rows, stale_steps, stale_back
    lens_s = jnp.sum(
        jnp.where(rows_s[0][None, :] == jnp.arange(ROWS)[:, None], lengths[:, None], 0),
        axis=0,
        keepdims=True,
    )
    at = lens_s + steps_s - back_s % (lens_s + steps_s + 1)
    place = jnp.where(
        at >= lens_s, ROWS * CTX + (at - lens_s) * ROWS + rows_s, rows_s * CTX + at
    ).astype(jnp.int32)
    token = (steps_s * ROWS + rows_s).astype(jnp.int32)

    query_gain = query_gain.reshape(1, HEAD)
    key_gain = key_gain.reshape(1, HEAD)
    cache = cache_keys.reshape(ROWS * CTX, HEAD)
    values = cache_values.reshape(ROWS * CTX, HEAD)

    normed, keys, one_q, one_f, old = pl.pallas_call(
        prepare_kernel,
        name="prepare",
        out_shape=(
            shape((TOKENS, WIDTH), BF16),
            shape((TOKENS, HEAD), F32),
            shape((TOKENS, TOKENS), BF16),
            shape((TOKENS, TOKENS), BF16),
            shape((2, TOKENS, HEAD), F32),
        ),
        in_specs=[whole()] * 12,
        out_specs=(whole(),) * 5,
        scratch_shapes=[
            VMEM((1, TOKENS), F32),
            VMEM((2 * TOKENS, HEAD), F32),
            VMEM((2 * TOKENS, HEAD), F32),
        ],
        compiler_params=params(32),
    )(
        xt, norm_gain.reshape(1, WIDTH), query_gain, key_gain, cosine, sine, lens, token, place,
        base_query, base_key, cache,
    )

    parts = pl.pallas_call(
        main_kernel,
        name="attend",
        out_shape=shape((PARTS, OWN + TAIL, TOKENS), BF16),
        in_specs=[whole(), pl.BlockSpec(memory_space=pl.ANY)] + [whole()] * 11,
        out_specs=whole(),
        scratch_shapes=[
            VMEM((WIDTH, COLS), BF16),
            VMEM((2 * TOKENS, HEAD), F32),
            VMEM((2 * TOKENS, HEAD), F32),
            VMEM((2 * TOKENS, HEAD), F32),
            pltpu.SemaphoreType.DMA((CHUNKS,)),
        ],
        compiler_params=params(40),
    )(normed, weight, query_gain, key_gain, cosine, sine, lens, cache, values, keys, one_q, one_f, old)

    landed = lax.all_to_all(parts, "shard", split_axis=0, concat_axis=0, tiled=False)
    out, ratio = pl.pallas_call(
        finish_kernel,
        name="finish",
        out_shape=(shape((TOKENS, OWN), BF16), shape((1, TOKENS), F32)),
        in_specs=[whole()],
        out_specs=(whole(), whole()),
        compiler_params=params(16),
    )(landed)
    return out.reshape(STEPS, ROWS, OWN), ratio


def solution(mesh):
    return jax.shard_map(
        local,
        mesh=mesh,
        in_specs=(
            P(None, "replica", "shard"),
            P(),
            P(),
            P(),
            P(None, "shard"),
            P(None, "shard"),
            P(None, "shard"),
            P(None, "shard"),
            P(("replica", "shard"), None),
            P(("replica", "shard"), None),
            P(("replica", "shard"), None),
            P(("replica", "shard"), None),
            P(("replica", "shard"), None),
            P(("replica", "shard"), None),
            P(("replica", "shard"), None),
            P(("replica", "shard"), None),
            P("replica", None, "shard"),
            P("replica", None, "shard"),
            P("replica"),
            P("replica", None),
            P("replica", None),
            P("replica", None),
        ),
        out_specs=(P(None, "replica", "shard"), P("replica", None)),
        check_vma=False,
    )
```

time: 593 us -> 177 us (0.30); the launches traced: 585 us -> 175 us
  waiting for transfers between devices: 267 us -> 58.7 us
  local copies, waits for them, and re-layouts: 132 us -> 25.7 us
  blocking collectives: 84.7 us -> 45 us
  other arithmetic: 32.7 us -> 1.16 us
  matrix products: 21.8 us -> 0 us
  starting transfers between devices: 32.5 us -> 16.6 us
  Pallas kernels: 0 us -> 14.1 us
    unnamed x5 -> x1, waiting for transfers between devices: 138 us -> 0.02 us
    all_gather x3 -> x1, waiting for transfers between devices: 68.9 us -> 11 us  [local(): weight = lax.all_gather(fresh_rows, 'replica', axis=0, tiled=True)]
    all_gather x2 -> x0, blocking collectives: 45.5 us -> none  [the longest x1 23.2 us: local(): lax.all_gather(narrow[1], 'replica', axis=0, tiled=True)]
    all_to_all x0 -> x1, blocking collectives: none -> 45 us  [local(): lax.all_to_all(parts, 'shard', split_axis=0, concat_axis=0, tiled=False)]
    convert_element_type x11 -> x1, local copies, waits for them, and re-layouts: 41.3 us -> 0.08 us  [local(): angle = position.astype(F32)[:, None] * freq]
    psum x1 -> x0, blocking collectives: 39.3 us -> none  [local(): summed = lax.psum(local_terms, 'shard')]
    gather x10 -> x0, local copies, waits for them, and re-layouts: 34.8 us -> none  [the longest x2 15.5 us: local(): normed[:, rows_s]]
    dot_general x12 -> x0, matrix products: 21.8 us -> none  [the longest x4 11.6 us: project(): jnp.dot(normed.reshape(-1, normed.shape[-1]), weight, preferred_element_t...]
  transfers between devices with their start and end apart: 8 -> 3, of which waited for: 5 -> 3; matrix products, arithmetic and copies ran while one was open for 24% -> 2% of each run, Pallas kernels for 0% -> 2%
where the time goes in v1:
time: 177 us; the launch traced here: 175 us
  waiting for transfers between devices  58.7 us (33%)
  blocking collectives  45 us (25%)
  local copies, waits for them, and re-layouts  25.7 us (15%)
  starting transfers between devices  16.6 us (9%)
  between operations  14.2 us (8%)
  Pallas kernels  14.1 us (8%)
    all_to_all x1, blocking collectives, local(): lax.all_to_all(parts, 'shard', split_axis=0, concat_axis=0, tiled=False)  45 us
    all_to_all x1, waiting for transfers between devices, local(): lax.all_to_all(spread, 'shard', split_axis=0, concat_axis=0, tiled=False)  31.9 us
    unnamed x60, local copies, waits for them, and re-layouts  24.1 us
    all_to_all x1, waiting for transfers between devices, local(): lax.all_to_all(packed, 'shard', split_axis=0, concat_axis=0, tiled=False)  15.8 us
    all_to_all x1, starting transfers between devices, local(): lax.all_to_all(packed, 'shard', split_axis=0, concat_axis=0, tiled=False)  11 us
    all_gather x1, waiting for transfers between devices, local(): weight = lax.all_gather(fresh_rows, 'replica', axis=0, tiled=True)  11 us
    pallas_call x1, Pallas kernels, local(): pl.pallas_call(main_kernel, name='attend', out_shape=shape((PARTS, OWN +...  6.89 us
    all_to_all x1, starting transfers between devices, local(): lax.all_to_all(spread, 'shard', split_axis=0, concat_axis=0, tiled=False)  5.52 us
  transfers between devices with their start and end apart: 3, of which 3 were waited for; matrix products, arithmetic and copies ran while one was open for 2% of the time, Pallas kernels for 2%

profile of v1, /device:TPU:32, one launch (start us, length us, event | category | flops | bytes accessed | tf_op | source)
XLA Modules:
  0.0 175.5 jit_solution(12180225916633965449)
XLA Ops:
  7.2 0.9 copy.24.sk
  8.8 0.9 copy-done.11
  9.8 0.9 copy-done.12
  11.5 0.8 copy-done.14
  13.7 1.3 pack.1
  15.0 11.0 %all-to-all-start = ((bf16[16,120,128]{2,1,0:T(8,128)(2,1)}), bf16[16,120,128]{2,1,0:T(8,128)(2,1)S(1)}, u32[]{:S(2)}, u32[]{:S(2)}) async-start(bf16[16,120,128]{2,1,0:T(8,128)(2,1)} %pack.1), calls=%async_computation | async-start | bytes 983040 | tf_op jit(solution)/shard_map/all_to_all | solution.py:302
  26.1 15.8 %all-to-all-done.recv = bf16[16,120,128]{2,1,0:T(8,128)(2,1)S(1)} async-done(((bf16[16,120,128]{2,1,0:T(8,128)(2,1)}), bf16[16,120,128]{2,1,0:T(8,128)(2,1)S(1)}, u32[]{:S(2)}, u32[]{:S(2)}) %all-to-all-start) | async-done | bytes 491552 | tf_op jit(solution)/shard_map/all_to_all | solution.py:302
  41.9 1.7 copy-done
  43.6 1.7 copy-done.5
  45.4 1.3 copy-done.7
  46.7 1.1 refresh.1
  47.9 1.3 broadcast_in_dim.13
  49.3 5.5 %all-to-all-start.1 = ((bf16[16,320,128]{2,1,0:T(8,128)(2,1)}), bf16[16,320,128]{2,1,0:T(8,128)(2,1)}, u32[]{:S(2)}, u32[]{:S(2)}) async-start(bf16[16,320,128]{2,1,0:T(8,128)(2,1)} %broadcast_in_dim.13), calls=%async_computation.1 | async-start | bytes 2621440 | tf_op jit(solution)/shard_map/all_to_all | solution.py:330
  56.1 31.9 %all-to-all-done.1 = bf16[16,320,128]{2,1,0:T(8,128)(2,1)} async-done(((bf16[16,320,128]{2,1,0:T(8,128)(2,1)}), bf16[16,320,128]{2,1,0:T(8,128)(2,1)}, u32[]{:S(2)}, u32[]{:S(2)}) %all-to-all-start.1) | async-done | bytes 1310752 | tf_op jit(solution)/shard_map/all_to_all | solution.py:330
  88.1 1.4 copy-done.4
  92.8 4.0 %prepare.1 = (bf16[128,5120]{1,0:T(8,128)(2,1)S(1)}, f32[128,128]{1,0:T(8,128)S(1)}, bf16[128,128]{1,0:T(8,128)(2,1)S(1)}, bf16[128,128]{1,0:T(8,128)(2,1)S(1)}, f32[2,128,128]{2,1,0:T(8,128)S(1)}) custom-call(bf16[5120,128]{1,0:T(8,128)(2,1)} %bitcast.2.xt, f32[1,5120]{1,0:T(1,128)S(1)} %bitcast.29, f32[1,128]{1,0:T(1,128)S(1)} %bitcast.30, ...), custom_call_target="tpu_custom_call" | custom-call | tf_op jit(solution)/shard_map/prepare/pallas_call | solution.py:358
  96.8 1.1 copy-done.8
  97.9 11.0 %all-gather.2.cloned.1.call-done.weight = bf16[5120,768]{1,0:T(8,128)(2,1)} async-done(((bf16[320,768]{1,0:T(8,128)(2,1)}), bf16[5120,768]{1,0:T(8,128)(2,1)}) %all-gather.2.cloned.1.call-update) | async-done | bytes 7864336 | tf_op jit(solution)/shard_map/all_gather | solution.py:326
  109.0 3.2 %copy-done.2 = bf16[5120,768]{1,0:T(8,128)(2,1)S(1)} copy-done((bf16[5120,768]{1,0:T(8,128)(2,1)S(1)}, bf16[5120,768]{1,0:T(8,128)(2,1)}, u32[]{:S(2)}) %copy-start.2) | copy-done | bytes 7864344
  112.2 1.3 copy-done.9
  113.5 1.0 copy-done.10
  115.9 6.9 %attend.1 = bf16[16,336,128]{2,1,0:T(8,128)(2,1)S(1)} custom-call(bf16[128,5120]{1,0:T(8,128)(2,1)S(1)} %copy-done.9, bf16[5120,768]{1,0:T(8,128)(2,1)S(1)} %copy-done.2, f32[1,128]{1,0:T(1,128)S(1)} %bitcast.31, f32[1,128]{1,0:T(1,128)S(1)} %bitcast.33, f32[128,128]{1,0:T(8,128)S(1)} %get-tuple-element.33.cosine, f32[128,128]{1,0:T(8,128)S(1)} %get-tuple-element.34.sine, ...), custom_call_target="tpu_custom_call" | custom-call | tf_op jit(solution)/shard_map/attend/pallas_call | solution.py:381
  122.8 45.0 %all_to_all.15.recv = bf16[16,336,128]{2,1,0:T(8,128)(2,1)S(1)} all-to-all(bf16[16,336,128]{2,1,0:T(8,128)(2,1)S(1)} %attend.1), channel_id=1, replica_groups=mesh['replica'=16,'shard'=16] {'shard'}, dimensions={0} | all-to-all | bytes 2752512 | tf_op jit(solution)/shard_map/all_to_all | solution.py:397
  167.7 0.9 finish.1
  (59 shorter events, 9.2 us)
Async XLA Ops:
  7.2 34.7 %copy-start.3 = (bf16[5120,128]{1,0:T(8,128)(2,1)S(1)}, bf16[5120,128]{1,0:T(8,128)(2,1)}, u32[]{:S(2)}) copy-start(bf16[5120,128]{1,0:T(8,128)(2,1)} %bk.1) | copy-start | bytes 3932164
  8.8 0.9 copy-start.11
  9.7 0.9 copy-start.12
  10.7 0.8 copy-start.13
  11.5 0.8 copy-start.14
  15.0 26.9 %all-to-all-start = ((bf16[16,120,128]{2,1,0:T(8,128)(2,1)}), bf16[16,120,128]{2,1,0:T(8,128)(2,1)S(1)}, u32[]{:S(2)}, u32[]{:S(2)}) async-start(bf16[16,120,128]{2,1,0:T(8,128)(2,1)} %pack.1), calls=%async_computation | async-start | bytes 983040 | tf_op jit(solution)/shard_map/all_to_all | solution.py:302
  26.1 82.9 %all-gather.2.cloned.1.call-start = ((), (), s32[]{:S(2)}) async-start(), calls=%async_computation.3 | async-start | bytes 8355840 | tf_op jit(solution)/shard_map/all_gather | solution.py:326
  41.9 1.7 copy-start
  43.6 1.7 copy-start.5
  45.4 1.3 copy-start.7
  46.7 1.1 copy-start.24
  47.9 6.9 %copy-start.25 = (s32[32]{0:T(128)S(1)}, s32[32]{0:T(128)}, u32[]{:S(2)}) copy-start(s32[32]{0:T(128)} %param.40) | copy-start | bytes 388
  47.9 7.0 %copy-start.26 = (s32[1,128]{1,0:T(1,128)S(1)}, s32[1,128]{1,0:T(1,128)}, u32[]{:S(2)}) copy-start(s32[1,128]{1,0:T(1,128)} %param.41) | copy-start | bytes 1540
  49.3 6.2 %copy-start.27 = (s32[1,128]{1,0:T(1,128)S(1)}, s32[1,128]{1,0:T(1,128)}, u32[]{:S(2)}) copy-start(s32[1,128]{1,0:T(1,128)} %param.43) | copy-start | bytes 1540
  49.3 6.2 %copy-start.28 = (s32[1,128]{1,0:T(1,128)S(1)}, s32[1,128]{1,0:T(1,128)}, u32[]{:S(2)}) copy-start(s32[1,128]{1,0:T(1,128)} %param.42) | copy-start | bytes 1540
  49.3 38.8 %copy-start.1 = (bf16[5120,256]{1,0:T(8,128)(2,1)S(1)}, bf16[5120,256]{1,0:T(8,128)(2,1)}, u32[]{:S(2)}) copy-start(bf16[5120,256]{1,0:T(8,128)(2,1)} %bq.1) | copy-start | bytes 7864324
  49.3 38.8 %copy-start.6 = (bf16[32,64,128]{2,1,0:T(8,128)(2,1)S(1)}, bf16[32,64,128]{2,1,0:T(8,128)(2,1)}, u32[]{:S(2)}) copy-start(bf16[32,64,128]{2,1,0:T(8,128)(2,1)} %param.38) | copy-start | bytes 1572868
  49.3 38.7 %all-to-all-start.1 = ((bf16[16,320,128]{2,1,0:T(8,128)(2,1)}), bf16[16,320,128]{2,1,0:T(8,128)(2,1)}, u32[]{:S(2)}, u32[]{:S(2)}) async-start(bf16[16,320,128]{2,1,0:T(8,128)(2,1)} %broadcast_in_dim.13), calls=%async_computation.1 | async-start | bytes 2621440 | tf_op jit(solution)/shard_map/all_to_all | solution.py:330
  88.1 1.4 copy-start.4
  89.4 0.7 copy-start.15
  96.8 1.1 copy-start.8
  109.0 3.2 %copy-start.2 = (bf16[5120,768]{1,0:T(8,128)(2,1)S(1)}, bf16[5120,768]{1,0:T(8,128)(2,1)}, u32[]{:S(2)}) copy-start(bf16[5120,768]{1,0:T(8,128)(2,1)} %all-gather.2.cloned.1.call-done.weight) | copy-start | bytes 23592964
  112.2 1.3 copy-start.9
  113.5 1.0 copy-start.10
  (8 other events, 5.3 us)
Sparse Core Ops, SparseCore 0:
  47.9 61.0 all-gather.1

commit v2 on v1

--- a/solution.py
+++ b/solution.py
@@ -1,5 +1,3 @@
-import functools
-
 import jax
 import jax.numpy as jnp
 from jax import lax
@@ -25,11 +23,50 @@
 THETA = 1000000.0
 SCALE = HEAD ** (-0.5)
 NEG = -1e30
-CHUNKS = 8
-CHUNK = WIDTH // CHUNKS
+TILES = ((0, 128), (128, 128), (256, 64))
+BLOCK = 448
+THIRDS = ((0, 112), (112, 112), (224, 96))
 F32 = jnp.float32
 BF16 = jnp.bfloat16
 VMEM = pltpu.VMEM
+
+
+PIECES = []
+PLACES = []
+for _dc in range(2):
+    for _dx in range(2):
+        for _dy in range(4):
+            _rows = THIRDS if (_dx, _dy) == (1, 2) else ((0, OWN),)
+            PLACES.append(((_dx, _dy, _dc), tuple(range(len(PIECES), len(PIECES) + len(_rows)))))
+            PIECES += [((_dx, _dy, _dc), r) for r in _rows]
+
+
+def fetch(value, dx, dy, dc):
+    pairs = []
+    for i in range(16):
+        x, y, c = i >> 3, (i >> 1) & 3, i & 1
+        pairs.append((((x ^ dx) << 3) + (((y + dy) & 3) << 1) + (c ^ dc), i))
+    return lax.ppermute(value, "replica", pairs)
+
+
+def gather_pieces(own):
+    held = {(0, 0): [own]}
+    over = fetch(own, 1, 0, 0)
+    up = fetch(own, 0, 1, 0)
+    down = fetch(own, 0, -1, 0)
+    held[1, 0], held[0, 1], held[0, 3] = [over], [up], [down]
+    far = fetch(up, 0, 1, 0)
+    over_up = fetch(up, 1, 0, 0)
+    over_down = fetch(over, 0, -1, 0)
+    held[0, 2], held[1, 1], held[1, 3] = [far], [over_up], [over_down]
+    cuts = [slice(at, at + n) for at, n in THIRDS]
+    held[1, 2] = [
+        fetch(far[cuts[0]], 1, 0, 0),
+        fetch(over_up[cuts[1]], 0, 1, 0),
+        fetch(over_down[cuts[2]], 0, -1, 0),
+    ]
+    same = [v for dx in range(2) for dy in range(4) for v in held[dx, dy]]
+    return same + [fetch(v, 0, 0, 1) for v in same]
 
 
 def factors(codes):
@@ -39,30 +76,36 @@
     return out
 
 
-def pack_kernel(dq, sq, dk, sk, dv, sv, do, so, out, buf):
-    fq, fk, fv, fo = factors(sq[...]), factors(sk[...]), factors(sv[...]), factors(so[...])
-
-    def piece(codes, factor, head):
-        return codes[:, head * HEAD : (head + 1) * HEAD].astype(F32) * factor[:, head : head + 1]
-
+def pack_kernel(hidden, dq, dk, dv, do, scales, out, buf):
+    factor = factors(scales[...])
+
+    def piece(codes, head, column):
+        value = codes[:, head * HEAD : (head + 1) * HEAD].astype(F32)
+        return value * factor[:, column : column + 1]
+
+    for at, n in TILES:
+        buf[at : at + n, :] = hidden[:, at : at + n].astype(F32).T
+    mine = buf[0:OWN, :].astype(BF16)
+    buf[OWN + 6 * CUT : BLOCK, :] = jnp.zeros((BLOCK - OWN - 6 * CUT, HEAD), F32)
     for dest in range(PARTS):
         half = dest // 2
         pieces = (
-            piece(dq, fq, 2 * dest),
-            piece(dq, fq, 2 * dest + 1),
-            piece(dk, fk, half),
-            piece(dv, fv, half),
-            piece(do, fo, 2 * dest),
-            piece(do, fo, 2 * dest + 1),
+            piece(dq, 2 * dest, 2 * dest),
+            piece(dq, 2 * dest + 1, 2 * dest + 1),
+            piece(dk, half, 32 + half),
+            piece(dv, half, 40 + half),
+            piece(do, 2 * dest, 48 + 2 * dest),
+            piece(do, 2 * dest + 1, 49 + 2 * dest),
         )
         for c, value in enumerate(pieces):
-            buf[dest % 2, CUT * c : CUT * (c + 1), :] = value
-        out[dest] = buf[dest % 2].astype(BF16)
+            buf[OWN + CUT * c : OWN + CUT * (c + 1), :] = value
+        out[dest, 0:OWN, :] = mine
+        out[dest, OWN:BLOCK, :] = buf[OWN:BLOCK, :].astype(BF16)
 
 
 def refresh_kernel(block, recv, bq, bk, bv, bo, out, buf, delta):
     for src in range(PARTS):
-        buf[src % 2] = recv[src].astype(F32)
+        buf[src % 2] = recv[src, OWN:BLOCK, :].astype(F32)
         for c in range(6):
             delta[CUT * src : CUT * (src + 1), HEAD * c : HEAD * (c + 1)] = buf[
                 src % 2, CUT * c : CUT * (c + 1), :
@@ -135,22 +178,24 @@
 
 
 def prepare_kernel(
-    xt, gain, qg, kg, cosine, sine, lens, token, place, base_q, base_k, cache,
+    recv, gain, qg, kg, cosine, sine, lens, token, place, base_q, base_k, cache,
     normed, keys_out, one_q_out, one_f_out, old_out,
-    total, query, lse,
+    query, lse,
 ):
-    total[...] = jnp.zeros_like(total)
-    for k in range(WIDTH // HEAD):
-        x = xt[k * HEAD : (k + 1) * HEAD, :].astype(F32)
-        total[...] += jnp.sum(x * x, axis=0, keepdims=True)
-    scale = lax.rsqrt(total[...] * (1.0 / WIDTH) + EPSILON)
-    for k in range(WIDTH // HEAD):
-        x = xt[k * HEAD : (k + 1) * HEAD, :].astype(F32) * scale
-        normed[:, k * HEAD : (k + 1) * HEAD] = (
-            x.T * gain[:, k * HEAD : (k + 1) * HEAD]
-        ).astype(BF16)
-    raw = dot(normed[...], base_q[...])
-    raw_k = dot(normed[...], base_k[...])
+    total = jnp.zeros((1, TOKENS), F32)
+    for src in range(PARTS):
+        x = recv[src, 0:OWN, :].astype(F32)
+        total = total + jnp.sum(x * x, axis=0, keepdims=True)
+    scale = lax.rsqrt(total * (1.0 / WIDTH) + EPSILON)
+    for src in range(PARTS):
+        for at, n in TILES:
+            x = recv[src, at : at + n, :].astype(F32) * scale
+            normed[src, :, at : at + n] = (x.T * gain[src : src + 1, at : at + n]).astype(BF16)
+    raw = jnp.zeros((TOKENS, 256), F32)
+    raw_k = jnp.zeros((TOKENS, HEAD), F32)
+    for src in range(PARTS):
+        raw = raw + dot(normed[src], base_q[src * OWN : (src + 1) * OWN, :])
+        raw_k = raw_k + dot(normed[src], base_k[src * OWN : (src + 1) * OWN, :])
     cos, sin = cosine[...], sine[...]
     for h in range(2):
         query[h * TOKENS : (h + 1) * TOKENS, :] = (
@@ -182,24 +227,31 @@
 
 
 def main_kernel(
-    normed, weight, qg, kg, cosine, sine, lens, cache, values, keys, one_q, one_f, old,
-    out,
-    held, query, lse, mixed, sems,
+    here, normed, qg, kg, cosine, sine, lens, cache_hbm, values_hbm, keys, one_q, one_f, old,
+    *rest,
 ):
-    copies = [
-        pltpu.make_async_copy(
-            weight.at[pl.ds(c * CHUNK, CHUNK)], held.at[pl.ds(c * CHUNK, CHUNK)], sems.at[c]
-        )
-        for c in range(CHUNKS)
-    ]
+    pieces = rest[: len(PIECES)]
+    out, cache, values, query, lse, mixed, sems = rest[len(PIECES) :]
+    copies = (
+        pltpu.make_async_copy(cache_hbm, cache, sems.at[0]),
+        pltpu.make_async_copy(values_hbm, values, sems.at[1]),
+    )
     for copy in copies:
         copy.start()
+    me = here[0]
+
+    def owner(place):
+        dx, dy, dc = place
+        return (((me >> 3) ^ dx) << 3) + ((((me >> 1) + dy) & 3) << 1) + ((me & 1) ^ dc)
+
     raw = jnp.zeros((TOKENS, 512), F32)
-    for c in range(CHUNKS):
-        copies[c].wait()
-        raw = raw + dot(
-            normed[:, c * CHUNK : (c + 1) * CHUNK], held[c * CHUNK : (c + 1) * CHUNK, 0:512]
-        )
+    for place, parts in PLACES:
+        block = owner(place)
+        if len(parts) == 1:
+            raw = raw + dot(normed[block], pieces[parts[0]][:, 0:512])
+        else:
+            whole_block = jnp.concatenate([pieces[i][:, 0:512] for i in parts], axis=0)
+            raw = raw + dot(normed[block], whole_block)
     cos, sin = cosine[...], sine[...]
     for h in range(2):
         query[h * TOKENS : (h + 1) * TOKENS, :] = (
@@ -209,6 +261,8 @@
         )
     fresh = head_norm_rotate(raw[:, 256:384], kg[...], cos, sin).astype(BF16)
     fresh_v = raw[:, 384:512].astype(BF16)
+    for copy in copies:
+        copy.wait()
     for g in range(GROUPS):
         at = slice(g * GROUP * CTX, (g + 1) * GROUP * CTX)
         past, new, total, log_sum = group_scores(g, query, cache[at, :], fresh, lens)
@@ -217,9 +271,12 @@
         mix = mix + dot((new / total).astype(BF16), fresh_v)
         put_groups(g, mixed, mix)
     attended = jnp.concatenate([mixed[0:TOKENS, :], mixed[TOKENS:, :]], axis=1).astype(BF16)
-    for p in range(PARTS):
-        part = dot_nt(held[p * OWN : (p + 1) * OWN, 512:768], attended)
-        out[p, 0:OWN, :] = part.astype(BF16)
+    for place, parts in PLACES:
+        block = owner(place)
+        for i in parts:
+            at, n = PIECES[i][1]
+            part = dot_nt(pieces[i][:, 512:768], attended)
+            out[block, at : at + n, :] = part.astype(BF16)
     now = sample_logp(query, keys[...] + dot(one_f[...], fresh), one_q[...], lse)
     term = (now[0] - old[0]) + (now[1] - old[1])
     line = term.T[0:1, :]
@@ -251,6 +308,10 @@
 
 def shape(dims, dtype):
     return jax.ShapeDtypeStruct(dims, dtype)
+
+
+def block(dims):
+    return pl.BlockSpec(dims, lambda i: (0,) * len(dims))
 
 
 def whole():
@@ -281,29 +342,22 @@
     stale_steps,
     stale_back,
 ):
+    scales = jnp.concatenate([scale_query, key_scale_codes, value_scale_codes, scale_output], axis=1)
     packed = pl.pallas_call(
         pack_kernel,
         name="pack",
-        out_shape=shape((PARTS, 6 * CUT, HEAD), BF16),
-        in_specs=[whole()] * 8,
+        out_shape=shape((PARTS, BLOCK, HEAD), BF16),
+        grid=(1,),
+        in_specs=[block((TOKENS, OWN)), block((CUT, 4096)), block((CUT, 1024)), block((CUT, 1024)), block((CUT, 4096)), block((CUT, 80))],
         out_specs=whole(),
-        scratch_shapes=[VMEM((2, 6 * CUT, HEAD), F32)],
-        compiler_params=params(16),
-    )(
-        delta_query,
-        scale_query,
-        key_delta_codes,
-        key_scale_codes,
-        value_delta_codes,
-        value_scale_codes,
-        delta_output,
-        scale_output,
-    )
+        scratch_shapes=[VMEM((BLOCK, HEAD), F32)],
+        compiler_params=params(8),
+    )(hidden.reshape(TOKENS, OWN), delta_query, key_delta_codes, value_delta_codes, delta_output, scales)
     arrived = lax.all_to_all(packed, "shard", split_axis=0, concat_axis=0, tiled=False)
-    arrived, hidden, lengths, stale_rows, stale_steps, stale_back = lax.optimization_barrier(
-        (arrived, hidden, lengths, stale_rows, stale_steps, stale_back)
-    )
-    block = lax.axis_index("replica").astype(jnp.int32).reshape(1)
+    arrived, lengths, stale_rows, stale_steps, stale_back = lax.optimization_barrier(
+        (arrived, lengths, stale_rows, stale_steps, stale_back)
+    )
+    here = lax.axis_index("replica").astype(jnp.int32).reshape(1)
     fresh_rows = pl.pallas_call(
         refresh_kernel,
         name="refresh",
@@ -312,23 +366,18 @@
             num_scalar_prefetch=1,
             grid=(1,),
             in_specs=[
-                pl.BlockSpec((PARTS, 6 * CUT, HEAD), lambda i, b: (0, 0, 0)),
+                whole(),
                 pl.BlockSpec((OWN, 256), lambda i, b: (b[0], 0)),
                 pl.BlockSpec((OWN, 128), lambda i, b: (b[0], 0)),
                 pl.BlockSpec((OWN, 128), lambda i, b: (b[0], 0)),
                 pl.BlockSpec((OWN, 256), lambda i, b: (b[0], 0)),
             ],
-            out_specs=pl.BlockSpec((OWN, COLS), lambda i, b: (0, 0)),
-            scratch_shapes=[VMEM((2, 6 * CUT, HEAD), F32), VMEM((OWN, COLS), F32)],
+            out_specs=whole(),
+            scratch_shapes=[VMEM((2, BLOCK - OWN, HEAD), F32), VMEM((OWN, COLS), F32)],
         ),
-        compiler_params=params(16),
-    )(block, arrived, base_query, base_key, base_value, base_output)
-    weight = lax.all_gather(fresh_rows, "replica", axis=0, tiled=True)
-
-    mine = hidden.reshape(TOKENS, OWN).T
-    spread = jnp.broadcast_to(mine[None], (PARTS, OWN, TOKENS))
-    xt = lax.all_to_all(spread, "shard", split_axis=0, concat_axis=0, tiled=False)
-    xt = xt.reshape(WIDTH, TOKENS)
+        compiler_params=params(8),
+    )(here, arrived, base_query, base_key, base_value, base_output)
+    pieces = gather_pieces(fresh_rows)
 
     position = (lengths[None, :] + jnp.arange(STEPS)[:, None]).reshape(TOKENS)
     freq = THETA ** (-(jnp.arange(HEAD // 2).astype(F32) * 2.0) / HEAD)
@@ -359,40 +408,58 @@
         prepare_kernel,
         name="prepare",
         out_shape=(
-            shape((TOKENS, WIDTH), BF16),
+            shape((PARTS, TOKENS, OWN), BF16),
             shape((TOKENS, HEAD), F32),
             shape((TOKENS, TOKENS), BF16),
             shape((TOKENS, TOKENS), BF16),
             shape((2, TOKENS, HEAD), F32),
         ),
-        in_specs=[whole()] * 12,
+        grid=(1,),
+        in_specs=[
+            whole(),
+            block((PARTS, OWN)),
+            block((1, HEAD)),
+            block((1, HEAD)),
+            block((TOKENS, HEAD)),
+            block((TOKENS, HEAD)),
+            block((ROWS, HEAD)),
+            block((1, TOKENS)),
+            block((1, TOKENS)),
+            block((WIDTH, 256)),
+            block((WIDTH, HEAD)),
+            block((ROWS * CTX, HEAD)),
+        ],
         out_specs=(whole(),) * 5,
-        scratch_shapes=[
-            VMEM((1, TOKENS), F32),
-            VMEM((2 * TOKENS, HEAD), F32),
-            VMEM((2 * TOKENS, HEAD), F32),
-        ],
-        compiler_params=params(32),
+        scratch_shapes=[VMEM((2 * TOKENS, HEAD), F32), VMEM((2 * TOKENS, HEAD), F32)],
+        compiler_params=params(20),
     )(
-        xt, norm_gain.reshape(1, WIDTH), query_gain, key_gain, cosine, sine, lens, token, place,
+        arrived, norm_gain.reshape(PARTS, OWN), query_gain, key_gain, cosine, sine, lens, token, place,
         base_query, base_key, cache,
     )
 
+    anywhere = pl.BlockSpec(memory_space=pl.ANY)
     parts = pl.pallas_call(
         main_kernel,
         name="attend",
         out_shape=shape((PARTS, OWN + TAIL, TOKENS), BF16),
-        in_specs=[whole(), pl.BlockSpec(memory_space=pl.ANY)] + [whole()] * 11,
+        in_specs=[pl.BlockSpec(memory_space=pltpu.SMEM)]
+        + [whole()] * 6
+        + [anywhere] * 2
+        + [whole()] * (4 + len(PIECES)),
         out_specs=whole(),
         scratch_shapes=[
-            VMEM((WIDTH, COLS), BF16),
+            VMEM((ROWS * CTX, HEAD), BF16),
+            VMEM((ROWS * CTX, HEAD), BF16),
             VMEM((2 * TOKENS, HEAD), F32),
             VMEM((2 * TOKENS, HEAD), F32),
             VMEM((2 * TOKENS, HEAD), F32),
-            pltpu.SemaphoreType.DMA((CHUNKS,)),
+            pltpu.SemaphoreType.DMA((2,)),
         ],
-        compiler_params=params(40),
-    )(normed, weight, query_gain, key_gain, cosine, sine, lens, cache, values, keys, one_q, one_f, old)
+        compiler_params=params(16),
+    )(
+        here, normed, query_gain, key_gain, cosine, sine, lens, cache, values, keys, one_q, one_f, old,
+        *pieces,
+    )
 
     landed = lax.all_to_all(parts, "shard", split_axis=0, concat_axis=0, tiled=False)
     out, ratio = pl.pallas_call(

time: 177 us -> 177 us (level)
  waiting for transfers between devices: 58.7 us -> 77.9 us
  between operations: 14.2 us -> 0.82 us
  local copies, waits for them, and re-layouts: 25.7 us -> 16.8 us
  starting transfers between devices: 16.6 us -> 23.8 us
    ppermute x0 -> x19, waiting for transfers between devices: none -> 33.4 us  [fetch(): return lax.ppermute(value, 'replica', pairs)]
    all_to_all x1 -> x0, waiting for transfers between devices: 31.9 us -> none  [local(): lax.all_to_all(spread, 'shard', split_axis=0, concat_axis=0, tiled=False)]
    all_to_all x1, waiting for transfers between devices: 15.8 us -> 44.5 us  [local(): lax.all_to_all(packed, 'shard', split_axis=0, concat_axis=0, tiled=False)]
    ppermute x0 -> x19, starting transfers between devices: none -> 12.6 us  [fetch(): return lax.ppermute(value, 'replica', pairs)]
    all_gather x1 -> x0, waiting for transfers between devices: 11 us -> none  [local(): weight = lax.all_gather(fresh_rows, 'replica', axis=0, tiled=True)]
    unnamed x60 -> x42, local copies, waits for them, and re-layouts: 24.1 us -> 13.7 us
    all_to_all x1 -> x0, starting transfers between devices: 5.52 us -> none  [local(): lax.all_to_all(spread, 'shard', split_axis=0, concat_axis=0, tiled=False)]
    slice x0 -> x3, local copies, waits for them, and re-layouts: none -> 2.84 us  [the longest x1 0.98 us: gather_pieces(): over_down[cuts[2]]]
  transfers between devices with their start and end apart: 3 -> 20, of which waited for: 3 -> 7; matrix products, arithmetic and copies ran while one was open for 2% -> 2% of each run, Pallas kernels for 2% -> 2%
where the time goes in v2:
time: 177 us
  waiting for transfers between devices  77.9 us (44%)
  blocking collectives  43.5 us (25%)
  starting transfers between devices  23.8 us (13%)
  local copies, waits for them, and re-layouts  16.8 us (9%)
  Pallas kernels  12.4 us (7%)
    all_to_all x1, waiting for transfers between devices, local(): lax.all_to_all(packed, 'shard', split_axis=0, concat_axis=0, tiled=False)  44.5 us
    all_to_all x1, blocking collectives, local(): lax.all_to_all(parts, 'shard', split_axis=0, concat_axis=0, tiled=False)  43.5 us
    ppermute x19, waiting for transfers between devices, fetch(): return lax.ppermute(value, 'replica', pairs)  33.4 us
    unnamed x42, local copies, waits for them, and re-layouts  13.7 us
    ppermute x19, starting transfers between devices, fetch(): return lax.ppermute(value, 'replica', pairs)  12.6 us
    all_to_all x1, starting transfers between devices, local(): lax.all_to_all(packed, 'shard', split_axis=0, concat_axis=0, tiled=False)  11.2 us
    pallas_call x1, Pallas kernels, local(): pl.pallas_call(main_kernel, name='attend', out_shape=shape((PARTS, OWN +...  6.83 us
  transfers between devices with their start and end apart: 20, of which 7 were waited for; matrix products, arithmetic and copies ran while one was open for 2% of the time, Pallas kernels for 2%

profile of v2, /device:TPU:32, one launch (start us, length us, event | category | flops | bytes accessed | tf_op | source)
XLA Modules:
  0.0 176.6 jit_solution(3317920763698314697)
XLA Ops:
  8.0 1.2 copy-done.2
  9.2 11.2 %all-to-all-start = ((bf16[16,448,128]{2,1,0:T(8,128)(2,1)}), bf16[16,448,128]{2,1,0:T(8,128)(2,1)S(1)}, u32[]{:S(2)}, u32[]{:S(2)}) async-start(bf16[16,448,128]{2,1,0:T(8,128)(2,1)} %copy-done.2), calls=%async_computation | async-start | bytes 3670016 | tf_op jit(solution)/shard_map/all_to_all | solution.py:356
  20.4 44.5 %all-to-all-done.recv = bf16[16,448,128]{2,1,0:T(8,128)(2,1)S(1)} async-done(((bf16[16,448,128]{2,1,0:T(8,128)(2,1)}), bf16[16,448,128]{2,1,0:T(8,128)(2,1)S(1)}, u32[]{:S(2)}, u32[]{:S(2)}) %all-to-all-start) | async-done | bytes 1835040 | tf_op jit(solution)/shard_map/all_to_all | solution.py:356
  64.9 1.7 copy-done
  66.6 1.7 copy-done.4
  68.4 1.3 copy-done.6
  69.7 1.0 refresh.1.rest_0_
  71.4 3.0 %collective-permute-start = (bf16[320,768]{1,0:T(8,128)(2,1)}, bf16[320,768]{1,0:T(8,128)(2,1)}, u32[]{:S(2)}, u32[]{:S(2)}) collective-permute-start(bf16[320,768]{1,0:T(8,128)(2,1)} %refresh.1.rest_0_), channel_id=1, source_target_pairs={{32,0},{48,16},{64,32},{80,48},{96,64},{112,80},{0,96},{16,112},{1... | collective-permute-start | bytes 1474568 | tf_op jit(solution)/shard_map/ppermute | solution.py:49
  74.4 8.2 %collective-permute-done.3.rest_4_ = bf16[320,768]{1,0:T(8,128)(2,1)} collective-permute-done((bf16[320,768]{1,0:T(8,128)(2,1)}, bf16[320,768]{1,0:T(8,128)(2,1)}, u32[]{:S(2)}, u32[]{:S(2)}) %collective-permute-start.3) | collective-permute-done | bytes 491552 | tf_op jit(solution)/shard_map/ppermute | solution.py:49
  82.6 1.6 collective-permute-start.7
  85.4 4.0 %collective-permute-done.2.rest_3_ = bf16[320,768]{1,0:T(8,128)(2,1)} collective-permute-done((bf16[320,768]{1,0:T(8,128)(2,1)}, bf16[320,768]{1,0:T(8,128)(2,1)}, u32[]{:S(2)}, u32[]{:S(2)}) %collective-permute-start.2) | collective-permute-done | bytes 491552 | tf_op jit(solution)/shard_map/ppermute | solution.py:49
  89.4 8.0 %collective-permute-done.7.rest_9_ = bf16[320,768]{1,0:T(8,128)(2,1)} collective-permute-done((bf16[320,768]{1,0:T(8,128)(2,1)}, bf16[320,768]{1,0:T(8,128)(2,1)}, u32[]{:S(2)}, u32[]{:S(2)}) %collective-permute-start.7) | collective-permute-done | bytes 491552 | tf_op jit(solution)/shard_map/ppermute | solution.py:49
  97.9 1.0 slice.14
  98.9 0.9 slice.13
  99.9 1.7 collective-permute-start.8
  101.6 1.6 collective-permute-start.6
  103.7 8.0 %collective-permute-done.1.rest_2_ = bf16[320,768]{1,0:T(8,128)(2,1)} collective-permute-done((bf16[320,768]{1,0:T(8,128)(2,1)}, bf16[320,768]{1,0:T(8,128)(2,1)}, u32[]{:S(2)}, u32[]{:S(2)}) %collective-permute-start.1) | collective-permute-done | bytes 491552 | tf_op jit(solution)/shard_map/ppermute | solution.py:49
  112.0 0.9 slice.12
  113.0 1.5 collective-permute-start.5
  115.1 4.7 %collective-permute-done.5.rest_6_ = bf16[112,768]{1,0:T(8,128)(2,1)S(1)} collective-permute-done((bf16[112,768]{1,0:T(8,128)(2,1)S(1)}, bf16[112,768]{1,0:T(8,128)(2,1)S(1)}, u32[]{:S(2)}, u32[]{:S(2)}) %collective-permute-start.5) | collective-permute-done | bytes 172064 | tf_op jit(solution)/shard_map/ppermute | solution.py:49
  120.6 1.7 copy-done.1
  122.3 3.0 %prepare.1 = (bf16[16,128,320]{2,1,0:T(8,128)(2,1)S(1)}, f32[128,128]{1,0:T(8,128)S(1)}, bf16[128,128]{1,0:T(8,128)(2,1)S(1)}, bf16[128,128]{1,0:T(8,128)(2,1)S(1)}, f32[2,128,128]{2,1,0:T(8,128)S(1)}) custom-call(bf16[16,448,128]{2,1,0:T(8,128)(2,1)S(1)} %all-to-all-done.recv, f32[16,320]{1,0:T(8,128)S(1)} %reshape.55.gain, f32[1,128]{1,0:T(1,128)S(1)} %bitcast.26, ...), custom_call_target="tpu_custom_call" | custom-call | tf_op jit(solution)/shard_map/prepare/pallas_call | solution.py:407
  125.4 6.8 %attend.1 = bf16[16,336,128]{2,1,0:T(8,128)(2,1)S(1)} custom-call(s32[1]{0:T(128)} %bitcast.block.here, bf16[16,128,320]{2,1,0:T(8,128)(2,1)S(1)} %get-tuple-element.19.normed, f32[1,128]{1,0:T(1,128)S(1)} %bitcast.27, f32[1,128]{1,0:T(1,128)S(1)} %bitcast.29, f32[128,128]{1,0:T(8,128)S(1)} %get-tuple-element.31.cosine, ...), custom_call_target="tpu_custom_call" | custom-call | tf_op jit(solution)/shard_map/attend/pallas_call | solution.py:441
  132.3 43.5 %all_to_all.10.recv = bf16[16,336,128]{2,1,0:T(8,128)(2,1)S(1)} all-to-all(bf16[16,336,128]{2,1,0:T(8,128)(2,1)S(1)} %attend.1), channel_id=1, replica_groups=mesh['replica'=16,'shard'=16] {'shard'}, dimensions={0} | all-to-all | bytes 2752512 | tf_op jit(solution)/shard_map/all_to_all | solution.py:464
  (77 shorter events, 12.8 us)
Async XLA Ops:
  9.2 55.7 %copy-start.3 = (bf16[5120,128]{1,0:T(8,128)(2,1)S(1)}, bf16[5120,128]{1,0:T(8,128)(2,1)}, u32[]{:S(2)}) copy-start(bf16[5120,128]{1,0:T(8,128)(2,1)} %bk.1) | copy-start | bytes 3932164
  9.2 55.7 %all-to-all-start = ((bf16[16,448,128]{2,1,0:T(8,128)(2,1)}), bf16[16,448,128]{2,1,0:T(8,128)(2,1)S(1)}, u32[]{:S(2)}, u32[]{:S(2)}) async-start(bf16[16,448,128]{2,1,0:T(8,128)(2,1)} %copy-done.2), calls=%async_computation | async-start | bytes 3670016 | tf_op jit(solution)/shard_map/all_to_all | solution.py:356
  69.7 50.7 %copy-start.18 = (s32[1,128]{1,0:T(1,128)S(1)}, s32[1,128]{1,0:T(1,128)}, u32[]{:S(2)}) copy-start(s32[1,128]{1,0:T(1,128)} %param.43) | copy-start | bytes 1540
  69.7 50.7 %copy-start.19 = (s32[1,128]{1,0:T(1,128)S(1)}, s32[1,128]{1,0:T(1,128)}, u32[]{:S(2)}) copy-start(s32[1,128]{1,0:T(1,128)} %param.42) | copy-start | bytes 1540
  70.8 49.8 %copy-start.14 = (f32[128]{0:T(128)S(1)}, f32[128]{0:T(128)}, u32[]{:S(2)}) copy-start(f32[128]{0:T(128)} %param.25) | copy-start | bytes 1540
  70.8 11.8 %collective-permute-start.3 = (bf16[320,768]{1,0:T(8,128)(2,1)}, bf16[320,768]{1,0:T(8,128)(2,1)}, u32[]{:S(2)}, u32[]{:S(2)}) collective-permute-start(bf16[320,768]{1,0:T(8,128)(2,1)} %refresh.1.rest_0_), channel_id=1, source_target_pairs={{128,0},{144,16},{160,32},{176,48},{192,64},{208,80},{224,96},{240... | collective-permute-start | bytes 1474568 | tf_op jit(solution)/shard_map/ppermute | solution.py:49
  71.4 12.8 %collective-permute-start = (bf16[320,768]{1,0:T(8,128)(2,1)}, bf16[320,768]{1,0:T(8,128)(2,1)}, u32[]{:S(2)}, u32[]{:S(2)}) collective-permute-start(bf16[320,768]{1,0:T(8,128)(2,1)} %refresh.1.rest_0_), channel_id=1, source_target_pairs={{32,0},{48,16},{64,32},{80,48},{96,64},{112,80},{0,96},{16,112},{1... | collective-permute-start | bytes 1474568 | tf_op jit(solution)/shard_map/ppermute | solution.py:49
  74.4 15.0 %collective-permute-start.2 = (bf16[320,768]{1,0:T(8,128)(2,1)}, bf16[320,768]{1,0:T(8,128)(2,1)}, u32[]{:S(2)}, u32[]{:S(2)}) collective-permute-start(bf16[320,768]{1,0:T(8,128)(2,1)} %refresh.1.rest_0_), channel_id=1, source_target_pairs={{96,0},{112,16},{0,32},{16,48},{32,64},{48,80},{64,96},{80,112},{2... | collective-permute-start | bytes 1474568 | tf_op jit(solution)/shard_map/ppermute | solution.py:49
  82.6 14.8 %collective-permute-start.7 = (bf16[320,768]{1,0:T(8,128)(2,1)}, bf16[320,768]{1,0:T(8,128)(2,1)}, u32[]{:S(2)}, u32[]{:S(2)}) collective-permute-start(bf16[320,768]{1,0:T(8,128)(2,1)} %collective-permute-done.3.rest_4_), channel_id=1, source_target_pairs={{96,0},{112,16},{0,32},{16,48},{32,64},{48,80},{64,96},{80,112},{2... | collective-permute-start | bytes 1474568 | tf_op jit(solution)/shard_map/ppermute | solution.py:49
  84.2 13.2 %collective-permute-start.4 = (bf16[320,768]{1,0:T(8,128)(2,1)}, bf16[320,768]{1,0:T(8,128)(2,1)}, u32[]{:S(2)}, u32[]{:S(2)}) collective-permute-start(bf16[320,768]{1,0:T(8,128)(2,1)} %collective-permute-done.rest_1_), channel_id=1, source_target_pairs={{128,0},{144,16},{160,32},{176,48},{192,64},{208,80},{224,96},{240... | collective-permute-start | bytes 1474568 | tf_op jit(solution)/shard_map/ppermute | solution.py:49
  84.9 15.0 %collective-permute-start.9 = (bf16[320,768]{1,0:T(8,128)(2,1)}, bf16[320,768]{1,0:T(8,128)(2,1)}, u32[]{:S(2)}, u32[]{:S(2)}) collective-permute-start(bf16[320,768]{1,0:T(8,128)(2,1)} %refresh.1.rest_0_), channel_id=1, source_target_pairs={{16,0},{0,16},{48,32},{32,48},{80,64},{64,80},{112,96},{96,112},{1... | collective-permute-start | bytes 1474568 | tf_op jit(solution)/shard_map/ppermute | solution.py:49
  84.9 16.7 %collective-permute-start.13 = (bf16[320,768]{1,0:T(8,128)(2,1)}, bf16[320,768]{1,0:T(8,128)(2,1)}, u32[]{:S(2)}, u32[]{:S(2)}) collective-permute-start(bf16[320,768]{1,0:T(8,128)(2,1)} %collective-permute-done.3.rest_4_), channel_id=1, source_target_pairs={{16,0},{0,16},{48,32},{32,48},{80,64},{64,80},{112,96},{96,112},{1... | collective-permute-start | bytes 1474568 | tf_op jit(solution)/shard_map/ppermute | solution.py:49
  89.4 13.8 %collective-permute-start.12 = (bf16[320,768]{1,0:T(8,128)(2,1)}, bf16[320,768]{1,0:T(8,128)(2,1)}, u32[]{:S(2)}, u32[]{:S(2)}) collective-permute-start(bf16[320,768]{1,0:T(8,128)(2,1)} %collective-permute-done.2.rest_3_), channel_id=1, source_target_pairs={{16,0},{0,16},{48,32},{32,48},{80,64},{64,80},{112,96},{96,112},{1... | collective-permute-start | bytes 1474568 | tf_op jit(solution)/shard_map/ppermute | solution.py:49
  97.4 5.8 %collective-permute-start.10 = (bf16[320,768]{1,0:T(8,128)(2,1)}, bf16[320,768]{1,0:T(8,128)(2,1)}, u32[]{:S(2)}, u32[]{:S(2)}) collective-permute-start(bf16[320,768]{1,0:T(8,128)(2,1)} %collective-permute-done.rest_1_), channel_id=1, source_target_pairs={{16,0},{0,16},{48,32},{32,48},{80,64},{64,80},{112,96},{96,112},{1... | collective-permute-start | bytes 1474568 | tf_op jit(solution)/shard_map/ppermute | solution.py:49
  97.4 14.3 %collective-permute-start.1 = (bf16[320,768]{1,0:T(8,128)(2,1)}, bf16[320,768]{1,0:T(8,128)(2,1)}, u32[]{:S(2)}, u32[]{:S(2)}) collective-permute-start(bf16[320,768]{1,0:T(8,128)(2,1)} %collective-permute-done.rest_1_), channel_id=1, source_target_pairs={{32,0},{48,16},{64,32},{80,48},{96,64},{112,80},{0,96},{16,112},{1... | collective-permute-start | bytes 1474568 | tf_op jit(solution)/shard_map/ppermute | solution.py:49
  99.9 13.1 %collective-permute-start.8 = (bf16[96,768]{1,0:T(8,128)(2,1)S(1)}, bf16[96,768]{1,0:T(8,128)(2,1)S(1)}, u32[]{:S(2)}, u32[]{:S(2)}) collective-permute-start(bf16[96,768]{1,0:T(8,128)(2,1)S(1)} %slice.14), channel_id=1, source_target_pairs={{96,0},{112,16},{0,32},{16,48},{32,64},{48,80},{64,96},{80,112},{2... | collective-permute-start | bytes 442376 | tf_op jit(solution)/shard_map/ppermute | solution.py:49
  101.6 13.3 %collective-permute-start.6 = (bf16[112,768]{1,0:T(8,128)(2,1)S(1)}, bf16[112,768]{1,0:T(8,128)(2,1)S(1)}, u32[]{:S(2)}, u32[]{:S(2)}) collective-permute-start(bf16[112,768]{1,0:T(8,128)(2,1)S(1)} %slice.13), channel_id=1, source_target_pairs={{32,0},{48,16},{64,32},{80,48},{96,64},{112,80},{0,96},{16,112},{1... | collective-permute-start | bytes 516104 | tf_op jit(solution)/shard_map/ppermute | solution.py:49
  103.2 22.2 %collective-permute-start.18 = (bf16[320,768]{1,0:T(8,128)(2,1)}, bf16[320,768]{1,0:T(8,128)(2,1)S(1)}, u32[]{:S(2)}, u32[]{:S(2)}) collective-permute-start(bf16[320,768]{1,0:T(8,128)(2,1)} %collective-permute-done.7.rest_9_), channel_id=1, source_target_pairs={{16,0},{0,16},{48,32},{32,48},{80,64},{64,80},{112,96},{96,112},{1... | collective-permute-start | bytes 1474568 | tf_op jit(solution)/shard_map/ppermute | solution.py:49
  103.2 22.2 %collective-permute-start.14 = (bf16[320,768]{1,0:T(8,128)(2,1)}, bf16[320,768]{1,0:T(8,128)(2,1)S(1)}, u32[]{:S(2)}, u32[]{:S(2)}) collective-permute-start(bf16[320,768]{1,0:T(8,128)(2,1)} %collective-permute-done.4.rest_5_), channel_id=1, source_target_pairs={{16,0},{0,16},{48,32},{32,48},{80,64},{64,80},{112,96},{96,112},{1... | collective-permute-start | bytes 1474568 | tf_op jit(solution)/shard_map/ppermute | solution.py:49
  111.7 13.7 %collective-permute-start.11 = (bf16[320,768]{1,0:T(8,128)(2,1)}, bf16[320,768]{1,0:T(8,128)(2,1)S(1)}, u32[]{:S(2)}, u32[]{:S(2)}) collective-permute-start(bf16[320,768]{1,0:T(8,128)(2,1)} %collective-permute-done.1.rest_2_), channel_id=1, source_target_pairs={{16,0},{0,16},{48,32},{32,48},{80,64},{64,80},{112,96},{96,112},{1... | collective-permute-start | bytes 1474568 | tf_op jit(solution)/shard_map/ppermute | solution.py:49
  113.0 6.9 %collective-permute-start.5 = (bf16[112,768]{1,0:T(8,128)(2,1)S(1)}, bf16[112,768]{1,0:T(8,128)(2,1)S(1)}, u32[]{:S(2)}, u32[]{:S(2)}) collective-permute-start(bf16[112,768]{1,0:T(8,128)(2,1)S(1)} %slice.12), channel_id=1, source_target_pairs={{128,0},{144,16},{160,32},{176,48},{192,64},{208,80},{224,96},{240... | collective-permute-start | bytes 516104 | tf_op jit(solution)/shard_map/ppermute | solution.py:49
  114.9 4.9 %collective-permute-start.17 = (bf16[96,768]{1,0:T(8,128)(2,1)S(1)}, bf16[96,768]{1,0:T(8,128)(2,1)S(1)}, u32[]{:S(2)}, u32[]{:S(2)}) collective-permute-start(bf16[96,768]{1,0:T(8,128)(2,1)S(1)} %collective-permute-done.8.rest_8_), channel_id=1, source_target_pairs={{16,0},{0,16},{48,32},{32,48},{80,64},{64,80},{112,96},{96,112},{1... | collective-permute-start | bytes 442376 | tf_op jit(solution)/shard_map/ppermute | solution.py:49
  119.9 5.5 %collective-permute-start.16 = (bf16[112,768]{1,0:T(8,128)(2,1)S(1)}, bf16[112,768]{1,0:T(8,128)(2,1)S(1)}, u32[]{:S(2)}, u32[]{:S(2)}) collective-permute-start(bf16[112,768]{1,0:T(8,128)(2,1)S(1)} %collective-permute-done.6.rest_7_), channel_id=1, source_target_pairs={{16,0},{0,16},{48,32},{32,48},{80,64},{64,80},{112,96},{96,112},{1... | collective-permute-start | bytes 516104 | tf_op jit(solution)/shard_map/ppermute | solution.py:49
  119.9 5.5 %collective-permute-start.15 = (bf16[112,768]{1,0:T(8,128)(2,1)S(1)}, bf16[112,768]{1,0:T(8,128)(2,1)S(1)}, u32[]{:S(2)}, u32[]{:S(2)}) collective-permute-start(bf16[112,768]{1,0:T(8,128)(2,1)S(1)} %collective-permute-done.5.rest_6_), channel_id=1, source_target_pairs={{16,0},{0,16},{48,32},{32,48},{80,64},{64,80},{112,96},{96,112},{1... | collective-permute-start | bytes 516104 | tf_op jit(solution)/shard_map/ppermute | solution.py:49
  (16 other events, 189.1 us)

commit v3 on v2

--- a/solution.py
+++ b/solution.py
@@ -24,7 +24,7 @@
 SCALE = HEAD ** (-0.5)
 NEG = -1e30
 TILES = ((0, 128), (128, 128), (256, 64))
-BLOCK = 448
+BLOCK = 128
 THIRDS = ((0, 112), (112, 112), (224, 96))
 F32 = jnp.float32
 BF16 = jnp.bfloat16
@@ -55,9 +55,11 @@
     up = fetch(own, 0, 1, 0)
     down = fetch(own, 0, -1, 0)
     held[1, 0], held[0, 1], held[0, 3] = [over], [up], [down]
+    over, up, down = lax.optimization_barrier((over, up, down))
     far = fetch(up, 0, 1, 0)
     over_up = fetch(up, 1, 0, 0)
     over_down = fetch(over, 0, -1, 0)
+    far, over_up, over_down = lax.optimization_barrier((far, over_up, over_down))
     held[0, 2], held[1, 1], held[1, 3] = [far], [over_up], [over_down]
     cuts = [slice(at, at + n) for at, n in THIRDS]
     held[1, 2] = [
@@ -69,6 +71,24 @@
     return same + [fetch(v, 0, 0, 1) for v in same]
 
 
+def along_shard(value, dx, dz):
+    pairs = [((((i >> 3) ^ dx) << 3) + ((i + dz) & 7), i) for i in range(16)]
+    return lax.ppermute(value, "shard", pairs)
+
+
+def gather_pairs(own):
+    pair = jnp.concatenate([own, along_shard(own, 1, 0)], axis=0)
+    held = {0: pair}
+    up, down = pair, pair
+    for k in range(1, 5):
+        up = along_shard(up, 0, 1)
+        held[k] = up
+        if k < 4:
+            down = along_shard(down, 0, -1)
+            held[8 - k] = down
+    return [held[k] for k in range(8)]
+
+
 def factors(codes):
     out = jnp.ones(codes.shape, F32)
     for bit in range(5):
@@ -76,7 +96,7 @@
     return out
 
 
-def pack_kernel(hidden, dq, dk, dv, do, scales, out, buf):
+def pack_kernel(hidden, dq, dk, dv, do, scales, out, turned, buf):
     factor = factors(scales[...])
 
     def piece(codes, head, column):
@@ -84,9 +104,8 @@
         return value * factor[:, column : column + 1]
 
     for at, n in TILES:
-        buf[at : at + n, :] = hidden[:, at : at + n].astype(F32).T
-    mine = buf[0:OWN, :].astype(BF16)
-    buf[OWN + 6 * CUT : BLOCK, :] = jnp.zeros((BLOCK - OWN - 6 * CUT, HEAD), F32)
+        turned[at : at + n, :] = hidden[:, at : at + n].astype(F32).T.astype(BF16)
+    buf[6 * CUT : BLOCK, :] = jnp.zeros((BLOCK - 6 * CUT, HEAD), F32)
     for dest in range(PARTS):
         half = dest // 2
         pieces = (
@@ -98,14 +117,13 @@
             piece(do, 2 * dest + 1, 49 + 2 * dest),
         )
         for c, value in enumerate(pieces):
-            buf[OWN + CUT * c : OWN + CUT * (c + 1), :] = value
-        out[dest, 0:OWN, :] = mine
-        out[dest, OWN:BLOCK, :] = buf[OWN:BLOCK, :].astype(BF16)
+            buf[CUT * c : CUT * (c + 1), :] = value
+        out[dest] = buf[...].astype(BF16)
 
 
 def refresh_kernel(block, recv, bq, bk, bv, bo, out, buf, delta):
     for src in range(PARTS):
-        buf[src % 2] = recv[src, OWN:BLOCK, :].astype(F32)
+        buf[src % 2] = recv[src].astype(F32)
         for c in range(6):
             delta[CUT * src : CUT * (src + 1), HEAD * c : HEAD * (c + 1)] = buf[
                 src % 2, CUT * c : CUT * (c + 1), :
@@ -178,19 +196,23 @@
 
 
 def prepare_kernel(
-    recv, gain, qg, kg, cosine, sine, lens, token, place, base_q, base_k, cache,
-    normed, keys_out, one_q_out, one_f_out, old_out,
+    seat, gain, qg, kg, cosine, sine, lens, token, place, base_q, base_k, cache,
+    p0, p1, p2, p3, p4, p5, p6, p7, normed, keys_out, one_q_out, one_f_out, old_out,
     query, lse,
 ):
     total = jnp.zeros((1, TOKENS), F32)
-    for src in range(PARTS):
-        x = recv[src, 0:OWN, :].astype(F32)
+    pairs = (p0, p1, p2, p3, p4, p5, p6, p7)
+    for pair in pairs:
+        x = pair[...].astype(F32)
         total = total + jnp.sum(x * x, axis=0, keepdims=True)
     scale = lax.rsqrt(total * (1.0 / WIDTH) + EPSILON)
-    for src in range(PARTS):
-        for at, n in TILES:
-            x = recv[src, at : at + n, :].astype(F32) * scale
-            normed[src, :, at : at + n] = (x.T * gain[src : src + 1, at : at + n]).astype(BF16)
+    me = seat[0]
+    for step, pair in enumerate(pairs):
+        for half in range(2):
+            src = (((me >> 3) ^ half) << 3) + ((me + step) & 7)
+            for at, n in TILES:
+                x = pair[half * OWN + at : half * OWN + at + n, :].astype(F32) * scale
+                normed[src, :, at : at + n] = (x.T * gain[src, :, at : at + n]).astype(BF16)
     raw = jnp.zeros((TOKENS, 256), F32)
     raw_k = jnp.zeros((TOKENS, HEAD), F32)
     for src in range(PARTS):
@@ -343,19 +365,19 @@
     stale_back,
 ):
     scales = jnp.concatenate([scale_query, key_scale_codes, value_scale_codes, scale_output], axis=1)
-    packed = pl.pallas_call(
+    packed, turned = pl.pallas_call(
         pack_kernel,
         name="pack",
-        out_shape=shape((PARTS, BLOCK, HEAD), BF16),
+        out_shape=(shape((PARTS, BLOCK, HEAD), BF16), shape((OWN, TOKENS), BF16)),
         grid=(1,),
         in_specs=[block((TOKENS, OWN)), block((CUT, 4096)), block((CUT, 1024)), block((CUT, 1024)), block((CUT, 4096)), block((CUT, 80))],
-        out_specs=whole(),
+        out_specs=(whole(), whole()),
         scratch_shapes=[VMEM((BLOCK, HEAD), F32)],
         compiler_params=params(8),
     )(hidden.reshape(TOKENS, OWN), delta_query, key_delta_codes, value_delta_codes, delta_output, scales)
     arrived = lax.all_to_all(packed, "shard", split_axis=0, concat_axis=0, tiled=False)
-    arrived, lengths, stale_rows, stale_steps, stale_back = lax.optimization_barrier(
-        (arrived, lengths, stale_rows, stale_steps, stale_back)
+    arrived, turned, lengths, stale_rows, stale_steps, stale_back = lax.optimization_barrier(
+        (arrived, turned, lengths, stale_rows, stale_steps, stale_back)
     )
     here = lax.axis_index("replica").astype(jnp.int32).reshape(1)
     fresh_rows = pl.pallas_call(
@@ -373,11 +395,13 @@
                 pl.BlockSpec((OWN, 256), lambda i, b: (b[0], 0)),
             ],
             out_specs=whole(),
-            scratch_shapes=[VMEM((2, BLOCK - OWN, HEAD), F32), VMEM((OWN, COLS), F32)],
+            scratch_shapes=[VMEM((2, BLOCK, HEAD), F32), VMEM((OWN, COLS), F32)],
         ),
         compiler_params=params(8),
     )(here, arrived, base_query, base_key, base_value, base_output)
     pieces = gather_pieces(fresh_rows)
+    features = gather_pairs(turned)
+    seat = lax.axis_index("shard").astype(jnp.int32).reshape(1)
 
     position = (lengths[None, :] + jnp.arange(STEPS)[:, None]).reshape(TOKENS)
     freq = THETA ** (-(jnp.arange(HEAD // 2).astype(F32) * 2.0) / HEAD)
@@ -416,8 +440,8 @@
         ),
         grid=(1,),
         in_specs=[
-            whole(),
-            block((PARTS, OWN)),
+            pl.BlockSpec(memory_space=pltpu.SMEM),
+            block((PARTS, 1, OWN)),
             block((1, HEAD)),
             block((1, HEAD)),
             block((TOKENS, HEAD)),
@@ -428,13 +452,14 @@
             block((WIDTH, 256)),
             block((WIDTH, HEAD)),
             block((ROWS * CTX, HEAD)),
-        ],
+        ]
+        + [whole()] * 8,
         out_specs=(whole(),) * 5,
         scratch_shapes=[VMEM((2 * TOKENS, HEAD), F32), VMEM((2 * TOKENS, HEAD), F32)],
         compiler_params=params(20),
     )(
-        arrived, norm_gain.reshape(PARTS, OWN), query_gain, key_gain, cosine, sine, lens, token, place,
-        base_query, base_key, cache,
+        seat, norm_gain.reshape(PARTS, 1, OWN), query_gain, key_gain, cosine, sine, lens, token, place,
+        base_query, base_key, cache, *features,
     )
 
     anywhere = pl.BlockSpec(memory_space=pl.ANY)

time: 177 us -> 164 us (0.927)
  waiting for transfers between devices: 77.9 us -> 48.3 us
  starting transfers between devices: 23.8 us -> 33.3 us
  local copies, waits for them, and re-layouts: 16.8 us -> 22.4 us
    all_to_all x1, waiting for transfers between devices: 44.5 us -> 16.4 us  [local(): lax.all_to_all(packed, 'shard', split_axis=0, concat_axis=0, tiled=False)]
    ppermute x19, waiting for transfers between devices: 33.4 us -> 10.8 us  [fetch(): return lax.ppermute(value, 'replica', pairs)]
    ppermute x0 -> x8, waiting for transfers between devices: none -> 21.2 us  [along_shard(): return lax.ppermute(value, 'shard', pairs)]
    ppermute x0 -> x8, starting transfers between devices: none -> 10.2 us  [along_shard(): return lax.ppermute(value, 'shard', pairs)]
    unnamed x42 -> x67, local copies, waits for them, and re-layouts: 13.7 us -> 19.3 us
  transfers between devices with their start and end apart: 20 -> 28, of which waited for: 7 -> 13; matrix products, arithmetic and copies ran while one was open for 2% -> 2% of each run, Pallas kernels for 2% -> 3%
where the time goes in v3:
time: 164 us; the launch traced here: 163 us
  waiting for transfers between devices  48.3 us (29%)
  blocking collectives  42.8 us (26%)
  starting transfers between devices  33.3 us (20%)
  local copies, waits for them, and re-layouts  22.4 us (14%)
  Pallas kernels  13.7 us (8%)
    all_to_all x1, blocking collectives, local(): lax.all_to_all(parts, 'shard', split_axis=0, concat_axis=0, tiled=False)  42.8 us
    ppermute x8, waiting for transfers between devices, along_shard(): return lax.ppermute(value, 'shard', pairs)  21.2 us
    unnamed x67, local copies, waits for them, and re-layouts  19.3 us
    all_to_all x1, waiting for transfers between devices, local(): lax.all_to_all(packed, 'shard', split_axis=0, concat_axis=0, tiled=False)  16.4 us
    ppermute x19, starting transfers between devices, fetch(): return lax.ppermute(value, 'replica', pairs)  12 us
    all_to_all x1, starting transfers between devices, local(): lax.all_to_all(packed, 'shard', split_axis=0, concat_axis=0, tiled=False)  11 us
    ppermute x19, waiting for transfers between devices, fetch(): return lax.ppermute(value, 'replica', pairs)  10.8 us
    ppermute x8, starting transfers between devices, along_shard(): return lax.ppermute(value, 'shard', pairs)  10.2 us
  transfers between devices with their start and end apart: 28, of which 13 were waited for; matrix products, arithmetic and copies ran while one was open for 2% of the time, Pallas kernels for 3%

profile of v3, /device:TPU:32, one launch (start us, length us, event | category | flops | bytes accessed | tf_op | source)
XLA Modules:
  0.0 162.8 jit_solution(1529134336502153432)
XLA Ops:
  8.7 11.0 %all-to-all-start = ((bf16[16,128,128]{2,1,0:T(8,128)(2,1)}), bf16[16,128,128]{2,1,0:T(8,128)(2,1)S(1)}, u32[]{:S(2)}, u32[]{:S(2)}) async-start(bf16[16,128,128]{2,1,0:T(8,128)(2,1)} %get-tuple-element.22), calls=%async_computation | async-start | bytes 1048576 | tf_op jit(solution)/shard_map/all_to_all | solution.py:378
  19.8 16.4 %all-to-all-done.recv = bf16[16,128,128]{2,1,0:T(8,128)(2,1)S(1)} async-done(((bf16[16,128,128]{2,1,0:T(8,128)(2,1)}), bf16[16,128,128]{2,1,0:T(8,128)(2,1)S(1)}, u32[]{:S(2)}, u32[]{:S(2)}) %all-to-all-start) | async-done | bytes 524320 | tf_op jit(solution)/shard_map/all_to_all | solution.py:378
  36.1 1.7 %copy-done = bf16[5120,256]{1,0:T(8,128)(2,1)S(1)} copy-done((bf16[5120,256]{1,0:T(8,128)(2,1)S(1)}, bf16[5120,256]{1,0:T(8,128)(2,1)}, u32[]{:S(2)}) %copy-start) | copy-done | bytes 2621464
  39.2 1.7 %copy-done.4 = bf16[5120,256]{1,0:T(8,128)(2,1)S(1)} copy-done((bf16[5120,256]{1,0:T(8,128)(2,1)S(1)}, bf16[5120,256]{1,0:T(8,128)(2,1)}, u32[]{:S(2)}) %copy-start.4) | copy-done | bytes 2621464
  42.6 1.7 %collective-permute-start.10 = (bf16[320,768]{1,0:T(8,128)(2,1)S(1)}, bf16[320,768]{1,0:T(8,128)(2,1)}, u32[]{:S(2)}, u32[]{:S(2)}) collective-permute-start(bf16[320,768]{1,0:T(8,128)(2,1)S(1)} %refresh.1.rest_0_), channel_id=1, source_target_pairs={{96,0},{112,16},{0,32},{16,48},{32,64},{48,80},{64,96},{80,112},{2... | collective-permute-start | bytes 1474568 | tf_op jit(solution)/shard_map/ppermute | solution.py:49
  44.9 1.7 %collective-permute-start.8 = (bf16[320,768]{1,0:T(8,128)(2,1)S(1)}, bf16[320,768]{1,0:T(8,128)(2,1)}, u32[]{:S(2)}, u32[]{:S(2)}) collective-permute-start(bf16[320,768]{1,0:T(8,128)(2,1)S(1)} %refresh.1.rest_0_), channel_id=1, source_target_pairs={{32,0},{48,16},{64,32},{80,48},{96,64},{112,80},{0,96},{16,112},{1... | collective-permute-start | bytes 1474568 | tf_op jit(solution)/shard_map/ppermute | solution.py:49
  46.5 2.3 %collective-permute-start = (bf16[320,128]{1,0:T(8,128)(2,1)S(1)}, bf16[320,128]{1,0:T(8,128)(2,1)S(1)}, u32[]{:S(2)}, u32[]{:S(2)}) collective-permute-start(bf16[320,128]{1,0:T(8,128)(2,1)S(1)} %get-tuple-element.28), channel_id=1, source_target_pairs={{8,0},{9,1},{10,2},{11,3},{12,4},{13,5},{14,6},{15,7},{0,8},{1,9},... | collective-permute-start | bytes 245768 | tf_op jit(solution)/shard_map/ppermute | solution.py:76
  48.9 9.8 %collective-permute-done = bf16[320,128]{1,0:T(8,128)(2,1)S(1)} collective-permute-done((bf16[320,128]{1,0:T(8,128)(2,1)S(1)}, bf16[320,128]{1,0:T(8,128)(2,1)S(1)}, u32[]{:S(2)}, u32[]{:S(2)}) %collective-permute-start) | collective-permute-done | bytes 81952 | tf_op jit(solution)/shard_map/ppermute | solution.py:76
  59.9 1.6 collective-permute-start.1
  61.5 1.6 collective-permute-start.13
  64.4 2.1 %collective-permute-done.1.p1 = bf16[640,128]{1,0:T(8,128)(2,1)S(1)} collective-permute-done((bf16[640,128]{1,0:T(8,128)(2,1)S(1)}, bf16[640,128]{1,0:T(8,128)(2,1)S(1)}, u32[]{:S(2)}, u32[]{:S(2)}) %collective-permute-start.1) | collective-permute-done | bytes 163872 | tf_op jit(solution)/shard_map/ppermute | solution.py:76
  66.5 1.6 collective-permute-start.2
  69.4 1.8 %collective-permute-start.11 = (bf16[320,768]{1,0:T(8,128)(2,1)}, bf16[320,768]{1,0:T(8,128)(2,1)}, u32[]{:S(2)}, u32[]{:S(2)}) collective-permute-start(bf16[320,768]{1,0:T(8,128)(2,1)} %collective-permute-done.8.rest_1_), channel_id=1, source_target_pairs={{32,0},{48,16},{64,32},{80,48},{96,64},{112,80},{0,96},{16,112},{1... | collective-permute-start | bytes 1474568 | tf_op jit(solution)/shard_map/ppermute | solution.py:49
  72.3 1.7 %collective-permute-start.3 = (bf16[640,128]{1,0:T(8,128)(2,1)S(1)}, bf16[640,128]{1,0:T(8,128)(2,1)S(1)}, u32[]{:S(2)}, u32[]{:S(2)}) collective-permute-start(bf16[640,128]{1,0:T(8,128)(2,1)S(1)} %collective-permute-done.2.p2), channel_id=1, source_target_pairs={{1,0},{2,1},{3,2},{4,3},{5,4},{6,5},{7,6},{0,7},{9,8},{10,9},{11,1... | collective-permute-start | bytes 491528 | tf_op jit(solution)/shard_map/ppermute | solution.py:76
  75.5 2.8 %collective-permute-done.3.p3 = bf16[640,128]{1,0:T(8,128)(2,1)S(1)} collective-permute-done((bf16[640,128]{1,0:T(8,128)(2,1)S(1)}, bf16[640,128]{1,0:T(8,128)(2,1)S(1)}, u32[]{:S(2)}, u32[]{:S(2)}) %collective-permute-start.3) | collective-permute-done | bytes 163872 | tf_op jit(solution)/shard_map/ppermute | solution.py:76
  79.6 2.2 %collective-permute-done.12.rest_5_ = bf16[320,768]{1,0:T(8,128)(2,1)} collective-permute-done((bf16[320,768]{1,0:T(8,128)(2,1)}, bf16[320,768]{1,0:T(8,128)(2,1)}, u32[]{:S(2)}, u32[]{:S(2)}) %collective-permute-start.12) | collective-permute-done | bytes 491552 | tf_op jit(solution)/shard_map/ppermute | solution.py:49
  85.9 1.5 collective-permute-done.7.p5
  87.4 2.6 %collective-permute-done.4.p4 = bf16[640,128]{1,0:T(8,128)(2,1)} collective-permute-done((bf16[640,128]{1,0:T(8,128)(2,1)}, bf16[640,128]{1,0:T(8,128)(2,1)}, u32[]{:S(2)}, u32[]{:S(2)}) %collective-permute-start.4) | collective-permute-done | bytes 163872 | tf_op jit(solution)/shard_map/ppermute | solution.py:76
  91.5 1.8 %collective-permute-start.15 = (bf16[112,768]{1,0:T(8,128)(2,1)S(1)}, bf16[112,768]{1,0:T(8,128)(2,1)S(1)}, u32[]{:S(2)}, u32[]{:S(2)}) collective-permute-start(bf16[112,768]{1,0:T(8,128)(2,1)S(1)} %slice.10), channel_id=1, source_target_pairs={{32,0},{48,16},{64,32},{80,48},{96,64},{112,80},{0,96},{16,112},{1... | collective-permute-start | bytes 516104 | tf_op jit(solution)/shard_map/ppermute | solution.py:49
  94.5 3.0 %collective-permute-done.16.rest_8_ = bf16[96,768]{1,0:T(8,128)(2,1)S(1)} collective-permute-done((bf16[96,768]{1,0:T(8,128)(2,1)S(1)}, bf16[96,768]{1,0:T(8,128)(2,1)S(1)}, u32[]{:S(2)}, u32[]{:S(2)}) %collective-permute-start.16) | collective-permute-done | bytes 147488 | tf_op jit(solution)/shard_map/ppermute | solution.py:49
  98.2 5.3 %collective-permute-done.14.rest_6_ = bf16[112,768]{1,0:T(8,128)(2,1)S(1)} collective-permute-done((bf16[112,768]{1,0:T(8,128)(2,1)S(1)}, bf16[112,768]{1,0:T(8,128)(2,1)S(1)}, u32[]{:S(2)}, u32[]{:S(2)}) %collective-permute-start.14) | collective-permute-done | bytes 172064 | tf_op jit(solution)/shard_map/ppermute | solution.py:49
  107.9 4.7 %prepare.1 = (bf16[16,128,320]{2,1,0:T(8,128)(2,1)S(1)}, f32[128,128]{1,0:T(8,128)S(1)}, bf16[128,128]{1,0:T(8,128)(2,1)S(1)}, bf16[128,128]{1,0:T(8,128)(2,1)S(1)}, f32[2,128,128]{2,1,0:T(8,128)S(1)}) custom-call(s32[1]{0:T(128)} %bitcast.1.seat, f32[16,1,320]{2,1,0:T(1,128)S(1)} %reshape.58.gain, f32[1,128]{1,0:T(1,128)S(1)} %bitcast.27, ...), custom_call_target="tpu_custom_call" | custom-call | tf_op jit(solution)/shard_map/prepare/pallas_call | solution.py:431
  112.7 6.5 %attend.1 = bf16[16,336,128]{2,1,0:T(8,128)(2,1)S(1)} custom-call(s32[1]{0:T(128)} %bitcast.block.here, bf16[16,128,320]{2,1,0:T(8,128)(2,1)S(1)} %get-tuple-element.29.normed, f32[1,128]{1,0:T(1,128)S(1)} %bitcast.28, f32[1,128]{1,0:T(1,128)S(1)} %bitcast.30, f32[128,128]{1,0:T(8,128)S(1)} %get-tuple-element.47.cosine, ...), custom_call_target="tpu_custom_call" | custom-call | tf_op jit(solution)/shard_map/attend/pallas_call | solution.py:466
  119.2 42.8 %all_to_all.10.recv = bf16[16,336,128]{2,1,0:T(8,128)(2,1)S(1)} all-to-all(bf16[16,336,128]{2,1,0:T(8,128)(2,1)S(1)} %attend.1), channel_id=1, replica_groups=mesh['replica'=16,'shard'=16] {'shard'}, dimensions={0} | all-to-all | bytes 2752512 | tf_op jit(solution)/shard_map/all_to_all | solution.py:489
  (119 shorter events, 32.2 us)
Async XLA Ops:
  8.7 27.4 %all-to-all-start = ((bf16[16,128,128]{2,1,0:T(8,128)(2,1)}), bf16[16,128,128]{2,1,0:T(8,128)(2,1)S(1)}, u32[]{:S(2)}, u32[]{:S(2)}) async-start(bf16[16,128,128]{2,1,0:T(8,128)(2,1)} %get-tuple-element.22), calls=%async_computation | async-start | bytes 1048576 | tf_op jit(solution)/shard_map/all_to_all | solution.py:378
  42.6 17.3 %collective-permute-start.10 = (bf16[320,768]{1,0:T(8,128)(2,1)S(1)}, bf16[320,768]{1,0:T(8,128)(2,1)}, u32[]{:S(2)}, u32[]{:S(2)}) collective-permute-start(bf16[320,768]{1,0:T(8,128)(2,1)S(1)} %refresh.1.rest_0_), channel_id=1, source_target_pairs={{96,0},{112,16},{0,32},{16,48},{32,64},{48,80},{64,96},{80,112},{2... | collective-permute-start | bytes 1474568 | tf_op jit(solution)/shard_map/ppermute | solution.py:49
  44.3 17.3 %collective-permute-start.9 = (bf16[320,768]{1,0:T(8,128)(2,1)S(1)}, bf16[320,768]{1,0:T(8,128)(2,1)}, u32[]{:S(2)}, u32[]{:S(2)}) collective-permute-start(bf16[320,768]{1,0:T(8,128)(2,1)S(1)} %refresh.1.rest_0_), channel_id=1, source_target_pairs={{128,0},{144,16},{160,32},{176,48},{192,64},{208,80},{224,96},{240... | collective-permute-start | bytes 1474568 | tf_op jit(solution)/shard_map/ppermute | solution.py:49
  44.9 16.7 %collective-permute-start.8 = (bf16[320,768]{1,0:T(8,128)(2,1)S(1)}, bf16[320,768]{1,0:T(8,128)(2,1)}, u32[]{:S(2)}, u32[]{:S(2)}) collective-permute-start(bf16[320,768]{1,0:T(8,128)(2,1)S(1)} %refresh.1.rest_0_), channel_id=1, source_target_pairs={{32,0},{48,16},{64,32},{80,48},{96,64},{112,80},{0,96},{16,112},{1... | collective-permute-start | bytes 1474568 | tf_op jit(solution)/shard_map/ppermute | solution.py:49
  46.5 12.1 %collective-permute-start = (bf16[320,128]{1,0:T(8,128)(2,1)S(1)}, bf16[320,128]{1,0:T(8,128)(2,1)S(1)}, u32[]{:S(2)}, u32[]{:S(2)}) collective-permute-start(bf16[320,128]{1,0:T(8,128)(2,1)S(1)} %get-tuple-element.28), channel_id=1, source_target_pairs={{8,0},{9,1},{10,2},{11,3},{12,4},{13,5},{14,6},{15,7},{0,8},{1,9},... | collective-permute-start | bytes 245768 | tf_op jit(solution)/shard_map/ppermute | solution.py:76
  59.1 15.6 %collective-permute-start.17 = (bf16[320,768]{1,0:T(8,128)(2,1)S(1)}, bf16[320,768]{1,0:T(8,128)(2,1)S(1)}, u32[]{:S(2)}, u32[]{:S(2)}) collective-permute-start(bf16[320,768]{1,0:T(8,128)(2,1)S(1)} %refresh.1.rest_0_), channel_id=1, source_target_pairs={{16,0},{0,16},{48,32},{32,48},{80,64},{64,80},{112,96},{96,112},{1... | collective-permute-start | bytes 1474568 | tf_op jit(solution)/shard_map/ppermute | solution.py:49
  59.9 6.6 %collective-permute-start.1 = (bf16[640,128]{1,0:T(8,128)(2,1)S(1)}, bf16[640,128]{1,0:T(8,128)(2,1)S(1)}, u32[]{:S(2)}, u32[]{:S(2)}) collective-permute-start(bf16[640,128]{1,0:T(8,128)(2,1)S(1)} %constant_dynamic-update-slice_fusion.p0), channel_id=1, source_target_pairs={{1,0},{2,1},{3,2},{4,3},{5,4},{6,5},{7,6},{0,7},{9,8},{10,9},{11,1... | collective-permute-start | bytes 491528 | tf_op jit(solution)/shard_map/ppermute | solution.py:76
  61.5 17.4 %collective-permute-start.13 = (bf16[320,768]{1,0:T(8,128)(2,1)}, bf16[320,768]{1,0:T(8,128)(2,1)}, u32[]{:S(2)}, u32[]{:S(2)}) collective-permute-start(bf16[320,768]{1,0:T(8,128)(2,1)} %collective-permute-done.9.rest_4_), channel_id=1, source_target_pairs={{96,0},{112,16},{0,32},{16,48},{32,64},{48,80},{64,96},{80,112},{2... | collective-permute-start | bytes 1474568 | tf_op jit(solution)/shard_map/ppermute | solution.py:49
  66.5 5.8 %collective-permute-start.2 = (bf16[640,128]{1,0:T(8,128)(2,1)S(1)}, bf16[640,128]{1,0:T(8,128)(2,1)S(1)}, u32[]{:S(2)}, u32[]{:S(2)}) collective-permute-start(bf16[640,128]{1,0:T(8,128)(2,1)S(1)} %collective-permute-done.1.p1), channel_id=1, source_target_pairs={{1,0},{2,1},{3,2},{4,3},{5,4},{6,5},{7,6},{0,7},{9,8},{10,9},{11,1... | collective-permute-start | bytes 491528 | tf_op jit(solution)/shard_map/ppermute | solution.py:76
  68.8 13.0 %collective-permute-start.12 = (bf16[320,768]{1,0:T(8,128)(2,1)}, bf16[320,768]{1,0:T(8,128)(2,1)}, u32[]{:S(2)}, u32[]{:S(2)}) collective-permute-start(bf16[320,768]{1,0:T(8,128)(2,1)} %collective-permute-done.8.rest_1_), channel_id=1, source_target_pairs={{128,0},{144,16},{160,32},{176,48},{192,64},{208,80},{224,96},{240... | collective-permute-start | bytes 1474568 | tf_op jit(solution)/shard_map/ppermute | solution.py:49
  69.4 13.1 %collective-permute-start.11 = (bf16[320,768]{1,0:T(8,128)(2,1)}, bf16[320,768]{1,0:T(8,128)(2,1)}, u32[]{:S(2)}, u32[]{:S(2)}) collective-permute-start(bf16[320,768]{1,0:T(8,128)(2,1)} %collective-permute-done.8.rest_1_), channel_id=1, source_target_pairs={{32,0},{48,16},{64,32},{80,48},{96,64},{112,80},{0,96},{16,112},{1... | collective-permute-start | bytes 1474568 | tf_op jit(solution)/shard_map/ppermute | solution.py:49
  72.3 6.0 %collective-permute-start.3 = (bf16[640,128]{1,0:T(8,128)(2,1)S(1)}, bf16[640,128]{1,0:T(8,128)(2,1)S(1)}, u32[]{:S(2)}, u32[]{:S(2)}) collective-permute-start(bf16[640,128]{1,0:T(8,128)(2,1)S(1)} %collective-permute-done.2.p2), channel_id=1, source_target_pairs={{1,0},{2,1},{3,2},{4,3},{5,4},{6,5},{7,6},{0,7},{9,8},{10,9},{11,1... | collective-permute-start | bytes 491528 | tf_op jit(solution)/shard_map/ppermute | solution.py:76
  75.5 14.5 %collective-permute-start.20 = (bf16[320,768]{1,0:T(8,128)(2,1)}, bf16[320,768]{1,0:T(8,128)(2,1)}, u32[]{:S(2)}, u32[]{:S(2)}) collective-permute-start(bf16[320,768]{1,0:T(8,128)(2,1)} %collective-permute-done.10.rest_3_), channel_id=1, source_target_pairs={{16,0},{0,16},{48,32},{32,48},{80,64},{64,80},{112,96},{96,112},{1... | collective-permute-start | bytes 1474568 | tf_op jit(solution)/shard_map/ppermute | solution.py:49
  79.0 12.5 %collective-permute-start.21 = (bf16[320,768]{1,0:T(8,128)(2,1)}, bf16[320,768]{1,0:T(8,128)(2,1)}, u32[]{:S(2)}, u32[]{:S(2)}) collective-permute-start(bf16[320,768]{1,0:T(8,128)(2,1)} %collective-permute-done.9.rest_4_), channel_id=1, source_target_pairs={{16,0},{0,16},{48,32},{32,48},{80,64},{64,80},{112,96},{96,112},{1... | collective-permute-start | bytes 1474568 | tf_op jit(solution)/shard_map/ppermute | solution.py:49
  79.0 14.3 %collective-permute-start.18 = (bf16[320,768]{1,0:T(8,128)(2,1)}, bf16[320,768]{1,0:T(8,128)(2,1)}, u32[]{:S(2)}, u32[]{:S(2)}) collective-permute-start(bf16[320,768]{1,0:T(8,128)(2,1)} %collective-permute-done.8.rest_1_), channel_id=1, source_target_pairs={{16,0},{0,16},{48,32},{32,48},{80,64},{64,80},{112,96},{96,112},{1... | collective-permute-start | bytes 1474568 | tf_op jit(solution)/shard_map/ppermute | solution.py:49
  82.5 7.5 %collective-permute-start.4 = (bf16[640,128]{1,0:T(8,128)(2,1)}, bf16[640,128]{1,0:T(8,128)(2,1)}, u32[]{:S(2)}, u32[]{:S(2)}) collective-permute-start(bf16[640,128]{1,0:T(8,128)(2,1)} %copy-done.20), channel_id=1, source_target_pairs={{1,0},{2,1},{3,2},{4,3},{5,4},{6,5},{7,6},{0,7},{9,8},{10,9},{11,1... | collective-permute-start | bytes 491528 | tf_op jit(solution)/shard_map/ppermute | solution.py:76
  87.4 25.2 %collective-permute-start.22 = (bf16[320,768]{1,0:T(8,128)(2,1)}, bf16[320,768]{1,0:T(8,128)(2,1)S(1)}, u32[]{:S(2)}, u32[]{:S(2)}) collective-permute-start(bf16[320,768]{1,0:T(8,128)(2,1)} %collective-permute-done.12.rest_5_), channel_id=1, source_target_pairs={{16,0},{0,16},{48,32},{32,48},{80,64},{64,80},{112,96},{96,112},{1... | collective-permute-start | bytes 1474568 | tf_op jit(solution)/shard_map/ppermute | solution.py:49
  90.0 22.6 %collective-permute-start.26 = (bf16[320,768]{1,0:T(8,128)(2,1)}, bf16[320,768]{1,0:T(8,128)(2,1)S(1)}, u32[]{:S(2)}, u32[]{:S(2)}) collective-permute-start(bf16[320,768]{1,0:T(8,128)(2,1)} %collective-permute-done.13.rest_9_), channel_id=1, source_target_pairs={{16,0},{0,16},{48,32},{32,48},{80,64},{64,80},{112,96},{96,112},{1... | collective-permute-start | bytes 1474568 | tf_op jit(solution)/shard_map/ppermute | solution.py:49
  90.0 7.5 %collective-permute-start.16 = (bf16[96,768]{1,0:T(8,128)(2,1)S(1)}, bf16[96,768]{1,0:T(8,128)(2,1)S(1)}, u32[]{:S(2)}, u32[]{:S(2)}) collective-permute-start(bf16[96,768]{1,0:T(8,128)(2,1)S(1)} %slice.11), channel_id=1, source_target_pairs={{96,0},{112,16},{0,32},{16,48},{32,64},{48,80},{64,96},{80,112},{2... | collective-permute-start | bytes 442376 | tf_op jit(solution)/shard_map/ppermute | solution.py:49
  91.5 6.5 %collective-permute-start.15 = (bf16[112,768]{1,0:T(8,128)(2,1)S(1)}, bf16[112,768]{1,0:T(8,128)(2,1)S(1)}, u32[]{:S(2)}, u32[]{:S(2)}) collective-permute-start(bf16[112,768]{1,0:T(8,128)(2,1)S(1)} %slice.10), channel_id=1, source_target_pairs={{32,0},{48,16},{64,32},{80,48},{96,64},{112,80},{0,96},{16,112},{1... | collective-permute-start | bytes 516104 | tf_op jit(solution)/shard_map/ppermute | solution.py:49
  93.2 19.4 %collective-permute-start.19 = (bf16[320,768]{1,0:T(8,128)(2,1)}, bf16[320,768]{1,0:T(8,128)(2,1)S(1)}, u32[]{:S(2)}, u32[]{:S(2)}) collective-permute-start(bf16[320,768]{1,0:T(8,128)(2,1)} %collective-permute-done.11.rest_2_), channel_id=1, source_target_pairs={{16,0},{0,16},{48,32},{32,48},{80,64},{64,80},{112,96},{96,112},{1... | collective-permute-start | bytes 1474568 | tf_op jit(solution)/shard_map/ppermute | solution.py:49
  97.5 6.0 %collective-permute-start.14 = (bf16[112,768]{1,0:T(8,128)(2,1)S(1)}, bf16[112,768]{1,0:T(8,128)(2,1)S(1)}, u32[]{:S(2)}, u32[]{:S(2)}) collective-permute-start(bf16[112,768]{1,0:T(8,128)(2,1)S(1)} %slice.9), channel_id=1, source_target_pairs={{128,0},{144,16},{160,32},{176,48},{192,64},{208,80},{224,96},{240... | collective-permute-start | bytes 516104 | tf_op jit(solution)/shard_map/ppermute | solution.py:49
  103.5 9.1 %collective-permute-start.24 = (bf16[112,768]{1,0:T(8,128)(2,1)S(1)}, bf16[112,768]{1,0:T(8,128)(2,1)S(1)}, u32[]{:S(2)}, u32[]{:S(2)}) collective-permute-start(bf16[112,768]{1,0:T(8,128)(2,1)S(1)} %collective-permute-done.15.rest_7_), channel_id=1, source_target_pairs={{16,0},{0,16},{48,32},{32,48},{80,64},{64,80},{112,96},{96,112},{1... | collective-permute-start | bytes 516104 | tf_op jit(solution)/shard_map/ppermute | solution.py:49
  103.5 9.1 %collective-permute-start.23 = (bf16[112,768]{1,0:T(8,128)(2,1)S(1)}, bf16[112,768]{1,0:T(8,128)(2,1)S(1)}, u32[]{:S(2)}, u32[]{:S(2)}) collective-permute-start(bf16[112,768]{1,0:T(8,128)(2,1)S(1)} %collective-permute-done.14.rest_6_), channel_id=1, source_target_pairs={{16,0},{0,16},{48,32},{32,48},{80,64},{64,80},{112,96},{96,112},{1... | collective-permute-start | bytes 516104 | tf_op jit(solution)/shard_map/ppermute | solution.py:49
  (36 other events, 583.4 us)

commit v4 on v1

v4 whole, which is shorter than its diff:
```python
import jax
import jax.numpy as jnp
from jax import lax
from jax.experimental import pallas as pl
from jax.experimental.pallas import tpu as pltpu
from jax.sharding import PartitionSpec as P

HQ = 32
KV = 8
HEAD = 128
WIDTH = 5120
STEPS = 4
ROWS = 32
TOKENS = STEPS * ROWS
CTX = 64
PARTS = 16
OWN = WIDTH // PARTS
CUT = 20
GROUP = 8
GROUPS = ROWS // GROUP
TAIL = 16
EPSILON = 1e-06
THETA = 1000000.0
SCALE = HEAD ** (-0.5)
NEG = -1e30
TILES = ((0, 128), (128, 128), (256, 64))
BLOCK = 128
HALF = PARTS // 2
LIFT = 32
SENT = 2 * TOKENS + TAIL
THIRDS = ((0, 112), (112, 112), (224, 96))
F32 = jnp.float32
BF16 = jnp.bfloat16
VMEM = pltpu.VMEM


PLACES = tuple((dx, dy) for dx in range(2) for dy in range(4))


def fetch(value, dx, dy, dc):
    pairs = []
    for i in range(16):
        x, y, c = i >> 3, (i >> 1) & 3, i & 1
        pairs.append((((x ^ dx) << 3) + (((y + dy) & 3) << 1) + (c ^ dc), i))
    return lax.ppermute(value, "replica", pairs)


def along_shard(value, dx, dz):
    pairs = [((((i >> 3) ^ dx) << 3) + ((i + dz) & 7), i) for i in range(16)]
    return lax.ppermute(value, "shard", pairs)


def owner(here, place):
    return (((here >> 3) ^ place[0]) << 2) + (((here >> 1) + place[1]) & 3)


def factors(codes):
    out = jnp.ones(codes.shape, F32)
    for bit in range(5):
        out = out * jnp.where((codes >> bit) & 1 == 1, F32(2.0 ** -(2**bit)), F32(1.0))
    return out


def start_all(copies):
    for copy in copies:
        copy.start()


def pack_kernel(
    here, hidden, dq, dk, dv, do, sq, so, skt, svt, base,
    out, turned, moved,
    vh, vq, vk, vv, vo, vsq, vso, vsk, vsv, rows, buf, sems,
):
    shift = CUT * here[0]
    first = (shift >> 4) << 4
    pairs = [(hidden, vh), (sq, vsq), (so, vso), (skt, vsk), (svt, vsv)]
    pairs += [(dq, vq), (dk, vk), (dv, vv), (do, vo)]
    copies = [pltpu.make_async_copy(a, b, sems.at[i]) for i, (a, b) in enumerate(pairs)]
    for dest in range(PARTS):
        at = pl.multiple_of(OWN * dest + first, 16)
        copies.append(
            pltpu.make_async_copy(
                base.at[pl.ds(at, LIFT), :], rows.at[dest], sems.at[len(pairs) + dest]
            )
        )
    start_all(copies)
    for copy in copies[:5]:
        copy.wait()
    for at, n in TILES:
        turned[at : at + n, :] = vh[:, at : at + n].astype(F32).T.astype(BF16)
    fq, fo, fk, fv = factors(vsq[...]), factors(vso[...]), factors(vsk[...]), factors(vsv[...])
    line = lax.broadcasted_iota(jnp.int32, (CUT, CUT), 0)
    lane = lax.broadcasted_iota(jnp.int32, (CUT, CUT), 1)

    def column(factor, head):
        spread = jnp.where(line == lane, factor[head : head + 1, :], 0.0)
        return jnp.sum(spread, axis=1, keepdims=True)

    def piece(codes, head, factor):
        return codes[:, head * HEAD : (head + 1) * HEAD].astype(F32) * factor

    for copy in copies[5:]:
        copy.wait()
    for head in range(HQ):
        moved[:, head * HEAD : (head + 1) * HEAD] = piece(vo, head, fo[:, head : head + 1]).astype(BF16)
    buf[6 * CUT : BLOCK, :] = jnp.zeros((BLOCK - 6 * CUT, HEAD), F32)
    turn = (LIFT - (shift - first)) & (LIFT - 1)
    for half in range(PARTS // 2):
        key, value = piece(vk, half, column(fk, half)), piece(vv, half, column(fv, half))
        for dest in (2 * half, 2 * half + 1):
            mine = pltpu.roll(rows[dest].astype(F32), turn, 0)[0:CUT, :]
            pieces = (
                piece(vq, 2 * dest, fq[:, 2 * dest : 2 * dest + 1]),
                piece(vq, 2 * dest + 1, fq[:, 2 * dest + 1 : 2 * dest + 2]),
                key,
                value,
                mine[:, 0:HEAD],
                mine[:, HEAD:],
            )
            for c, item in enumerate(pieces):
                buf[CUT * c : CUT * (c + 1), :] = item
            out[dest] = buf[...].astype(BF16)


def refresh_kernel(here, recv, bq, bk, bv, out, vq, vk, vv, buf, delta, sems):
    at = pl.ds(pl.multiple_of(OWN * here[0], 64), OWN)
    copies = [
        pltpu.make_async_copy(a.at[at, :], b, sems.at[i])
        for i, (a, b) in enumerate(((bq, vq), (bk, vk), (bv, vv)))
    ]
    start_all(copies)
    for src in range(PARTS):
        buf[src % 2] = recv[src].astype(F32)
        for c in range(4):
            delta[CUT * src : CUT * (src + 1), HEAD * c : HEAD * (c + 1)] = buf[
                src % 2, CUT * c : CUT * (c + 1), :
            ]
    for copy in copies:
        copy.wait()
    out[:, 0:256] = (vq[...].astype(F32) + delta[:, 0:256]).astype(BF16)
    out[:, 256:384] = (vk[...].astype(F32) + delta[:, 256:384]).astype(BF16)
    out[:, 384:512] = (vv[...].astype(F32) + delta[:, 384:512]).astype(BF16)


def refresh_out_kernel(recv, moved, out, buf):
    for src in range(PARTS):
        buf[src % 2] = recv[src].astype(F32)
        for h in range(2):
            at = (2 * src + h) * HEAD
            base = buf[src % 2, CUT * (4 + h) : CUT * (5 + h), :]
            out[:, at : at + HEAD] = (base + moved[:, at : at + HEAD].astype(F32)).astype(BF16)


def dot_nt(a, b):
    return lax.dot_general(a, b, (((1,), (1,)), ((), ())), preferred_element_type=F32)


def dot(a, b):
    return jnp.dot(a, b, preferred_element_type=F32)


def head_norm_rotate(raw, gain, cosine, sine):
    value = raw * lax.rsqrt(jnp.mean(raw * raw, axis=-1, keepdims=True) + EPSILON) * gain
    swapped = jnp.concatenate([value[:, HEAD // 2 :], value[:, : HEAD // 2]], axis=-1)
    return value * cosine + swapped * sine


def group_scores(group, query, cache, fresh, lens):
    picked = [
        query[h * TOKENS + t * ROWS + group * GROUP : h * TOKENS + t * ROWS + (group + 1) * GROUP, :]
        for h in range(2)
        for t in range(STEPS)
    ]
    q = jnp.concatenate(picked, axis=0).astype(BF16)
    past = dot_nt(q, cache) * SCALE
    new = dot_nt(q, fresh) * SCALE
    n = 2 * STEPS * GROUP
    length = jnp.concatenate([lens[group * GROUP : (group + 1) * GROUP, :]] * (2 * STEPS), axis=0)
    column = lax.broadcasted_iota(jnp.int32, past.shape, 1)
    line = lax.broadcasted_iota(jnp.int32, past.shape, 0)
    past_ok = ((column >> 6) == (line & 7)) & ((column & 63) < length[:, 0:1])
    column = lax.broadcasted_iota(jnp.int32, (n, TOKENS), 1)
    line = lax.broadcasted_iota(jnp.int32, (n, TOKENS), 0)
    new_ok = ((column & 31) == group * GROUP + (line & 7)) & ((column >> 5) <= ((line >> 3) & 3))
    past = jnp.where(past_ok, past, NEG)
    new = jnp.where(new_ok, new, NEG)
    top = jnp.maximum(
        jnp.max(past, axis=-1, keepdims=True), jnp.max(new, axis=-1, keepdims=True)
    )
    past = jnp.exp(past - top)
    new = jnp.exp(new - top)
    total = jnp.sum(past, axis=-1, keepdims=True) + jnp.sum(new, axis=-1, keepdims=True)
    return past, new, total, top + jnp.log(total)


def put_groups(group, ref, value):
    for h in range(2):
        for t in range(STEPS):
            at = h * TOKENS + t * ROWS + group * GROUP
            i = (h * STEPS + t) * GROUP
            ref[at : at + GROUP, :] = value[i : i + GROUP, :]


def sample_logp(query, keys, one_query, lse):
    out = []
    for h in range(2):
        q = dot(one_query, query[h * TOKENS : (h + 1) * TOKENS, :].astype(BF16))
        score = jnp.sum(q * keys, axis=-1, keepdims=True) * SCALE
        line = lse[h * TOKENS : (h + 1) * TOKENS, :].T
        picked = jnp.sum(one_query.astype(F32) * line, axis=-1, keepdims=True)
        out.append(jnp.broadcast_to(score - picked, (TOKENS, HEAD)))
    return out


def normalise_kernel(
    here, seat, gain, p0, p1, p2, p3, p4, p5, p6, p7, normed, keep, give,
):
    total = jnp.zeros((1, TOKENS), F32)
    pairs = (p0, p1, p2, p3, p4, p5, p6, p7)
    for pair in pairs:
        x = pair[...].astype(F32)
        total = total + jnp.sum(x * x, axis=0, keepdims=True)
    scale = lax.rsqrt(total * (1.0 / WIDTH) + EPSILON)
    me = seat[0]
    for step, pair in enumerate(pairs):
        for half in range(2):
            src = (((me >> 3) ^ half) << 3) + ((me + step) & 7)
            for at, n in TILES:
                x = pair[half * OWN + at : half * OWN + at + n, :].astype(F32) * scale
                normed[src, :, at : at + n] = (x.T * gain[src, :, at : at + n]).astype(BF16)
    core = here[0] & 1
    for j in range(HALF):
        keep[j] = normed[2 * j + core]
        give[j] = normed[2 * j + 1 - core]


def old_kernel(
    normed, table, marks, base_q, base_k, cache_hbm,
    keys_out, one_q_out, one_f_out, old_out,
    wq, wk, cache, query, lse, sems,
):
    copies = [
        pltpu.make_async_copy(a, b, sems.at[i])
        for i, (a, b) in enumerate(((base_q, wq), (base_k, wk), (cache_hbm, cache)))
    ]
    start_all(copies)
    for copy in copies:
        copy.wait()
    raw = jnp.zeros((TOKENS, 256), F32)
    raw_k = jnp.zeros((TOKENS, HEAD), F32)
    for src in range(PARTS):
        raw = raw + dot(normed[src], wq[src * OWN : (src + 1) * OWN, :])
        raw_k = raw_k + dot(normed[src], wk[src * OWN : (src + 1) * OWN, :])
    cos, sin = table[0:TOKENS, :], table[TOKENS : 2 * TOKENS, :]
    qg, kg = table[2 * TOKENS : 2 * TOKENS + 1, :], table[2 * TOKENS + 1 : 2 * TOKENS + 2, :]
    lens = marks
    for h in range(2):
        query[h * TOKENS : (h + 1) * TOKENS, :] = (
            head_norm_rotate(raw[:, h * HEAD : (h + 1) * HEAD], qg, cos, sin)
            .astype(BF16)
            .astype(F32)
        )
    fresh = head_norm_rotate(raw_k, kg, cos, sin).astype(BF16)
    for g in range(GROUPS):
        _, _, _, log_sum = group_scores(
            g, query, cache[g * GROUP * CTX : (g + 1) * GROUP * CTX, :], fresh, lens
        )
        put_groups(g, lse, jnp.broadcast_to(log_sum, (log_sum.shape[0], HEAD)))
    tokens = jnp.broadcast_to(marks[ROWS : ROWS + 1, :], (TOKENS, TOKENS)).T
    places = jnp.broadcast_to(marks[ROWS + 1 : ROWS + 2, :], (TOKENS, TOKENS)).T
    lane = lax.broadcasted_iota(jnp.int32, (TOKENS, TOKENS), 1)
    one_q = jnp.where(tokens == lane, F32(1.0), F32(0.0)).astype(BF16)
    one_f = jnp.where(places == lane + ROWS * CTX, F32(1.0), F32(0.0)).astype(BF16)
    keys = jnp.zeros((TOKENS, HEAD), F32)
    for k in range(ROWS * CTX // HEAD):
        one = jnp.where(places == lane + k * HEAD, F32(1.0), F32(0.0)).astype(BF16)
        keys = keys + dot(one, cache[k * HEAD : (k + 1) * HEAD, :])
    keys_out[...] = keys
    one_q_out[...] = one_q
    one_f_out[...] = one_f
    old = sample_logp(query, keys + dot(one_f, fresh), one_q, lse)
    old_out[0] = old[0]
    old_out[1] = old[1]


def project_kernel(here, keep, given, w00, w01, w02, w03, w10, w11, wa, wb, wc, w13, own, other):
    raw = jnp.zeros((2 * TOKENS, 512), F32)
    weights = (w00, w01, w02, w03, w10, w11, (wa, wb, wc), w13)
    for place, weight in zip(PLACES, weights):
        j = owner(here[0], place)
        lines = jnp.concatenate([keep[j], given[j]], axis=0)
        if isinstance(weight, tuple):
            value = jnp.concatenate([w[...] for w in weight], axis=0)
        else:
            value = weight[...]
        raw = raw + dot(lines, value)
    own[...] = raw[0:TOKENS, :]
    other[...] = raw[TOKENS:, :]


def attend_kernel(
    own, other, table, marks, cache_hbm, values_hbm, keys, one_q, one_f, old,
    out,
    cache, values, query, lse, mixed, sems,
):
    copies = (
        pltpu.make_async_copy(cache_hbm, cache, sems.at[0]),
        pltpu.make_async_copy(values_hbm, values, sems.at[1]),
    )
    start_all(copies)
    raw = own[...] + other[...]
    cos, sin = table[0:TOKENS, :], table[TOKENS : 2 * TOKENS, :]
    qg, kg = table[2 * TOKENS : 2 * TOKENS + 1, :], table[2 * TOKENS + 1 : 2 * TOKENS + 2, :]
    lens = marks
    for h in range(2):
        query[h * TOKENS : (h + 1) * TOKENS, :] = (
            head_norm_rotate(raw[:, h * HEAD : (h + 1) * HEAD], qg, cos, sin)
            .astype(BF16)
            .astype(F32)
        )
    fresh = head_norm_rotate(raw[:, 256:384], kg, cos, sin).astype(BF16)
    fresh_v = raw[:, 384:512].astype(BF16)
    for copy in copies:
        copy.wait()
    for g in range(GROUPS):
        at = slice(g * GROUP * CTX, (g + 1) * GROUP * CTX)
        past, new, total, log_sum = group_scores(g, query, cache[at, :], fresh, lens)
        put_groups(g, lse, jnp.broadcast_to(log_sum, (log_sum.shape[0], HEAD)))
        mix = dot((past / total).astype(BF16), values[at, :])
        mix = mix + dot((new / total).astype(BF16), fresh_v)
        put_groups(g, mixed, mix)
    attended = mixed[...].astype(BF16)
    now = sample_logp(query, keys[...] + dot(one_f[...], fresh), one_q[...], lse)
    term = (now[0] - old[0]) + (now[1] - old[1])
    line = term.T[0:1, :]
    high = line.astype(BF16).astype(F32)
    middle = (line - high).astype(BF16).astype(F32)
    low = line - high - middle
    tail = jnp.concatenate([high, middle, low, jnp.zeros((TAIL - 3, TOKENS), F32)], axis=0)
    tail = tail.astype(BF16)
    for p in range(PARTS):
        out[p, 0 : 2 * TOKENS, :] = attended
        out[p, 2 * TOKENS : SENT, :] = tail


def collect_kernel(here, w0, w1, w2, w3, w4, w5, w6, w7, out, buf):
    buf[...] = jnp.zeros_like(buf)
    for place, weight in zip(PLACES, (w0, w1, w2, w3, w4, w5, w6, w7)):
        buf[0:CUT, :] = weight[...].astype(F32)
        out[owner(here[0], place)] = buf[...].astype(BF16)


def finish_kernel(here, recv, mine, theirs, out, ratio, lines, blocks, features):
    tail = jnp.zeros((TAIL, TOKENS), F32)
    for src in range(PARTS):
        for h in range(2):
            at = (2 * src + h) * HEAD
            lines[:, at : at + HEAD] = recv[src, h * TOKENS : (h + 1) * TOKENS, :]
        tail = tail + recv[src, 2 * TOKENS : SENT, :].astype(F32)
    ratio[...] = ((tail[2:3, :] + tail[1:2, :]) + tail[0:1, :]) * (1.0 / HQ)
    core = here[0] & 1
    for weight, parity in ((mine, core), (theirs, 1 - core)):
        result = dot_nt(weight[...].reshape(HALF * LIFT, 2 * PARTS * HEAD), lines[...])
        for j in range(HALF):
            blocks[2 * j + parity] = result[LIFT * j : LIFT * (j + 1), :]
    for b in range(PARTS):
        features[CUT * b : CUT * (b + 1), :] = blocks[b, 0:CUT, :]
    for at, n in TILES:
        out[:, at : at + n] = features[at : at + n, :].T.astype(BF16)


def params(mib):
    return pltpu.CompilerParams(vmem_limit_bytes=mib * 1024 * 1024)


def shape(dims, dtype):
    return jax.ShapeDtypeStruct(dims, dtype)


def whole(n=1):
    return [pl.BlockSpec(memory_space=VMEM)] * n


def scalars(n=1):
    return [pl.BlockSpec(memory_space=pltpu.SMEM)] * n


def far_away(n=1):
    return [pl.BlockSpec(memory_space=pltpu.HBM)] * n


def call(kernel, name, out_shape, in_specs, scratch, mib):
    several = isinstance(out_shape, tuple)
    return pl.pallas_call(
        kernel,
        name=name,
        out_shape=out_shape,
        in_specs=in_specs,
        out_specs=tuple(whole(len(out_shape))) if several else whole()[0],
        scratch_shapes=scratch,
        compiler_params=params(mib),
    )


def local(
    hidden,
    norm_gain,
    query_gain,
    key_gain,
    base_query,
    base_key,
    base_value,
    base_output,
    delta_query,
    scale_query,
    key_delta_codes,
    key_scale_codes,
    value_delta_codes,
    value_scale_codes,
    delta_output,
    scale_output,
    cache_keys,
    cache_values,
    lengths,
    stale_rows,
    stale_steps,
    stale_back,
):
    here = lax.axis_index("replica").astype(jnp.int32).reshape(1)
    seat = lax.axis_index("shard").astype(jnp.int32).reshape(1)
    dma = pltpu.SemaphoreType.DMA
    packed, turned, moved = call(
        pack_kernel,
        "pack",
        (
            shape((PARTS, BLOCK, HEAD), BF16),
            shape((OWN, TOKENS), BF16),
            shape((CUT, HQ * HEAD), BF16),
        ),
        scalars() + far_away(10),
        [
            VMEM((TOKENS, OWN), BF16),
            VMEM((CUT, HQ * HEAD), BF16),
            VMEM((CUT, KV * HEAD), BF16),
            VMEM((CUT, KV * HEAD), BF16),
            VMEM((CUT, HQ * HEAD), BF16),
            VMEM((CUT, HQ), jnp.int32),
            VMEM((CUT, HQ), jnp.int32),
            VMEM((KV, CUT), jnp.int32),
            VMEM((KV, CUT), jnp.int32),
            VMEM((PARTS, LIFT, 2 * HEAD), BF16),
            VMEM((BLOCK, HEAD), F32),
            dma((9 + PARTS,)),
        ],
        16,
    )(
        here, hidden.reshape(TOKENS, OWN), delta_query, key_delta_codes, value_delta_codes, delta_output,
        scale_query, scale_output, key_scale_codes.T, value_scale_codes.T, base_output,
    )
    mirrored = [(r * PARTS + s, s * PARTS + r) for r in range(PARTS) for s in range(PARTS)]
    moved = lax.ppermute(moved, ("replica", "shard"), mirrored)
    across = along_shard(turned, 1, 0)
    arrived = lax.all_to_all(packed, "shard", split_axis=0, concat_axis=0, tiled=False)
    arrived, moved, across, turned, lengths, stale_rows, stale_steps, stale_back = (
        lax.optimization_barrier(
            (arrived, moved, across, turned, lengths, stale_rows, stale_steps, stale_back)
        )
    )
    fresh_rows = call(
        refresh_kernel,
        "refresh",
        shape((OWN, 512), BF16),
        scalars() + whole() + far_away(3),
        [
            VMEM((OWN, 256), BF16),
            VMEM((OWN, 128), BF16),
            VMEM((OWN, 128), BF16),
            VMEM((2, BLOCK, HEAD), F32),
            VMEM((OWN, 512), F32),
            dma((3,)),
        ],
        8,
    )(here, arrived, base_query, base_key, base_value)
    pair = jnp.concatenate([turned, across], axis=0)
    fresh_out = call(
        refresh_out_kernel,
        "refresh_out",
        shape((CUT, HQ * HEAD), BF16),
        whole(2),
        [VMEM((2, BLOCK, HEAD), F32)],
        8,
    )(arrived, moved)

    over = fetch(fresh_rows, 1, 0, 0)
    up = fetch(fresh_rows, 0, 1, 0)
    down = fetch(fresh_rows, 0, -1, 0)
    z1, z7 = along_shard(pair, 0, 1), along_shard(pair, 0, -1)
    z2, z6 = along_shard(pair, 0, 2), along_shard(pair, 0, -2)
    over, up, down, z1, z7, z2, z6 = lax.optimization_barrier((over, up, down, z1, z7, z2, z6))
    over_up = fetch(up, 1, 0, 0)
    far = fetch(up, 0, 1, 0)
    over_down = fetch(over, 0, -1, 0)
    z3, z5 = along_shard(z2, 0, 1), along_shard(z6, 0, -1)
    z4 = along_shard(z2, 0, 2)
    over_up, far, over_down, z3, z4, z5, fresh_out = lax.optimization_barrier(
        (over_up, far, over_down, z3, z4, z5, fresh_out)
    )
    cuts = [slice(at, at + n) for at, n in THIRDS]
    far_over = [
        fetch(far[cuts[0]], 1, 0, 0),
        fetch(over_up[cuts[1]], 0, 1, 0),
        fetch(over_down[cuts[2]], 0, -1, 0),
    ]

    normed, keep, give = call(
        normalise_kernel,
        "normalise",
        (
            shape((PARTS, TOKENS, OWN), BF16),
            shape((HALF, TOKENS, OWN), BF16),
            shape((HALF, TOKENS, OWN), BF16),
        ),
        scalars(2) + whole(9),
        [],
        8,
    )(here, seat, norm_gain.reshape(PARTS, 1, OWN), pair, z1, z2, z3, z4, z5, z6, z7)
    given = fetch(give, 0, 0, 1)

    position = (lengths[None, :] + jnp.arange(STEPS)[:, None]).reshape(TOKENS)
    freq = THETA ** (-(jnp.arange(HEAD // 2).astype(F32) * 2.0) / HEAD)
    angle = position.astype(F32)[:, None] * freq
    cos, sin = jnp.cos(angle), jnp.sin(angle)
    table = jnp.concatenate(
        [
            jnp.concatenate([cos, cos], axis=1),
            jnp.concatenate([-sin, sin], axis=1),
            query_gain.reshape(1, HEAD),
            key_gain.reshape(1, HEAD),
            jnp.zeros((6, HEAD), F32),
        ],
        axis=0,
    )
    rows_s, steps_s, back_s = stale_rows, stale_steps, stale_back
    lens_s = jnp.sum(
        jnp.where(rows_s[0][None, :] == jnp.arange(ROWS)[:, None], lengths[:, None], 0),
        axis=0,
        keepdims=True,
    )
    at = lens_s + steps_s - back_s % (lens_s + steps_s + 1)
    place = jnp.where(
        at >= lens_s, ROWS * CTX + (at - lens_s) * ROWS + rows_s, rows_s * CTX + at
    ).astype(jnp.int32)
    token = (steps_s * ROWS + rows_s).astype(jnp.int32)
    marks = jnp.concatenate(
        [
            jnp.broadcast_to(lengths[:, None], (ROWS, HEAD)),
            token,
            place,
            jnp.zeros((6, HEAD), jnp.int32),
        ],
        axis=0,
    )
    cache = cache_keys.reshape(ROWS * CTX, HEAD)
    values = cache_values.reshape(ROWS * CTX, HEAD)

    keys, one_q, one_f, old = call(
        old_kernel,
        "old",
        (
            shape((TOKENS, HEAD), F32),
            shape((TOKENS, TOKENS), BF16),
            shape((TOKENS, TOKENS), BF16),
            shape((2, TOKENS, HEAD), F32),
        ),
        whole(3) + far_away(3),
        [
            VMEM((WIDTH, 256), BF16),
            VMEM((WIDTH, HEAD), BF16),
            VMEM((ROWS * CTX, HEAD), BF16),
            VMEM((2 * TOKENS, HEAD), F32),
            VMEM((2 * TOKENS, HEAD), F32),
            dma((3,)),
        ],
        16,
    )(normed, table, marks, base_query, base_key, cache)

    own, other = call(
        project_kernel,
        "project",
        (shape((TOKENS, 512), F32), shape((TOKENS, 512), F32)),
        scalars() + whole(12),
        [],
        12,
    )(here, keep, given, fresh_rows, up, far, down, over, over_up, *far_over, over_down)
    other = fetch(other, 0, 0, 1)

    out_over = fetch(fresh_out, 1, 0, 0)
    out_up = fetch(fresh_out, 0, 1, 0)
    out_down = fetch(fresh_out, 0, -1, 0)
    out_over_up = fetch(out_up, 1, 0, 0)
    out_far = fetch(out_up, 0, 1, 0)
    out_over_down = fetch(out_over, 0, -1, 0)
    out_far_over = fetch(out_far, 1, 0, 0)
    mine = call(
        collect_kernel,
        "collect",
        shape((HALF, LIFT, HQ * HEAD), BF16),
        scalars() + whole(8),
        [VMEM((LIFT, HQ * HEAD), F32)],
        8,
    )(here, fresh_out, out_up, out_far, out_down, out_over, out_over_up, out_far_over, out_over_down)
    theirs = fetch(mine, 0, 0, 1)

    sent = call(
        attend_kernel,
        "attend",
        shape((PARTS, SENT, HEAD), BF16),
        whole(4) + far_away(2) + whole(4),
        [
            VMEM((ROWS * CTX, HEAD), BF16),
            VMEM((ROWS * CTX, HEAD), BF16),
            VMEM((2 * TOKENS, HEAD), F32),
            VMEM((2 * TOKENS, HEAD), F32),
            VMEM((2 * TOKENS, HEAD), F32),
            dma((2,)),
        ],
        12,
    )(own, other, table, marks, cache, values, keys, one_q, one_f, old)
    landed = lax.all_to_all(sent, "shard", split_axis=0, concat_axis=0, tiled=False)
    out, ratio = call(
        finish_kernel,
        "finish",
        (shape((TOKENS, OWN), BF16), shape((1, TOKENS), F32)),
        scalars() + whole(3),
        [
            VMEM((TOKENS, HQ * HEAD), BF16),
            VMEM((PARTS, LIFT, TOKENS), F32),
            VMEM((OWN, TOKENS), F32),
        ],
        12,
    )(here, landed, mine, theirs)
    return out.reshape(STEPS, ROWS, OWN), ratio


def solution(mesh):
    return jax.shard_map(
        local,
        mesh=mesh,
        in_specs=(
            P(None, "replica", "shard"),
            P(),
            P(),
            P(),
            P(None, "shard"),
            P(None, "shard"),
            P(None, "shard"),
            P(None, "shard"),
            P(("replica", "shard"), None),
            P(("replica", "shard"), None),
            P(("replica", "shard"), None),
            P(("replica", "shard"), None),
            P(("replica", "shard"), None),
            P(("replica", "shard"), None),
            P(("replica", "shard"), None),
            P(("replica", "shard"), None),
            P("replica", None, "shard"),
            P("replica", None, "shard"),
            P("replica"),
            P("replica", None),
            P("replica", None),
            P("replica", None),
        ),
        out_specs=(P(None, "replica", "shard"), P("replica", None)),
        check_vma=False,
    )
```

time: 177 us -> 192 us (1.085)
  blocking collectives: 45 us -> 0 us
  starting transfers between devices: 16.6 us -> 51.1 us
  local copies, waits for them, and re-layouts: 25.7 us -> 41.3 us
  between operations: 14.2 us -> 0.98 us
  waiting for transfers between devices: 58.7 us -> 70.7 us
  Pallas kernels: 14.1 us -> 21.8 us
    all_to_all x1 -> x0, blocking collectives: 45 us -> none  [local(): lax.all_to_all(parts, 'shard', split_axis=0, concat_axis=0, tiled=False)]
    ppermute x0 -> x28, starting transfers between devices: none -> 32.7 us  [the longest x19 18.7 us: fetch(): return lax.ppermute(value, 'replica', pairs)]
    ppermute x0 -> x28, waiting for transfers between devices: none -> 31.1 us  [the longest x8 23.3 us: along_shard(): return lax.ppermute(value, 'shard', pairs)]
    all_gather x1 -> x0, waiting for transfers between devices: 11 us -> none  [local(): weight = lax.all_gather(fresh_rows, 'replica', axis=0, tiled=True)]
    unnamed x60 -> x107, local copies, waits for them, and re-layouts: 24.1 us -> 32.1 us
    pallas_call x5 -> x9, Pallas kernels: 14.1 us -> 21.8 us  [the longest x1 4.3 us: local(): call(finish_kernel, 'finish', (shape((TOKENS, OWN), BF16), shape((1, TOKE...]
    all_to_all x1, waiting for transfers between devices: 15.8 us -> 10.2 us  [local(): lax.all_to_all(packed, 'shard', split_axis=0, concat_axis=0, tiled=False)]
    slice x0 -> x3, local copies, waits for them, and re-layouts: none -> 4.65 us  [the longest x1 1.56 us: local(): far[cuts[0]]]
  transfers between devices with their start and end apart: 3 -> 30, of which waited for: 3 -> 11; matrix products, arithmetic and copies ran while one was open for 2% -> 6% of each run, Pallas kernels for 2% -> 7%
where the time goes in v4:
time: 192 us; the launch traced here: 189 us
  waiting for transfers between devices  70.7 us (37%)
  starting transfers between devices  51.1 us (27%)
  local copies, waits for them, and re-layouts  41.3 us (22%)
  Pallas kernels  21.8 us (11%)
  other arithmetic  2.72 us (1%)
    unnamed x107, local copies, waits for them, and re-layouts  32.1 us
    all_to_all x1, waiting for transfers between devices, local(): lax.all_to_all(sent, 'shard', split_axis=0, concat_axis=0, tiled=False)  29.4 us
    ppermute x8, waiting for transfers between devices, along_shard(): return lax.ppermute(value, 'shard', pairs)  23.3 us
    ppermute x19, starting transfers between devices, fetch(): return lax.ppermute(value, 'replica', pairs)  18.7 us
    ppermute x8, starting transfers between devices, along_shard(): return lax.ppermute(value, 'shard', pairs)  12.1 us
    all_to_all x1, starting transfers between devices, local(): lax.all_to_all(packed, 'shard', split_axis=0, concat_axis=0, tiled=False)  11 us
    all_to_all x1, waiting for transfers between devices, local(): lax.all_to_all(packed, 'shard', split_axis=0, concat_axis=0, tiled=False)  10.2 us
    all_to_all x1, starting transfers between devices, local(): lax.all_to_all(sent, 'shard', split_axis=0, concat_axis=0, tiled=False)  7.36 us
  transfers between devices with their start and end apart: 30, of which 11 were waited for; matrix products, arithmetic and copies ran while one was open for 6% of the time, Pallas kernels for 7%

profile of v4, /device:TPU:32, one launch (start us, length us, event | category | flops | bytes accessed | tf_op | source)
XLA Modules:
  0.0 188.6 jit_solution(10809492108443497298)
XLA Ops:
  9.5 2.4 %pack.1 = (bf16[16,128,128]{2,1,0:T(8,128)(2,1)S(1)}, bf16[320,128]{1,0:T(8,128)(2,1)S(1)}, bf16[20,4096]{1,0:T(8,128)(2,1)S(1)}) custom-call(s32[1]{0:T(128)} %bitcast.here, bf16[128,320]{1,0:T(8,128)(2,1)S(1)} %bitcast.28, bf16[20,4096]{1,0:T(8,128)(2,1)S(1)} %copy-done.26, bf16[20,1024]{1,0:T(8,128)(2,1)S(1)} %copy-done.36, ...), custom_call_target="tpu_custom_call" | custom-call | tf_op jit(solution)/shard_map/pack/pallas_call | solution.py:432
  12.7 11.0 %all-to-all-start = ((bf16[16,128,128]{2,1,0:T(8,128)(2,1)}), bf16[16,128,128]{2,1,0:T(8,128)(2,1)S(1)}, u32[]{:S(2)}, u32[]{:S(2)}) async-start(bf16[16,128,128]{2,1,0:T(8,128)(2,1)} %copy-done.16), calls=%async_computation | async-start | bytes 1048576 | tf_op jit(solution)/shard_map/all_to_all | solution.py:463
  25.7 3.1 %collective-permute-start.1 = (bf16[320,128]{1,0:T(8,128)(2,1)S(1)}, bf16[320,128]{1,0:T(8,128)(2,1)S(1)}, u32[]{:S(2)}, u32[]{:S(2)}) collective-permute-start(bf16[320,128]{1,0:T(8,128)(2,1)S(1)} %get-tuple-element.41), channel_id=1, source_target_pairs={{8,0},{9,1},{10,2},{11,3},{12,4},{13,5},{14,6},{15,7},{0,8},{1,9},... | collective-permute-start | bytes 245768 | tf_op jit(solution)/shard_map/ppermute | solution.py:50
  28.7 4.4 %collective-permute-done.1 = bf16[320,128]{1,0:T(8,128)(2,1)S(1)} collective-permute-done((bf16[320,128]{1,0:T(8,128)(2,1)S(1)}, bf16[320,128]{1,0:T(8,128)(2,1)S(1)}, u32[]{:S(2)}, u32[]{:S(2)}) %collective-permute-start.1) | collective-permute-done | bytes 81952 | tf_op jit(solution)/shard_map/ppermute | solution.py:50
  33.2 5.8 %collective-permute-done.moved = bf16[20,4096]{1,0:T(8,128)(2,1)S(1)} collective-permute-done((bf16[20,4096]{1,0:T(8,128)(2,1)S(1)}, bf16[20,4096]{1,0:T(8,128)(2,1)S(1)}, u32[]{:S(2)}, u32[]{:S(2)}) %collective-permute-start) | collective-permute-done | bytes 163872 | tf_op jit(solution)/shard_map/ppermute | solution.py:461
  39.6 10.2 %all-to-all-done.recv = bf16[16,128,128]{2,1,0:T(8,128)(2,1)S(1)} async-done(((bf16[16,128,128]{2,1,0:T(8,128)(2,1)}), bf16[16,128,128]{2,1,0:T(8,128)(2,1)S(1)}, u32[]{:S(2)}, u32[]{:S(2)}) %all-to-all-start) | async-done | bytes 524320 | tf_op jit(solution)/shard_map/all_to_all | solution.py:463
  50.0 2.0 %collective-permute-start.6 = (bf16[640,128]{1,0:T(8,128)(2,1)S(1)}, bf16[640,128]{1,0:T(8,128)(2,1)S(1)}, u32[]{:S(2)}, u32[]{:S(2)}) collective-permute-start(bf16[640,128]{1,0:T(8,128)(2,1)S(1)} %constant_dynamic-update-slice_fusion.p0), channel_id=1, source_target_pairs={{7,0},{0,1},{1,2},{2,3},{3,4},{4,5},{5,6},{6,7},{15,8},{8,9},{9,10... | collective-permute-start | bytes 491528 | tf_op jit(solution)/shard_map/ppermute | solution.py:50
  56.4 2.7 %collective-permute-start.3 = (bf16[320,512]{1,0:T(8,128)(2,1)S(1)}, bf16[320,512]{1,0:T(8,128)(2,1)}, u32[]{:S(2)}, u32[]{:S(2)}) collective-permute-start(bf16[320,512]{1,0:T(8,128)(2,1)S(1)} %refresh.1.w00), channel_id=1, source_target_pairs={{32,0},{48,16},{64,32},{80,48},{96,64},{112,80},{0,96},{16,112},{1... | collective-permute-start | bytes 983048 | tf_op jit(solution)/shard_map/ppermute | solution.py:45
  59.1 2.7 %collective-permute-start.4 = (bf16[320,512]{1,0:T(8,128)(2,1)S(1)}, bf16[320,512]{1,0:T(8,128)(2,1)S(1)}, u32[]{:S(2)}, u32[]{:S(2)}) collective-permute-start(bf16[320,512]{1,0:T(8,128)(2,1)S(1)} %refresh.1.w00), channel_id=1, source_target_pairs={{96,0},{112,16},{0,32},{16,48},{32,64},{48,80},{64,96},{80,112},{2... | collective-permute-start | bytes 983048 | tf_op jit(solution)/shard_map/ppermute | solution.py:45
  63.2 5.4 %collective-permute-start.7 = (bf16[640,128]{1,0:T(8,128)(2,1)S(1)}, bf16[640,128]{1,0:T(8,128)(2,1)}, u32[]{:S(2)}, u32[]{:S(2)}) collective-permute-start(bf16[640,128]{1,0:T(8,128)(2,1)S(1)} %constant_dynamic-update-slice_fusion.p0), channel_id=1, source_target_pairs={{2,0},{3,1},{4,2},{5,3},{6,4},{7,5},{0,6},{1,7},{10,8},{11,9},{12,... | collective-permute-start | bytes 491528 | tf_op jit(solution)/shard_map/ppermute | solution.py:50
  69.3 3.7 %collective-permute-done.7.p2 = bf16[640,128]{1,0:T(8,128)(2,1)} collective-permute-done((bf16[640,128]{1,0:T(8,128)(2,1)S(1)}, bf16[640,128]{1,0:T(8,128)(2,1)}, u32[]{:S(2)}, u32[]{:S(2)}) %collective-permute-start.7) | collective-permute-done | bytes 163872 | tf_op jit(solution)/shard_map/ppermute | solution.py:50
  73.0 5.6 %collective-permute-done.8.p6 = bf16[640,128]{1,0:T(8,128)(2,1)} collective-permute-done((bf16[640,128]{1,0:T(8,128)(2,1)S(1)}, bf16[640,128]{1,0:T(8,128)(2,1)}, u32[]{:S(2)}, u32[]{:S(2)}) %collective-permute-start.8) | collective-permute-done | bytes 163872 | tf_op jit(solution)/shard_map/ppermute | solution.py:50
  82.9 5.8 %collective-permute-done.12.p3 = bf16[640,128]{1,0:T(8,128)(2,1)S(1)} collective-permute-done((bf16[640,128]{1,0:T(8,128)(2,1)}, bf16[640,128]{1,0:T(8,128)(2,1)S(1)}, u32[]{:S(2)}, u32[]{:S(2)}) %collective-permute-start.12) | collective-permute-done | bytes 163872 | tf_op jit(solution)/shard_map/ppermute | solution.py:50
  91.2 3.8 %collective-permute-done.14.p5 = bf16[640,128]{1,0:T(8,128)(2,1)} collective-permute-done((bf16[640,128]{1,0:T(8,128)(2,1)}, bf16[640,128]{1,0:T(8,128)(2,1)}, u32[]{:S(2)}, u32[]{:S(2)}) %collective-permute-start.14) | collective-permute-done | bytes 163872 | tf_op jit(solution)/shard_map/ppermute | solution.py:50
  99.4 2.5 %normalise.1 = (bf16[16,128,320]{2,1,0:T(8,128)(2,1)S(1)}, bf16[8,128,320]{2,1,0:T(8,128)(2,1)S(1)}, bf16[8,128,320]{2,1,0:T(8,128)(2,1)S(1)}) custom-call(s32[1]{0:T(128)} %bitcast.here, s32[1]{0:T(128)} %bitcast.1.seat, f32[16,1,320]{2,1,0:T(1,128)S(1)} %reshape.58.gain, bf16[640,128]{1,0:T(8,128)(2,1)S(1)} %copy-done.19, bf16[640,128]{1,0:T(8,128)(2,1)S(1)} %copy-done.30, ...), custom_call_target="tpu_custom_call" | custom-call | tf_op jit(solution)/shard_map/normalise/pallas_call | solution.py:515
  111.5 2.6 %collective-permute-start.17 = (bf16[112,512]{1,0:T(8,128)(2,1)}, bf16[112,512]{1,0:T(8,128)(2,1)}, u32[]{:S(2)}, u32[]{:S(2)}) collective-permute-start(bf16[112,512]{1,0:T(8,128)(2,1)} %slice.10), channel_id=1, source_target_pairs={{32,0},{48,16},{64,32},{80,48},{96,64},{112,80},{0,96},{16,112},{1... | collective-permute-start | bytes 344072 | tf_op jit(solution)/shard_map/ppermute | solution.py:45
  115.7 3.2 %collective-permute-start.21 = (bf16[20,4096]{1,0:T(8,128)(2,1)}, bf16[20,4096]{1,0:T(8,128)(2,1)}, u32[]{:S(2)}, u32[]{:S(2)}) collective-permute-start(bf16[20,4096]{1,0:T(8,128)(2,1)} %collective-permute-done.20.w1), channel_id=1, source_target_pairs={{32,0},{48,16},{64,32},{80,48},{96,64},{112,80},{0,96},{16,112},{1... | collective-permute-start | bytes 491528 | tf_op jit(solution)/shard_map/ppermute | solution.py:45
  128.2 3.3 %project.1 = (f32[128,512]{1,0:T(8,128)S(1)}, f32[128,512]{1,0:T(8,128)}) custom-call(s32[1]{0:T(128)} %bitcast.here, bf16[8,128,320]{2,1,0:T(8,128)(2,1)S(1)} %copy-done.11, bf16[8,128,320]{2,1,0:T(8,128)(2,1)S(1)} %copy.25.given, bf16[320,512]{1,0:T(8,128)(2,1)S(1)} %copy-done.8, bf16[320,512]{1,0:T(8,128)(2,1)} %collective-permute-done.3.w01, ...), custom_call_target="tpu_custom_call" | custom-call | tf_op jit(solution)/shard_map/project/pallas_call | solution.py:587
  132.5 2.7 %collect.1.mine = bf16[8,32,4096]{2,1,0:T(8,128)(2,1)} custom-call(s32[1]{0:T(128)} %bitcast.here, bf16[20,4096]{1,0:T(8,128)(2,1)S(1)} %copy-done.13, bf16[20,4096]{1,0:T(8,128)(2,1)} %collective-permute-done.20.w1, bf16[20,4096]{1,0:T(8,128)(2,1)} %collective-permute-done.21.w2, bf16[20,4096]{1,0:T(8,128)(2,1)S(1)} %collective-permute-done.22.w3, ...), custom_call_target="tpu_custom_call" | custom-call | tf_op jit(solution)/shard_map/collect/pallas_call | solution.py:604
  141.6 2.7 %old.1 = (f32[128,128]{1,0:T(8,128)S(1)}, bf16[128,128]{1,0:T(8,128)(2,1)S(1)}, bf16[128,128]{1,0:T(8,128)(2,1)S(1)}, f32[2,128,128]{2,1,0:T(8,128)S(1)}) custom-call(bf16[16,128,320]{2,1,0:T(8,128)(2,1)S(1)} %copy-done.6, f32[264,128]{1,0:T(8,128)S(1)} %concatenate.18.table, s32[40,128]{1,0:T(8,128)S(1)} %copy-done.28, bf16[5120,256]{1,0:T(8,128)(2,1)S(1)} %copy-done, ...), custom_call_target="tpu_custom_call" | custom-call | tf_op jit(solution)/shard_map/old/pallas_call | solution.py:566
  144.3 3.3 %attend.1 = bf16[16,272,128]{2,1,0:T(8,128)(2,1)} custom-call(f32[128,512]{1,0:T(8,128)S(1)} %copy-done.23, f32[128,512]{1,0:T(8,128)S(1)} %collective-permute-done.19.other, f32[264,128]{1,0:T(8,128)S(1)} %concatenate.18.table, s32[40,128]{1,0:T(8,128)S(1)} %copy-done.28, bf16[2048,128]{1,0:T(8,128)(2,1)S(1)} %bitcast.26, bf16[2048,128]{1,0:T(8,128)(2,1)S(1)} %bitcast.27, ...), custom_call_target="tpu_custom_call" | custom-call | tf_op jit(solution)/shard_map/attend/pallas_call | solution.py:614
  147.6 7.4 %all-to-all-start.1 = ((bf16[16,272,128]{2,1,0:T(8,128)(2,1)}), bf16[16,272,128]{2,1,0:T(8,128)(2,1)S(1)}, u32[]{:S(2)}, u32[]{:S(2)}) async-start(bf16[16,272,128]{2,1,0:T(8,128)(2,1)} %attend.1), calls=%async_computation.1 | async-start | bytes 2228224 | tf_op jit(solution)/shard_map/all_to_all | solution.py:629
  154.9 29.4 %all-to-all-done.1.recv = bf16[16,272,128]{2,1,0:T(8,128)(2,1)S(1)} async-done(((bf16[16,272,128]{2,1,0:T(8,128)(2,1)}), bf16[16,272,128]{2,1,0:T(8,128)(2,1)S(1)}, u32[]{:S(2)}, u32[]{:S(2)}) %all-to-all-start.1) | async-done | bytes 1114144 | tf_op jit(solution)/shard_map/all_to_all | solution.py:629
  184.3 4.3 %finish.1 = (bf16[128,320]{1,0:T(8,128)(2,1)}, f32[1,128]{1,0:T(1,128)}) custom-call(s32[1]{0:T(128)} %bitcast.here, bf16[16,272,128]{2,1,0:T(8,128)(2,1)S(1)} %all-to-all-done.1.recv, bf16[8,32,4096]{2,1,0:T(8,128)(2,1)} %collect.1.mine, bf16[8,32,4096]{2,1,0:T(8,128)(2,1)} %collective-permute-done.27.theirs), custom_call_target="tpu_custom_call" | custom-call | tf_op jit(solution)/shard_map/finish/pallas_call | solution.py:630
  (172 shorter events, 57.7 us)
Async XLA Ops:
  12.7 37.2 %all-to-all-start = ((bf16[16,128,128]{2,1,0:T(8,128)(2,1)}), bf16[16,128,128]{2,1,0:T(8,128)(2,1)S(1)}, u32[]{:S(2)}, u32[]{:S(2)}) async-start(bf16[16,128,128]{2,1,0:T(8,128)(2,1)} %copy-done.16), calls=%async_computation | async-start | bytes 1048576 | tf_op jit(solution)/shard_map/all_to_all | solution.py:463
  23.8 15.2 %collective-permute-start = (bf16[20,4096]{1,0:T(8,128)(2,1)S(1)}, bf16[20,4096]{1,0:T(8,128)(2,1)S(1)}, u32[]{:S(2)}, u32[]{:S(2)}) collective-permute-start(bf16[20,4096]{1,0:T(8,128)(2,1)S(1)} %get-tuple-element.39), channel_id=1, source_target_pairs={{0,0},{1,16},{2,32},{3,48},{4,64},{5,80},{6,96},{7,112},{8,128},{9... | collective-permute-start | bytes 491528 | tf_op jit(solution)/shard_map/ppermute | solution.py:461
  49.9 12.6 %collective-permute-start.5 = (bf16[640,128]{1,0:T(8,128)(2,1)S(1)}, bf16[640,128]{1,0:T(8,128)(2,1)S(1)}, u32[]{:S(2)}, u32[]{:S(2)}) collective-permute-start(bf16[640,128]{1,0:T(8,128)(2,1)S(1)} %constant_dynamic-update-slice_fusion.p0), channel_id=1, source_target_pairs={{1,0},{2,1},{3,2},{4,3},{5,4},{6,5},{7,6},{0,7},{9,8},{10,9},{11,1... | collective-permute-start | bytes 491528 | tf_op jit(solution)/shard_map/ppermute | solution.py:50
  50.0 18.6 %collective-permute-start.6 = (bf16[640,128]{1,0:T(8,128)(2,1)S(1)}, bf16[640,128]{1,0:T(8,128)(2,1)S(1)}, u32[]{:S(2)}, u32[]{:S(2)}) collective-permute-start(bf16[640,128]{1,0:T(8,128)(2,1)S(1)} %constant_dynamic-update-slice_fusion.p0), channel_id=1, source_target_pairs={{7,0},{0,1},{1,2},{2,3},{3,4},{4,5},{5,6},{6,7},{15,8},{8,9},{9,10... | collective-permute-start | bytes 491528 | tf_op jit(solution)/shard_map/ppermute | solution.py:50
  55.3 23.3 %collective-permute-start.2 = (bf16[320,512]{1,0:T(8,128)(2,1)S(1)}, bf16[320,512]{1,0:T(8,128)(2,1)}, u32[]{:S(2)}, u32[]{:S(2)}) collective-permute-start(bf16[320,512]{1,0:T(8,128)(2,1)S(1)} %refresh.1.w00), channel_id=1, source_target_pairs={{128,0},{144,16},{160,32},{176,48},{192,64},{208,80},{224,96},{240... | collective-permute-start | bytes 983048 | tf_op jit(solution)/shard_map/ppermute | solution.py:45
  56.4 22.2 %collective-permute-start.3 = (bf16[320,512]{1,0:T(8,128)(2,1)S(1)}, bf16[320,512]{1,0:T(8,128)(2,1)}, u32[]{:S(2)}, u32[]{:S(2)}) collective-permute-start(bf16[320,512]{1,0:T(8,128)(2,1)S(1)} %refresh.1.w00), channel_id=1, source_target_pairs={{32,0},{48,16},{64,32},{80,48},{96,64},{112,80},{0,96},{16,112},{1... | collective-permute-start | bytes 983048 | tf_op jit(solution)/shard_map/ppermute | solution.py:45
  59.1 19.4 %collective-permute-start.4 = (bf16[320,512]{1,0:T(8,128)(2,1)S(1)}, bf16[320,512]{1,0:T(8,128)(2,1)S(1)}, u32[]{:S(2)}, u32[]{:S(2)}) collective-permute-start(bf16[320,512]{1,0:T(8,128)(2,1)S(1)} %refresh.1.w00), channel_id=1, source_target_pairs={{96,0},{112,16},{0,32},{16,48},{32,64},{48,80},{64,96},{80,112},{2... | collective-permute-start | bytes 983048 | tf_op jit(solution)/shard_map/ppermute | solution.py:45
  63.2 9.8 %collective-permute-start.7 = (bf16[640,128]{1,0:T(8,128)(2,1)S(1)}, bf16[640,128]{1,0:T(8,128)(2,1)}, u32[]{:S(2)}, u32[]{:S(2)}) collective-permute-start(bf16[640,128]{1,0:T(8,128)(2,1)S(1)} %constant_dynamic-update-slice_fusion.p0), channel_id=1, source_target_pairs={{2,0},{3,1},{4,2},{5,3},{6,4},{7,5},{0,6},{1,7},{10,8},{11,9},{12,... | collective-permute-start | bytes 491528 | tf_op jit(solution)/shard_map/ppermute | solution.py:50
  79.3 9.3 %collective-permute-start.12 = (bf16[640,128]{1,0:T(8,128)(2,1)}, bf16[640,128]{1,0:T(8,128)(2,1)S(1)}, u32[]{:S(2)}, u32[]{:S(2)}) collective-permute-start(bf16[640,128]{1,0:T(8,128)(2,1)} %collective-permute-done.7.p2), channel_id=1, source_target_pairs={{1,0},{2,1},{3,2},{4,3},{5,4},{6,5},{7,6},{0,7},{9,8},{10,9},{11,1... | collective-permute-start | bytes 491528 | tf_op jit(solution)/shard_map/ppermute | solution.py:50
  79.9 15.1 %collective-permute-start.9 = (bf16[320,512]{1,0:T(8,128)(2,1)}, bf16[320,512]{1,0:T(8,128)(2,1)S(1)}, u32[]{:S(2)}, u32[]{:S(2)}) collective-permute-start(bf16[320,512]{1,0:T(8,128)(2,1)} %collective-permute-done.3.w01), channel_id=1, source_target_pairs={{128,0},{144,16},{160,32},{176,48},{192,64},{208,80},{224,96},{240... | collective-permute-start | bytes 983048 | tf_op jit(solution)/shard_map/ppermute | solution.py:45
  79.9 15.1 %collective-permute-start.10 = (bf16[320,512]{1,0:T(8,128)(2,1)}, bf16[320,512]{1,0:T(8,128)(2,1)}, u32[]{:S(2)}, u32[]{:S(2)}) collective-permute-start(bf16[320,512]{1,0:T(8,128)(2,1)} %collective-permute-done.3.w01), channel_id=1, source_target_pairs={{32,0},{48,16},{64,32},{80,48},{96,64},{112,80},{0,96},{16,112},{1... | collective-permute-start | bytes 983048 | tf_op jit(solution)/shard_map/ppermute | solution.py:45
  81.8 13.2 %collective-permute-start.11 = (bf16[320,512]{1,0:T(8,128)(2,1)}, bf16[320,512]{1,0:T(8,128)(2,1)}, u32[]{:S(2)}, u32[]{:S(2)}) collective-permute-start(bf16[320,512]{1,0:T(8,128)(2,1)} %collective-permute-done.2.w10), channel_id=1, source_target_pairs={{96,0},{112,16},{0,32},{16,48},{32,64},{48,80},{64,96},{80,112},{2... | collective-permute-start | bytes 983048 | tf_op jit(solution)/shard_map/ppermute | solution.py:45
  105.1 10.6 %collective-permute-start.15 = (bf16[8,128,320]{1,2,0:T(8,128)(2,1)}, bf16[8,128,320]{1,2,0:T(8,128)(2,1)S(1)}, u32[]{:S(2)}, u32[]{:S(2)}) collective-permute-start(bf16[8,128,320]{1,2,0:T(8,128)(2,1)} %copy.24), channel_id=1, source_target_pairs={{16,0},{0,16},{48,32},{32,48},{80,64},{64,80},{112,96},{96,112},{1... | collective-permute-start | bytes 1966088 | tf_op jit(solution)/shard_map/ppermute | solution.py:45
  105.2 10.5 %collective-permute-start.20 = (bf16[20,4096]{1,0:T(8,128)(2,1)}, bf16[20,4096]{1,0:T(8,128)(2,1)}, u32[]{:S(2)}, u32[]{:S(2)}) collective-permute-start(bf16[20,4096]{1,0:T(8,128)(2,1)} %copy-done.12), channel_id=1, source_target_pairs={{32,0},{48,16},{64,32},{80,48},{96,64},{112,80},{0,96},{16,112},{1... | collective-permute-start | bytes 491528 | tf_op jit(solution)/shard_map/ppermute | solution.py:45
  106.4 15.5 %collective-permute-start.23 = (bf16[20,4096]{1,0:T(8,128)(2,1)}, bf16[20,4096]{1,0:T(8,128)(2,1)}, u32[]{:S(2)}, u32[]{:S(2)}) collective-permute-start(bf16[20,4096]{1,0:T(8,128)(2,1)} %copy-done.12), channel_id=1, source_target_pairs={{128,0},{144,16},{160,32},{176,48},{192,64},{208,80},{224,96},{240... | collective-permute-start | bytes 491528 | tf_op jit(solution)/shard_map/ppermute | solution.py:45
  108.6 13.3 %collective-permute-start.16 = (bf16[112,512]{1,0:T(8,128)(2,1)}, bf16[112,512]{1,0:T(8,128)(2,1)S(1)}, u32[]{:S(2)}, u32[]{:S(2)}) collective-permute-start(bf16[112,512]{1,0:T(8,128)(2,1)} %slice.9), channel_id=1, source_target_pairs={{128,0},{144,16},{160,32},{176,48},{192,64},{208,80},{224,96},{240... | collective-permute-start | bytes 344072 | tf_op jit(solution)/shard_map/ppermute | solution.py:45
  111.5 12.6 %collective-permute-start.17 = (bf16[112,512]{1,0:T(8,128)(2,1)}, bf16[112,512]{1,0:T(8,128)(2,1)}, u32[]{:S(2)}, u32[]{:S(2)}) collective-permute-start(bf16[112,512]{1,0:T(8,128)(2,1)} %slice.10), channel_id=1, source_target_pairs={{32,0},{48,16},{64,32},{80,48},{96,64},{112,80},{0,96},{16,112},{1... | collective-permute-start | bytes 344072 | tf_op jit(solution)/shard_map/ppermute | solution.py:45
  121.8 10.5 %collective-permute-start.22 = (bf16[20,4096]{1,0:T(8,128)(2,1)}, bf16[20,4096]{1,0:T(8,128)(2,1)S(1)}, u32[]{:S(2)}, u32[]{:S(2)}) collective-permute-start(bf16[20,4096]{1,0:T(8,128)(2,1)} %copy-done.12), channel_id=1, source_target_pairs={{96,0},{112,16},{0,32},{16,48},{32,64},{48,80},{64,96},{80,112},{2... | collective-permute-start | bytes 491528 | tf_op jit(solution)/shard_map/ppermute | solution.py:45
  121.8 10.5 %collective-permute-start.24 = (bf16[20,4096]{1,0:T(8,128)(2,1)}, bf16[20,4096]{1,0:T(8,128)(2,1)S(1)}, u32[]{:S(2)}, u32[]{:S(2)}) collective-permute-start(bf16[20,4096]{1,0:T(8,128)(2,1)} %collective-permute-done.20.w1), channel_id=1, source_target_pairs={{128,0},{144,16},{160,32},{176,48},{192,64},{208,80},{224,96},{240... | collective-permute-start | bytes 491528 | tf_op jit(solution)/shard_map/ppermute | solution.py:45
  121.8 10.6 %collective-permute-start.26 = (bf16[20,4096]{1,0:T(8,128)(2,1)}, bf16[20,4096]{1,0:T(8,128)(2,1)S(1)}, u32[]{:S(2)}, u32[]{:S(2)}) collective-permute-start(bf16[20,4096]{1,0:T(8,128)(2,1)} %collective-permute-done.23.w4), channel_id=1, source_target_pairs={{96,0},{112,16},{0,32},{16,48},{32,64},{48,80},{64,96},{80,112},{2... | collective-permute-start | bytes 491528 | tf_op jit(solution)/shard_map/ppermute | solution.py:45
  122.7 9.8 %collective-permute-start.25 = (bf16[20,4096]{1,0:T(8,128)(2,1)}, bf16[20,4096]{1,0:T(8,128)(2,1)S(1)}, u32[]{:S(2)}, u32[]{:S(2)}) collective-permute-start(bf16[20,4096]{1,0:T(8,128)(2,1)} %collective-permute-done.21.w2), channel_id=1, source_target_pairs={{128,0},{144,16},{160,32},{176,48},{192,64},{208,80},{224,96},{240... | collective-permute-start | bytes 491528 | tf_op jit(solution)/shard_map/ppermute | solution.py:45
  131.5 12.8 %collective-permute-start.19 = (f32[128,512]{1,0:T(8,128)}, f32[128,512]{1,0:T(8,128)S(1)}, u32[]{:S(2)}, u32[]{:S(2)}) collective-permute-start(f32[128,512]{1,0:T(8,128)} %get-tuple-element.61), channel_id=1, source_target_pairs={{16,0},{0,16},{48,32},{32,48},{80,64},{64,80},{112,96},{96,112},{1... | collective-permute-start | bytes 786440 | tf_op jit(solution)/shard_map/ppermute | solution.py:45
  135.2 19.7 %collective-permute-start.27 = (bf16[8,32,4096]{2,1,0:T(8,128)(2,1)}, bf16[8,32,4096]{2,1,0:T(8,128)(2,1)}, u32[]{:S(2)}, u32[]{:S(2)}) collective-permute-start(bf16[8,32,4096]{2,1,0:T(8,128)(2,1)} %collect.1.mine), channel_id=1, source_target_pairs={{16,0},{0,16},{48,32},{32,48},{80,64},{64,80},{112,96},{96,112},{1... | collective-permute-start | bytes 6291464 | tf_op jit(solution)/shard_map/ppermute | solution.py:45
  147.6 36.8 %all-to-all-start.1 = ((bf16[16,272,128]{2,1,0:T(8,128)(2,1)}), bf16[16,272,128]{2,1,0:T(8,128)(2,1)S(1)}, u32[]{:S(2)}, u32[]{:S(2)}) async-start(bf16[16,272,128]{2,1,0:T(8,128)(2,1)} %attend.1), calls=%async_computation.1 | async-start | bytes 2228224 | tf_op jit(solution)/shard_map/all_to_all | solution.py:629
  (59 other events, 286.7 us)

commit v5 on v4

v5 whole, which is shorter than its diff:
```python
import jax
import jax.numpy as jnp
from jax import lax
from jax.experimental import pallas as pl
from jax.experimental.pallas import tpu as pltpu
from jax.sharding import PartitionSpec as P

HQ = 32
KV = 8
HEAD = 128
WIDTH = 5120
STEPS = 4
ROWS = 32
TOKENS = STEPS * ROWS
CTX = 64
PARTS = 16
OWN = WIDTH // PARTS
CUT = 20
GROUP = 8
GROUPS = ROWS // GROUP
TAIL = 16
EPSILON = 1e-06
THETA = 1000000.0
SCALE = HEAD ** (-0.5)
NEG = -1e30
TILES = ((0, 128), (128, 128), (256, 64))
BLOCK = 128
HALF = PARTS // 2
FOLD = OWN // 2
TALL = OWN + FOLD
WIDE = 384
SENT = OWN + TAIL
F32 = jnp.float32
BF16 = jnp.bfloat16
VMEM = pltpu.VMEM


def fetch(value, dx, dy, dc):
    pairs = []
    for i in range(16):
        x, y, c = i >> 3, (i >> 1) & 3, i & 1
        pairs.append((((x ^ dx) << 3) + (((y + dy) & 3) << 1) + (c ^ dc), i))
    return lax.ppermute(value, "replica", pairs)


def along_shard(value, dx, dz):
    pairs = [((((i >> 3) ^ dx) << 3) + ((i + dz) & 7), i) for i in range(16)]
    return lax.ppermute(value, "shard", pairs)


def factors(codes):
    out = jnp.ones(codes.shape, F32)
    for bit in range(5):
        out = out * jnp.where((codes >> bit) & 1 == 1, F32(2.0 ** -(2**bit)), F32(1.0))
    return out


def start_all(copies):
    for copy in copies:
        copy.start()


def pack_kernel(
    hidden, dq, dk, dv, do, sq, so, skt, svt,
    out, turned,
    vh, vq, vk, vv, vo, vsq, vso, vsk, vsv, buf, sems,
):
    pairs = [(hidden, vh), (sq, vsq), (so, vso), (skt, vsk), (svt, vsv)]
    pairs += [(dq, vq), (dk, vk), (dv, vv), (do, vo)]
    copies = [pltpu.make_async_copy(a, b, sems.at[i]) for i, (a, b) in enumerate(pairs)]
    start_all(copies)
    for copy in copies[:5]:
        copy.wait()
    for at, n in TILES:
        turned[at : at + n, :] = vh[:, at : at + n].astype(F32).T.astype(BF16)
    fq, fo, fk, fv = factors(vsq[...]), factors(vso[...]), factors(vsk[...]), factors(vsv[...])
    line = lax.broadcasted_iota(jnp.int32, (CUT, CUT), 0)
    lane = lax.broadcasted_iota(jnp.int32, (CUT, CUT), 1)

    def column(factor, head):
        spread = jnp.where(line == lane, factor[head : head + 1, :], 0.0)
        return jnp.sum(spread, axis=1, keepdims=True)

    def piece(codes, head, factor):
        return codes[:, head * HEAD : (head + 1) * HEAD].astype(F32) * factor

    for copy in copies[5:]:
        copy.wait()
    buf[6 * CUT : BLOCK, :] = jnp.zeros((BLOCK - 6 * CUT, HEAD), F32)
    for half in range(PARTS // 2):
        key, value = piece(vk, half, column(fk, half)), piece(vv, half, column(fv, half))
        for dest in (2 * half, 2 * half + 1):
            pieces = (
                piece(vq, 2 * dest, fq[:, 2 * dest : 2 * dest + 1]),
                piece(vq, 2 * dest + 1, fq[:, 2 * dest + 1 : 2 * dest + 2]),
                key,
                value,
                piece(vo, 2 * dest, fo[:, 2 * dest : 2 * dest + 1]),
                piece(vo, 2 * dest + 1, fo[:, 2 * dest + 1 : 2 * dest + 2]),
            )
            for c, item in enumerate(pieces):
                buf[CUT * c : CUT * (c + 1), :] = item
            out[dest] = buf[...].astype(BF16)


def refresh_kernel(
    here, recv, bq, bk, bv, bo, out, vq, vk, vv, vo, buf, delta, fresh, sems,
):
    at = pl.ds(pl.multiple_of(OWN * here[0], 64), OWN)
    bases = ((bq, vq), (bk, vk), (bv, vv), (bo, vo))
    copies = [
        pltpu.make_async_copy(a.at[at, :], b, sems.at[i]) for i, (a, b) in enumerate(bases)
    ]
    start_all(copies)
    for src in range(PARTS):
        buf[src % 2] = recv[src].astype(F32)
        for c in range(6):
            delta[CUT * src : CUT * (src + 1), HEAD * c : HEAD * (c + 1)] = buf[
                src % 2, CUT * c : CUT * (c + 1), :
            ]
    for copy in copies:
        copy.wait()
    for at, n, base in ((0, 256, vq), (256, 128, vk), (384, 128, vv)):
        fresh[0:OWN, at : at + n] = (base[...].astype(F32) + delta[:, at : at + n]).astype(BF16)
    for half in range(2):
        at = slice(half * FOLD, (half + 1) * FOLD)
        value = vo[at, :].astype(F32) + delta[at, 512:768]
        fresh[OWN:, half * 256 : (half + 1) * 256] = value.astype(BF16)
    copies = [pltpu.make_async_copy(fresh, out.at[j], sems.at[4 + j]) for j in range(HALF)]
    start_all(copies)
    for copy in copies:
        copy.wait()


def dot_nt(a, b):
    return lax.dot_general(a, b, (((1,), (1,)), ((), ())), preferred_element_type=F32)


def dot(a, b):
    return jnp.dot(a, b, preferred_element_type=F32)


def head_norm_rotate(raw, gain, cosine, sine):
    value = raw * lax.rsqrt(jnp.mean(raw * raw, axis=-1, keepdims=True) + EPSILON) * gain
    swapped = jnp.concatenate([value[:, HEAD // 2 :], value[:, : HEAD // 2]], axis=-1)
    return value * cosine + swapped * sine


def group_scores(group, query, cache, fresh, lens):
    picked = [
        query[h * TOKENS + t * ROWS + group * GROUP : h * TOKENS + t * ROWS + (group + 1) * GROUP, :]
        for h in range(2)
        for t in range(STEPS)
    ]
    q = jnp.concatenate(picked, axis=0).astype(BF16)
    past = dot_nt(q, cache) * SCALE
    new = dot_nt(q, fresh) * SCALE
    n = 2 * STEPS * GROUP
    length = jnp.concatenate([lens[group * GROUP : (group + 1) * GROUP, :]] * (2 * STEPS), axis=0)
    column = lax.broadcasted_iota(jnp.int32, past.shape, 1)
    line = lax.broadcasted_iota(jnp.int32, past.shape, 0)
    past_ok = ((column >> 6) == (line & 7)) & ((column & 63) < length[:, 0:1])
    column = lax.broadcasted_iota(jnp.int32, (n, TOKENS), 1)
    line = lax.broadcasted_iota(jnp.int32, (n, TOKENS), 0)
    new_ok = ((column & 31) == group * GROUP + (line & 7)) & ((column >> 5) <= ((line >> 3) & 3))
    past = jnp.where(past_ok, past, NEG)
    new = jnp.where(new_ok, new, NEG)
    top = jnp.maximum(
        jnp.max(past, axis=-1, keepdims=True), jnp.max(new, axis=-1, keepdims=True)
    )
    past = jnp.exp(past - top)
    new = jnp.exp(new - top)
    total = jnp.sum(past, axis=-1, keepdims=True) + jnp.sum(new, axis=-1, keepdims=True)
    return past, new, total, top + jnp.log(total)


def put_groups(group, ref, value):
    for h in range(2):
        for t in range(STEPS):
            at = h * TOKENS + t * ROWS + group * GROUP
            i = (h * STEPS + t) * GROUP
            ref[at : at + GROUP, :] = value[i : i + GROUP, :]


def sample_logp(query, keys, one_query, lse):
    out = []
    for h in range(2):
        q = dot(one_query, query[h * TOKENS : (h + 1) * TOKENS, :].astype(BF16))
        score = jnp.sum(q * keys, axis=-1, keepdims=True) * SCALE
        line = lse[h * TOKENS : (h + 1) * TOKENS, :].T
        picked = jnp.sum(one_query.astype(F32) * line, axis=-1, keepdims=True)
        out.append(jnp.broadcast_to(score - picked, (TOKENS, HEAD)))
    return out


def normalise_kernel(here, seat, gain, p0, p1, p2, p3, p4, p5, p6, p7, keep, give):
    total = jnp.zeros((1, TOKENS), F32)
    pairs = (p0, p1, p2, p3, p4, p5, p6, p7)
    for pair in pairs:
        x = pair[...].astype(F32)
        total = total + jnp.sum(x * x, axis=0, keepdims=True)
    scale = lax.rsqrt(total * (1.0 / WIDTH) + EPSILON)
    me, core = seat[0], here[0] & 1

    def put(step, pair, target):
        for half in range(2):
            src = (((me >> 3) ^ half) << 3) + ((me + step) & 7)
            for at, n in TILES:
                x = pair[half * OWN + at : half * OWN + at + n, :].astype(F32) * scale
                value = (x.T * gain[src, :, at : at + n]).astype(BF16)
                target[src >> 1, :, at : at + n] = value
            target[src >> 1, :, OWN:] = jnp.zeros((TOKENS, WIDE - OWN), BF16)

    for step, pair in enumerate(pairs):
        same = ((me + step) & 1) == core
        pl.when(same)(lambda step=step, pair=pair: put(step, pair, keep))
        pl.when(jnp.logical_not(same))(lambda step=step, pair=pair: put(step, pair, give))


def select_kernel(marks, cache_hbm, keys_out, one_q_out, one_f_out, cache, sems):
    copy = pltpu.make_async_copy(cache_hbm, cache, sems.at[0])
    copy.start()
    tokens = jnp.broadcast_to(marks[ROWS : ROWS + 1, :], (TOKENS, TOKENS)).T
    places = jnp.broadcast_to(marks[ROWS + 1 : ROWS + 2, :], (TOKENS, TOKENS)).T
    lane = lax.broadcasted_iota(jnp.int32, (TOKENS, TOKENS), 1)
    one_q = jnp.where(tokens == lane, F32(1.0), F32(0.0)).astype(BF16)
    one_f = jnp.where(places == lane + ROWS * CTX, F32(1.0), F32(0.0)).astype(BF16)
    copy.wait()
    keys = jnp.zeros((TOKENS, HEAD), F32)
    for k in range(ROWS * CTX // HEAD):
        one = jnp.where(places == lane + k * HEAD, F32(1.0), F32(0.0)).astype(BF16)
        keys = keys + dot(one, cache[k * HEAD : (k + 1) * HEAD, :])
    keys_out[...] = keys
    one_q_out[...] = one_q
    one_f_out[...] = one_f


def old_kernel(
    here, keep, give, table, marks, keys, one_q, one_f, base_q, base_k, cache_hbm,
    old_out,
    wq, wk, cache, query, lse, sems,
):
    quarter = WIDTH // 4
    copies = []
    for i in range(4):
        at = pl.ds(i * quarter, quarter)
        copies += [
            pltpu.make_async_copy(base_q.at[at, :], wq.at[at, :], sems.at[2 * i]),
            pltpu.make_async_copy(base_k.at[at, :], wk.at[at, :], sems.at[2 * i + 1]),
        ]
    copies.append(pltpu.make_async_copy(cache_hbm, cache, sems.at[8]))
    start_all(copies)
    core = here[0] & 1
    raw = jnp.zeros((TOKENS, 256), F32)
    raw_k = jnp.zeros((TOKENS, HEAD), F32)
    for j in range(HALF):
        if j % 2 == 0:
            copies[j].wait()
            copies[j + 1].wait()
        for lines, src in ((keep, 2 * j + core), (give, 2 * j + 1 - core)):
            at = pl.ds(pl.multiple_of(OWN * src, 64), OWN)
            raw = raw + dot(lines[j, :, 0:OWN], wq[at, :])
            raw_k = raw_k + dot(lines[j, :, 0:OWN], wk[at, :])
    copies[8].wait()
    cos, sin = table[0:TOKENS, :], table[TOKENS : 2 * TOKENS, :]
    qg, kg = table[2 * TOKENS : 2 * TOKENS + 1, :], table[2 * TOKENS + 1 : 2 * TOKENS + 2, :]
    lens = marks
    for h in range(2):
        query[h * TOKENS : (h + 1) * TOKENS, :] = (
            head_norm_rotate(raw[:, h * HEAD : (h + 1) * HEAD], qg, cos, sin)
            .astype(BF16)
            .astype(F32)
        )
    fresh = head_norm_rotate(raw_k, kg, cos, sin).astype(BF16)
    for g in range(GROUPS):
        _, _, _, log_sum = group_scores(
            g, query, cache[g * GROUP * CTX : (g + 1) * GROUP * CTX, :], fresh, lens
        )
        put_groups(g, lse, jnp.broadcast_to(log_sum, (log_sum.shape[0], HEAD)))
    old = sample_logp(query, keys[...] + dot(one_f[...], fresh), one_q[...], lse)
    old_out[0] = old[0]
    old_out[1] = old[1]


def project_kernel(keep, given, weight, own, other, below):
    raw = jnp.zeros((2 * TOKENS, 512), F32)
    for j in range(HALF):
        lines = jnp.concatenate([keep[j, :, 0:OWN], given[j, :, 0:OWN]], axis=0)
        raw = raw + dot(lines, weight[j, 0:OWN, :])
        below[j] = weight[j, OWN:, :]
    own[...] = raw[0:TOKENS, :]
    other[...] = raw[TOKENS:, :]


def attend_kernel(
    here, own, other, table, marks, cache_hbm, values_hbm, keys, one_q, one_f, old, mine, theirs,
    out,
    cache, values, query, lse, mixed, sems,
):
    copies = (
        pltpu.make_async_copy(cache_hbm, cache, sems.at[0]),
        pltpu.make_async_copy(values_hbm, values, sems.at[1]),
    )
    start_all(copies)
    raw = own[...] + other[...]
    cos, sin = table[0:TOKENS, :], table[TOKENS : 2 * TOKENS, :]
    qg, kg = table[2 * TOKENS : 2 * TOKENS + 1, :], table[2 * TOKENS + 1 : 2 * TOKENS + 2, :]
    lens = marks
    for h in range(2):
        query[h * TOKENS : (h + 1) * TOKENS, :] = (
            head_norm_rotate(raw[:, h * HEAD : (h + 1) * HEAD], qg, cos, sin)
            .astype(BF16)
            .astype(F32)
        )
    fresh = head_norm_rotate(raw[:, 256:384], kg, cos, sin).astype(BF16)
    fresh_v = raw[:, 384:512].astype(BF16)
    for copy in copies:
        copy.wait()
    for g in range(GROUPS):
        at = slice(g * GROUP * CTX, (g + 1) * GROUP * CTX)
        past, new, total, log_sum = group_scores(g, query, cache[at, :], fresh, lens)
        put_groups(g, lse, jnp.broadcast_to(log_sum, (log_sum.shape[0], HEAD)))
        mix = dot((past / total).astype(BF16), values[at, :])
        mix = mix + dot((new / total).astype(BF16), fresh_v)
        put_groups(g, mixed, mix)
    attended = jnp.concatenate([mixed[0:TOKENS, :], mixed[TOKENS:, :]], axis=1).astype(BF16)
    core = here[0] & 1
    for rows, parity in ((mine, core), (theirs, 1 - core)):
        for j in range(HALF):
            for half in range(2):
                part = dot_nt(rows[j, :, half * 256 : (half + 1) * 256], attended)
                at = slice(half * FOLD, (half + 1) * FOLD)
                out[2 * j + parity, at, :] = part.astype(BF16)
    now = sample_logp(query, keys[...] + dot(one_f[...], fresh), one_q[...], lse)
    term = (now[0] - old[0]) + (now[1] - old[1])
    line = term.T[0:1, :]
    high = line.astype(BF16).astype(F32)
    middle = (line - high).astype(BF16).astype(F32)
    low = line - high - middle
    tail = jnp.concatenate([high, middle, low, jnp.zeros((TAIL - 3, TOKENS), F32)], axis=0)
    tail = tail.astype(BF16)
    for p in range(PARTS):
        out[p, OWN:SENT, :] = tail


def finish_kernel(recv, out, ratio):
    for k, n in ((0, 128), (128, 128), (256, 80)):
        total = recv[0, k : k + n, :].astype(F32)
        for src in range(1, PARTS):
            total = total + recv[src, k : k + n, :].astype(F32)
        if n == 128:
            out[:, k : k + n] = total.T.astype(BF16)
        else:
            tail = total[64:67, :]
            ratio[...] = ((tail[2:3, :] + tail[1:2, :]) + tail[0:1, :]) * (1.0 / HQ)
            out[:, k : k + 64] = total[0:64, :].T.astype(BF16)


def params(mib):
    return pltpu.CompilerParams(vmem_limit_bytes=mib * 1024 * 1024)


def shape(dims, dtype):
    return jax.ShapeDtypeStruct(dims, dtype)


def whole(*dims):
    return pl.BlockSpec(dims, lambda i: (0,) * len(dims))


def scalars(n=1):
    return [pl.BlockSpec(memory_space=pltpu.SMEM)] * n


def far_away(n=1):
    return [pl.BlockSpec(memory_space=pltpu.HBM)] * n


def spec_of(out):
    return whole(*out.shape)


def call(kernel, name, outs, in_specs, scratch, far=False, mib=56):
    several = isinstance(outs, tuple)
    return pl.pallas_call(
        kernel,
        name=name,
        grid=(1,),
        out_shape=outs,
        in_specs=in_specs,
        out_specs=far_away()[0] if far else tuple(map(spec_of, outs)) if several else spec_of(outs),
        scratch_shapes=scratch,
        compiler_params=params(mib),
    )


def local(
    hidden,
    norm_gain,
    query_gain,
    key_gain,
    base_query,
    base_key,
    base_value,
    base_output,
    delta_query,
    scale_query,
    key_delta_codes,
    key_scale_codes,
    value_delta_codes,
    value_scale_codes,
    delta_output,
    scale_output,
    cache_keys,
    cache_values,
    lengths,
    stale_rows,
    stale_steps,
    stale_back,
):
    here = lax.axis_index("replica").astype(jnp.int32).reshape(1)
    seat = lax.axis_index("shard").astype(jnp.int32).reshape(1)
    dma = pltpu.SemaphoreType.DMA
    packed, turned = call(
        pack_kernel,
        "pack",
        (shape((PARTS, BLOCK, HEAD), BF16), shape((OWN, TOKENS), BF16)),
        far_away(9),
        [
            VMEM((TOKENS, OWN), BF16),
            VMEM((CUT, HQ * HEAD), BF16),
            VMEM((CUT, KV * HEAD), BF16),
            VMEM((CUT, KV * HEAD), BF16),
            VMEM((CUT, HQ * HEAD), BF16),
            VMEM((CUT, HQ), jnp.int32),
            VMEM((CUT, HQ), jnp.int32),
            VMEM((KV, CUT), jnp.int32),
            VMEM((KV, CUT), jnp.int32),
            VMEM((BLOCK, HEAD), F32),
            dma((9,)),
        ],
        mib=56,
    )(
        hidden.reshape(TOKENS, OWN), delta_query, key_delta_codes, value_delta_codes, delta_output,
        scale_query, scale_output, key_scale_codes.T, value_scale_codes.T,
    )
    across = along_shard(turned, 1, 0)
    arrived = lax.all_to_all(packed, "shard", split_axis=0, concat_axis=0, tiled=False)
    arrived, across, lengths, stale_rows, stale_steps, stale_back = lax.optimization_barrier(
        (arrived, across, lengths, stale_rows, stale_steps, stale_back)
    )
    copies = call(
        refresh_kernel,
        "refresh",
        shape((HALF, TALL, 512), BF16),
        scalars() + [whole(PARTS, BLOCK, HEAD)] + far_away(4),
        [
            VMEM((OWN, 256), BF16),
            VMEM((OWN, 128), BF16),
            VMEM((OWN, 128), BF16),
            VMEM((OWN, 256), BF16),
            VMEM((2, BLOCK, HEAD), F32),
            VMEM((OWN, 768), F32),
            VMEM((TALL, 512), BF16),
            dma((4 + HALF,)),
        ],
        True,
        mib=56,
    )(here, arrived, base_query, base_key, base_value, base_output)
    groups = [[2 * j + core for j in range(HALF)] for core in range(2)]
    pair = jnp.concatenate([turned, across], axis=0)
    copies, pair = lax.optimization_barrier((copies, pair))
    weight = lax.all_to_all(
        copies, "replica", split_axis=0, concat_axis=0, tiled=False, axis_index_groups=groups
    )
    position = (lengths[None, :] + jnp.arange(STEPS)[:, None]).reshape(TOKENS)
    freq = THETA ** (-(jnp.arange(HEAD // 2).astype(F32) * 2.0) / HEAD)
    angle = position.astype(F32)[:, None] * freq
    cos, sin = jnp.cos(angle), jnp.sin(angle)
    table = jnp.concatenate(
        [
            jnp.concatenate([cos, cos], axis=1),
            jnp.concatenate([-sin, sin], axis=1),
            query_gain.reshape(1, HEAD),
            key_gain.reshape(1, HEAD),
            jnp.zeros((6, HEAD), F32),
        ],
        axis=0,
    )
    rows_s, steps_s, back_s = stale_rows, stale_steps, stale_back
    lens_s = jnp.sum(
        jnp.where(rows_s[0][None, :] == jnp.arange(ROWS)[:, None], lengths[:, None], 0),
        axis=0,
        keepdims=True,
    )
    at = lens_s + steps_s - back_s % (lens_s + steps_s + 1)
    place = jnp.where(
        at >= lens_s, ROWS * CTX + (at - lens_s) * ROWS + rows_s, rows_s * CTX + at
    ).astype(jnp.int32)
    token = (steps_s * ROWS + rows_s).astype(jnp.int32)
    marks = jnp.concatenate(
        [
            jnp.broadcast_to(lengths[:, None], (ROWS, HEAD)),
            token,
            place,
            jnp.zeros((6, HEAD), jnp.int32),
        ],
        axis=0,
    )
    cache = cache_keys.reshape(ROWS * CTX, HEAD)
    values = cache_values.reshape(ROWS * CTX, HEAD)

    keys, one_q, one_f = call(
        select_kernel,
        "select",
        (
            shape((TOKENS, HEAD), F32),
            shape((TOKENS, TOKENS), BF16),
            shape((TOKENS, TOKENS), BF16),
        ),
        [whole(ROWS + 8, HEAD)] + far_away(),
        [VMEM((ROWS * CTX, HEAD), BF16), dma((1,))],
    )(marks, cache)
    z1, z7 = along_shard(pair, 0, 1), along_shard(pair, 0, -1)
    z2, z6 = along_shard(pair, 0, 2), along_shard(pair, 0, -2)
    z2, z6, keys, one_q, one_f, table = lax.optimization_barrier(
        (z2, z6, keys, one_q, one_f, table)
    )
    z3, z5 = along_shard(z2, 0, 1), along_shard(z6, 0, -1)
    z4 = along_shard(z2, 0, 2)

    keep, give = call(
        normalise_kernel,
        "normalise",
        (
            shape((HALF, TOKENS, WIDE), BF16),
            shape((HALF, TOKENS, WIDE), BF16),
        ),
        scalars(2) + [whole(PARTS, 1, OWN)] + [whole(2 * OWN, TOKENS)] * 8,
        [],
    )(here, seat, norm_gain.reshape(PARTS, 1, OWN), pair, z1, z2, z3, z4, z5, z6, z7)
    given = fetch(give, 0, 0, 1)

    old = call(
        old_kernel,
        "old",
        shape((2, TOKENS, HEAD), F32),
        scalars()
        + [whole(HALF, TOKENS, WIDE)] * 2
        + [whole(2 * TOKENS + 8, HEAD), whole(ROWS + 8, HEAD)]
        + [whole(TOKENS, HEAD)] * 3
        + far_away(3),
        [
            VMEM((WIDTH, 256), BF16),
            VMEM((WIDTH, HEAD), BF16),
            VMEM((ROWS * CTX, HEAD), BF16),
            VMEM((2 * TOKENS, HEAD), F32),
            VMEM((2 * TOKENS, HEAD), F32),
            dma((9,)),
        ],
    )(here, keep, give, table, marks, keys, one_q, one_f, base_query, base_key, cache)

    weight, keep, given, old = lax.optimization_barrier((weight, keep, given, old))
    own, other, mine = call(
        project_kernel,
        "project",
        (
            shape((TOKENS, 512), F32),
            shape((TOKENS, 512), F32),
            shape((HALF, FOLD, 512), BF16),
        ),
        [whole(HALF, TOKENS, WIDE)] * 2 + [whole(HALF, TALL, 512)],
        [],
        mib=20,
    )(keep, given, weight)
    other = fetch(other, 0, 0, 1)
    theirs = fetch(mine, 0, 0, 1)

    sent = call(
        attend_kernel,
        "attend",
        shape((PARTS, SENT, HEAD), BF16),
        scalars()
        + [whole(TOKENS, 512)] * 2
        + [whole(2 * TOKENS + 8, HEAD), whole(ROWS + 8, HEAD)]
        + far_away(2)
        + [whole(TOKENS, HEAD)] * 3
        + [whole(2, TOKENS, HEAD)]
        + [whole(HALF, FOLD, 512)] * 2,
        [
            VMEM((ROWS * CTX, HEAD), BF16),
            VMEM((ROWS * CTX, HEAD), BF16),
            VMEM((2 * TOKENS, HEAD), F32),
            VMEM((2 * TOKENS, HEAD), F32),
            VMEM((2 * TOKENS, HEAD), F32),
            dma((2,)),
        ],
        mib=24,
    )(here, own, other, table, marks, cache, values, keys, one_q, one_f, old, mine, theirs)
    landed = lax.all_to_all(sent, "shard", split_axis=0, concat_axis=0, tiled=False)
    out, ratio = call(
        finish_kernel,
        "finish",
        (shape((TOKENS, OWN), BF16), shape((1, TOKENS), F32)),
        [whole(PARTS, SENT, HEAD)],
        [],
        mib=20,
    )(landed)
    return out.reshape(STEPS, ROWS, OWN), ratio


def solution(mesh):
    return jax.shard_map(
        local,
        mesh=mesh,
        in_specs=(
            P(None, "replica", "shard"),
            P(),
            P(),
            P(),
            P(None, "shard"),
            P(None, "shard"),
            P(None, "shard"),
            P(None, "shard"),
            P(("replica", "shard"), None),
            P(("replica", "shard"), None),
            P(("replica", "shard"), None),
            P(("replica", "shard"), None),
            P(("replica", "shard"), None),
            P(("replica", "shard"), None),
            P(("replica", "shard"), None),
            P(("replica", "shard"), None),
            P("replica", None, "shard"),
            P("replica", None, "shard"),
            P("replica"),
            P("replica", None),
            P("replica", None),
            P("replica", None),
        ),
        out_specs=(P(None, "replica", "shard"), P("replica", None)),
        check_vma=False,
    )
```

time: 192 us -> 139 us (0.72); the launches traced: 189 us -> 139 us
  blocking collectives: 0 us -> 42.6 us
  waiting for transfers between devices: 70.7 us -> 31.9 us
  local copies, waits for them, and re-layouts: 41.3 us -> 3.57 us
  starting transfers between devices: 51.1 us -> 29.7 us
  Pallas kernels: 21.8 us -> 27.6 us
    all_to_all x0 -> x1, blocking collectives: none -> 42.6 us  [local(): lax.all_to_all(sent, 'shard', split_axis=0, concat_axis=0, tiled=False)]
    unnamed x107 -> x50, local copies, waits for them, and re-layouts: 32.1 us -> 0.79 us
    all_to_all x1, waiting for transfers between devices: 29.4 us -> 9.48 us  [local(): lax.all_to_all(copies, 'replica', split_axis=0, concat_axis=0, tiled=Fals...]
    ppermute x19 -> x3, starting transfers between devices: 18.7 us -> 0.59 us  [fetch(): return lax.ppermute(value, 'replica', pairs)]
    ppermute x8, waiting for transfers between devices: 23.3 us -> 9.91 us  [along_shard(): return lax.ppermute(value, 'shard', pairs)]
    pallas_call x6 -> x5, Pallas kernels: 11.8 us -> 20.5 us  [the longest x1 6.14 us: local(): call(old_kernel, 'old', shape((2, TOKENS, HEAD), F32), scalars() + [whole...]
    ppermute x1 -> x0, waiting for transfers between devices: 5.79 us -> none  [local(): moved = lax.ppermute(moved, ('replica', 'shard'), mirrored)]
    slice x3 -> x0, local copies, waits for them, and re-layouts: 4.65 us -> none  [the longest x1 1.56 us: local(): far[cuts[0]]]
  transfers between devices with their start and end apart: 30 -> 13, of which waited for: 11 -> 7; matrix products, arithmetic and copies ran while one was open for 6% -> 3% of each run, Pallas kernels for 7% -> 9%
where the time goes in v5:
time: 139 us
  blocking collectives  42.6 us (31%)
  waiting for transfers between devices  31.9 us (23%)
  starting transfers between devices  29.7 us (21%)
  Pallas kernels  27.6 us (20%)
  local copies, waits for them, and re-layouts  3.57 us (3%)
  other arithmetic  2.29 us (2%)
    all_to_all x1, blocking collectives, local(): lax.all_to_all(sent, 'shard', split_axis=0, concat_axis=0, tiled=False)  42.6 us
    ppermute x8, starting transfers between devices, along_shard(): return lax.ppermute(value, 'shard', pairs)  13.4 us
    all_to_all x1, starting transfers between devices, local(): lax.all_to_all(packed, 'shard', split_axis=0, concat_axis=0, tiled=False)  11.1 us
    ppermute x8, waiting for transfers between devices, along_shard(): return lax.ppermute(value, 'shard', pairs)  9.91 us
    all_to_all x1, waiting for transfers between devices, local(): lax.all_to_all(packed, 'shard', split_axis=0, concat_axis=0, tiled=False)  9.65 us
    all_to_all x1, waiting for transfers between devices, local(): lax.all_to_all(copies, 'replica', split_axis=0, concat_axis=0, tiled=Fals...  9.48 us
    pallas_call x1, Pallas kernels, local(): call(old_kernel, 'old', shape((2, TOKENS, HEAD), F32), scalars() + [whole...  6.14 us
    all_to_all x1, starting transfers between devices, local(): lax.all_to_all(copies, 'replica', split_axis=0, concat_axis=0, tiled=Fals...  4.65 us
  transfers between devices with their start and end apart: 13, of which 7 were waited for; matrix products, arithmetic and copies ran while one was open for 3% of the time, Pallas kernels for 9%

profile of v5, /device:TPU:32, one launch (start us, length us, event | category | flops | bytes accessed | tf_op | source)
XLA Modules:
  0.0 138.8 jit_solution(1518361958027457691)
XLA Ops:
  0.6 2.8 %pack.1 = (bf16[16,128,128]{2,1,0:T(8,128)(2,1)}, bf16[320,128]{1,0:T(8,128)(2,1)}) custom-call(bf16[128,320]{1,0:T(8,128)(2,1)} %bitcast.29, bf16[20,4096]{1,0:T(8,128)(2,1)} %dq.1, bf16[20,1024]{1,0:T(8,128)(2,1)} %dk.1, bf16[20,1024]{1,0:T(8,128)(2,1)} %dv.1, bf16[20,4096]{1,0:T(8,128)(2,1)} %do.1, s32[20,32]{1,0:T(8,128)} %sq.1, s32[20,32]{1,0:T(8,128)} %so.1, ...), custom_call_target="tpu_custom_call" | custom-call | tf_op jit(solution)/shard_map/pack/pallas_call | solution.py:424
  3.5 11.1 %all-to-all-start = ((bf16[16,128,128]{2,1,0:T(8,128)(2,1)}), bf16[16,128,128]{2,1,0:T(8,128)(2,1)S(1)}, u32[]{:S(2)}, u32[]{:S(2)}) async-start(bf16[16,128,128]{2,1,0:T(8,128)(2,1)} %get-tuple-element.32), calls=%async_computation | async-start | bytes 1048576 | tf_op jit(solution)/shard_map/all_to_all | solution.py:448
  14.5 3.0 %collective-permute-start = (bf16[320,128]{1,0:T(8,128)(2,1)}, bf16[320,128]{1,0:T(8,128)(2,1)S(1)}, u32[]{:S(2)}, u32[]{:S(2)}) collective-permute-start(bf16[320,128]{1,0:T(8,128)(2,1)} %get-tuple-element.33), channel_id=1, source_target_pairs={{8,0},{9,1},{10,2},{11,3},{12,4},{13,5},{14,6},{15,7},{0,8},{1,9},... | collective-permute-start | bytes 245768 | tf_op jit(solution)/shard_map/ppermute | solution.py:48
  17.5 3.7 %collective-permute-done = bf16[320,128]{1,0:T(8,128)(2,1)S(1)} collective-permute-done((bf16[320,128]{1,0:T(8,128)(2,1)}, bf16[320,128]{1,0:T(8,128)(2,1)S(1)}, u32[]{:S(2)}, u32[]{:S(2)}) %collective-permute-start) | collective-permute-done | bytes 81952 | tf_op jit(solution)/shard_map/ppermute | solution.py:48
  21.2 9.7 %all-to-all-done.recv = bf16[16,128,128]{2,1,0:T(8,128)(2,1)S(1)} async-done(((bf16[16,128,128]{2,1,0:T(8,128)(2,1)}), bf16[16,128,128]{2,1,0:T(8,128)(2,1)S(1)}, u32[]{:S(2)}, u32[]{:S(2)}) %all-to-all-start) | async-done | bytes 524320 | tf_op jit(solution)/shard_map/all_to_all | solution.py:448
  30.9 1.0 pad_maximum_fusion.p0
  31.9 4.3 %refresh.1 = bf16[8,480,512]{2,1,0:T(8,128)(2,1)} custom-call(s32[1]{0:T(128)} %bitcast.here, bf16[16,128,128]{2,1,0:T(8,128)(2,1)} %copy-done.9, bf16[5120,256]{1,0:T(8,128)(2,1)} %base_q.1, bf16[5120,128]{1,0:T(8,128)(2,1)} %base_k.1, bf16[5120,128]{1,0:T(8,128)(2,1)} %bv.1, bf16[5120,256]{1,0:T(8,128)(2,1)} %bo.1), custom_call_target="tpu_custom_call" | custom-call | tf_op jit(solution)/shard_map/refresh/pallas_call | solution.py:452
  36.2 4.7 %all-to-all-start.1 = ((bf16[8,480,512]{2,1,0:T(8,128)(2,1)}), bf16[8,480,512]{2,1,0:T(8,128)(2,1)}, u32[]{:S(2)}, u32[]{:S(2)}) async-start(bf16[8,480,512]{2,1,0:T(8,128)(2,1)} %refresh.1), calls=%async_computation.1 | async-start | bytes 7864320 | tf_op jit(solution)/shard_map/all_to_all | solution.py:473
  41.9 2.3 %collective-permute-start.2 = (bf16[640,128]{1,0:T(8,128)(2,1)S(1)}, bf16[640,128]{1,0:T(8,128)(2,1)S(1)}, u32[]{:S(2)}, u32[]{:S(2)}) collective-permute-start(bf16[640,128]{1,0:T(8,128)(2,1)S(1)} %pad_maximum_fusion.p0), channel_id=1, source_target_pairs={{2,0},{3,1},{4,2},{5,3},{6,4},{7,5},{0,6},{1,7},{10,8},{11,9},{12,... | collective-permute-start | bytes 491528 | tf_op jit(solution)/shard_map/ppermute | solution.py:48
  44.9 2.3 %collective-permute-start.7 = (bf16[640,128]{1,0:T(8,128)(2,1)S(1)}, bf16[640,128]{1,0:T(8,128)(2,1)S(1)}, u32[]{:S(2)}, u32[]{:S(2)}) collective-permute-start(bf16[640,128]{1,0:T(8,128)(2,1)S(1)} %pad_maximum_fusion.p0), channel_id=1, source_target_pairs={{7,0},{0,1},{1,2},{2,3},{3,4},{4,5},{5,6},{6,7},{15,8},{8,9},{9,10... | collective-permute-start | bytes 491528 | tf_op jit(solution)/shard_map/ppermute | solution.py:48
  48.6 2.7 %select.1 = (f32[128,128]{1,0:T(8,128)}, bf16[128,128]{1,0:T(8,128)(2,1)}, bf16[128,128]{1,0:T(8,128)(2,1)}) custom-call(s32[40,128]{1,0:T(8,128)} %add_add_fusion.marks, bf16[2048,128]{1,0:T(8,128)(2,1)} %bitcast.25), custom_call_target="tpu_custom_call" | custom-call | tf_op jit(solution)/shard_map/select/pallas_call | solution.py:513
  51.4 1.8 %concatenate.19.table = f32[264,128]{1,0:T(8,128)} concatenate(f32[128,128]{1,0:T(8,128)S(1)} %get-tuple-element.67, f32[128,128]{1,0:T(8,128)S(1)} %get-tuple-element.68, f32[1,128]{1,0:T(1,128)S(1)} %bitcast.32, f32[1,128]{1,0:T(1,128)S(1)} %bitcast.33, f32[6,128]{1,0:T(8,128)S(1)} %broadcast_in_dim.37), dimensions={0} | concatenate | bytes 270336 | tf_op jit(solution)/shard_map/concatenate | solution.py:480
  54.2 1.7 %collective-permute-start.4 = (bf16[640,128]{1,0:T(8,128)(2,1)S(1)}, bf16[640,128]{1,0:T(8,128)(2,1)S(1)}, u32[]{:S(2)}, u32[]{:S(2)}) collective-permute-start(bf16[640,128]{1,0:T(8,128)(2,1)S(1)} %collective-permute-done.2.p2), channel_id=1, source_target_pairs={{1,0},{2,1},{3,2},{4,3},{5,4},{6,5},{7,6},{0,7},{9,8},{10,9},{11,1... | collective-permute-start | bytes 491528 | tf_op jit(solution)/shard_map/ppermute | solution.py:48
  55.9 1.2 collective-permute-start.5
  57.1 1.3 collective-permute-start.6
  59.1 1.2 collective-permute-done.4.p3
  60.3 4.1 %collective-permute-done.5.p4 = bf16[640,128]{1,0:T(8,128)(2,1)S(1)} collective-permute-done((bf16[640,128]{1,0:T(8,128)(2,1)S(1)}, bf16[640,128]{1,0:T(8,128)(2,1)S(1)}, u32[]{:S(2)}, u32[]{:S(2)}) %collective-permute-start.5) | collective-permute-done | bytes 163872 | tf_op jit(solution)/shard_map/ppermute | solution.py:48
  65.1 4.3 %normalise.1 = (bf16[8,128,384]{2,1,0:T(8,128)(2,1)}, bf16[8,128,384]{2,1,0:T(8,128)(2,1)}) custom-call(s32[1]{0:T(128)} %bitcast.here, s32[1]{0:T(128)} %bitcast.4.seat, f32[16,1,320]{2,1,0:T(1,128)} %reshape.59.gain, bf16[640,128]{1,0:T(8,128)(2,1)} %copy-done.10, bf16[640,128]{1,0:T(8,128)(2,1)} %copy-done.11, bf16[640,128]{1,0:T(8,128)(2,1)} %copy-done.12, ...), custom_call_target="tpu_custom_call" | custom-call | tf_op jit(solution)/shard_map/normalise/pallas_call | solution.py:532
  69.4 6.1 %old.1 = f32[2,128,128]{2,1,0:T(8,128)} custom-call(s32[1]{0:T(128)} %bitcast.here, bf16[8,128,384]{2,1,0:T(8,128)(2,1)} %get-tuple-element.53.keep, bf16[8,128,384]{2,1,0:T(8,128)(2,1)} %get-tuple-element.48.give, f32[264,128]{1,0:T(8,128)} %concatenate.19.table, s32[40,128]{1,0:T(8,128)} %add_add_fusion.marks, f32[128,128]{1,0:T(8,128)} %get-tuple-element.50.keys, ...), custom_call_target="tpu_custom_call" | custom-call | tf_op jit(solution)/shard_map/old/pallas_call | solution.py:544
  75.7 9.5 %all-to-all-done.1.weight = bf16[8,480,512]{2,1,0:T(8,128)(2,1)} async-done(((bf16[8,480,512]{2,1,0:T(8,128)(2,1)}), bf16[8,480,512]{2,1,0:T(8,128)(2,1)}, u32[]{:S(2)}, u32[]{:S(2)}) %all-to-all-start.1) | async-done | bytes 3932192 | tf_op jit(solution)/shard_map/all_to_all | solution.py:473
  85.1 3.4 %project.1 = (f32[128,512]{1,0:T(8,128)S(1)}, f32[128,512]{1,0:T(8,128)S(1)}, bf16[8,160,512]{2,1,0:T(8,128)(2,1)S(1)}) custom-call(bf16[8,128,384]{2,1,0:T(8,128)(2,1)S(1)} %copy-done.1, bf16[8,128,384]{2,1,0:T(8,128)(2,1)S(1)} %collective-permute-done.8.given, bf16[8,480,512]{2,1,0:T(8,128)(2,1)} %all-to-all-done.1.weight), custom_call_target="tpu_custom_call" | custom-call | tf_op jit(solution)/shard_map/project/pallas_call | solution.py:564
  89.2 2.9 %collective-permute-done.9.other = f32[128,512]{1,0:T(8,128)S(1)} collective-permute-done((f32[128,512]{1,0:T(8,128)S(1)}, f32[128,512]{1,0:T(8,128)S(1)}, u32[]{:S(2)}, u32[]{:S(2)}) %collective-permute-start.9) | collective-permute-done | bytes 262176 | tf_op jit(solution)/shard_map/ppermute | solution.py:43
  92.1 3.1 %attend.1 = bf16[16,336,128]{2,1,0:T(8,128)(2,1)S(1)} custom-call(s32[1]{0:T(128)} %bitcast.here, f32[128,512]{1,0:T(8,128)S(1)} %get-tuple-element.56.own, f32[128,512]{1,0:T(8,128)S(1)} %collective-permute-done.9.other, f32[264,128]{1,0:T(8,128)S(1)} %copy-done.2, s32[40,128]{1,0:T(8,128)S(1)} %copy-done.5, bf16[2048,128]{1,0:T(8,128)(2,1)S(1)} %bitcast.27, ...), custom_call_target="tpu_custom_call" | custom-call | tf_op jit(solution)/shard_map/attend/pallas_call | solution.py:579
  95.3 42.6 %all_to_all.15.recv = bf16[16,336,128]{2,1,0:T(8,128)(2,1)S(1)} all-to-all(bf16[16,336,128]{2,1,0:T(8,128)(2,1)S(1)} %attend.1), channel_id=1, replica_groups=mesh['replica'=16,'shard'=16] {'shard'}, dimensions={0} | all-to-all | bytes 2752512 | tf_op jit(solution)/shard_map/all_to_all | solution.py:600
  (76 shorter events, 7.0 us)
Async XLA Ops:
  3.5 27.4 %all-to-all-start = ((bf16[16,128,128]{2,1,0:T(8,128)(2,1)}), bf16[16,128,128]{2,1,0:T(8,128)(2,1)S(1)}, u32[]{:S(2)}, u32[]{:S(2)}) async-start(bf16[16,128,128]{2,1,0:T(8,128)(2,1)} %get-tuple-element.32), calls=%async_computation | async-start | bytes 1048576 | tf_op jit(solution)/shard_map/all_to_all | solution.py:448
  14.5 6.7 %collective-permute-start = (bf16[320,128]{1,0:T(8,128)(2,1)}, bf16[320,128]{1,0:T(8,128)(2,1)S(1)}, u32[]{:S(2)}, u32[]{:S(2)}) collective-permute-start(bf16[320,128]{1,0:T(8,128)(2,1)} %get-tuple-element.33), channel_id=1, source_target_pairs={{8,0},{9,1},{10,2},{11,3},{12,4},{13,5},{14,6},{15,7},{0,8},{1,9},... | collective-permute-start | bytes 245768 | tf_op jit(solution)/shard_map/ppermute | solution.py:48
  36.2 15.2 %copy-start.20 = (f32[128]{0:T(128)S(1)}, f32[128]{0:T(128)}, u32[]{:S(2)}) copy-start(f32[128]{0:T(128)} %param.24) | copy-start | bytes 1540
  36.2 48.9 %all-to-all-start.1 = ((bf16[8,480,512]{2,1,0:T(8,128)(2,1)}), bf16[8,480,512]{2,1,0:T(8,128)(2,1)}, u32[]{:S(2)}, u32[]{:S(2)}) async-start(bf16[8,480,512]{2,1,0:T(8,128)(2,1)} %refresh.1), calls=%async_computation.1 | async-start | bytes 7864320 | tf_op jit(solution)/shard_map/all_to_all | solution.py:473
  40.9 17.5 %copy-start.18 = (f32[5120]{0:T(1024)S(1)}, f32[5120]{0:T(1024)}, u32[]{:S(2)}) copy-start(f32[5120]{0:T(1024)} %param.23) | copy-start | bytes 61444
  41.0 18.1 %collective-permute-start.1 = (bf16[640,128]{1,0:T(8,128)(2,1)S(1)}, bf16[640,128]{1,0:T(8,128)(2,1)S(1)}, u32[]{:S(2)}, u32[]{:S(2)}) collective-permute-start(bf16[640,128]{1,0:T(8,128)(2,1)S(1)} %pad_maximum_fusion.p0), channel_id=1, source_target_pairs={{1,0},{2,1},{3,2},{4,3},{5,4},{6,5},{7,6},{0,7},{9,8},{10,9},{11,1... | collective-permute-start | bytes 491528 | tf_op jit(solution)/shard_map/ppermute | solution.py:48
  41.9 11.3 %collective-permute-start.2 = (bf16[640,128]{1,0:T(8,128)(2,1)S(1)}, bf16[640,128]{1,0:T(8,128)(2,1)S(1)}, u32[]{:S(2)}, u32[]{:S(2)}) collective-permute-start(bf16[640,128]{1,0:T(8,128)(2,1)S(1)} %pad_maximum_fusion.p0), channel_id=1, source_target_pairs={{2,0},{3,1},{4,2},{5,3},{6,4},{7,5},{0,6},{1,7},{10,8},{11,9},{12,... | collective-permute-start | bytes 491528 | tf_op jit(solution)/shard_map/ppermute | solution.py:48
  44.3 9.9 %collective-permute-start.3 = (bf16[640,128]{1,0:T(8,128)(2,1)S(1)}, bf16[640,128]{1,0:T(8,128)(2,1)S(1)}, u32[]{:S(2)}, u32[]{:S(2)}) collective-permute-start(bf16[640,128]{1,0:T(8,128)(2,1)S(1)} %pad_maximum_fusion.p0), channel_id=1, source_target_pairs={{6,0},{7,1},{0,2},{1,3},{2,4},{3,5},{4,6},{5,7},{14,8},{15,9},{8,1... | collective-permute-start | bytes 491528 | tf_op jit(solution)/shard_map/ppermute | solution.py:48
  44.9 14.2 %collective-permute-start.7 = (bf16[640,128]{1,0:T(8,128)(2,1)S(1)}, bf16[640,128]{1,0:T(8,128)(2,1)S(1)}, u32[]{:S(2)}, u32[]{:S(2)}) collective-permute-start(bf16[640,128]{1,0:T(8,128)(2,1)S(1)} %pad_maximum_fusion.p0), channel_id=1, source_target_pairs={{7,0},{0,1},{1,2},{2,3},{3,4},{4,5},{5,6},{6,7},{15,8},{8,9},{9,10... | collective-permute-start | bytes 491528 | tf_op jit(solution)/shard_map/ppermute | solution.py:48
  54.2 6.1 %collective-permute-start.4 = (bf16[640,128]{1,0:T(8,128)(2,1)S(1)}, bf16[640,128]{1,0:T(8,128)(2,1)S(1)}, u32[]{:S(2)}, u32[]{:S(2)}) collective-permute-start(bf16[640,128]{1,0:T(8,128)(2,1)S(1)} %collective-permute-done.2.p2), channel_id=1, source_target_pairs={{1,0},{2,1},{3,2},{4,3},{5,4},{6,5},{7,6},{0,7},{9,8},{10,9},{11,1... | collective-permute-start | bytes 491528 | tf_op jit(solution)/shard_map/ppermute | solution.py:48
  55.9 8.5 %collective-permute-start.5 = (bf16[640,128]{1,0:T(8,128)(2,1)S(1)}, bf16[640,128]{1,0:T(8,128)(2,1)S(1)}, u32[]{:S(2)}, u32[]{:S(2)}) collective-permute-start(bf16[640,128]{1,0:T(8,128)(2,1)S(1)} %collective-permute-done.2.p2), channel_id=1, source_target_pairs={{2,0},{3,1},{4,2},{5,3},{6,4},{7,5},{0,6},{1,7},{10,8},{11,9},{12,... | collective-permute-start | bytes 491528 | tf_op jit(solution)/shard_map/ppermute | solution.py:48
  57.1 7.3 %collective-permute-start.6 = (bf16[640,128]{1,0:T(8,128)(2,1)S(1)}, bf16[640,128]{1,0:T(8,128)(2,1)S(1)}, u32[]{:S(2)}, u32[]{:S(2)}) collective-permute-start(bf16[640,128]{1,0:T(8,128)(2,1)S(1)} %collective-permute-done.3.p6), channel_id=1, source_target_pairs={{7,0},{0,1},{1,2},{2,3},{3,4},{4,5},{5,6},{6,7},{15,8},{8,9},{9,10... | collective-permute-start | bytes 491528 | tf_op jit(solution)/shard_map/ppermute | solution.py:48
  69.4 6.2 %collective-permute-start.8 = (bf16[8,128,384]{2,1,0:T(8,128)(2,1)}, bf16[8,128,384]{2,1,0:T(8,128)(2,1)S(1)}, u32[]{:S(2)}, u32[]{:S(2)}) collective-permute-start(bf16[8,128,384]{2,1,0:T(8,128)(2,1)} %get-tuple-element.48.give), channel_id=1, source_target_pairs={{16,0},{0,16},{48,32},{32,48},{80,64},{64,80},{112,96},{96,112},{1... | collective-permute-start | bytes 2359304 | tf_op jit(solution)/shard_map/ppermute | solution.py:43
  69.4 15.7 %copy-start.1 = (bf16[8,128,384]{2,1,0:T(8,128)(2,1)S(1)}, bf16[8,128,384]{2,1,0:T(8,128)(2,1)}, u32[]{:S(2)}) copy-start(bf16[8,128,384]{2,1,0:T(8,128)(2,1)} %get-tuple-element.53.keep) | copy-start | bytes 2359300
  75.6 16.5 %copy-start = (bf16[32,64,128]{2,1,0:T(8,128)(2,1)S(1)}, bf16[32,64,128]{2,1,0:T(8,128)(2,1)}, u32[]{:S(2)}) copy-start(bf16[32,64,128]{2,1,0:T(8,128)(2,1)} %param.38) | copy-start | bytes 1572868
  75.6 16.5 %copy-start.2 = (f32[264,128]{1,0:T(8,128)S(1)}, f32[264,128]{1,0:T(8,128)}, u32[]{:S(2)}) copy-start(f32[264,128]{1,0:T(8,128)} %concatenate.19.table) | copy-start | bytes 405508
  75.6 16.5 %copy-start.3 = (bf16[32,64,128]{2,1,0:T(8,128)(2,1)S(1)}, bf16[32,64,128]{2,1,0:T(8,128)(2,1)}, u32[]{:S(2)}) copy-start(bf16[32,64,128]{2,1,0:T(8,128)(2,1)} %param.39) | copy-start | bytes 1572868
  75.6 16.5 %copy-start.4 = (f32[2,128,128]{2,1,0:T(8,128)S(1)}, f32[2,128,128]{2,1,0:T(8,128)}, u32[]{:S(2)}) copy-start(f32[2,128,128]{2,1,0:T(8,128)} %old.1) | copy-start | bytes 393220
  75.6 16.5 %copy-start.5 = (s32[40,128]{1,0:T(8,128)S(1)}, s32[40,128]{1,0:T(8,128)}, u32[]{:S(2)}) copy-start(s32[40,128]{1,0:T(8,128)} %add_add_fusion.marks) | copy-start | bytes 61444
  75.6 16.5 %copy-start.6 = (f32[128,128]{1,0:T(8,128)S(1)}, f32[128,128]{1,0:T(8,128)}, u32[]{:S(2)}) copy-start(f32[128,128]{1,0:T(8,128)} %get-tuple-element.50.keys) | copy-start | bytes 196612
  75.6 16.5 %copy-start.7 = (bf16[128,128]{1,0:T(8,128)(2,1)S(1)}, bf16[128,128]{1,0:T(8,128)(2,1)}, u32[]{:S(2)}) copy-start(bf16[128,128]{1,0:T(8,128)(2,1)} %get-tuple-element.51.one_q) | copy-start | bytes 98308
  75.6 16.5 %copy-start.8 = (bf16[128,128]{1,0:T(8,128)(2,1)S(1)}, bf16[128,128]{1,0:T(8,128)(2,1)}, u32[]{:S(2)}) copy-start(bf16[128,128]{1,0:T(8,128)(2,1)} %get-tuple-element.52.one_f) | copy-start | bytes 98308
  88.6 3.5 %collective-permute-start.10 = (bf16[8,160,512]{2,1,0:T(8,128)(2,1)S(1)}, bf16[8,160,512]{2,1,0:T(8,128)(2,1)S(1)}, u32[]{:S(2)}, u32[]{:S(2)}) collective-permute-start(bf16[8,160,512]{2,1,0:T(8,128)(2,1)S(1)} %get-tuple-element.59.mine), channel_id=1, source_target_pairs={{16,0},{0,16},{48,32},{32,48},{80,64},{64,80},{112,96},{96,112},{1... | collective-permute-start | bytes 3932168 | tf_op jit(solution)/shard_map/ppermute | solution.py:43
  88.7 3.4 %collective-permute-start.9 = (f32[128,512]{1,0:T(8,128)S(1)}, f32[128,512]{1,0:T(8,128)S(1)}, u32[]{:S(2)}, u32[]{:S(2)}) collective-permute-start(f32[128,512]{1,0:T(8,128)S(1)} %get-tuple-element.57), channel_id=1, source_target_pairs={{16,0},{0,16},{48,32},{32,48},{80,64},{64,80},{112,96},{96,112},{1... | collective-permute-start | bytes 786440 | tf_op jit(solution)/shard_map/ppermute | solution.py:43
  (14 other events, 111.2 us)

commit v6 on v5

--- a/solution.py
+++ b/solution.py
@@ -27,7 +27,8 @@
 BLOCK = 128
 HALF = PARTS // 2
 FOLD = OWN // 2
-TALL = OWN + FOLD
+UPPER = 256
+LOWER = OWN - UPPER + FOLD
 WIDE = 384
 SENT = OWN + TAIL
 F32 = jnp.float32
@@ -41,6 +42,25 @@
         x, y, c = i >> 3, (i >> 1) & 3, i & 1
         pairs.append((((x ^ dx) << 3) + (((y + dy) & 3) << 1) + (c ^ dc), i))
     return lax.ppermute(value, "replica", pairs)
+
+
+PLACES = tuple((dx, dy) for dx in range(2) for dy in range(4))
+
+
+def owner(here, place):
+    return (((here >> 3) ^ place[0]) << 2) + (((here >> 1) + place[1]) & 3)
+
+
+def gather_blocks(own, turn):
+    over, first, back = fetch(own, 1, 0, 0), fetch(own, 0, turn, 0), fetch(own, 0, -turn, 0)
+    over_first, far, over_back = fetch(first, 1, 0, 0), fetch(first, 0, turn, 0), fetch(over, 0, -turn, 0)
+    held = {(0, 0): own, (1, 0): over, (0, turn & 3): first, (0, -turn & 3): back}
+    held.update({(1, turn & 3): over_first, (0, 2): far, (1, -turn & 3): over_back})
+    if turn == 1:
+        held[1, 2] = fetch(far, 1, 0, 0)
+    else:
+        held[1, 2] = fetch(over_back, 0, 1, 0)
+    return [held[place] for place in PLACES]
 
 
 def along_shard(value, dx, dz):
@@ -104,7 +124,7 @@
 
 
 def refresh_kernel(
-    here, recv, bq, bk, bv, bo, out, vq, vk, vv, vo, buf, delta, fresh, sems,
+    here, recv, bq, bk, bv, bo, upper, lower, vq, vk, vv, vo, buf, delta, sems,
 ):
     at = pl.ds(pl.multiple_of(OWN * here[0], 64), OWN)
     bases = ((bq, vq), (bk, vk), (bv, vv), (bo, vo))
@@ -121,15 +141,13 @@
     for copy in copies:
         copy.wait()
     for at, n, base in ((0, 256, vq), (256, 128, vk), (384, 128, vv)):
-        fresh[0:OWN, at : at + n] = (base[...].astype(F32) + delta[:, at : at + n]).astype(BF16)
+        value = (base[...].astype(F32) + delta[:, at : at + n]).astype(BF16)
+        upper[:, at : at + n] = value[0:UPPER]
+        lower[0 : OWN - UPPER, at : at + n] = value[UPPER:]
     for half in range(2):
         at = slice(half * FOLD, (half + 1) * FOLD)
         value = vo[at, :].astype(F32) + delta[at, 512:768]
-        fresh[OWN:, half * 256 : (half + 1) * 256] = value.astype(BF16)
-    copies = [pltpu.make_async_copy(fresh, out.at[j], sems.at[4 + j]) for j in range(HALF)]
-    start_all(copies)
-    for copy in copies:
-        copy.wait()
+        lower[OWN - UPPER :, half * 256 : (half + 1) * 256] = value.astype(BF16)
 
 
 def dot_nt(a, b):
@@ -193,28 +211,26 @@
     return out
 
 
-def normalise_kernel(here, seat, gain, p0, p1, p2, p3, p4, p5, p6, p7, keep, give):
+def normalise_kernel(here, seat, gain, pairs, keep, give):
     total = jnp.zeros((1, TOKENS), F32)
-    pairs = (p0, p1, p2, p3, p4, p5, p6, p7)
-    for pair in pairs:
-        x = pair[...].astype(F32)
+    for z in range(8):
+        x = pairs[z].astype(F32)
         total = total + jnp.sum(x * x, axis=0, keepdims=True)
     scale = lax.rsqrt(total * (1.0 / WIDTH) + EPSILON)
     me, core = seat[0], here[0] & 1
 
-    def put(step, pair, target):
+    def put(z, target):
         for half in range(2):
-            src = (((me >> 3) ^ half) << 3) + ((me + step) & 7)
+            src = (((me >> 3) ^ half) << 3) + z
             for at, n in TILES:
-                x = pair[half * OWN + at : half * OWN + at + n, :].astype(F32) * scale
+                x = pairs[z, half * OWN + at : half * OWN + at + n, :].astype(F32) * scale
                 value = (x.T * gain[src, :, at : at + n]).astype(BF16)
                 target[src >> 1, :, at : at + n] = value
             target[src >> 1, :, OWN:] = jnp.zeros((TOKENS, WIDE - OWN), BF16)
 
-    for step, pair in enumerate(pairs):
-        same = ((me + step) & 1) == core
-        pl.when(same)(lambda step=step, pair=pair: put(step, pair, keep))
-        pl.when(jnp.logical_not(same))(lambda step=step, pair=pair: put(step, pair, give))
+    for z in range(8):
+        pl.when(core == z & 1)(lambda z=z: put(z, keep))
+        pl.when(core != z & 1)(lambda z=z: put(z, give))
 
 
 def select_kernel(marks, cache_hbm, keys_out, one_q_out, one_f_out, cache, sems):
@@ -282,12 +298,15 @@
     old_out[1] = old[1]
 
 
-def project_kernel(keep, given, weight, own, other, below):
+def project_kernel(here, keep, given, *rest):
+    uppers, lowers, (own, other, below) = rest[0:8], rest[8:16], rest[16:]
     raw = jnp.zeros((2 * TOKENS, 512), F32)
-    for j in range(HALF):
-        lines = jnp.concatenate([keep[j, :, 0:OWN], given[j, :, 0:OWN]], axis=0)
-        raw = raw + dot(lines, weight[j, 0:OWN, :])
-        below[j] = weight[j, OWN:, :]
+    for place, upper, lower in zip(PLACES, uppers, lowers):
+        j = owner(here[0], place)
+        for at, n, weight in ((0, UPPER, upper), (UPPER, OWN - UPPER, lower)):
+            lines = jnp.concatenate([keep[j, :, at : at + n], given[j, :, at : at + n]], axis=0)
+            raw = raw + dot(lines, weight[0:n, :])
+        below[j] = lower[OWN - UPPER :, :]
     own[...] = raw[0:TOKENS, :]
     other[...] = raw[TOKENS:, :]
 
@@ -446,13 +465,15 @@
     )
     across = along_shard(turned, 1, 0)
     arrived = lax.all_to_all(packed, "shard", split_axis=0, concat_axis=0, tiled=False)
-    arrived, across, lengths, stale_rows, stale_steps, stale_back = lax.optimization_barrier(
-        (arrived, across, lengths, stale_rows, stale_steps, stale_back)
-    )
-    copies = call(
+    spread = jnp.concatenate([turned, across], axis=0)
+    spread = jnp.broadcast_to(spread[None], (8, 2 * OWN, TOKENS))
+    arrived, spread, lengths, stale_rows, stale_steps, stale_back = lax.optimization_barrier(
+        (arrived, spread, lengths, stale_rows, stale_steps, stale_back)
+    )
+    upper, lower = call(
         refresh_kernel,
         "refresh",
-        shape((HALF, TALL, 512), BF16),
+        (shape((UPPER, 512), BF16), shape((LOWER, 512), BF16)),
         scalars() + [whole(PARTS, BLOCK, HEAD)] + far_away(4),
         [
             VMEM((OWN, 256), BF16),
@@ -461,18 +482,22 @@
             VMEM((OWN, 256), BF16),
             VMEM((2, BLOCK, HEAD), F32),
             VMEM((OWN, 768), F32),
-            VMEM((TALL, 512), BF16),
-            dma((4 + HALF,)),
+            dma((4,)),
         ],
-        True,
         mib=56,
     )(here, arrived, base_query, base_key, base_value, base_output)
-    groups = [[2 * j + core for j in range(HALF)] for core in range(2)]
-    pair = jnp.concatenate([turned, across], axis=0)
-    copies, pair = lax.optimization_barrier((copies, pair))
-    weight = lax.all_to_all(
-        copies, "replica", split_axis=0, concat_axis=0, tiled=False, axis_index_groups=groups
-    )
+    upper, lower, spread = lax.optimization_barrier((upper, lower, spread))
+    uppers, lowers = gather_blocks(upper, 1), gather_blocks(lower, -1)
+    rings = [[8 * x + z for z in range(8)] for x in range(2)]
+    hidden_t = lax.all_to_all(
+        spread,
+        "shard",
+        split_axis=0,
+        concat_axis=0,
+        tiled=False,
+        axis_index_groups=rings,
+    )
+
     position = (lengths[None, :] + jnp.arange(STEPS)[:, None]).reshape(TOKENS)
     freq = THETA ** (-(jnp.arange(HEAD // 2).astype(F32) * 2.0) / HEAD)
     angle = position.astype(F32)[:, None] * freq
@@ -520,15 +545,12 @@
         ),
         [whole(ROWS + 8, HEAD)] + far_away(),
         [VMEM((ROWS * CTX, HEAD), BF16), dma((1,))],
+        mib=8,
     )(marks, cache)
-    z1, z7 = along_shard(pair, 0, 1), along_shard(pair, 0, -1)
-    z2, z6 = along_shard(pair, 0, 2), along_shard(pair, 0, -2)
-    z2, z6, keys, one_q, one_f, table = lax.optimization_barrier(
-        (z2, z6, keys, one_q, one_f, table)
-    )
-    z3, z5 = along_shard(z2, 0, 1), along_shard(z6, 0, -1)
-    z4 = along_shard(z2, 0, 2)
-
+    later = uppers + lowers
+    hidden_t, keys, one_q, one_f, table, _ = lax.optimization_barrier(
+        (hidden_t, keys, one_q, one_f, table, later)
+    )
     keep, give = call(
         normalise_kernel,
         "normalise",
@@ -536,9 +558,10 @@
             shape((HALF, TOKENS, WIDE), BF16),
             shape((HALF, TOKENS, WIDE), BF16),
         ),
-        scalars(2) + [whole(PARTS, 1, OWN)] + [whole(2 * OWN, TOKENS)] * 8,
+        scalars(2) + [whole(PARTS, 1, OWN)] + [whole(8, 2 * OWN, TOKENS)],
         [],
-    )(here, seat, norm_gain.reshape(PARTS, 1, OWN), pair, z1, z2, z3, z4, z5, z6, z7)
+        mib=16,
+    )(here, seat, norm_gain.reshape(PARTS, 1, OWN), hidden_t)
     given = fetch(give, 0, 0, 1)
 
     old = call(
@@ -558,9 +581,9 @@
             VMEM((2 * TOKENS, HEAD), F32),
             dma((9,)),
         ],
+        mib=24,
     )(here, keep, give, table, marks, keys, one_q, one_f, base_query, base_key, cache)
 
-    weight, keep, given, old = lax.optimization_barrier((weight, keep, given, old))
     own, other, mine = call(
         project_kernel,
         "project",
@@ -569,10 +592,13 @@
             shape((TOKENS, 512), F32),
             shape((HALF, FOLD, 512), BF16),
         ),
-        [whole(HALF, TOKENS, WIDE)] * 2 + [whole(HALF, TALL, 512)],
+        scalars()
+        + [whole(HALF, TOKENS, WIDE)] * 2
+        + [whole(UPPER, 512)] * 8
+        + [whole(LOWER, 512)] * 8,
         [],
-        mib=20,
-    )(keep, given, weight)
+        mib=24,
+    )(here, keep, given, *uppers, *lowers)
     other = fetch(other, 0, 0, 1)
     theirs = fetch(mine, 0, 0, 1)
 

time: 139 us -> 136 us (0.978)
  starting transfers between devices: 29.7 us -> 39.8 us
  Pallas kernels: 27.6 us -> 19 us
  waiting for transfers between devices: 31.9 us -> 25.7 us
  blocking collectives: 42.6 us -> 45.2 us
    ppermute x3 -> x17, starting transfers between devices: 0.59 us -> 20.7 us  [fetch(): return lax.ppermute(value, 'replica', pairs)]
    ppermute x8 -> x1, starting transfers between devices: 13.4 us -> 2.97 us  [along_shard(): return lax.ppermute(value, 'shard', pairs)]
    ppermute x3 -> x17, waiting for transfers between devices: 2.9 us -> 13.2 us  [fetch(): return lax.ppermute(value, 'replica', pairs)]
    all_to_all x1, waiting for transfers between devices: 9.48 us -> 0.01 us  [local(): lax.all_to_all(spread, 'shard', split_axis=0, concat_axis=0, tiled=False,...]
    ppermute x8 -> x1, waiting for transfers between devices: 9.91 us -> 3.75 us  [along_shard(): return lax.ppermute(value, 'shard', pairs)]
    pallas_call x1, Pallas kernels: 4.31 us -> 1.7 us  [local(): call(normalise_kernel, 'normalise', (shape((HALF, TOKENS, WIDE), BF16), s...]
    all_to_all x1, blocking collectives: 42.6 us -> 45.2 us  [local(): lax.all_to_all(sent, 'shard', split_axis=0, concat_axis=0, tiled=False)]
    pallas_call x1, Pallas kernels: 2.7 us -> 0.44 us  [local(): call(select_kernel, 'select', (shape((TOKENS, HEAD), F32), shape((TOKENS,...]
  transfers between devices with their start and end apart: 13 -> 20, of which waited for: 7 -> 8; matrix products, arithmetic and copies ran while one was open for 3% -> 3% of each run, Pallas kernels for 9% -> 3%
where the time goes in v6:
time: 136 us; the launch traced here: 135 us
  blocking collectives  45.2 us (33%)
  starting transfers between devices  39.8 us (29%)
  waiting for transfers between devices  25.7 us (19%)
  Pallas kernels  19 us (14%)
  local copies, waits for them, and re-layouts  2.55 us (2%)
  other arithmetic  2.24 us (2%)
    all_to_all x1, blocking collectives, local(): lax.all_to_all(sent, 'shard', split_axis=0, concat_axis=0, tiled=False)  45.2 us
    ppermute x17, starting transfers between devices, fetch(): return lax.ppermute(value, 'replica', pairs)  20.7 us
    ppermute x17, waiting for transfers between devices, fetch(): return lax.ppermute(value, 'replica', pairs)  13.2 us
    all_to_all x1, starting transfers between devices, local(): lax.all_to_all(packed, 'shard', split_axis=0, concat_axis=0, tiled=False)  11.1 us
    all_to_all x1, waiting for transfers between devices, local(): lax.all_to_all(packed, 'shard', split_axis=0, concat_axis=0, tiled=False)  8.75 us
    all_to_all x1, starting transfers between devices, local(): lax.all_to_all(spread, 'shard', split_axis=0, concat_axis=0, tiled=False,...  5.16 us
    pallas_call x1, Pallas kernels, local(): call(old_kernel, 'old', shape((2, TOKENS, HEAD), F32), scalars() + [whole...  4.11 us
    ppermute x1, waiting for transfers between devices, along_shard(): return lax.ppermute(value, 'shard', pairs)  3.75 us
  transfers between devices with their start and end apart: 20, of which 8 were waited for; matrix products, arithmetic and copies ran while one was open for 3% of the time, Pallas kernels for 3%

profile of v6, /device:TPU:32, one launch (start us, length us, event | category | flops | bytes accessed | tf_op | source)
XLA Modules:
  0.0 135.4 jit_solution(17353931282910812141)
XLA Ops:
  0.6 2.8 %pack.1 = (bf16[16,128,128]{2,1,0:T(8,128)(2,1)}, bf16[320,128]{1,0:T(8,128)(2,1)}) custom-call(bf16[128,320]{1,0:T(8,128)(2,1)} %bitcast.29, bf16[20,4096]{1,0:T(8,128)(2,1)} %dq.1, bf16[20,1024]{1,0:T(8,128)(2,1)} %dk.1, bf16[20,1024]{1,0:T(8,128)(2,1)} %dv.1, bf16[20,4096]{1,0:T(8,128)(2,1)} %do.1, s32[20,32]{1,0:T(8,128)} %sq.1, s32[20,32]{1,0:T(8,128)} %so.1, ...), custom_call_target="tpu_custom_call" | custom-call | tf_op jit(solution)/shard_map/pack/pallas_call | solution.py:443
  3.5 11.1 %all-to-all-start = ((bf16[16,128,128]{2,1,0:T(8,128)(2,1)}), bf16[16,128,128]{2,1,0:T(8,128)(2,1)S(1)}, u32[]{:S(2)}, u32[]{:S(2)}) async-start(bf16[16,128,128]{2,1,0:T(8,128)(2,1)} %get-tuple-element.30), calls=%async_computation | async-start | bytes 1048576 | tf_op jit(solution)/shard_map/all_to_all | solution.py:467
  14.5 3.0 %collective-permute-start = (bf16[320,128]{1,0:T(8,128)(2,1)}, bf16[320,128]{1,0:T(8,128)(2,1)S(1)}, u32[]{:S(2)}, u32[]{:S(2)}) collective-permute-start(bf16[320,128]{1,0:T(8,128)(2,1)} %get-tuple-element.31), channel_id=1, source_target_pairs={{8,0},{9,1},{10,2},{11,3},{12,4},{13,5},{14,6},{15,7},{0,8},{1,9},... | collective-permute-start | bytes 245768 | tf_op jit(solution)/shard_map/ppermute | solution.py:68
  17.5 3.7 %collective-permute-done = bf16[320,128]{1,0:T(8,128)(2,1)S(1)} collective-permute-done((bf16[320,128]{1,0:T(8,128)(2,1)}, bf16[320,128]{1,0:T(8,128)(2,1)S(1)}, u32[]{:S(2)}, u32[]{:S(2)}) %collective-permute-start) | collective-permute-done | bytes 81952 | tf_op jit(solution)/shard_map/ppermute | solution.py:68
  22.1 8.8 %all-to-all-done.recv = bf16[16,128,128]{2,1,0:T(8,128)(2,1)S(1)} async-done(((bf16[16,128,128]{2,1,0:T(8,128)(2,1)}), bf16[16,128,128]{2,1,0:T(8,128)(2,1)S(1)}, u32[]{:S(2)}, u32[]{:S(2)}) %all-to-all-start) | async-done | bytes 524320 | tf_op jit(solution)/shard_map/all_to_all | solution.py:467
  32.2 3.0 %refresh.1 = (bf16[256,512]{1,0:T(8,128)(2,1)}, bf16[224,512]{1,0:T(8,128)(2,1)}) custom-call(s32[1]{0:T(128)} %bitcast.here, bf16[16,128,128]{2,1,0:T(8,128)(2,1)} %copy-done.9, bf16[5120,256]{1,0:T(8,128)(2,1)} %base_q.1, bf16[5120,128]{1,0:T(8,128)(2,1)} %base_k.1, bf16[5120,128]{1,0:T(8,128)(2,1)} %bv.1, bf16[5120,256]{1,0:T(8,128)(2,1)} %bo.1), custom_call_target="tpu_custom_call" | custom-call | tf_op jit(solution)/shard_map/refresh/pallas_call | solution.py:473
  35.3 5.2 %all-to-all-start.1 = ((bf16[8,640,128]{2,1,0:T(8,128)(2,1)}), bf16[8,640,128]{2,1,0:T(8,128)(2,1)S(1)}, u32[]{:S(2)}, u32[]{:S(2)}) async-start(bf16[8,640,128]{2,1,0:T(8,128)(2,1)} %broadcast_in_dim.21), calls=%async_computation.1 | async-start | bytes 2621440 | tf_op jit(solution)/shard_map/all_to_all | solution.py:492
  41.3 1.6 %collective-permute-start.9 = (bf16[224,512]{1,0:T(8,128)(2,1)}, bf16[224,512]{1,0:T(8,128)(2,1)}, u32[]{:S(2)}, u32[]{:S(2)}) collective-permute-start(bf16[224,512]{1,0:T(8,128)(2,1)} %get-tuple-element.45.rest_8_), channel_id=1, source_target_pairs={{96,0},{112,16},{0,32},{16,48},{32,64},{48,80},{64,96},{80,112},{2... | collective-permute-start | bytes 688136 | tf_op jit(solution)/shard_map/ppermute | solution.py:44
  42.9 1.7 %collective-permute-start.8 = (bf16[224,512]{1,0:T(8,128)(2,1)}, bf16[224,512]{1,0:T(8,128)(2,1)}, u32[]{:S(2)}, u32[]{:S(2)}) collective-permute-start(bf16[224,512]{1,0:T(8,128)(2,1)} %get-tuple-element.45.rest_8_), channel_id=1, source_target_pairs={{32,0},{48,16},{64,32},{80,48},{96,64},{112,80},{0,96},{16,112},{1... | collective-permute-start | bytes 688136 | tf_op jit(solution)/shard_map/ppermute | solution.py:44
  46.0 1.8 %collective-permute-start.1 = (bf16[256,512]{1,0:T(8,128)(2,1)S(1)}, bf16[256,512]{1,0:T(8,128)(2,1)S(1)}, u32[]{:S(2)}, u32[]{:S(2)}) collective-permute-start(bf16[256,512]{1,0:T(8,128)(2,1)S(1)} %copy-done.4), channel_id=1, source_target_pairs={{32,0},{48,16},{64,32},{80,48},{96,64},{112,80},{0,96},{16,112},{1... | collective-permute-start | bytes 786440 | tf_op jit(solution)/shard_map/ppermute | solution.py:44
  49.4 1.5 %collective-permute-start.3 = (bf16[256,512]{1,0:T(8,128)(2,1)S(1)}, bf16[256,512]{1,0:T(8,128)(2,1)S(1)}, u32[]{:S(2)}, u32[]{:S(2)}) collective-permute-start(bf16[256,512]{1,0:T(8,128)(2,1)S(1)} %copy-done.4), channel_id=1, source_target_pairs={{96,0},{112,16},{0,32},{16,48},{32,64},{48,80},{64,96},{80,112},{2... | collective-permute-start | bytes 786440 | tf_op jit(solution)/shard_map/ppermute | solution.py:44
  50.9 3.5 %collective-permute-done.1.rest_1_ = bf16[256,512]{1,0:T(8,128)(2,1)S(1)} collective-permute-done((bf16[256,512]{1,0:T(8,128)(2,1)S(1)}, bf16[256,512]{1,0:T(8,128)(2,1)S(1)}, u32[]{:S(2)}, u32[]{:S(2)}) %collective-permute-start.1) | collective-permute-done | bytes 262176 | tf_op jit(solution)/shard_map/ppermute | solution.py:44
  54.4 2.2 %collective-permute-start.2 = (bf16[256,512]{1,0:T(8,128)(2,1)S(1)}, bf16[256,512]{1,0:T(8,128)(2,1)S(1)}, u32[]{:S(2)}, u32[]{:S(2)}) collective-permute-start(bf16[256,512]{1,0:T(8,128)(2,1)S(1)} %collective-permute-done.1.rest_1_), channel_id=1, source_target_pairs={{32,0},{48,16},{64,32},{80,48},{96,64},{112,80},{0,96},{16,112},{1... | collective-permute-start | bytes 786440 | tf_op jit(solution)/shard_map/ppermute | solution.py:44
  61.2 3.2 %collective-permute-done.12.rest_13_ = bf16[224,512]{1,0:T(8,128)(2,1)} collective-permute-done((bf16[224,512]{1,0:T(8,128)(2,1)S(1)}, bf16[224,512]{1,0:T(8,128)(2,1)}, u32[]{:S(2)}, u32[]{:S(2)}) %collective-permute-start.12) | collective-permute-done | bytes 229408 | tf_op jit(solution)/shard_map/ppermute | solution.py:44
  64.4 1.6 %collective-permute-start.7 = (bf16[256,512]{1,0:T(8,128)(2,1)S(1)}, bf16[256,512]{1,0:T(8,128)(2,1)}, u32[]{:S(2)}, u32[]{:S(2)}) collective-permute-start(bf16[256,512]{1,0:T(8,128)(2,1)S(1)} %collective-permute-done.4.rest_4_), channel_id=1, source_target_pairs={{96,0},{112,16},{0,32},{16,48},{32,64},{48,80},{64,96},{80,112},{2... | collective-permute-start | bytes 786440 | tf_op jit(solution)/shard_map/ppermute | solution.py:44
  66.0 1.9 %collective-permute-start.13 = (bf16[224,512]{1,0:T(8,128)(2,1)}, bf16[224,512]{1,0:T(8,128)(2,1)}, u32[]{:S(2)}, u32[]{:S(2)}) collective-permute-start(bf16[224,512]{1,0:T(8,128)(2,1)} %collective-permute-done.12.rest_13_), channel_id=1, source_target_pairs={{32,0},{48,16},{64,32},{80,48},{96,64},{112,80},{0,96},{16,112},{1... | collective-permute-start | bytes 688136 | tf_op jit(solution)/shard_map/ppermute | solution.py:44
  67.9 1.4 %collective-permute-start.6 = (bf16[256,512]{1,0:T(8,128)(2,1)S(1)}, bf16[256,512]{1,0:T(8,128)(2,1)}, u32[]{:S(2)}, u32[]{:S(2)}) collective-permute-start(bf16[256,512]{1,0:T(8,128)(2,1)S(1)} %collective-permute-done.2.rest_2_), channel_id=1, source_target_pairs={{128,0},{144,16},{160,32},{176,48},{192,64},{208,80},{224,96},{240... | collective-permute-start | bytes 786440 | tf_op jit(solution)/shard_map/ppermute | solution.py:44
  72.5 1.9 %collective-permute-done.6.rest_6_ = bf16[256,512]{1,0:T(8,128)(2,1)} collective-permute-done((bf16[256,512]{1,0:T(8,128)(2,1)S(1)}, bf16[256,512]{1,0:T(8,128)(2,1)}, u32[]{:S(2)}, u32[]{:S(2)}) %collective-permute-start.6) | collective-permute-done | bytes 262176 | tf_op jit(solution)/shard_map/ppermute | solution.py:44
  74.4 1.7 %normalise.1 = (bf16[8,128,384]{2,1,0:T(8,128)(2,1)S(1)}, bf16[8,128,384]{2,1,0:T(8,128)(2,1)S(1)}) custom-call(s32[1]{0:T(128)} %bitcast.here, s32[1]{0:T(128)} %bitcast.1.seat, f32[16,1,320]{2,1,0:T(1,128)S(1)} %reshape.59.gain, bf16[8,640,128]{2,1,0:T(8,128)(2,1)S(1)} %all-to-all-done.1.pairs), custom_call_target="tpu_custom_call" | custom-call | tf_op jit(solution)/shard_map/normalise/pallas_call | solution.py:554
  76.2 2.3 %collective-permute-done.15.given = bf16[8,128,384]{2,1,0:T(8,128)(2,1)S(1)} collective-permute-done((bf16[8,128,384]{2,1,0:T(8,128)(2,1)S(1)}, bf16[8,128,384]{2,1,0:T(8,128)(2,1)S(1)}, u32[]{:S(2)}, u32[]{:S(2)}) %collective-permute-start.15) | collective-permute-done | bytes 786464 | tf_op jit(solution)/shard_map/ppermute | solution.py:44
  78.5 3.0 %project.1 = (f32[128,512]{1,0:T(8,128)S(1)}, f32[128,512]{1,0:T(8,128)S(1)}, bf16[8,160,512]{2,1,0:T(8,128)(2,1)S(1)}) custom-call(s32[1]{0:T(128)} %bitcast.here, bf16[8,128,384]{2,1,0:T(8,128)(2,1)S(1)} %get-tuple-element.47.keep, bf16[8,128,384]{2,1,0:T(8,128)(2,1)S(1)} %collective-permute-done.15.given, bf16[256,512]{1,0:T(8,128)(2,1)S(1)} %copy-done.4, ...), custom_call_target="tpu_custom_call" | custom-call | tf_op jit(solution)/shard_map/project/pallas_call | solution.py:587
  82.1 4.1 %old.1 = f32[2,128,128]{2,1,0:T(8,128)S(1)} custom-call(s32[1]{0:T(128)} %bitcast.here, bf16[8,128,384]{2,1,0:T(8,128)(2,1)S(1)} %get-tuple-element.47.keep, bf16[8,128,384]{2,1,0:T(8,128)(2,1)S(1)} %get-tuple-element.48.give, f32[264,128]{1,0:T(8,128)S(1)} %concatenate.19.table, s32[40,128]{1,0:T(8,128)S(1)} %add_add_fusion.marks, ...), custom_call_target="tpu_custom_call" | custom-call | tf_op jit(solution)/shard_map/old/pallas_call | solution.py:567
  86.2 3.1 %attend.1 = bf16[16,336,128]{2,1,0:T(8,128)(2,1)S(1)} custom-call(s32[1]{0:T(128)} %bitcast.here, f32[128,512]{1,0:T(8,128)S(1)} %get-tuple-element.49.own, f32[128,512]{1,0:T(8,128)S(1)} %collective-permute-done.16.other, f32[264,128]{1,0:T(8,128)S(1)} %concatenate.19.table, s32[40,128]{1,0:T(8,128)S(1)} %add_add_fusion.marks, ...), custom_call_target="tpu_custom_call" | custom-call | tf_op jit(solution)/shard_map/attend/pallas_call | solution.py:605
  89.3 45.2 %all_to_all.15.recv = bf16[16,336,128]{2,1,0:T(8,128)(2,1)S(1)} all-to-all(bf16[16,336,128]{2,1,0:T(8,128)(2,1)S(1)} %attend.1), channel_id=1, replica_groups=mesh['replica'=16,'shard'=16] {'shard'}, dimensions={0} | all-to-all | bytes 2752512 | tf_op jit(solution)/shard_map/all_to_all | solution.py:626
  (75 shorter events, 15.4 us)
Async XLA Ops:
  3.5 27.4 %all-to-all-start = ((bf16[16,128,128]{2,1,0:T(8,128)(2,1)}), bf16[16,128,128]{2,1,0:T(8,128)(2,1)S(1)}, u32[]{:S(2)}, u32[]{:S(2)}) async-start(bf16[16,128,128]{2,1,0:T(8,128)(2,1)} %get-tuple-element.30), calls=%async_computation | async-start | bytes 1048576 | tf_op jit(solution)/shard_map/all_to_all | solution.py:467
  14.5 6.7 %collective-permute-start = (bf16[320,128]{1,0:T(8,128)(2,1)}, bf16[320,128]{1,0:T(8,128)(2,1)S(1)}, u32[]{:S(2)}, u32[]{:S(2)}) collective-permute-start(bf16[320,128]{1,0:T(8,128)(2,1)} %get-tuple-element.31), channel_id=1, source_target_pairs={{8,0},{9,1},{10,2},{11,3},{12,4},{13,5},{14,6},{15,7},{0,8},{1,9},... | collective-permute-start | bytes 245768 | tf_op jit(solution)/shard_map/ppermute | solution.py:68
  35.2 34.3 %copy-start.2 = (bf16[32,64,128]{2,1,0:T(8,128)(2,1)S(1)}, bf16[32,64,128]{2,1,0:T(8,128)(2,1)}, u32[]{:S(2)}) copy-start(bf16[32,64,128]{2,1,0:T(8,128)(2,1)} %param.38) | copy-start | bytes 1572868
  35.3 35.4 %copy-start.12 = (f32[128]{0:T(128)S(1)}, f32[128]{0:T(128)}, u32[]{:S(2)}) copy-start(f32[128]{0:T(128)} %param.24) | copy-start | bytes 1540
  35.3 35.4 %copy-start.13 = (f32[128]{0:T(128)S(1)}, f32[128]{0:T(128)}, u32[]{:S(2)}) copy-start(f32[128]{0:T(128)} %param.25) | copy-start | bytes 1540
  35.3 39.1 %all-to-all-start.1 = ((bf16[8,640,128]{2,1,0:T(8,128)(2,1)}), bf16[8,640,128]{2,1,0:T(8,128)(2,1)S(1)}, u32[]{:S(2)}, u32[]{:S(2)}) async-start(bf16[8,640,128]{2,1,0:T(8,128)(2,1)} %broadcast_in_dim.21), calls=%async_computation.1 | async-start | bytes 2621440 | tf_op jit(solution)/shard_map/all_to_all | solution.py:492
  40.6 8.8 %collective-permute-start.11 = (bf16[224,512]{1,0:T(8,128)(2,1)}, bf16[224,512]{1,0:T(8,128)(2,1)S(1)}, u32[]{:S(2)}, u32[]{:S(2)}) collective-permute-start(bf16[224,512]{1,0:T(8,128)(2,1)} %get-tuple-element.45.rest_8_), channel_id=1, source_target_pairs={{128,0},{144,16},{160,32},{176,48},{192,64},{208,80},{224,96},{240... | collective-permute-start | bytes 688136 | tf_op jit(solution)/shard_map/ppermute | solution.py:44
  41.3 15.4 %collective-permute-start.9 = (bf16[224,512]{1,0:T(8,128)(2,1)}, bf16[224,512]{1,0:T(8,128)(2,1)}, u32[]{:S(2)}, u32[]{:S(2)}) collective-permute-start(bf16[224,512]{1,0:T(8,128)(2,1)} %get-tuple-element.45.rest_8_), channel_id=1, source_target_pairs={{96,0},{112,16},{0,32},{16,48},{32,64},{48,80},{64,96},{80,112},{2... | collective-permute-start | bytes 688136 | tf_op jit(solution)/shard_map/ppermute | solution.py:44
  42.9 15.1 %collective-permute-start.8 = (bf16[224,512]{1,0:T(8,128)(2,1)}, bf16[224,512]{1,0:T(8,128)(2,1)}, u32[]{:S(2)}, u32[]{:S(2)}) collective-permute-start(bf16[224,512]{1,0:T(8,128)(2,1)} %get-tuple-element.45.rest_8_), channel_id=1, source_target_pairs={{32,0},{48,16},{64,32},{80,48},{96,64},{112,80},{0,96},{16,112},{1... | collective-permute-start | bytes 688136 | tf_op jit(solution)/shard_map/ppermute | solution.py:44
  44.5 15.2 %collective-permute-start.4 = (bf16[256,512]{1,0:T(8,128)(2,1)S(1)}, bf16[256,512]{1,0:T(8,128)(2,1)S(1)}, u32[]{:S(2)}, u32[]{:S(2)}) collective-permute-start(bf16[256,512]{1,0:T(8,128)(2,1)S(1)} %copy-done.4), channel_id=1, source_target_pairs={{128,0},{144,16},{160,32},{176,48},{192,64},{208,80},{224,96},{240... | collective-permute-start | bytes 786440 | tf_op jit(solution)/shard_map/ppermute | solution.py:44
  46.0 8.4 %collective-permute-start.1 = (bf16[256,512]{1,0:T(8,128)(2,1)S(1)}, bf16[256,512]{1,0:T(8,128)(2,1)S(1)}, u32[]{:S(2)}, u32[]{:S(2)}) collective-permute-start(bf16[256,512]{1,0:T(8,128)(2,1)S(1)} %copy-done.4), channel_id=1, source_target_pairs={{32,0},{48,16},{64,32},{80,48},{96,64},{112,80},{0,96},{16,112},{1... | collective-permute-start | bytes 786440 | tf_op jit(solution)/shard_map/ppermute | solution.py:44
  49.4 20.0 %copy-start.5 = (bf16[224,512]{1,0:T(8,128)(2,1)}, bf16[224,512]{1,0:T(8,128)(2,1)S(1)}, u32[]{:S(2)}) copy-start(bf16[224,512]{1,0:T(8,128)(2,1)S(1)} %collective-permute-done.11.rest_12_) | copy-start | bytes 688132
  49.4 11.2 %collective-permute-start.3 = (bf16[256,512]{1,0:T(8,128)(2,1)S(1)}, bf16[256,512]{1,0:T(8,128)(2,1)S(1)}, u32[]{:S(2)}, u32[]{:S(2)}) collective-permute-start(bf16[256,512]{1,0:T(8,128)(2,1)S(1)} %copy-done.4), channel_id=1, source_target_pairs={{96,0},{112,16},{0,32},{16,48},{32,64},{48,80},{64,96},{80,112},{2... | collective-permute-start | bytes 786440 | tf_op jit(solution)/shard_map/ppermute | solution.py:44
  54.4 13.5 %collective-permute-start.2 = (bf16[256,512]{1,0:T(8,128)(2,1)S(1)}, bf16[256,512]{1,0:T(8,128)(2,1)S(1)}, u32[]{:S(2)}, u32[]{:S(2)}) collective-permute-start(bf16[256,512]{1,0:T(8,128)(2,1)S(1)} %collective-permute-done.1.rest_1_), channel_id=1, source_target_pairs={{32,0},{48,16},{64,32},{80,48},{96,64},{112,80},{0,96},{16,112},{1... | collective-permute-start | bytes 786440 | tf_op jit(solution)/shard_map/ppermute | solution.py:44
  56.7 7.6 %collective-permute-start.12 = (bf16[224,512]{1,0:T(8,128)(2,1)S(1)}, bf16[224,512]{1,0:T(8,128)(2,1)}, u32[]{:S(2)}, u32[]{:S(2)}) collective-permute-start(bf16[224,512]{1,0:T(8,128)(2,1)S(1)} %collective-permute-done.11.rest_12_), channel_id=1, source_target_pairs={{32,0},{48,16},{64,32},{80,48},{96,64},{112,80},{0,96},{16,112},{1... | collective-permute-start | bytes 688136 | tf_op jit(solution)/shard_map/ppermute | solution.py:44
  57.9 8.0 %collective-permute-start.14 = (bf16[224,512]{1,0:T(8,128)(2,1)}, bf16[224,512]{1,0:T(8,128)(2,1)S(1)}, u32[]{:S(2)}, u32[]{:S(2)}) collective-permute-start(bf16[224,512]{1,0:T(8,128)(2,1)} %collective-permute-done.9.rest_11_), channel_id=1, source_target_pairs={{128,0},{144,16},{160,32},{176,48},{192,64},{208,80},{224,96},{240... | collective-permute-start | bytes 688136 | tf_op jit(solution)/shard_map/ppermute | solution.py:44
  59.7 11.9 %collective-permute-start.10 = (bf16[224,512]{1,0:T(8,128)(2,1)}, bf16[224,512]{1,0:T(8,128)(2,1)}, u32[]{:S(2)}, u32[]{:S(2)}) collective-permute-start(bf16[224,512]{1,0:T(8,128)(2,1)} %collective-permute-done.9.rest_11_), channel_id=1, source_target_pairs={{96,0},{112,16},{0,32},{16,48},{32,64},{48,80},{64,96},{80,112},{2... | collective-permute-start | bytes 688136 | tf_op jit(solution)/shard_map/ppermute | solution.py:44
  60.6 11.9 %collective-permute-start.5 = (bf16[256,512]{1,0:T(8,128)(2,1)S(1)}, bf16[256,512]{1,0:T(8,128)(2,1)}, u32[]{:S(2)}, u32[]{:S(2)}) collective-permute-start(bf16[256,512]{1,0:T(8,128)(2,1)S(1)} %collective-permute-done.1.rest_1_), channel_id=1, source_target_pairs={{128,0},{144,16},{160,32},{176,48},{192,64},{208,80},{224,96},{240... | collective-permute-start | bytes 786440 | tf_op jit(solution)/shard_map/ppermute | solution.py:44
  64.4 8.1 %collective-permute-start.7 = (bf16[256,512]{1,0:T(8,128)(2,1)S(1)}, bf16[256,512]{1,0:T(8,128)(2,1)}, u32[]{:S(2)}, u32[]{:S(2)}) collective-permute-start(bf16[256,512]{1,0:T(8,128)(2,1)S(1)} %collective-permute-done.4.rest_4_), channel_id=1, source_target_pairs={{96,0},{112,16},{0,32},{16,48},{32,64},{48,80},{64,96},{80,112},{2... | collective-permute-start | bytes 786440 | tf_op jit(solution)/shard_map/ppermute | solution.py:44
  66.0 6.5 %collective-permute-start.13 = (bf16[224,512]{1,0:T(8,128)(2,1)}, bf16[224,512]{1,0:T(8,128)(2,1)}, u32[]{:S(2)}, u32[]{:S(2)}) collective-permute-start(bf16[224,512]{1,0:T(8,128)(2,1)} %collective-permute-done.12.rest_13_), channel_id=1, source_target_pairs={{32,0},{48,16},{64,32},{80,48},{96,64},{112,80},{0,96},{16,112},{1... | collective-permute-start | bytes 688136 | tf_op jit(solution)/shard_map/ppermute | solution.py:44
  67.9 6.5 %collective-permute-start.6 = (bf16[256,512]{1,0:T(8,128)(2,1)S(1)}, bf16[256,512]{1,0:T(8,128)(2,1)}, u32[]{:S(2)}, u32[]{:S(2)}) collective-permute-start(bf16[256,512]{1,0:T(8,128)(2,1)S(1)} %collective-permute-done.2.rest_2_), channel_id=1, source_target_pairs={{128,0},{144,16},{160,32},{176,48},{192,64},{208,80},{224,96},{240... | collective-permute-start | bytes 786440 | tf_op jit(solution)/shard_map/ppermute | solution.py:44
  76.1 2.4 %collective-permute-start.15 = (bf16[8,128,384]{2,1,0:T(8,128)(2,1)S(1)}, bf16[8,128,384]{2,1,0:T(8,128)(2,1)S(1)}, u32[]{:S(2)}, u32[]{:S(2)}) collective-permute-start(bf16[8,128,384]{2,1,0:T(8,128)(2,1)S(1)} %get-tuple-element.48.give), channel_id=1, source_target_pairs={{16,0},{0,16},{48,32},{32,48},{80,64},{64,80},{112,96},{96,112},{1... | collective-permute-start | bytes 2359304 | tf_op jit(solution)/shard_map/ppermute | solution.py:44
  81.5 4.7 %collective-permute-start.17 = (bf16[8,160,512]{2,1,0:T(8,128)(2,1)S(1)}, bf16[8,160,512]{2,1,0:T(8,128)(2,1)S(1)}, u32[]{:S(2)}, u32[]{:S(2)}) collective-permute-start(bf16[8,160,512]{2,1,0:T(8,128)(2,1)S(1)} %get-tuple-element.55.mine), channel_id=1, source_target_pairs={{16,0},{0,16},{48,32},{32,48},{80,64},{64,80},{112,96},{96,112},{1... | collective-permute-start | bytes 3932168 | tf_op jit(solution)/shard_map/ppermute | solution.py:44
  81.7 4.5 %collective-permute-start.16 = (f32[128,512]{1,0:T(8,128)S(1)}, f32[128,512]{1,0:T(8,128)S(1)}, u32[]{:S(2)}, u32[]{:S(2)}) collective-permute-start(f32[128,512]{1,0:T(8,128)S(1)} %get-tuple-element.50), channel_id=1, source_target_pairs={{16,0},{0,16},{48,32},{32,48},{80,64},{64,80},{112,96},{96,112},{1... | collective-permute-start | bytes 786440 | tf_op jit(solution)/shard_map/ppermute | solution.py:44
  (13 other events, 91.1 us)

commit v7 on v6

--- a/solution.py
+++ b/solution.py
@@ -31,6 +31,7 @@
 LOWER = OWN - UPPER + FOLD
 WIDE = 384
 SENT = OWN + TAIL
+TRIPS = ((3, -3), (4, 2), (-2, 1), (-1, 0))
 F32 = jnp.float32
 BF16 = jnp.bfloat16
 VMEM = pltpu.VMEM
@@ -312,8 +313,8 @@
 
 
 def attend_kernel(
-    here, own, other, table, marks, cache_hbm, values_hbm, keys, one_q, one_f, old, mine, theirs,
-    out,
+    here, seat, own, other, table, marks, cache_hbm, values_hbm, keys, one_q, one_f, old, mine, theirs,
+    give0, give1, give2, give3, keep0, keep1, keep2, keep3,
     cache, values, query, lse, mixed, sems,
 ):
     copies = (
@@ -343,30 +344,51 @@
         mix = mix + dot((new / total).astype(BF16), fresh_v)
         put_groups(g, mixed, mix)
     attended = jnp.concatenate([mixed[0:TOKENS, :], mixed[TOKENS:, :]], axis=1).astype(BF16)
-    core = here[0] & 1
-    for rows, parity in ((mine, core), (theirs, 1 - core)):
-        for j in range(HALF):
-            for half in range(2):
-                part = dot_nt(rows[j, :, half * 256 : (half + 1) * 256], attended)
-                at = slice(half * FOLD, (half + 1) * FOLD)
-                out[2 * j + parity, at, :] = part.astype(BF16)
+    gives, keeps = (give0, give1, give2, give3), (keep0, keep1, keep2, keep3)
+    me = seat[0]
+
+    def place_parts(even, odd):
+        for c, trips in enumerate(TRIPS):
+            for i, dz in enumerate(trips):
+                rows = odd if dz & 1 else even
+                for dx, target in ((1, gives[c]), (0, keeps[c])):
+                    j = (((me >> 3) ^ dx) << 2) + (((me + dz) & 7) >> 1)
+                    for half in range(2):
+                        part = dot_nt(rows[j, :, half * 256 : (half + 1) * 256], attended)
+                        at = slice(half * FOLD, (half + 1) * FOLD)
+                        target[i, at, :] = part.astype(target.dtype)
+
+    same = ((here[0] ^ me) & 1) == 0
+    pl.when(same)(lambda: place_parts(mine, theirs))
+    pl.when(jnp.logical_not(same))(lambda: place_parts(theirs, mine))
     now = sample_logp(query, keys[...] + dot(one_f[...], fresh), one_q[...], lse)
     term = (now[0] - old[0]) + (now[1] - old[1])
-    line = term.T[0:1, :]
+    tail = split_line(term.T[0:1, :])
+    for target in gives + keeps:
+        for i in range(2):
+            target[i, OWN:SENT, :] = tail.astype(target.dtype)
+
+
+def split_line(line):
     high = line.astype(BF16).astype(F32)
     middle = (line - high).astype(BF16).astype(F32)
     low = line - high - middle
-    tail = jnp.concatenate([high, middle, low, jnp.zeros((TAIL - 3, TOKENS), F32)], axis=0)
-    tail = tail.astype(BF16)
-    for p in range(PARTS):
-        out[p, OWN:SENT, :] = tail
-
-
-def finish_kernel(recv, out, ratio):
+    return jnp.concatenate([high, middle, low, jnp.zeros((TAIL - 3, TOKENS), F32)], axis=0)
+
+
+def merge_kernel(keep, recv, first, second):
+    for i, out in enumerate((first, second)):
+        total = keep[i] + recv[i].astype(F32)
+        out[0:OWN, :] = total[0:OWN, :].astype(out.dtype)
+        line = (total[OWN + 2 : OWN + 3, :] + total[OWN + 1 : OWN + 2, :]) + total[OWN : OWN + 1, :]
+        out[OWN:SENT, :] = split_line(line).astype(out.dtype)
+
+
+def finish_kernel(own, r1, r2, r3, r4, r5, r6, r7, out, ratio):
     for k, n in ((0, 128), (128, 128), (256, 80)):
-        total = recv[0, k : k + n, :].astype(F32)
-        for src in range(1, PARTS):
-            total = total + recv[src, k : k + n, :].astype(F32)
+        total = own[k : k + n, :]
+        for part in (r1, r2, r3, r4, r5, r6, r7):
+            total = total + part[k : k + n, :].astype(F32)
         if n == 128:
             out[:, k : k + n] = total.T.astype(BF16)
         else:
@@ -602,11 +624,11 @@
     other = fetch(other, 0, 0, 1)
     theirs = fetch(mine, 0, 0, 1)
 
-    sent = call(
+    parts = call(
         attend_kernel,
         "attend",
-        shape((PARTS, SENT, HEAD), BF16),
-        scalars()
+        (shape((2, SENT, HEAD), BF16),) * 4 + (shape((2, SENT, HEAD), F32),) * 4,
+        scalars(2)
         + [whole(TOKENS, 512)] * 2
         + [whole(2 * TOKENS + 8, HEAD), whole(ROWS + 8, HEAD)]
         + far_away(2)
@@ -622,16 +644,23 @@
             dma((2,)),
         ],
         mib=24,
-    )(here, own, other, table, marks, cache, values, keys, one_q, one_f, old, mine, theirs)
-    landed = lax.all_to_all(sent, "shard", split_axis=0, concat_axis=0, tiled=False)
+    )(here, seat, own, other, table, marks, cache, values, keys, one_q, one_f, old, mine, theirs)
+    crossed = [along_shard(give, 1, 0) for give in parts[:4]]
+    landed = []
+    for trips, keep_part, recv in zip(TRIPS, parts[4:], crossed):
+        kinds = tuple(shape((SENT, HEAD), BF16 if dz else F32) for dz in trips)
+        sums = call(
+            merge_kernel, "merge", kinds, [whole(2, SENT, HEAD)] * 2, [], mib=8
+        )(keep_part, recv)
+        landed += [along_shard(part, 0, -dz) if dz else part for dz, part in zip(trips, sums)]
     out, ratio = call(
         finish_kernel,
         "finish",
         (shape((TOKENS, OWN), BF16), shape((1, TOKENS), F32)),
-        [whole(PARTS, SENT, HEAD)],
+        [whole(SENT, HEAD)] * 8,
         [],
-        mib=20,
-    )(landed)
+        mib=16,
+    )(landed[-1], *landed[:-1])
     return out.reshape(STEPS, ROWS, OWN), ratio
 
 

time: 136 us -> 124 us (0.912)
  blocking collectives: 45.2 us -> 0 us
  starting transfers between devices: 39.8 us -> 61.5 us
  waiting for transfers between devices: 25.7 us -> 36.6 us
    all_to_all x1 -> x0, blocking collectives: 45.2 us -> none  [local(): lax.all_to_all(sent, 'shard', split_axis=0, concat_axis=0, tiled=False)]
    ppermute x1 -> x12, starting transfers between devices: 2.97 us -> 24.6 us  [along_shard(): return lax.ppermute(value, 'shard', pairs)]
    ppermute x1 -> x12, waiting for transfers between devices: 3.75 us -> 14.7 us  [along_shard(): return lax.ppermute(value, 'shard', pairs)]
    pallas_call x1 -> x5, Pallas kernels: 3.1 us -> 3.47 us  [the longest x1 3.27 us: local(): call(attend_kernel, 'attend', (shape((2, SENT, HEAD), BF16),) * 4 + (shap...]
  transfers between devices with their start and end apart: 20 -> 31, of which waited for: 8 -> 11; matrix products, arithmetic and copies ran while one was open for 3% -> 3% of each run, Pallas kernels for 3% -> 4%
where the time goes in v7:
time: 124 us; the launch traced here: 123 us
  starting transfers between devices  61.5 us (50%)
  waiting for transfers between devices  36.6 us (30%)
  Pallas kernels  19.3 us (16%)
  local copies, waits for them, and re-layouts  2.54 us (2%)
  other arithmetic  2.24 us (2%)
    ppermute x12, starting transfers between devices, along_shard(): return lax.ppermute(value, 'shard', pairs)  24.6 us
    ppermute x17, starting transfers between devices, fetch(): return lax.ppermute(value, 'replica', pairs)  20.7 us
    ppermute x12, waiting for transfers between devices, along_shard(): return lax.ppermute(value, 'shard', pairs)  14.7 us
    ppermute x17, waiting for transfers between devices, fetch(): return lax.ppermute(value, 'replica', pairs)  13.2 us
    all_to_all x1, starting transfers between devices, local(): lax.all_to_all(packed, 'shard', split_axis=0, concat_axis=0, tiled=False)  11.1 us
    all_to_all x1, waiting for transfers between devices, local(): lax.all_to_all(packed, 'shard', split_axis=0, concat_axis=0, tiled=False)  8.75 us
    all_to_all x1, starting transfers between devices, local(): lax.all_to_all(spread, 'shard', split_axis=0, concat_axis=0, tiled=False,...  5.16 us
    pallas_call x1, Pallas kernels, local(): call(old_kernel, 'old', shape((2, TOKENS, HEAD), F32), scalars() + [whole...  4.11 us
  transfers between devices with their start and end apart: 31, of which 11 were waited for; matrix products, arithmetic and copies ran while one was open for 3% of the time, Pallas kernels for 4%

profile of v7, /device:TPU:32, one launch (start us, length us, event | category | flops | bytes accessed | tf_op | source)
XLA Modules:
  0.0 123.1 jit_solution(10744788909451592284)
XLA Ops:
  0.6 2.8 %pack.1 = (bf16[16,128,128]{2,1,0:T(8,128)(2,1)}, bf16[320,128]{1,0:T(8,128)(2,1)}) custom-call(bf16[128,320]{1,0:T(8,128)(2,1)} %bitcast.29, bf16[20,4096]{1,0:T(8,128)(2,1)} %dq.1, bf16[20,1024]{1,0:T(8,128)(2,1)} %dk.1, bf16[20,1024]{1,0:T(8,128)(2,1)} %dv.1, bf16[20,4096]{1,0:T(8,128)(2,1)} %do.1, s32[20,32]{1,0:T(8,128)} %sq.1, s32[20,32]{1,0:T(8,128)} %so.1, ...), custom_call_target="tpu_custom_call" | custom-call | tf_op jit(solution)/shard_map/pack/pallas_call | solution.py:465
  3.5 11.1 %all-to-all-start = ((bf16[16,128,128]{2,1,0:T(8,128)(2,1)}), bf16[16,128,128]{2,1,0:T(8,128)(2,1)S(1)}, u32[]{:S(2)}, u32[]{:S(2)}) async-start(bf16[16,128,128]{2,1,0:T(8,128)(2,1)} %get-tuple-element.46), calls=%async_computation | async-start | bytes 1048576 | tf_op jit(solution)/shard_map/all_to_all | solution.py:489
  14.5 3.0 %collective-permute-start = (bf16[320,128]{1,0:T(8,128)(2,1)}, bf16[320,128]{1,0:T(8,128)(2,1)S(1)}, u32[]{:S(2)}, u32[]{:S(2)}) collective-permute-start(bf16[320,128]{1,0:T(8,128)(2,1)} %get-tuple-element.47), channel_id=1, source_target_pairs={{8,0},{9,1},{10,2},{11,3},{12,4},{13,5},{14,6},{15,7},{0,8},{1,9},... | collective-permute-start | bytes 245768 | tf_op jit(solution)/shard_map/ppermute | solution.py:69
  17.5 3.7 %collective-permute-done = bf16[320,128]{1,0:T(8,128)(2,1)S(1)} collective-permute-done((bf16[320,128]{1,0:T(8,128)(2,1)}, bf16[320,128]{1,0:T(8,128)(2,1)S(1)}, u32[]{:S(2)}, u32[]{:S(2)}) %collective-permute-start) | collective-permute-done | bytes 81952 | tf_op jit(solution)/shard_map/ppermute | solution.py:69
  22.2 8.8 %all-to-all-done.recv = bf16[16,128,128]{2,1,0:T(8,128)(2,1)S(1)} async-done(((bf16[16,128,128]{2,1,0:T(8,128)(2,1)}), bf16[16,128,128]{2,1,0:T(8,128)(2,1)S(1)}, u32[]{:S(2)}, u32[]{:S(2)}) %all-to-all-start) | async-done | bytes 524320 | tf_op jit(solution)/shard_map/all_to_all | solution.py:489
  32.2 3.0 %refresh.1 = (bf16[256,512]{1,0:T(8,128)(2,1)}, bf16[224,512]{1,0:T(8,128)(2,1)}) custom-call(s32[1]{0:T(128)} %bitcast.here, bf16[16,128,128]{2,1,0:T(8,128)(2,1)} %copy-done.9, bf16[5120,256]{1,0:T(8,128)(2,1)} %base_q.1, bf16[5120,128]{1,0:T(8,128)(2,1)} %base_k.1, bf16[5120,128]{1,0:T(8,128)(2,1)} %bv.1, bf16[5120,256]{1,0:T(8,128)(2,1)} %bo.1), custom_call_target="tpu_custom_call" | custom-call | tf_op jit(solution)/shard_map/refresh/pallas_call | solution.py:495
  35.3 5.2 %all-to-all-start.1 = ((bf16[8,640,128]{2,1,0:T(8,128)(2,1)}), bf16[8,640,128]{2,1,0:T(8,128)(2,1)S(1)}, u32[]{:S(2)}, u32[]{:S(2)}) async-start(bf16[8,640,128]{2,1,0:T(8,128)(2,1)} %broadcast_in_dim.21), calls=%async_computation.1 | async-start | bytes 2621440 | tf_op jit(solution)/shard_map/all_to_all | solution.py:514
  46.0 1.8 %collective-permute-start.1 = (bf16[256,512]{1,0:T(8,128)(2,1)S(1)}, bf16[256,512]{1,0:T(8,128)(2,1)S(1)}, u32[]{:S(2)}, u32[]{:S(2)}) collective-permute-start(bf16[256,512]{1,0:T(8,128)(2,1)S(1)} %copy-done.4), channel_id=1, source_target_pairs={{32,0},{48,16},{64,32},{80,48},{96,64},{112,80},{0,96},{16,112},{1... | collective-permute-start | bytes 786440 | tf_op jit(solution)/shard_map/ppermute | solution.py:45
  50.9 3.5 %collective-permute-done.1.rest_1_ = bf16[256,512]{1,0:T(8,128)(2,1)S(1)} collective-permute-done((bf16[256,512]{1,0:T(8,128)(2,1)S(1)}, bf16[256,512]{1,0:T(8,128)(2,1)S(1)}, u32[]{:S(2)}, u32[]{:S(2)}) %collective-permute-start.1) | collective-permute-done | bytes 262176 | tf_op jit(solution)/shard_map/ppermute | solution.py:45
  54.4 2.2 %collective-permute-start.2 = (bf16[256,512]{1,0:T(8,128)(2,1)S(1)}, bf16[256,512]{1,0:T(8,128)(2,1)S(1)}, u32[]{:S(2)}, u32[]{:S(2)}) collective-permute-start(bf16[256,512]{1,0:T(8,128)(2,1)S(1)} %collective-permute-done.1.rest_1_), channel_id=1, source_target_pairs={{32,0},{48,16},{64,32},{80,48},{96,64},{112,80},{0,96},{16,112},{1... | collective-permute-start | bytes 786440 | tf_op jit(solution)/shard_map/ppermute | solution.py:45
  61.2 3.2 %collective-permute-done.12.rest_13_ = bf16[224,512]{1,0:T(8,128)(2,1)} collective-permute-done((bf16[224,512]{1,0:T(8,128)(2,1)S(1)}, bf16[224,512]{1,0:T(8,128)(2,1)}, u32[]{:S(2)}, u32[]{:S(2)}) %collective-permute-start.12) | collective-permute-done | bytes 229408 | tf_op jit(solution)/shard_map/ppermute | solution.py:45
  66.0 1.9 %collective-permute-start.13 = (bf16[224,512]{1,0:T(8,128)(2,1)}, bf16[224,512]{1,0:T(8,128)(2,1)}, u32[]{:S(2)}, u32[]{:S(2)}) collective-permute-start(bf16[224,512]{1,0:T(8,128)(2,1)} %collective-permute-done.12.rest_13_), channel_id=1, source_target_pairs={{32,0},{48,16},{64,32},{80,48},{96,64},{112,80},{0,96},{16,112},{1... | collective-permute-start | bytes 688136 | tf_op jit(solution)/shard_map/ppermute | solution.py:45
  72.5 1.9 %collective-permute-done.6.rest_6_ = bf16[256,512]{1,0:T(8,128)(2,1)} collective-permute-done((bf16[256,512]{1,0:T(8,128)(2,1)S(1)}, bf16[256,512]{1,0:T(8,128)(2,1)}, u32[]{:S(2)}, u32[]{:S(2)}) %collective-permute-start.6) | collective-permute-done | bytes 262176 | tf_op jit(solution)/shard_map/ppermute | solution.py:45
  76.2 2.3 %collective-permute-done.15.given = bf16[8,128,384]{2,1,0:T(8,128)(2,1)S(1)} collective-permute-done((bf16[8,128,384]{2,1,0:T(8,128)(2,1)S(1)}, bf16[8,128,384]{2,1,0:T(8,128)(2,1)S(1)}, u32[]{:S(2)}, u32[]{:S(2)}) %collective-permute-start.15) | collective-permute-done | bytes 786464 | tf_op jit(solution)/shard_map/ppermute | solution.py:45
  78.5 3.0 %project.1 = (f32[128,512]{1,0:T(8,128)S(1)}, f32[128,512]{1,0:T(8,128)S(1)}, bf16[8,160,512]{2,1,0:T(8,128)(2,1)S(1)}) custom-call(s32[1]{0:T(128)} %bitcast.here, bf16[8,128,384]{2,1,0:T(8,128)(2,1)S(1)} %get-tuple-element.63.keep, bf16[8,128,384]{2,1,0:T(8,128)(2,1)S(1)} %collective-permute-done.15.given, bf16[256,512]{1,0:T(8,128)(2,1)S(1)} %copy-done.4, ...), custom_call_target="tpu_custom_call" | custom-call | tf_op jit(solution)/shard_map/project/pallas_call | solution.py:609
  82.1 4.1 %old.1 = f32[2,128,128]{2,1,0:T(8,128)S(1)} custom-call(s32[1]{0:T(128)} %bitcast.here, bf16[8,128,384]{2,1,0:T(8,128)(2,1)S(1)} %get-tuple-element.63.keep, bf16[8,128,384]{2,1,0:T(8,128)(2,1)S(1)} %get-tuple-element.64.give, f32[264,128]{1,0:T(8,128)S(1)} %concatenate.19.table, s32[40,128]{1,0:T(8,128)S(1)} %add_add_fusion.marks, ...), custom_call_target="tpu_custom_call" | custom-call | tf_op jit(solution)/shard_map/old/pallas_call | solution.py:589
  86.2 3.3 %attend.1 = (bf16[2,336,128]{2,1,0:T(8,128)(2,1)S(1)}, bf16[2,336,128]{2,1,0:T(8,128)(2,1)S(1)}, bf16[2,336,128]{2,1,0:T(8,128)(2,1)S(1)}, bf16[2,336,128]{2,1,0...) custom-call(s32[1]{0:T(128)} %bitcast.here, ...), custom_call_target="tpu_custom_call" | custom-call | tf_op jit(solution)/shard_map/attend/pallas_call | solution.py:627
  89.5 3.0 %collective-permute-start.18 = (bf16[2,336,128]{2,1,0:T(8,128)(2,1)S(1)}, bf16[2,336,128]{2,1,0:T(8,128)(2,1)S(1)}, u32[]{:S(2)}, u32[]{:S(2)}) collective-permute-start(bf16[2,336,128]{2,1,0:T(8,128)(2,1)S(1)} %get-tuple-element.73), channel_id=1, source_target_pairs={{8,0},{9,1},{10,2},{11,3},{12,4},{13,5},{14,6},{15,7},{0,8},{1,9},... | collective-permute-start | bytes 516104 | tf_op jit(solution)/shard_map/ppermute | solution.py:69
  93.1 2.9 %collective-permute-start.22 = (bf16[2,336,128]{2,1,0:T(8,128)(2,1)S(1)}, bf16[2,336,128]{2,1,0:T(8,128)(2,1)S(1)}, u32[]{:S(2)}, u32[]{:S(2)}) collective-permute-start(bf16[2,336,128]{2,1,0:T(8,128)(2,1)S(1)} %get-tuple-element.80), channel_id=1, source_target_pairs={{8,0},{9,1},{10,2},{11,3},{12,4},{13,5},{14,6},{15,7},{0,8},{1,9},... | collective-permute-start | bytes 516104 | tf_op jit(solution)/shard_map/ppermute | solution.py:69
  99.0 3.1 %collective-permute-done.19.recv = bf16[2,336,128]{2,1,0:T(8,128)(2,1)S(1)} collective-permute-done((bf16[2,336,128]{2,1,0:T(8,128)(2,1)S(1)}, bf16[2,336,128]{2,1,0:T(8,128)(2,1)S(1)}, u32[]{:S(2)}, u32[]{:S(2)}) %collective-permute-start.19) | collective-permute-done | bytes 172064 | tf_op jit(solution)/shard_map/ppermute | solution.py:69
  102.1 4.5 %collective-permute-start.20 = (bf16[336,128]{1,0:T(8,128)(2,1)S(1)}, bf16[336,128]{1,0:T(8,128)(2,1)S(1)}, u32[]{:S(2)}, u32[]{:S(2)}) collective-permute-start(bf16[336,128]{1,0:T(8,128)(2,1)S(1)} %get-tuple-element.77), channel_id=1, source_target_pairs={{5,0},{6,1},{7,2},{0,3},{1,4},{2,5},{3,6},{4,7},{13,8},{14,9},{15,... | collective-permute-start | bytes 258056 | tf_op jit(solution)/shard_map/ppermute | solution.py:69
  107.2 4.6 %collective-permute-start.23 = (bf16[336,128]{1,0:T(8,128)(2,1)S(1)}, bf16[336,128]{1,0:T(8,128)(2,1)S(1)}, u32[]{:S(2)}, u32[]{:S(2)}) collective-permute-start(bf16[336,128]{1,0:T(8,128)(2,1)S(1)} %get-tuple-element.81), channel_id=1, source_target_pairs={{4,0},{5,1},{6,2},{7,3},{0,4},{1,5},{2,6},{3,7},{12,8},{13,9},{14,... | collective-permute-start | bytes 258056 | tf_op jit(solution)/shard_map/ppermute | solution.py:69
  111.9 4.2 %collective-permute-start.26 = (bf16[336,128]{1,0:T(8,128)(2,1)S(1)}, bf16[336,128]{1,0:T(8,128)(2,1)S(1)}, u32[]{:S(2)}, u32[]{:S(2)}) collective-permute-start(bf16[336,128]{1,0:T(8,128)(2,1)S(1)} %get-tuple-element.85), channel_id=1, source_target_pairs={{2,0},{3,1},{4,2},{5,3},{6,4},{7,5},{0,6},{1,7},{10,8},{11,9},{12,... | collective-permute-start | bytes 258056 | tf_op jit(solution)/shard_map/ppermute | solution.py:69
  116.1 6.2 %collective-permute-done.21.r2 = bf16[336,128]{1,0:T(8,128)(2,1)S(1)} collective-permute-done((bf16[336,128]{1,0:T(8,128)(2,1)S(1)}, bf16[336,128]{1,0:T(8,128)(2,1)S(1)}, u32[]{:S(2)}, u32[]{:S(2)}) %collective-permute-start.21) | collective-permute-done | bytes 86048 | tf_op jit(solution)/shard_map/ppermute | solution.py:69
  (100 shorter events, 29.1 us)
Async XLA Ops:
  3.5 27.4 %all-to-all-start = ((bf16[16,128,128]{2,1,0:T(8,128)(2,1)}), bf16[16,128,128]{2,1,0:T(8,128)(2,1)S(1)}, u32[]{:S(2)}, u32[]{:S(2)}) async-start(bf16[16,128,128]{2,1,0:T(8,128)(2,1)} %get-tuple-element.46), calls=%async_computation | async-start | bytes 1048576 | tf_op jit(solution)/shard_map/all_to_all | solution.py:489
  35.3 39.1 %all-to-all-start.1 = ((bf16[8,640,128]{2,1,0:T(8,128)(2,1)}), bf16[8,640,128]{2,1,0:T(8,128)(2,1)S(1)}, u32[]{:S(2)}, u32[]{:S(2)}) async-start(bf16[8,640,128]{2,1,0:T(8,128)(2,1)} %broadcast_in_dim.21), calls=%async_computation.1 | async-start | bytes 2621440 | tf_op jit(solution)/shard_map/all_to_all | solution.py:514
  40.6 8.8 %collective-permute-start.11 = (bf16[224,512]{1,0:T(8,128)(2,1)}, bf16[224,512]{1,0:T(8,128)(2,1)S(1)}, u32[]{:S(2)}, u32[]{:S(2)}) collective-permute-start(bf16[224,512]{1,0:T(8,128)(2,1)} %get-tuple-element.61.rest_8_), channel_id=1, source_target_pairs={{128,0},{144,16},{160,32},{176,48},{192,64},{208,80},{224,96},{240... | collective-permute-start | bytes 688136 | tf_op jit(solution)/shard_map/ppermute | solution.py:45
  41.3 15.4 %collective-permute-start.9 = (bf16[224,512]{1,0:T(8,128)(2,1)}, bf16[224,512]{1,0:T(8,128)(2,1)}, u32[]{:S(2)}, u32[]{:S(2)}) collective-permute-start(bf16[224,512]{1,0:T(8,128)(2,1)} %get-tuple-element.61.rest_8_), channel_id=1, source_target_pairs={{96,0},{112,16},{0,32},{16,48},{32,64},{48,80},{64,96},{80,112},{2... | collective-permute-start | bytes 688136 | tf_op jit(solution)/shard_map/ppermute | solution.py:45
  42.9 15.1 %collective-permute-start.8 = (bf16[224,512]{1,0:T(8,128)(2,1)}, bf16[224,512]{1,0:T(8,128)(2,1)}, u32[]{:S(2)}, u32[]{:S(2)}) collective-permute-start(bf16[224,512]{1,0:T(8,128)(2,1)} %get-tuple-element.61.rest_8_), channel_id=1, source_target_pairs={{32,0},{48,16},{64,32},{80,48},{96,64},{112,80},{0,96},{16,112},{1... | collective-permute-start | bytes 688136 | tf_op jit(solution)/shard_map/ppermute | solution.py:45
  44.5 15.2 %collective-permute-start.4 = (bf16[256,512]{1,0:T(8,128)(2,1)S(1)}, bf16[256,512]{1,0:T(8,128)(2,1)S(1)}, u32[]{:S(2)}, u32[]{:S(2)}) collective-permute-start(bf16[256,512]{1,0:T(8,128)(2,1)S(1)} %copy-done.4), channel_id=1, source_target_pairs={{128,0},{144,16},{160,32},{176,48},{192,64},{208,80},{224,96},{240... | collective-permute-start | bytes 786440 | tf_op jit(solution)/shard_map/ppermute | solution.py:45
  46.0 8.4 %collective-permute-start.1 = (bf16[256,512]{1,0:T(8,128)(2,1)S(1)}, bf16[256,512]{1,0:T(8,128)(2,1)S(1)}, u32[]{:S(2)}, u32[]{:S(2)}) collective-permute-start(bf16[256,512]{1,0:T(8,128)(2,1)S(1)} %copy-done.4), channel_id=1, source_target_pairs={{32,0},{48,16},{64,32},{80,48},{96,64},{112,80},{0,96},{16,112},{1... | collective-permute-start | bytes 786440 | tf_op jit(solution)/shard_map/ppermute | solution.py:45
  49.4 11.2 %collective-permute-start.3 = (bf16[256,512]{1,0:T(8,128)(2,1)S(1)}, bf16[256,512]{1,0:T(8,128)(2,1)S(1)}, u32[]{:S(2)}, u32[]{:S(2)}) collective-permute-start(bf16[256,512]{1,0:T(8,128)(2,1)S(1)} %copy-done.4), channel_id=1, source_target_pairs={{96,0},{112,16},{0,32},{16,48},{32,64},{48,80},{64,96},{80,112},{2... | collective-permute-start | bytes 786440 | tf_op jit(solution)/shard_map/ppermute | solution.py:45
  54.4 13.5 %collective-permute-start.2 = (bf16[256,512]{1,0:T(8,128)(2,1)S(1)}, bf16[256,512]{1,0:T(8,128)(2,1)S(1)}, u32[]{:S(2)}, u32[]{:S(2)}) collective-permute-start(bf16[256,512]{1,0:T(8,128)(2,1)S(1)} %collective-permute-done.1.rest_1_), channel_id=1, source_target_pairs={{32,0},{48,16},{64,32},{80,48},{96,64},{112,80},{0,96},{16,112},{1... | collective-permute-start | bytes 786440 | tf_op jit(solution)/shard_map/ppermute | solution.py:45
  56.7 7.6 %collective-permute-start.12 = (bf16[224,512]{1,0:T(8,128)(2,1)S(1)}, bf16[224,512]{1,0:T(8,128)(2,1)}, u32[]{:S(2)}, u32[]{:S(2)}) collective-permute-start(bf16[224,512]{1,0:T(8,128)(2,1)S(1)} %collective-permute-done.11.rest_12_), channel_id=1, source_target_pairs={{32,0},{48,16},{64,32},{80,48},{96,64},{112,80},{0,96},{16,112},{1... | collective-permute-start | bytes 688136 | tf_op jit(solution)/shard_map/ppermute | solution.py:45
  58.0 8.0 %collective-permute-start.14 = (bf16[224,512]{1,0:T(8,128)(2,1)}, bf16[224,512]{1,0:T(8,128)(2,1)S(1)}, u32[]{:S(2)}, u32[]{:S(2)}) collective-permute-start(bf16[224,512]{1,0:T(8,128)(2,1)} %collective-permute-done.9.rest_11_), channel_id=1, source_target_pairs={{128,0},{144,16},{160,32},{176,48},{192,64},{208,80},{224,96},{240... | collective-permute-start | bytes 688136 | tf_op jit(solution)/shard_map/ppermute | solution.py:45
  59.7 11.9 %collective-permute-start.10 = (bf16[224,512]{1,0:T(8,128)(2,1)}, bf16[224,512]{1,0:T(8,128)(2,1)}, u32[]{:S(2)}, u32[]{:S(2)}) collective-permute-start(bf16[224,512]{1,0:T(8,128)(2,1)} %collective-permute-done.9.rest_11_), channel_id=1, source_target_pairs={{96,0},{112,16},{0,32},{16,48},{32,64},{48,80},{64,96},{80,112},{2... | collective-permute-start | bytes 688136 | tf_op jit(solution)/shard_map/ppermute | solution.py:45
  60.6 11.9 %collective-permute-start.5 = (bf16[256,512]{1,0:T(8,128)(2,1)S(1)}, bf16[256,512]{1,0:T(8,128)(2,1)}, u32[]{:S(2)}, u32[]{:S(2)}) collective-permute-start(bf16[256,512]{1,0:T(8,128)(2,1)S(1)} %collective-permute-done.1.rest_1_), channel_id=1, source_target_pairs={{128,0},{144,16},{160,32},{176,48},{192,64},{208,80},{224,96},{240... | collective-permute-start | bytes 786440 | tf_op jit(solution)/shard_map/ppermute | solution.py:45
  64.4 8.1 %collective-permute-start.7 = (bf16[256,512]{1,0:T(8,128)(2,1)S(1)}, bf16[256,512]{1,0:T(8,128)(2,1)}, u32[]{:S(2)}, u32[]{:S(2)}) collective-permute-start(bf16[256,512]{1,0:T(8,128)(2,1)S(1)} %collective-permute-done.4.rest_4_), channel_id=1, source_target_pairs={{96,0},{112,16},{0,32},{16,48},{32,64},{48,80},{64,96},{80,112},{2... | collective-permute-start | bytes 786440 | tf_op jit(solution)/shard_map/ppermute | solution.py:45
  89.5 8.8 %collective-permute-start.18 = (bf16[2,336,128]{2,1,0:T(8,128)(2,1)S(1)}, bf16[2,336,128]{2,1,0:T(8,128)(2,1)S(1)}, u32[]{:S(2)}, u32[]{:S(2)}) collective-permute-start(bf16[2,336,128]{2,1,0:T(8,128)(2,1)S(1)} %get-tuple-element.73), channel_id=1, source_target_pairs={{8,0},{9,1},{10,2},{11,3},{12,4},{13,5},{14,6},{15,7},{0,8},{1,9},... | collective-permute-start | bytes 516104 | tf_op jit(solution)/shard_map/ppermute | solution.py:69
  92.5 9.5 %collective-permute-start.19 = (bf16[2,336,128]{2,1,0:T(8,128)(2,1)S(1)}, bf16[2,336,128]{2,1,0:T(8,128)(2,1)S(1)}, u32[]{:S(2)}, u32[]{:S(2)}) collective-permute-start(bf16[2,336,128]{2,1,0:T(8,128)(2,1)S(1)} %get-tuple-element.76), channel_id=1, source_target_pairs={{8,0},{9,1},{10,2},{11,3},{12,4},{13,5},{14,6},{15,7},{0,8},{1,9},... | collective-permute-start | bytes 516104 | tf_op jit(solution)/shard_map/ppermute | solution.py:69
  93.1 14.1 %collective-permute-start.22 = (bf16[2,336,128]{2,1,0:T(8,128)(2,1)S(1)}, bf16[2,336,128]{2,1,0:T(8,128)(2,1)S(1)}, u32[]{:S(2)}, u32[]{:S(2)}) collective-permute-start(bf16[2,336,128]{2,1,0:T(8,128)(2,1)S(1)} %get-tuple-element.80), channel_id=1, source_target_pairs={{8,0},{9,1},{10,2},{11,3},{12,4},{13,5},{14,6},{15,7},{0,8},{1,9},... | collective-permute-start | bytes 516104 | tf_op jit(solution)/shard_map/ppermute | solution.py:69
  96.0 15.8 %collective-permute-start.25 = (bf16[2,336,128]{2,1,0:T(8,128)(2,1)S(1)}, bf16[2,336,128]{2,1,0:T(8,128)(2,1)S(1)}, u32[]{:S(2)}, u32[]{:S(2)}) collective-permute-start(bf16[2,336,128]{2,1,0:T(8,128)(2,1)S(1)} %get-tuple-element.84), channel_id=1, source_target_pairs={{8,0},{9,1},{10,2},{11,3},{12,4},{13,5},{14,6},{15,7},{0,8},{1,9},... | collective-permute-start | bytes 516104 | tf_op jit(solution)/shard_map/ppermute | solution.py:69
  98.4 13.5 %collective-permute-start.28 = (bf16[336,128]{1,0:T(8,128)(2,1)S(1)}, bf16[336,128]{1,0:T(8,128)(2,1)S(1)}, u32[]{:S(2)}, u32[]{:S(2)}) collective-permute-start(bf16[336,128]{1,0:T(8,128)(2,1)S(1)} %get-tuple-element.87), channel_id=1, source_target_pairs={{1,0},{2,1},{3,2},{4,3},{5,4},{6,5},{7,6},{0,7},{9,8},{10,9},{11,1... | collective-permute-start | bytes 258056 | tf_op jit(solution)/shard_map/ppermute | solution.py:69
  102.1 14.0 %collective-permute-start.20 = (bf16[336,128]{1,0:T(8,128)(2,1)S(1)}, bf16[336,128]{1,0:T(8,128)(2,1)S(1)}, u32[]{:S(2)}, u32[]{:S(2)}) collective-permute-start(bf16[336,128]{1,0:T(8,128)(2,1)S(1)} %get-tuple-element.77), channel_id=1, source_target_pairs={{5,0},{6,1},{7,2},{0,3},{1,4},{2,5},{3,6},{4,7},{13,8},{14,9},{15,... | collective-permute-start | bytes 258056 | tf_op jit(solution)/shard_map/ppermute | solution.py:69
  106.6 15.7 %collective-permute-start.21 = (bf16[336,128]{1,0:T(8,128)(2,1)S(1)}, bf16[336,128]{1,0:T(8,128)(2,1)S(1)}, u32[]{:S(2)}, u32[]{:S(2)}) collective-permute-start(bf16[336,128]{1,0:T(8,128)(2,1)S(1)} %get-tuple-element.78), channel_id=1, source_target_pairs={{3,0},{4,1},{5,2},{6,3},{7,4},{0,5},{1,6},{2,7},{11,8},{12,9},{13,... | collective-permute-start | bytes 258056 | tf_op jit(solution)/shard_map/ppermute | solution.py:69
  107.2 15.0 %collective-permute-start.23 = (bf16[336,128]{1,0:T(8,128)(2,1)S(1)}, bf16[336,128]{1,0:T(8,128)(2,1)S(1)}, u32[]{:S(2)}, u32[]{:S(2)}) collective-permute-start(bf16[336,128]{1,0:T(8,128)(2,1)S(1)} %get-tuple-element.81), channel_id=1, source_target_pairs={{4,0},{5,1},{6,2},{7,3},{0,4},{1,5},{2,6},{3,7},{12,8},{13,9},{14,... | collective-permute-start | bytes 258056 | tf_op jit(solution)/shard_map/ppermute | solution.py:69
  111.8 10.5 %collective-permute-start.24 = (bf16[336,128]{1,0:T(8,128)(2,1)S(1)}, bf16[336,128]{1,0:T(8,128)(2,1)S(1)}, u32[]{:S(2)}, u32[]{:S(2)}) collective-permute-start(bf16[336,128]{1,0:T(8,128)(2,1)S(1)} %get-tuple-element.82), channel_id=1, source_target_pairs={{6,0},{7,1},{0,2},{1,3},{2,4},{3,5},{4,6},{5,7},{14,8},{15,9},{8,1... | collective-permute-start | bytes 258056 | tf_op jit(solution)/shard_map/ppermute | solution.py:69
  111.9 10.4 %collective-permute-start.26 = (bf16[336,128]{1,0:T(8,128)(2,1)S(1)}, bf16[336,128]{1,0:T(8,128)(2,1)S(1)}, u32[]{:S(2)}, u32[]{:S(2)}) collective-permute-start(bf16[336,128]{1,0:T(8,128)(2,1)S(1)} %get-tuple-element.85), channel_id=1, source_target_pairs={{2,0},{3,1},{4,2},{5,3},{6,4},{7,5},{0,6},{1,7},{10,8},{11,9},{12,... | collective-permute-start | bytes 258056 | tf_op jit(solution)/shard_map/ppermute | solution.py:69
  (24 other events, 253.7 us)

commit v8 on v7

--- a/solution.py
+++ b/solution.py
@@ -122,6 +122,15 @@
             for c, item in enumerate(pieces):
                 buf[CUT * c : CUT * (c + 1), :] = item
             out[dest] = buf[...].astype(BF16)
+
+
+def spread_kernel(turned, across, out, pair, sems):
+    pair[0:OWN, :] = turned[...]
+    pair[OWN:, :] = across[...]
+    copies = [pltpu.make_async_copy(pair, out.at[z], sems.at[z]) for z in range(8)]
+    start_all(copies)
+    for copy in copies:
+        copy.wait()
 
 
 def refresh_kernel(
@@ -487,8 +496,15 @@
     )
     across = along_shard(turned, 1, 0)
     arrived = lax.all_to_all(packed, "shard", split_axis=0, concat_axis=0, tiled=False)
-    spread = jnp.concatenate([turned, across], axis=0)
-    spread = jnp.broadcast_to(spread[None], (8, 2 * OWN, TOKENS))
+    spread = call(
+        spread_kernel,
+        "spread",
+        shape((8, 2 * OWN, TOKENS), BF16),
+        [whole(OWN, TOKENS)] * 2,
+        [VMEM((2 * OWN, TOKENS), BF16), dma((8,))],
+        True,
+        mib=24,
+    )(turned, across)
     arrived, spread, lengths, stale_rows, stale_steps, stale_back = lax.optimization_barrier(
         (arrived, spread, lengths, stale_rows, stale_steps, stale_back)
     )
@@ -508,7 +524,6 @@
         ],
         mib=56,
     )(here, arrived, base_query, base_key, base_value, base_output)
-    upper, lower, spread = lax.optimization_barrier((upper, lower, spread))
     uppers, lowers = gather_blocks(upper, 1), gather_blocks(lower, -1)
     rings = [[8 * x + z for z in range(8)] for x in range(2)]
     hidden_t = lax.all_to_all(
@@ -646,8 +661,9 @@
         mib=24,
     )(here, seat, own, other, table, marks, cache, values, keys, one_q, one_f, old, mine, theirs)
     crossed = [along_shard(give, 1, 0) for give in parts[:4]]
-    landed = []
+    landed, sums = [], parts[4:5]
     for trips, keep_part, recv in zip(TRIPS, parts[4:], crossed):
+        keep_part, _ = lax.optimization_barrier((keep_part, tuple(sums)))
         kinds = tuple(shape((SENT, HEAD), BF16 if dz else F32) for dz in trips)
         sums = call(
             merge_kernel, "merge", kinds, [whole(2, SENT, HEAD)] * 2, [], mib=8

time: 124 us -> 124 us (level)
    unnamed x34 -> x38, local copies, waits for them, and re-layouts: 0.08 us -> 2.47 us
    ppermute x12, waiting for transfers between devices: 14.7 us -> 16 us  [along_shard(): return lax.ppermute(value, 'shard', pairs)]
    broadcast_in_dim x1 -> x0, local copies, waits for them, and re-layouts: 1.26 us -> none  [local(): spread = jnp.broadcast_to(spread[None], (8, 2 * OWN, TOKENS))]
  transfers between devices with their start and end apart: 31 -> 31, of which waited for: 11 -> 13; matrix products, arithmetic and copies ran while one was open for 3% -> 2% of each run, Pallas kernels for 4% -> 7%
where the time goes in v8:
time: 124 us; the launch traced here: 123 us
  starting transfers between devices  60.3 us (49%)
  waiting for transfers between devices  36.5 us (29%)
  Pallas kernels  20.5 us (17%)
  local copies, waits for them, and re-layouts  3.66 us (3%)
  other arithmetic  1.34 us (1%)
    ppermute x12, starting transfers between devices, along_shard(): return lax.ppermute(value, 'shard', pairs)  23.7 us
    ppermute x17, starting transfers between devices, fetch(): return lax.ppermute(value, 'replica', pairs)  20.5 us
    ppermute x12, waiting for transfers between devices, along_shard(): return lax.ppermute(value, 'shard', pairs)  16 us
    ppermute x17, waiting for transfers between devices, fetch(): return lax.ppermute(value, 'replica', pairs)  12.9 us
    all_to_all x1, starting transfers between devices, local(): lax.all_to_all(packed, 'shard', split_axis=0, concat_axis=0, tiled=False)  11.1 us
    all_to_all x1, waiting for transfers between devices, local(): lax.all_to_all(packed, 'shard', split_axis=0, concat_axis=0, tiled=False)  7.57 us
    all_to_all x1, starting transfers between devices, local(): lax.all_to_all(spread, 'shard', split_axis=0, concat_axis=0, tiled=False,...  5.01 us
    pallas_call x1, Pallas kernels, local(): call(old_kernel, 'old', shape((2, TOKENS, HEAD), F32), scalars() + [whole...  4.11 us
  transfers between devices with their start and end apart: 31, of which 13 were waited for; matrix products, arithmetic and copies ran while one was open for 2% of the time, Pallas kernels for 7%

profile of v8, /device:TPU:32, one launch (start us, length us, event | category | flops | bytes accessed | tf_op | source)
XLA Modules:
  0.0 123.2 jit_solution(9742551002161892461)
XLA Ops:
  0.6 2.8 %pack.1 = (bf16[16,128,128]{2,1,0:T(8,128)(2,1)}, bf16[320,128]{1,0:T(8,128)(2,1)}) custom-call(bf16[128,320]{1,0:T(8,128)(2,1)} %bitcast.29, bf16[20,4096]{1,0:T(8,128)(2,1)} %dq.1, bf16[20,1024]{1,0:T(8,128)(2,1)} %dk.1, bf16[20,1024]{1,0:T(8,128)(2,1)} %dv.1, bf16[20,4096]{1,0:T(8,128)(2,1)} %do.1, s32[20,32]{1,0:T(8,128)} %sq.1, s32[20,32]{1,0:T(8,128)} %so.1, ...), custom_call_target="tpu_custom_call" | custom-call | tf_op jit(solution)/shard_map/pack/pallas_call | solution.py:474
  3.5 11.1 %all-to-all-start = ((bf16[16,128,128]{2,1,0:T(8,128)(2,1)}), bf16[16,128,128]{2,1,0:T(8,128)(2,1)S(1)}, u32[]{:S(2)}, u32[]{:S(2)}) async-start(bf16[16,128,128]{2,1,0:T(8,128)(2,1)} %get-tuple-element.46), calls=%async_computation | async-start | bytes 1048576 | tf_op jit(solution)/shard_map/all_to_all | solution.py:498
  14.5 3.0 %collective-permute-start = (bf16[320,128]{1,0:T(8,128)(2,1)}, bf16[320,128]{1,0:T(8,128)(2,1)S(1)}, u32[]{:S(2)}, u32[]{:S(2)}) collective-permute-start(bf16[320,128]{1,0:T(8,128)(2,1)} %get-tuple-element.47.turned), channel_id=1, source_target_pairs={{8,0},{9,1},{10,2},{11,3},{12,4},{13,5},{14,6},{15,7},{0,8},{1,9},... | collective-permute-start | bytes 245768 | tf_op jit(solution)/shard_map/ppermute | solution.py:69
  17.5 3.7 %collective-permute-done.across = bf16[320,128]{1,0:T(8,128)(2,1)S(1)} collective-permute-done((bf16[320,128]{1,0:T(8,128)(2,1)}, bf16[320,128]{1,0:T(8,128)(2,1)S(1)}, u32[]{:S(2)}, u32[]{:S(2)}) %collective-permute-start) | collective-permute-done | bytes 81952 | tf_op jit(solution)/shard_map/ppermute | solution.py:69
  23.3 7.6 %all-to-all-done.recv = bf16[16,128,128]{2,1,0:T(8,128)(2,1)S(1)} async-done(((bf16[16,128,128]{2,1,0:T(8,128)(2,1)}), bf16[16,128,128]{2,1,0:T(8,128)(2,1)S(1)}, u32[]{:S(2)}, u32[]{:S(2)}) %all-to-all-start) | async-done | bytes 524320 | tf_op jit(solution)/shard_map/all_to_all | solution.py:498
  31.7 5.0 %all-to-all-start.1 = ((bf16[8,640,128]{2,1,0:T(8,128)(2,1)}), bf16[8,640,128]{2,1,0:T(8,128)(2,1)S(1)}, u32[]{:S(2)}, u32[]{:S(2)}) async-start(bf16[8,640,128]{2,1,0:T(8,128)(2,1)} %spread.1), calls=%async_computation.1 | async-start | bytes 2621440 | tf_op jit(solution)/shard_map/all_to_all | solution.py:529
  37.0 3.0 %refresh.1 = (bf16[256,512]{1,0:T(8,128)(2,1)}, bf16[224,512]{1,0:T(8,128)(2,1)}) custom-call(s32[1]{0:T(128)} %bitcast.here, bf16[16,128,128]{2,1,0:T(8,128)(2,1)} %copy-done.11, bf16[5120,256]{1,0:T(8,128)(2,1)} %base_q.1, bf16[5120,128]{1,0:T(8,128)(2,1)} %base_k.1, bf16[5120,128]{1,0:T(8,128)(2,1)} %bv.1, bf16[5120,256]{1,0:T(8,128)(2,1)} %bo.1), custom_call_target="tpu_custom_call" | custom-call | tf_op jit(solution)/shard_map/refresh/pallas_call | solution.py:511
  45.4 1.8 %collective-permute-start.1 = (bf16[256,512]{1,0:T(8,128)(2,1)}, bf16[256,512]{1,0:T(8,128)(2,1)S(1)}, u32[]{:S(2)}, u32[]{:S(2)}) collective-permute-start(bf16[256,512]{1,0:T(8,128)(2,1)} %get-tuple-element.57.rest_0_), channel_id=1, source_target_pairs={{32,0},{48,16},{64,32},{80,48},{96,64},{112,80},{0,96},{16,112},{1... | collective-permute-start | bytes 786440 | tf_op jit(solution)/shard_map/ppermute | solution.py:45
  50.4 3.4 %collective-permute-done.1.rest_1_ = bf16[256,512]{1,0:T(8,128)(2,1)S(1)} collective-permute-done((bf16[256,512]{1,0:T(8,128)(2,1)}, bf16[256,512]{1,0:T(8,128)(2,1)S(1)}, u32[]{:S(2)}, u32[]{:S(2)}) %collective-permute-start.1) | collective-permute-done | bytes 262176 | tf_op jit(solution)/shard_map/ppermute | solution.py:45
  53.8 2.4 %collective-permute-start.2 = (bf16[256,512]{1,0:T(8,128)(2,1)S(1)}, bf16[256,512]{1,0:T(8,128)(2,1)S(1)}, u32[]{:S(2)}, u32[]{:S(2)}) collective-permute-start(bf16[256,512]{1,0:T(8,128)(2,1)S(1)} %collective-permute-done.1.rest_1_), channel_id=1, source_target_pairs={{32,0},{48,16},{64,32},{80,48},{96,64},{112,80},{0,96},{16,112},{1... | collective-permute-start | bytes 786440 | tf_op jit(solution)/shard_map/ppermute | solution.py:45
  61.5 2.7 %collective-permute-done.12.rest_13_ = bf16[224,512]{1,0:T(8,128)(2,1)} collective-permute-done((bf16[224,512]{1,0:T(8,128)(2,1)}, bf16[224,512]{1,0:T(8,128)(2,1)}, u32[]{:S(2)}, u32[]{:S(2)}) %collective-permute-start.12) | collective-permute-done | bytes 229408 | tf_op jit(solution)/shard_map/ppermute | solution.py:45
  65.3 2.3 %collective-permute-start.13 = (bf16[224,512]{1,0:T(8,128)(2,1)}, bf16[224,512]{1,0:T(8,128)(2,1)}, u32[]{:S(2)}, u32[]{:S(2)}) collective-permute-start(bf16[224,512]{1,0:T(8,128)(2,1)} %collective-permute-done.12.rest_13_), channel_id=1, source_target_pairs={{32,0},{48,16},{64,32},{80,48},{96,64},{112,80},{0,96},{16,112},{1... | collective-permute-start | bytes 688136 | tf_op jit(solution)/shard_map/ppermute | solution.py:45
  74.1 1.7 %normalise.1 = (bf16[8,128,384]{2,1,0:T(8,128)(2,1)S(1)}, bf16[8,128,384]{2,1,0:T(8,128)(2,1)S(1)}) custom-call(s32[1]{0:T(128)} %bitcast.here, s32[1]{0:T(128)} %bitcast.1.seat, f32[16,1,320]{2,1,0:T(1,128)S(1)} %reshape.58.gain, bf16[8,640,128]{2,1,0:T(8,128)(2,1)S(1)} %all-to-all-done.1.pairs), custom_call_target="tpu_custom_call" | custom-call | tf_op jit(solution)/shard_map/normalise/pallas_call | solution.py:591
  75.9 2.3 %collective-permute-done.15.given = bf16[8,128,384]{2,1,0:T(8,128)(2,1)S(1)} collective-permute-done((bf16[8,128,384]{2,1,0:T(8,128)(2,1)S(1)}, bf16[8,128,384]{2,1,0:T(8,128)(2,1)S(1)}, u32[]{:S(2)}, u32[]{:S(2)}) %collective-permute-start.15) | collective-permute-done | bytes 786464 | tf_op jit(solution)/shard_map/ppermute | solution.py:45
  78.2 2.9 %project.1 = (f32[128,512]{1,0:T(8,128)S(1)}, f32[128,512]{1,0:T(8,128)S(1)}, bf16[8,160,512]{2,1,0:T(8,128)(2,1)S(1)}) custom-call(s32[1]{0:T(128)} %bitcast.here, bf16[8,128,384]{2,1,0:T(8,128)(2,1)S(1)} %get-tuple-element.60.keep, bf16[8,128,384]{2,1,0:T(8,128)(2,1)S(1)} %collective-permute-done.15.given, bf16[256,512]{1,0:T(8,128)(2,1)S(1)} %copy-done.4, ...), custom_call_target="tpu_custom_call" | custom-call | tf_op jit(solution)/shard_map/project/pallas_call | solution.py:624
  81.7 4.1 %old.1 = f32[2,128,128]{2,1,0:T(8,128)S(1)} custom-call(s32[1]{0:T(128)} %bitcast.here, bf16[8,128,384]{2,1,0:T(8,128)(2,1)S(1)} %get-tuple-element.60.keep, bf16[8,128,384]{2,1,0:T(8,128)(2,1)S(1)} %get-tuple-element.61.give, f32[264,128]{1,0:T(8,128)S(1)} %concatenate.15.table, s32[40,128]{1,0:T(8,128)S(1)} %add_add_fusion.marks, ...), custom_call_target="tpu_custom_call" | custom-call | tf_op jit(solution)/shard_map/old/pallas_call | solution.py:604
  85.9 3.3 %attend.1 = (bf16[2,336,128]{2,1,0:T(8,128)(2,1)S(1)}, bf16[2,336,128]{2,1,0:T(8,128)(2,1)S(1)}, bf16[2,336,128]{2,1,0:T(8,128)(2,1)S(1)}, bf16[2,336,128]{2,1,0...) custom-call(s32[1]{0:T(128)} %bitcast.here, ...), custom_call_target="tpu_custom_call" | custom-call | tf_op jit(solution)/shard_map/attend/pallas_call | solution.py:642
  89.2 2.6 %collective-permute-start.18 = (bf16[2,336,128]{2,1,0:T(8,128)(2,1)S(1)}, bf16[2,336,128]{2,1,0:T(8,128)(2,1)S(1)}, u32[]{:S(2)}, u32[]{:S(2)}) collective-permute-start(bf16[2,336,128]{2,1,0:T(8,128)(2,1)S(1)} %get-tuple-element.73), channel_id=1, source_target_pairs={{8,0},{9,1},{10,2},{11,3},{12,4},{13,5},{14,6},{15,7},{0,8},{1,9},... | collective-permute-start | bytes 516104 | tf_op jit(solution)/shard_map/ppermute | solution.py:69
  92.8 2.5 %collective-permute-start.20 = (bf16[2,336,128]{2,1,0:T(8,128)(2,1)S(1)}, bf16[2,336,128]{2,1,0:T(8,128)(2,1)S(1)}, u32[]{:S(2)}, u32[]{:S(2)}) collective-permute-start(bf16[2,336,128]{2,1,0:T(8,128)(2,1)S(1)} %get-tuple-element.81), channel_id=1, source_target_pairs={{8,0},{9,1},{10,2},{11,3},{12,4},{13,5},{14,6},{15,7},{0,8},{1,9},... | collective-permute-start | bytes 516104 | tf_op jit(solution)/shard_map/ppermute | solution.py:69
  98.0 4.5 %collective-permute-start.22 = (bf16[336,128]{1,0:T(8,128)(2,1)S(1)}, bf16[336,128]{1,0:T(8,128)(2,1)S(1)}, u32[]{:S(2)}, u32[]{:S(2)}) collective-permute-start(bf16[336,128]{1,0:T(8,128)(2,1)S(1)} %get-tuple-element.74), channel_id=1, source_target_pairs={{5,0},{6,1},{7,2},{0,3},{1,4},{2,5},{3,6},{4,7},{13,8},{14,9},{15,... | collective-permute-start | bytes 258056 | tf_op jit(solution)/shard_map/ppermute | solution.py:69
  103.2 4.6 %collective-permute-start.24 = (bf16[336,128]{1,0:T(8,128)(2,1)S(1)}, bf16[336,128]{1,0:T(8,128)(2,1)S(1)}, u32[]{:S(2)}, u32[]{:S(2)}) collective-permute-start(bf16[336,128]{1,0:T(8,128)(2,1)S(1)} %get-tuple-element.78), channel_id=1, source_target_pairs={{4,0},{5,1},{6,2},{7,3},{0,4},{1,5},{2,6},{3,7},{12,8},{13,9},{14,... | collective-permute-start | bytes 258056 | tf_op jit(solution)/shard_map/ppermute | solution.py:69
  108.2 3.8 %collective-permute-start.26 = (bf16[336,128]{1,0:T(8,128)(2,1)S(1)}, bf16[336,128]{1,0:T(8,128)(2,1)S(1)}, u32[]{:S(2)}, u32[]{:S(2)}) collective-permute-start(bf16[336,128]{1,0:T(8,128)(2,1)S(1)} %get-tuple-element.82), channel_id=1, source_target_pairs={{2,0},{3,1},{4,2},{5,3},{6,4},{7,5},{0,6},{1,7},{10,8},{11,9},{12,... | collective-permute-start | bytes 258056 | tf_op jit(solution)/shard_map/ppermute | solution.py:69
  112.2 5.7 %collective-permute-done.23.r2 = bf16[336,128]{1,0:T(8,128)(2,1)S(1)} collective-permute-done((bf16[336,128]{1,0:T(8,128)(2,1)S(1)}, bf16[336,128]{1,0:T(8,128)(2,1)S(1)}, u32[]{:S(2)}, u32[]{:S(2)}) %collective-permute-start.23) | collective-permute-done | bytes 86048 | tf_op jit(solution)/shard_map/ppermute | solution.py:69
  118.5 3.9 %collective-permute-done.28.r7 = bf16[336,128]{1,0:T(8,128)(2,1)S(1)} collective-permute-done((bf16[336,128]{1,0:T(8,128)(2,1)S(1)}, bf16[336,128]{1,0:T(8,128)(2,1)S(1)}, u32[]{:S(2)}, u32[]{:S(2)}) %collective-permute-start.28) | collective-permute-done | bytes 86048 | tf_op jit(solution)/shard_map/ppermute | solution.py:69
  (103 shorter events, 31.6 us)
Async XLA Ops:
  3.5 27.4 %all-to-all-start = ((bf16[16,128,128]{2,1,0:T(8,128)(2,1)}), bf16[16,128,128]{2,1,0:T(8,128)(2,1)S(1)}, u32[]{:S(2)}, u32[]{:S(2)}) async-start(bf16[16,128,128]{2,1,0:T(8,128)(2,1)} %get-tuple-element.46), calls=%async_computation | async-start | bytes 1048576 | tf_op jit(solution)/shard_map/all_to_all | solution.py:498
  31.7 42.4 %all-to-all-start.1 = ((bf16[8,640,128]{2,1,0:T(8,128)(2,1)}), bf16[8,640,128]{2,1,0:T(8,128)(2,1)S(1)}, u32[]{:S(2)}, u32[]{:S(2)}) async-start(bf16[8,640,128]{2,1,0:T(8,128)(2,1)} %spread.1), calls=%async_computation.1 | async-start | bytes 2621440 | tf_op jit(solution)/shard_map/all_to_all | solution.py:529
  40.0 8.8 %collective-permute-start.11 = (bf16[224,512]{1,0:T(8,128)(2,1)}, bf16[224,512]{1,0:T(8,128)(2,1)}, u32[]{:S(2)}, u32[]{:S(2)}) collective-permute-start(bf16[224,512]{1,0:T(8,128)(2,1)} %get-tuple-element.58.rest_8_), channel_id=1, source_target_pairs={{128,0},{144,16},{160,32},{176,48},{192,64},{208,80},{224,96},{240... | collective-permute-start | bytes 688136 | tf_op jit(solution)/shard_map/ppermute | solution.py:45
  40.7 15.6 %collective-permute-start.9 = (bf16[224,512]{1,0:T(8,128)(2,1)}, bf16[224,512]{1,0:T(8,128)(2,1)}, u32[]{:S(2)}, u32[]{:S(2)}) collective-permute-start(bf16[224,512]{1,0:T(8,128)(2,1)} %get-tuple-element.58.rest_8_), channel_id=1, source_target_pairs={{96,0},{112,16},{0,32},{16,48},{32,64},{48,80},{64,96},{80,112},{2... | collective-permute-start | bytes 688136 | tf_op jit(solution)/shard_map/ppermute | solution.py:45
  42.3 14.9 %collective-permute-start.8 = (bf16[224,512]{1,0:T(8,128)(2,1)}, bf16[224,512]{1,0:T(8,128)(2,1)S(1)}, u32[]{:S(2)}, u32[]{:S(2)}) collective-permute-start(bf16[224,512]{1,0:T(8,128)(2,1)} %get-tuple-element.58.rest_8_), channel_id=1, source_target_pairs={{32,0},{48,16},{64,32},{80,48},{96,64},{112,80},{0,96},{16,112},{1... | collective-permute-start | bytes 688136 | tf_op jit(solution)/shard_map/ppermute | solution.py:45
  44.0 16.0 %collective-permute-start.4 = (bf16[256,512]{1,0:T(8,128)(2,1)}, bf16[256,512]{1,0:T(8,128)(2,1)S(1)}, u32[]{:S(2)}, u32[]{:S(2)}) collective-permute-start(bf16[256,512]{1,0:T(8,128)(2,1)} %get-tuple-element.57.rest_0_), channel_id=1, source_target_pairs={{128,0},{144,16},{160,32},{176,48},{192,64},{208,80},{224,96},{240... | collective-permute-start | bytes 786440 | tf_op jit(solution)/shard_map/ppermute | solution.py:45
  45.4 8.4 %collective-permute-start.1 = (bf16[256,512]{1,0:T(8,128)(2,1)}, bf16[256,512]{1,0:T(8,128)(2,1)S(1)}, u32[]{:S(2)}, u32[]{:S(2)}) collective-permute-start(bf16[256,512]{1,0:T(8,128)(2,1)} %get-tuple-element.57.rest_0_), channel_id=1, source_target_pairs={{32,0},{48,16},{64,32},{80,48},{96,64},{112,80},{0,96},{16,112},{1... | collective-permute-start | bytes 786440 | tf_op jit(solution)/shard_map/ppermute | solution.py:45
  48.8 11.9 %collective-permute-start.3 = (bf16[256,512]{1,0:T(8,128)(2,1)}, bf16[256,512]{1,0:T(8,128)(2,1)S(1)}, u32[]{:S(2)}, u32[]{:S(2)}) collective-permute-start(bf16[256,512]{1,0:T(8,128)(2,1)} %get-tuple-element.57.rest_0_), channel_id=1, source_target_pairs={{96,0},{112,16},{0,32},{16,48},{32,64},{48,80},{64,96},{80,112},{2... | collective-permute-start | bytes 786440 | tf_op jit(solution)/shard_map/ppermute | solution.py:45
  53.8 13.8 %collective-permute-start.2 = (bf16[256,512]{1,0:T(8,128)(2,1)S(1)}, bf16[256,512]{1,0:T(8,128)(2,1)S(1)}, u32[]{:S(2)}, u32[]{:S(2)}) collective-permute-start(bf16[256,512]{1,0:T(8,128)(2,1)S(1)} %collective-permute-done.1.rest_1_), channel_id=1, source_target_pairs={{32,0},{48,16},{64,32},{80,48},{96,64},{112,80},{0,96},{16,112},{1... | collective-permute-start | bytes 786440 | tf_op jit(solution)/shard_map/ppermute | solution.py:45
  56.3 7.9 %collective-permute-start.12 = (bf16[224,512]{1,0:T(8,128)(2,1)}, bf16[224,512]{1,0:T(8,128)(2,1)}, u32[]{:S(2)}, u32[]{:S(2)}) collective-permute-start(bf16[224,512]{1,0:T(8,128)(2,1)} %collective-permute-done.11.rest_12_), channel_id=1, source_target_pairs={{32,0},{48,16},{64,32},{80,48},{96,64},{112,80},{0,96},{16,112},{1... | collective-permute-start | bytes 688136 | tf_op jit(solution)/shard_map/ppermute | solution.py:45
  57.9 7.4 %collective-permute-start.14 = (bf16[224,512]{1,0:T(8,128)(2,1)}, bf16[224,512]{1,0:T(8,128)(2,1)S(1)}, u32[]{:S(2)}, u32[]{:S(2)}) collective-permute-start(bf16[224,512]{1,0:T(8,128)(2,1)} %collective-permute-done.9.rest_11_), channel_id=1, source_target_pairs={{128,0},{144,16},{160,32},{176,48},{192,64},{208,80},{224,96},{240... | collective-permute-start | bytes 688136 | tf_op jit(solution)/shard_map/ppermute | solution.py:45
  59.9 11.0 %collective-permute-start.10 = (bf16[224,512]{1,0:T(8,128)(2,1)}, bf16[224,512]{1,0:T(8,128)(2,1)}, u32[]{:S(2)}, u32[]{:S(2)}) collective-permute-start(bf16[224,512]{1,0:T(8,128)(2,1)} %collective-permute-done.9.rest_11_), channel_id=1, source_target_pairs={{96,0},{112,16},{0,32},{16,48},{32,64},{48,80},{64,96},{80,112},{2... | collective-permute-start | bytes 688136 | tf_op jit(solution)/shard_map/ppermute | solution.py:45
  60.7 11.7 %collective-permute-start.5 = (bf16[256,512]{1,0:T(8,128)(2,1)S(1)}, bf16[256,512]{1,0:T(8,128)(2,1)}, u32[]{:S(2)}, u32[]{:S(2)}) collective-permute-start(bf16[256,512]{1,0:T(8,128)(2,1)S(1)} %collective-permute-done.1.rest_1_), channel_id=1, source_target_pairs={{128,0},{144,16},{160,32},{176,48},{192,64},{208,80},{224,96},{240... | collective-permute-start | bytes 786440 | tf_op jit(solution)/shard_map/ppermute | solution.py:45
  64.2 8.2 %collective-permute-start.7 = (bf16[256,512]{1,0:T(8,128)(2,1)S(1)}, bf16[256,512]{1,0:T(8,128)(2,1)}, u32[]{:S(2)}, u32[]{:S(2)}) collective-permute-start(bf16[256,512]{1,0:T(8,128)(2,1)S(1)} %collective-permute-done.4.rest_4_), channel_id=1, source_target_pairs={{96,0},{112,16},{0,32},{16,48},{32,64},{48,80},{64,96},{80,112},{2... | collective-permute-start | bytes 786440 | tf_op jit(solution)/shard_map/ppermute | solution.py:45
  65.3 7.1 %collective-permute-start.13 = (bf16[224,512]{1,0:T(8,128)(2,1)}, bf16[224,512]{1,0:T(8,128)(2,1)}, u32[]{:S(2)}, u32[]{:S(2)}) collective-permute-start(bf16[224,512]{1,0:T(8,128)(2,1)} %collective-permute-done.12.rest_13_), channel_id=1, source_target_pairs={{32,0},{48,16},{64,32},{80,48},{96,64},{112,80},{0,96},{16,112},{1... | collective-permute-start | bytes 688136 | tf_op jit(solution)/shard_map/ppermute | solution.py:45
  89.2 8.8 %collective-permute-start.18 = (bf16[2,336,128]{2,1,0:T(8,128)(2,1)S(1)}, bf16[2,336,128]{2,1,0:T(8,128)(2,1)S(1)}, u32[]{:S(2)}, u32[]{:S(2)}) collective-permute-start(bf16[2,336,128]{2,1,0:T(8,128)(2,1)S(1)} %get-tuple-element.73), channel_id=1, source_target_pairs={{8,0},{9,1},{10,2},{11,3},{12,4},{13,5},{14,6},{15,7},{0,8},{1,9},... | collective-permute-start | bytes 516104 | tf_op jit(solution)/shard_map/ppermute | solution.py:69
  91.8 11.4 %collective-permute-start.19 = (bf16[2,336,128]{2,1,0:T(8,128)(2,1)S(1)}, bf16[2,336,128]{2,1,0:T(8,128)(2,1)S(1)}, u32[]{:S(2)}, u32[]{:S(2)}) collective-permute-start(bf16[2,336,128]{2,1,0:T(8,128)(2,1)S(1)} %get-tuple-element.77), channel_id=1, source_target_pairs={{8,0},{9,1},{10,2},{11,3},{12,4},{13,5},{14,6},{15,7},{0,8},{1,9},... | collective-permute-start | bytes 516104 | tf_op jit(solution)/shard_map/ppermute | solution.py:69
  92.8 15.0 %collective-permute-start.20 = (bf16[2,336,128]{2,1,0:T(8,128)(2,1)S(1)}, bf16[2,336,128]{2,1,0:T(8,128)(2,1)S(1)}, u32[]{:S(2)}, u32[]{:S(2)}) collective-permute-start(bf16[2,336,128]{2,1,0:T(8,128)(2,1)S(1)} %get-tuple-element.81), channel_id=1, source_target_pairs={{8,0},{9,1},{10,2},{11,3},{12,4},{13,5},{14,6},{15,7},{0,8},{1,9},... | collective-permute-start | bytes 516104 | tf_op jit(solution)/shard_map/ppermute | solution.py:69
  95.3 12.9 %collective-permute-start.21 = (bf16[2,336,128]{2,1,0:T(8,128)(2,1)S(1)}, bf16[2,336,128]{2,1,0:T(8,128)(2,1)S(1)}, u32[]{:S(2)}, u32[]{:S(2)}) collective-permute-start(bf16[2,336,128]{2,1,0:T(8,128)(2,1)S(1)} %get-tuple-element.85), channel_id=1, source_target_pairs={{8,0},{9,1},{10,2},{11,3},{12,4},{13,5},{14,6},{15,7},{0,8},{1,9},... | collective-permute-start | bytes 516104 | tf_op jit(solution)/shard_map/ppermute | solution.py:69
  98.0 14.0 %collective-permute-start.22 = (bf16[336,128]{1,0:T(8,128)(2,1)S(1)}, bf16[336,128]{1,0:T(8,128)(2,1)S(1)}, u32[]{:S(2)}, u32[]{:S(2)}) collective-permute-start(bf16[336,128]{1,0:T(8,128)(2,1)S(1)} %get-tuple-element.74), channel_id=1, source_target_pairs={{5,0},{6,1},{7,2},{0,3},{1,4},{2,5},{3,6},{4,7},{13,8},{14,9},{15,... | collective-permute-start | bytes 258056 | tf_op jit(solution)/shard_map/ppermute | solution.py:69
  102.6 15.3 %collective-permute-start.23 = (bf16[336,128]{1,0:T(8,128)(2,1)S(1)}, bf16[336,128]{1,0:T(8,128)(2,1)S(1)}, u32[]{:S(2)}, u32[]{:S(2)}) collective-permute-start(bf16[336,128]{1,0:T(8,128)(2,1)S(1)} %get-tuple-element.75), channel_id=1, source_target_pairs={{3,0},{4,1},{5,2},{6,3},{7,4},{0,5},{1,6},{2,7},{11,8},{12,9},{13,... | collective-permute-start | bytes 258056 | tf_op jit(solution)/shard_map/ppermute | solution.py:69
  103.2 14.7 %collective-permute-start.24 = (bf16[336,128]{1,0:T(8,128)(2,1)S(1)}, bf16[336,128]{1,0:T(8,128)(2,1)S(1)}, u32[]{:S(2)}, u32[]{:S(2)}) collective-permute-start(bf16[336,128]{1,0:T(8,128)(2,1)S(1)} %get-tuple-element.78), channel_id=1, source_target_pairs={{4,0},{5,1},{6,2},{7,3},{0,4},{1,5},{2,6},{3,7},{12,8},{13,9},{14,... | collective-permute-start | bytes 258056 | tf_op jit(solution)/shard_map/ppermute | solution.py:69
  107.7 10.2 %collective-permute-start.25 = (bf16[336,128]{1,0:T(8,128)(2,1)S(1)}, bf16[336,128]{1,0:T(8,128)(2,1)S(1)}, u32[]{:S(2)}, u32[]{:S(2)}) collective-permute-start(bf16[336,128]{1,0:T(8,128)(2,1)S(1)} %get-tuple-element.79), channel_id=1, source_target_pairs={{6,0},{7,1},{0,2},{1,3},{2,4},{3,5},{4,6},{5,7},{14,8},{15,9},{8,1... | collective-permute-start | bytes 258056 | tf_op jit(solution)/shard_map/ppermute | solution.py:69
  108.2 10.3 %collective-permute-start.26 = (bf16[336,128]{1,0:T(8,128)(2,1)S(1)}, bf16[336,128]{1,0:T(8,128)(2,1)S(1)}, u32[]{:S(2)}, u32[]{:S(2)}) collective-permute-start(bf16[336,128]{1,0:T(8,128)(2,1)S(1)} %get-tuple-element.82), channel_id=1, source_target_pairs={{2,0},{3,1},{4,2},{5,3},{6,4},{7,5},{0,6},{1,7},{10,8},{11,9},{12,... | collective-permute-start | bytes 258056 | tf_op jit(solution)/shard_map/ppermute | solution.py:69
  (26 other events, 238.0 us)

commit v9 on v8

--- a/solution.py
+++ b/solution.py
@@ -16,6 +16,8 @@
 PARTS = 16
 OWN = WIDTH // PARTS
 CUT = 20
+FIRST = {"q": 0, "k": 32, "v": 40, "o": 48}
+TIDY = 32
 GROUP = 8
 GROUPS = ROWS // GROUP
 TAIL = 16
@@ -82,12 +84,12 @@
 
 
 def pack_kernel(
-    hidden, dq, dk, dv, do, sq, so, skt, svt,
+    hidden, codes, sq, so, skt, svt,
     out, turned,
-    vh, vq, vk, vv, vo, vsq, vso, vsk, vsv, buf, sems,
+    vh, rows, vsq, vso, vsk, vsv, buf, sems,
 ):
     pairs = [(hidden, vh), (sq, vsq), (so, vso), (skt, vsk), (svt, vsv)]
-    pairs += [(dq, vq), (dk, vk), (dv, vv), (do, vo)]
+    pairs.append((codes, rows))
     copies = [pltpu.make_async_copy(a, b, sems.at[i]) for i, (a, b) in enumerate(pairs)]
     start_all(copies)
     for copy in copies[:5]:
@@ -103,21 +105,22 @@
         return jnp.sum(spread, axis=1, keepdims=True)
 
     def piece(codes, head, factor):
-        return codes[:, head * HEAD : (head + 1) * HEAD].astype(F32) * factor
+        at = (FIRST[codes] + head) * HEAD
+        return rows[:, at : at + HEAD].astype(F32)[0:CUT] * factor
 
     for copy in copies[5:]:
         copy.wait()
     buf[6 * CUT : BLOCK, :] = jnp.zeros((BLOCK - 6 * CUT, HEAD), F32)
     for half in range(PARTS // 2):
-        key, value = piece(vk, half, column(fk, half)), piece(vv, half, column(fv, half))
+        key, value = piece("k", half, column(fk, half)), piece("v", half, column(fv, half))
         for dest in (2 * half, 2 * half + 1):
             pieces = (
-                piece(vq, 2 * dest, fq[:, 2 * dest : 2 * dest + 1]),
-                piece(vq, 2 * dest + 1, fq[:, 2 * dest + 1 : 2 * dest + 2]),
+                piece("q", 2 * dest, fq[:, 2 * dest : 2 * dest + 1]),
+                piece("q", 2 * dest + 1, fq[:, 2 * dest + 1 : 2 * dest + 2]),
                 key,
                 value,
-                piece(vo, 2 * dest, fo[:, 2 * dest : 2 * dest + 1]),
-                piece(vo, 2 * dest + 1, fo[:, 2 * dest + 1 : 2 * dest + 2]),
+                piece("o", 2 * dest, fo[:, 2 * dest : 2 * dest + 1]),
+                piece("o", 2 * dest + 1, fo[:, 2 * dest + 1 : 2 * dest + 2]),
             )
             for c, item in enumerate(pieces):
                 buf[CUT * c : CUT * (c + 1), :] = item
@@ -471,27 +474,26 @@
     here = lax.axis_index("replica").astype(jnp.int32).reshape(1)
     seat = lax.axis_index("shard").astype(jnp.int32).reshape(1)
     dma = pltpu.SemaphoreType.DMA
+    codes = [delta_query, key_delta_codes, value_delta_codes, delta_output]
+    codes = jnp.pad(jnp.concatenate(codes, axis=1), ((0, TIDY - CUT), (0, 0)))
     packed, turned = call(
         pack_kernel,
         "pack",
         (shape((PARTS, BLOCK, HEAD), BF16), shape((OWN, TOKENS), BF16)),
-        far_away(9),
+        far_away(6),
         [
             VMEM((TOKENS, OWN), BF16),
-            VMEM((CUT, HQ * HEAD), BF16),
-            VMEM((CUT, KV * HEAD), BF16),
-            VMEM((CUT, KV * HEAD), BF16),
-            VMEM((CUT, HQ * HEAD), BF16),
+            VMEM((TIDY, 80 * HEAD), BF16),
             VMEM((CUT, HQ), jnp.int32),
             VMEM((CUT, HQ), jnp.int32),
             VMEM((KV, CUT), jnp.int32),
             VMEM((KV, CUT), jnp.int32),
             VMEM((BLOCK, HEAD), F32),
-            dma((9,)),
+            dma((6,)),
         ],
         mib=56,
     )(
-        hidden.reshape(TOKENS, OWN), delta_query, key_delta_codes, value_delta_codes, delta_output,
+        hidden.reshape(TOKENS, OWN), codes,
         scale_query, scale_output, key_scale_codes.T, value_scale_codes.T,
     )
     across = along_shard(turned, 1, 0)

time: 124 us -> 125 us (level)
  other arithmetic: 1.34 us -> 3.33 us
    concatenate x0 -> x1, other arithmetic: none -> 1.99 us  [local(): codes = jnp.pad(jnp.concatenate(codes, axis=1), ((0, TIDY - CUT), (0, 0)))]
where the time goes in v9:
time: 125 us; the launch traced here: 124 us
  starting transfers between devices  60.3 us (48%)
  waiting for transfers between devices  36.6 us (29%)
  Pallas kernels  20.5 us (16%)
  other arithmetic  3.33 us (3%)
  local copies, waits for them, and re-layouts  2.86 us (2%)
    ppermute x12, starting transfers between devices, along_shard(): return lax.ppermute(value, 'shard', pairs)  23.7 us
    ppermute x17, starting transfers between devices, fetch(): return lax.ppermute(value, 'replica', pairs)  20.5 us
    ppermute x12, waiting for transfers between devices, along_shard(): return lax.ppermute(value, 'shard', pairs)  16.1 us
    ppermute x17, waiting for transfers between devices, fetch(): return lax.ppermute(value, 'replica', pairs)  12.9 us
    all_to_all x1, starting transfers between devices, local(): lax.all_to_all(packed, 'shard', split_axis=0, concat_axis=0, tiled=False)  11.1 us
    all_to_all x1, waiting for transfers between devices, local(): lax.all_to_all(packed, 'shard', split_axis=0, concat_axis=0, tiled=False)  7.57 us
    all_to_all x1, starting transfers between devices, local(): lax.all_to_all(spread, 'shard', split_axis=0, concat_axis=0, tiled=False,...  5.01 us
    pallas_call x1, Pallas kernels, local(): call(old_kernel, 'old', shape((2, TOKENS, HEAD), F32), scalars() + [whole...  4.12 us
  transfers between devices with their start and end apart: 31, of which 13 were waited for; matrix products, arithmetic and copies ran while one was open for 2% of the time, Pallas kernels for 7%

profile of v9, /device:TPU:32, one launch (start us, length us, event | category | flops | bytes accessed | tf_op | source)
XLA Modules:
  0.0 124.4 jit_solution(9353491917712621586)
XLA Ops:
  0.6 2.0 %fusion.6.codes = bf16[32,10240]{1,0:T(8,128)(2,1)} fusion(bf16[20,4096]{1,0:T(8,128)(2,1)} %param.36, bf16[20,1024]{1,0:T(8,128)(2,1)} %param.34, bf16[20,1024]{1,0:T(8,128)(2,1)} %param.32, bf16[20,4096]{1,0:T(8,128)(2,1)} %param.30), kind=kLoop, calls=%fused_computation.7 | loop fusion | flops 4259840 | bytes 1064960 | tf_op jit(solution)/shard_map/concatenate | solution.py:478
  2.6 2.8 %pack.1 = (bf16[16,128,128]{2,1,0:T(8,128)(2,1)}, bf16[320,128]{1,0:T(8,128)(2,1)}) custom-call(bf16[128,320]{1,0:T(8,128)(2,1)} %bitcast.29, bf16[32,10240]{1,0:T(8,128)(2,1)} %fusion.6.codes, s32[20,32]{1,0:T(8,128)} %sq.1, s32[20,32]{1,0:T(8,128)} %so.1, s32[8,20]{1,0:T(8,128)} %bitcast.30, s32[8,20]{1,0:T(8,128)} %bitcast.31), custom_call_target="tpu_custom_call" | custom-call | tf_op jit(solution)/shard_map/pack/pallas_call | solution.py:479
  5.4 11.1 %all-to-all-start = ((bf16[16,128,128]{2,1,0:T(8,128)(2,1)}), bf16[16,128,128]{2,1,0:T(8,128)(2,1)S(1)}, u32[]{:S(2)}, u32[]{:S(2)}) async-start(bf16[16,128,128]{2,1,0:T(8,128)(2,1)} %get-tuple-element.46), calls=%async_computation | async-start | bytes 1048576 | tf_op jit(solution)/shard_map/all_to_all | solution.py:500
  16.5 3.0 %collective-permute-start = (bf16[320,128]{1,0:T(8,128)(2,1)}, bf16[320,128]{1,0:T(8,128)(2,1)S(1)}, u32[]{:S(2)}, u32[]{:S(2)}) collective-permute-start(bf16[320,128]{1,0:T(8,128)(2,1)} %get-tuple-element.47.turned), channel_id=1, source_target_pairs={{8,0},{9,1},{10,2},{11,3},{12,4},{13,5},{14,6},{15,7},{0,8},{1,9},... | collective-permute-start | bytes 245768 | tf_op jit(solution)/shard_map/ppermute | solution.py:71
  19.5 3.7 %collective-permute-done.across = bf16[320,128]{1,0:T(8,128)(2,1)S(1)} collective-permute-done((bf16[320,128]{1,0:T(8,128)(2,1)}, bf16[320,128]{1,0:T(8,128)(2,1)S(1)}, u32[]{:S(2)}, u32[]{:S(2)}) %collective-permute-start) | collective-permute-done | bytes 81952 | tf_op jit(solution)/shard_map/ppermute | solution.py:71
  25.3 7.6 %all-to-all-done.recv = bf16[16,128,128]{2,1,0:T(8,128)(2,1)S(1)} async-done(((bf16[16,128,128]{2,1,0:T(8,128)(2,1)}), bf16[16,128,128]{2,1,0:T(8,128)(2,1)S(1)}, u32[]{:S(2)}, u32[]{:S(2)}) %all-to-all-start) | async-done | bytes 524320 | tf_op jit(solution)/shard_map/all_to_all | solution.py:500
  32.9 5.0 %all-to-all-start.1 = ((bf16[8,640,128]{2,1,0:T(8,128)(2,1)}), bf16[8,640,128]{2,1,0:T(8,128)(2,1)S(1)}, u32[]{:S(2)}, u32[]{:S(2)}) async-start(bf16[8,640,128]{2,1,0:T(8,128)(2,1)} %spread.1), calls=%async_computation.1 | async-start | bytes 2621440 | tf_op jit(solution)/shard_map/all_to_all | solution.py:531
  38.2 3.0 %refresh.1 = (bf16[256,512]{1,0:T(8,128)(2,1)}, bf16[224,512]{1,0:T(8,128)(2,1)}) custom-call(s32[1]{0:T(128)} %bitcast.here, bf16[16,128,128]{2,1,0:T(8,128)(2,1)} %copy-done.11, bf16[5120,256]{1,0:T(8,128)(2,1)} %base_q.1, bf16[5120,128]{1,0:T(8,128)(2,1)} %base_k.1, bf16[5120,128]{1,0:T(8,128)(2,1)} %bv.1, bf16[5120,256]{1,0:T(8,128)(2,1)} %bo.1), custom_call_target="tpu_custom_call" | custom-call | tf_op jit(solution)/shard_map/refresh/pallas_call | solution.py:513
  46.6 1.8 %collective-permute-start.1 = (bf16[256,512]{1,0:T(8,128)(2,1)}, bf16[256,512]{1,0:T(8,128)(2,1)S(1)}, u32[]{:S(2)}, u32[]{:S(2)}) collective-permute-start(bf16[256,512]{1,0:T(8,128)(2,1)} %get-tuple-element.57.rest_0_), channel_id=1, source_target_pairs={{32,0},{48,16},{64,32},{80,48},{96,64},{112,80},{0,96},{16,112},{1... | collective-permute-start | bytes 786440 | tf_op jit(solution)/shard_map/ppermute | solution.py:47
  51.5 3.4 %collective-permute-done.1.rest_1_ = bf16[256,512]{1,0:T(8,128)(2,1)S(1)} collective-permute-done((bf16[256,512]{1,0:T(8,128)(2,1)}, bf16[256,512]{1,0:T(8,128)(2,1)S(1)}, u32[]{:S(2)}, u32[]{:S(2)}) %collective-permute-start.1) | collective-permute-done | bytes 262176 | tf_op jit(solution)/shard_map/ppermute | solution.py:47
  55.0 2.4 %collective-permute-start.2 = (bf16[256,512]{1,0:T(8,128)(2,1)S(1)}, bf16[256,512]{1,0:T(8,128)(2,1)S(1)}, u32[]{:S(2)}, u32[]{:S(2)}) collective-permute-start(bf16[256,512]{1,0:T(8,128)(2,1)S(1)} %collective-permute-done.1.rest_1_), channel_id=1, source_target_pairs={{32,0},{48,16},{64,32},{80,48},{96,64},{112,80},{0,96},{16,112},{1... | collective-permute-start | bytes 786440 | tf_op jit(solution)/shard_map/ppermute | solution.py:47
  62.6 2.7 %collective-permute-done.12.rest_13_ = bf16[224,512]{1,0:T(8,128)(2,1)} collective-permute-done((bf16[224,512]{1,0:T(8,128)(2,1)}, bf16[224,512]{1,0:T(8,128)(2,1)}, u32[]{:S(2)}, u32[]{:S(2)}) %collective-permute-start.12) | collective-permute-done | bytes 229408 | tf_op jit(solution)/shard_map/ppermute | solution.py:47
  66.5 2.3 %collective-permute-start.13 = (bf16[224,512]{1,0:T(8,128)(2,1)}, bf16[224,512]{1,0:T(8,128)(2,1)}, u32[]{:S(2)}, u32[]{:S(2)}) collective-permute-start(bf16[224,512]{1,0:T(8,128)(2,1)} %collective-permute-done.12.rest_13_), channel_id=1, source_target_pairs={{32,0},{48,16},{64,32},{80,48},{96,64},{112,80},{0,96},{16,112},{1... | collective-permute-start | bytes 688136 | tf_op jit(solution)/shard_map/ppermute | solution.py:47
  77.1 2.3 %collective-permute-done.15.given = bf16[8,128,384]{2,1,0:T(8,128)(2,1)S(1)} collective-permute-done((bf16[8,128,384]{2,1,0:T(8,128)(2,1)S(1)}, bf16[8,128,384]{2,1,0:T(8,128)(2,1)S(1)}, u32[]{:S(2)}, u32[]{:S(2)}) %collective-permute-start.15) | collective-permute-done | bytes 786464 | tf_op jit(solution)/shard_map/ppermute | solution.py:47
  79.4 2.9 %project.1 = (f32[128,512]{1,0:T(8,128)S(1)}, f32[128,512]{1,0:T(8,128)S(1)}, bf16[8,160,512]{2,1,0:T(8,128)(2,1)S(1)}) custom-call(s32[1]{0:T(128)} %bitcast.here, bf16[8,128,384]{2,1,0:T(8,128)(2,1)S(1)} %get-tuple-element.60.keep, bf16[8,128,384]{2,1,0:T(8,128)(2,1)S(1)} %collective-permute-done.15.given, bf16[256,512]{1,0:T(8,128)(2,1)S(1)} %copy-done.4, ...), custom_call_target="tpu_custom_call" | custom-call | tf_op jit(solution)/shard_map/project/pallas_call | solution.py:626
  82.9 4.1 %old.1 = f32[2,128,128]{2,1,0:T(8,128)S(1)} custom-call(s32[1]{0:T(128)} %bitcast.here, bf16[8,128,384]{2,1,0:T(8,128)(2,1)S(1)} %get-tuple-element.60.keep, bf16[8,128,384]{2,1,0:T(8,128)(2,1)S(1)} %get-tuple-element.61.give, f32[264,128]{1,0:T(8,128)S(1)} %concatenate.19.table, s32[40,128]{1,0:T(8,128)S(1)} %add_add_fusion.marks, ...), custom_call_target="tpu_custom_call" | custom-call | tf_op jit(solution)/shard_map/old/pallas_call | solution.py:606
  87.1 3.3 %attend.1 = (bf16[2,336,128]{2,1,0:T(8,128)(2,1)S(1)}, bf16[2,336,128]{2,1,0:T(8,128)(2,1)S(1)}, bf16[2,336,128]{2,1,0:T(8,128)(2,1)S(1)}, bf16[2,336,128]{2,1,0...) custom-call(s32[1]{0:T(128)} %bitcast.here, ...), custom_call_target="tpu_custom_call" | custom-call | tf_op jit(solution)/shard_map/attend/pallas_call | solution.py:644
  90.4 2.6 %collective-permute-start.18 = (bf16[2,336,128]{2,1,0:T(8,128)(2,1)S(1)}, bf16[2,336,128]{2,1,0:T(8,128)(2,1)S(1)}, u32[]{:S(2)}, u32[]{:S(2)}) collective-permute-start(bf16[2,336,128]{2,1,0:T(8,128)(2,1)S(1)} %get-tuple-element.73), channel_id=1, source_target_pairs={{8,0},{9,1},{10,2},{11,3},{12,4},{13,5},{14,6},{15,7},{0,8},{1,9},... | collective-permute-start | bytes 516104 | tf_op jit(solution)/shard_map/ppermute | solution.py:71
  94.0 2.5 %collective-permute-start.20 = (bf16[2,336,128]{2,1,0:T(8,128)(2,1)S(1)}, bf16[2,336,128]{2,1,0:T(8,128)(2,1)S(1)}, u32[]{:S(2)}, u32[]{:S(2)}) collective-permute-start(bf16[2,336,128]{2,1,0:T(8,128)(2,1)S(1)} %get-tuple-element.81), channel_id=1, source_target_pairs={{8,0},{9,1},{10,2},{11,3},{12,4},{13,5},{14,6},{15,7},{0,8},{1,9},... | collective-permute-start | bytes 516104 | tf_op jit(solution)/shard_map/ppermute | solution.py:71
  99.2 4.6 %collective-permute-start.22 = (bf16[336,128]{1,0:T(8,128)(2,1)S(1)}, bf16[336,128]{1,0:T(8,128)(2,1)S(1)}, u32[]{:S(2)}, u32[]{:S(2)}) collective-permute-start(bf16[336,128]{1,0:T(8,128)(2,1)S(1)} %get-tuple-element.74), channel_id=1, source_target_pairs={{5,0},{6,1},{7,2},{0,3},{1,4},{2,5},{3,6},{4,7},{13,8},{14,9},{15,... | collective-permute-start | bytes 258056 | tf_op jit(solution)/shard_map/ppermute | solution.py:71
  104.4 4.6 %collective-permute-start.24 = (bf16[336,128]{1,0:T(8,128)(2,1)S(1)}, bf16[336,128]{1,0:T(8,128)(2,1)S(1)}, u32[]{:S(2)}, u32[]{:S(2)}) collective-permute-start(bf16[336,128]{1,0:T(8,128)(2,1)S(1)} %get-tuple-element.78), channel_id=1, source_target_pairs={{4,0},{5,1},{6,2},{7,3},{0,4},{1,5},{2,6},{3,7},{12,8},{13,9},{14,... | collective-permute-start | bytes 258056 | tf_op jit(solution)/shard_map/ppermute | solution.py:71
  109.4 3.8 %collective-permute-start.26 = (bf16[336,128]{1,0:T(8,128)(2,1)S(1)}, bf16[336,128]{1,0:T(8,128)(2,1)S(1)}, u32[]{:S(2)}, u32[]{:S(2)}) collective-permute-start(bf16[336,128]{1,0:T(8,128)(2,1)S(1)} %get-tuple-element.82), channel_id=1, source_target_pairs={{2,0},{3,1},{4,2},{5,3},{6,4},{7,5},{0,6},{1,7},{10,8},{11,9},{12,... | collective-permute-start | bytes 258056 | tf_op jit(solution)/shard_map/ppermute | solution.py:71
  113.4 5.8 %collective-permute-done.23.r2 = bf16[336,128]{1,0:T(8,128)(2,1)S(1)} collective-permute-done((bf16[336,128]{1,0:T(8,128)(2,1)S(1)}, bf16[336,128]{1,0:T(8,128)(2,1)S(1)}, u32[]{:S(2)}, u32[]{:S(2)}) %collective-permute-start.23) | collective-permute-done | bytes 86048 | tf_op jit(solution)/shard_map/ppermute | solution.py:71
  119.7 4.0 %collective-permute-done.28.r7 = bf16[336,128]{1,0:T(8,128)(2,1)S(1)} collective-permute-done((bf16[336,128]{1,0:T(8,128)(2,1)S(1)}, bf16[336,128]{1,0:T(8,128)(2,1)S(1)}, u32[]{:S(2)}, u32[]{:S(2)}) %collective-permute-start.28) | collective-permute-done | bytes 86048 | tf_op jit(solution)/shard_map/ppermute | solution.py:71
  (104 shorter events, 32.4 us)
Async XLA Ops:
  5.4 27.4 %all-to-all-start = ((bf16[16,128,128]{2,1,0:T(8,128)(2,1)}), bf16[16,128,128]{2,1,0:T(8,128)(2,1)S(1)}, u32[]{:S(2)}, u32[]{:S(2)}) async-start(bf16[16,128,128]{2,1,0:T(8,128)(2,1)} %get-tuple-element.46), calls=%async_computation | async-start | bytes 1048576 | tf_op jit(solution)/shard_map/all_to_all | solution.py:500
  32.9 42.4 %all-to-all-start.1 = ((bf16[8,640,128]{2,1,0:T(8,128)(2,1)}), bf16[8,640,128]{2,1,0:T(8,128)(2,1)S(1)}, u32[]{:S(2)}, u32[]{:S(2)}) async-start(bf16[8,640,128]{2,1,0:T(8,128)(2,1)} %spread.1), calls=%async_computation.1 | async-start | bytes 2621440 | tf_op jit(solution)/shard_map/all_to_all | solution.py:531
  41.2 8.8 %collective-permute-start.11 = (bf16[224,512]{1,0:T(8,128)(2,1)}, bf16[224,512]{1,0:T(8,128)(2,1)}, u32[]{:S(2)}, u32[]{:S(2)}) collective-permute-start(bf16[224,512]{1,0:T(8,128)(2,1)} %get-tuple-element.58.rest_8_), channel_id=1, source_target_pairs={{128,0},{144,16},{160,32},{176,48},{192,64},{208,80},{224,96},{240... | collective-permute-start | bytes 688136 | tf_op jit(solution)/shard_map/ppermute | solution.py:47
  41.9 15.6 %collective-permute-start.9 = (bf16[224,512]{1,0:T(8,128)(2,1)}, bf16[224,512]{1,0:T(8,128)(2,1)}, u32[]{:S(2)}, u32[]{:S(2)}) collective-permute-start(bf16[224,512]{1,0:T(8,128)(2,1)} %get-tuple-element.58.rest_8_), channel_id=1, source_target_pairs={{96,0},{112,16},{0,32},{16,48},{32,64},{48,80},{64,96},{80,112},{2... | collective-permute-start | bytes 688136 | tf_op jit(solution)/shard_map/ppermute | solution.py:47
  43.5 14.9 %collective-permute-start.8 = (bf16[224,512]{1,0:T(8,128)(2,1)}, bf16[224,512]{1,0:T(8,128)(2,1)S(1)}, u32[]{:S(2)}, u32[]{:S(2)}) collective-permute-start(bf16[224,512]{1,0:T(8,128)(2,1)} %get-tuple-element.58.rest_8_), channel_id=1, source_target_pairs={{32,0},{48,16},{64,32},{80,48},{96,64},{112,80},{0,96},{16,112},{1... | collective-permute-start | bytes 688136 | tf_op jit(solution)/shard_map/ppermute | solution.py:47
  45.1 16.0 %collective-permute-start.4 = (bf16[256,512]{1,0:T(8,128)(2,1)}, bf16[256,512]{1,0:T(8,128)(2,1)S(1)}, u32[]{:S(2)}, u32[]{:S(2)}) collective-permute-start(bf16[256,512]{1,0:T(8,128)(2,1)} %get-tuple-element.57.rest_0_), channel_id=1, source_target_pairs={{128,0},{144,16},{160,32},{176,48},{192,64},{208,80},{224,96},{240... | collective-permute-start | bytes 786440 | tf_op jit(solution)/shard_map/ppermute | solution.py:47
  46.6 8.4 %collective-permute-start.1 = (bf16[256,512]{1,0:T(8,128)(2,1)}, bf16[256,512]{1,0:T(8,128)(2,1)S(1)}, u32[]{:S(2)}, u32[]{:S(2)}) collective-permute-start(bf16[256,512]{1,0:T(8,128)(2,1)} %get-tuple-element.57.rest_0_), channel_id=1, source_target_pairs={{32,0},{48,16},{64,32},{80,48},{96,64},{112,80},{0,96},{16,112},{1... | collective-permute-start | bytes 786440 | tf_op jit(solution)/shard_map/ppermute | solution.py:47
  50.0 11.9 %collective-permute-start.3 = (bf16[256,512]{1,0:T(8,128)(2,1)}, bf16[256,512]{1,0:T(8,128)(2,1)S(1)}, u32[]{:S(2)}, u32[]{:S(2)}) collective-permute-start(bf16[256,512]{1,0:T(8,128)(2,1)} %get-tuple-element.57.rest_0_), channel_id=1, source_target_pairs={{96,0},{112,16},{0,32},{16,48},{32,64},{48,80},{64,96},{80,112},{2... | collective-permute-start | bytes 786440 | tf_op jit(solution)/shard_map/ppermute | solution.py:47
  55.0 13.8 %collective-permute-start.2 = (bf16[256,512]{1,0:T(8,128)(2,1)S(1)}, bf16[256,512]{1,0:T(8,128)(2,1)S(1)}, u32[]{:S(2)}, u32[]{:S(2)}) collective-permute-start(bf16[256,512]{1,0:T(8,128)(2,1)S(1)} %collective-permute-done.1.rest_1_), channel_id=1, source_target_pairs={{32,0},{48,16},{64,32},{80,48},{96,64},{112,80},{0,96},{16,112},{1... | collective-permute-start | bytes 786440 | tf_op jit(solution)/shard_map/ppermute | solution.py:47
  57.5 7.9 %collective-permute-start.12 = (bf16[224,512]{1,0:T(8,128)(2,1)}, bf16[224,512]{1,0:T(8,128)(2,1)}, u32[]{:S(2)}, u32[]{:S(2)}) collective-permute-start(bf16[224,512]{1,0:T(8,128)(2,1)} %collective-permute-done.11.rest_12_), channel_id=1, source_target_pairs={{32,0},{48,16},{64,32},{80,48},{96,64},{112,80},{0,96},{16,112},{1... | collective-permute-start | bytes 688136 | tf_op jit(solution)/shard_map/ppermute | solution.py:47
  59.1 7.4 %collective-permute-start.14 = (bf16[224,512]{1,0:T(8,128)(2,1)}, bf16[224,512]{1,0:T(8,128)(2,1)S(1)}, u32[]{:S(2)}, u32[]{:S(2)}) collective-permute-start(bf16[224,512]{1,0:T(8,128)(2,1)} %collective-permute-done.9.rest_11_), channel_id=1, source_target_pairs={{128,0},{144,16},{160,32},{176,48},{192,64},{208,80},{224,96},{240... | collective-permute-start | bytes 688136 | tf_op jit(solution)/shard_map/ppermute | solution.py:47
  61.1 11.0 %collective-permute-start.10 = (bf16[224,512]{1,0:T(8,128)(2,1)}, bf16[224,512]{1,0:T(8,128)(2,1)}, u32[]{:S(2)}, u32[]{:S(2)}) collective-permute-start(bf16[224,512]{1,0:T(8,128)(2,1)} %collective-permute-done.9.rest_11_), channel_id=1, source_target_pairs={{96,0},{112,16},{0,32},{16,48},{32,64},{48,80},{64,96},{80,112},{2... | collective-permute-start | bytes 688136 | tf_op jit(solution)/shard_map/ppermute | solution.py:47
  61.9 11.7 %collective-permute-start.5 = (bf16[256,512]{1,0:T(8,128)(2,1)S(1)}, bf16[256,512]{1,0:T(8,128)(2,1)}, u32[]{:S(2)}, u32[]{:S(2)}) collective-permute-start(bf16[256,512]{1,0:T(8,128)(2,1)S(1)} %collective-permute-done.1.rest_1_), channel_id=1, source_target_pairs={{128,0},{144,16},{160,32},{176,48},{192,64},{208,80},{224,96},{240... | collective-permute-start | bytes 786440 | tf_op jit(solution)/shard_map/ppermute | solution.py:47
  65.3 8.2 %collective-permute-start.7 = (bf16[256,512]{1,0:T(8,128)(2,1)S(1)}, bf16[256,512]{1,0:T(8,128)(2,1)}, u32[]{:S(2)}, u32[]{:S(2)}) collective-permute-start(bf16[256,512]{1,0:T(8,128)(2,1)S(1)} %collective-permute-done.4.rest_4_), channel_id=1, source_target_pairs={{96,0},{112,16},{0,32},{16,48},{32,64},{48,80},{64,96},{80,112},{2... | collective-permute-start | bytes 786440 | tf_op jit(solution)/shard_map/ppermute | solution.py:47
  66.5 7.1 %collective-permute-start.13 = (bf16[224,512]{1,0:T(8,128)(2,1)}, bf16[224,512]{1,0:T(8,128)(2,1)}, u32[]{:S(2)}, u32[]{:S(2)}) collective-permute-start(bf16[224,512]{1,0:T(8,128)(2,1)} %collective-permute-done.12.rest_13_), channel_id=1, source_target_pairs={{32,0},{48,16},{64,32},{80,48},{96,64},{112,80},{0,96},{16,112},{1... | collective-permute-start | bytes 688136 | tf_op jit(solution)/shard_map/ppermute | solution.py:47
  90.4 8.8 %collective-permute-start.18 = (bf16[2,336,128]{2,1,0:T(8,128)(2,1)S(1)}, bf16[2,336,128]{2,1,0:T(8,128)(2,1)S(1)}, u32[]{:S(2)}, u32[]{:S(2)}) collective-permute-start(bf16[2,336,128]{2,1,0:T(8,128)(2,1)S(1)} %get-tuple-element.73), channel_id=1, source_target_pairs={{8,0},{9,1},{10,2},{11,3},{12,4},{13,5},{14,6},{15,7},{0,8},{1,9},... | collective-permute-start | bytes 516104 | tf_op jit(solution)/shard_map/ppermute | solution.py:71
  93.0 11.4 %collective-permute-start.19 = (bf16[2,336,128]{2,1,0:T(8,128)(2,1)S(1)}, bf16[2,336,128]{2,1,0:T(8,128)(2,1)S(1)}, u32[]{:S(2)}, u32[]{:S(2)}) collective-permute-start(bf16[2,336,128]{2,1,0:T(8,128)(2,1)S(1)} %get-tuple-element.77), channel_id=1, source_target_pairs={{8,0},{9,1},{10,2},{11,3},{12,4},{13,5},{14,6},{15,7},{0,8},{1,9},... | collective-permute-start | bytes 516104 | tf_op jit(solution)/shard_map/ppermute | solution.py:71
  94.0 15.0 %collective-permute-start.20 = (bf16[2,336,128]{2,1,0:T(8,128)(2,1)S(1)}, bf16[2,336,128]{2,1,0:T(8,128)(2,1)S(1)}, u32[]{:S(2)}, u32[]{:S(2)}) collective-permute-start(bf16[2,336,128]{2,1,0:T(8,128)(2,1)S(1)} %get-tuple-element.81), channel_id=1, source_target_pairs={{8,0},{9,1},{10,2},{11,3},{12,4},{13,5},{14,6},{15,7},{0,8},{1,9},... | collective-permute-start | bytes 516104 | tf_op jit(solution)/shard_map/ppermute | solution.py:71
  96.5 12.9 %collective-permute-start.21 = (bf16[2,336,128]{2,1,0:T(8,128)(2,1)S(1)}, bf16[2,336,128]{2,1,0:T(8,128)(2,1)S(1)}, u32[]{:S(2)}, u32[]{:S(2)}) collective-permute-start(bf16[2,336,128]{2,1,0:T(8,128)(2,1)S(1)} %get-tuple-element.85), channel_id=1, source_target_pairs={{8,0},{9,1},{10,2},{11,3},{12,4},{13,5},{14,6},{15,7},{0,8},{1,9},... | collective-permute-start | bytes 516104 | tf_op jit(solution)/shard_map/ppermute | solution.py:71
  99.2 14.1 %collective-permute-start.22 = (bf16[336,128]{1,0:T(8,128)(2,1)S(1)}, bf16[336,128]{1,0:T(8,128)(2,1)S(1)}, u32[]{:S(2)}, u32[]{:S(2)}) collective-permute-start(bf16[336,128]{1,0:T(8,128)(2,1)S(1)} %get-tuple-element.74), channel_id=1, source_target_pairs={{5,0},{6,1},{7,2},{0,3},{1,4},{2,5},{3,6},{4,7},{13,8},{14,9},{15,... | collective-permute-start | bytes 258056 | tf_op jit(solution)/shard_map/ppermute | solution.py:71
  103.8 15.4 %collective-permute-start.23 = (bf16[336,128]{1,0:T(8,128)(2,1)S(1)}, bf16[336,128]{1,0:T(8,128)(2,1)S(1)}, u32[]{:S(2)}, u32[]{:S(2)}) collective-permute-start(bf16[336,128]{1,0:T(8,128)(2,1)S(1)} %get-tuple-element.75), channel_id=1, source_target_pairs={{3,0},{4,1},{5,2},{6,3},{7,4},{0,5},{1,6},{2,7},{11,8},{12,9},{13,... | collective-permute-start | bytes 258056 | tf_op jit(solution)/shard_map/ppermute | solution.py:71
  104.4 14.8 %collective-permute-start.24 = (bf16[336,128]{1,0:T(8,128)(2,1)S(1)}, bf16[336,128]{1,0:T(8,128)(2,1)S(1)}, u32[]{:S(2)}, u32[]{:S(2)}) collective-permute-start(bf16[336,128]{1,0:T(8,128)(2,1)S(1)} %get-tuple-element.78), channel_id=1, source_target_pairs={{4,0},{5,1},{6,2},{7,3},{0,4},{1,5},{2,6},{3,7},{12,8},{13,9},{14,... | collective-permute-start | bytes 258056 | tf_op jit(solution)/shard_map/ppermute | solution.py:71
  109.0 10.2 %collective-permute-start.25 = (bf16[336,128]{1,0:T(8,128)(2,1)S(1)}, bf16[336,128]{1,0:T(8,128)(2,1)S(1)}, u32[]{:S(2)}, u32[]{:S(2)}) collective-permute-start(bf16[336,128]{1,0:T(8,128)(2,1)S(1)} %get-tuple-element.79), channel_id=1, source_target_pairs={{6,0},{7,1},{0,2},{1,3},{2,4},{3,5},{4,6},{5,7},{14,8},{15,9},{8,1... | collective-permute-start | bytes 258056 | tf_op jit(solution)/shard_map/ppermute | solution.py:71
  109.4 10.2 %collective-permute-start.26 = (bf16[336,128]{1,0:T(8,128)(2,1)S(1)}, bf16[336,128]{1,0:T(8,128)(2,1)S(1)}, u32[]{:S(2)}, u32[]{:S(2)}) collective-permute-start(bf16[336,128]{1,0:T(8,128)(2,1)S(1)} %get-tuple-element.82), channel_id=1, source_target_pairs={{2,0},{3,1},{4,2},{5,3},{6,4},{7,5},{0,6},{1,7},{10,8},{11,9},{12,... | collective-permute-start | bytes 258056 | tf_op jit(solution)/shard_map/ppermute | solution.py:71
  (26 other events, 241.4 us)
